TPU v7x, 32 devices: a whole 2x2x4 slice. The times are simulated.
32 devices in a mesh: row: 16 (over z, x, core), col: 2 (over y).
Axes of the slice: x: 2, y: 2, z: 4, core: 2. Of those that a mesh axis runs over, the one named last changes fastest.
Arguments:
- x0_rows: bfloat16 [4096, 32768], P('row', 'col'), may hold values from -0.1875 to 0.1875
- x1_rows: bfloat16 [4096, 32768], P('row', 'col'), may hold values from -0.1875 to 0.1875
- x0_cols: bfloat16 [32768, 1536], P('row', 'col'), may hold values from -6 to 6
- x1_cols: bfloat16 [32768, 1536], P('row', 'col'), may hold values from -6 to 6
- mask0_rows: int32 [32, 256], P('row', 'col'), may hold values 0 or 1
- mask1_rows: int32 [32, 256], P('row', 'col'), may hold values 0 or 1
- mask0_cols: int32 [256, 12], P('row', 'col'), may hold values 0 or 1
- mask1_cols: int32 [256, 12], P('row', 'col'), may hold values 0 or 1
- keep_mask: int32 [32, 12], P('row', 'col'), may hold values 0 or 1
Outputs:
- x_square: bfloat16 [4096, 1536], P('row', 'col')
- x_tangent: bfloat16 [4096, 1536], P('row', 'col')
All inputs are finite; a program needn't handle non-finite values. No bound on the sum of `mask0_rows` or of `mask1_rows` or of `mask0_cols` or of `mask1_cols` or of `keep_mask` on one device may be relied on, other than what follows from the above.
Results may differ from a plain program's by a relative error of at most 0.001.
Values may be sent and summed in bfloat16 or wider, within the bound.
No kernel may reach another device: no remote copies, remote signals or barrier semaphores. Data moves between devices by JAX's collectives and lax.ppermute only.
A program may use at most 128 MiB of HBM per device.

v0:
```python
import jax
import jax.numpy as jnp
from jax import lax
from jax.sharding import PartitionSpec as P

BLOCK = 128


def passed_along(shard, axis, by):
    devices = lax.axis_size(axis)
    return lax.ppermute(shard, axis, [(i, (i + by) % devices) for i in range(devices)])


def masked(values, mask):
    rows_b, cols_b = mask.shape
    tiles = values.reshape(rows_b, BLOCK, cols_b, BLOCK)
    return (tiles * mask.astype(values.dtype)[:, None, :, None]).reshape(values.shape)


def per_device(
    x0_rows, x1_rows, x0_cols, x1_cols, mask0_rows, mask1_rows, mask0_cols, mask1_cols, keep_mask
):
    n_row = lax.axis_size("row")
    n_col = lax.axis_size("col")
    group = n_row // n_col
    row_index = lax.axis_index("row")
    col_index = lax.axis_index("col")
    panel = x0_cols.shape[0]
    start = row_index % group * panel
    block_start = row_index % group * (panel // BLOCK)
    left_zero = masked(
        lax.dynamic_slice_in_dim(x0_rows, start, panel, 1),
        lax.dynamic_slice_in_dim(mask0_rows, block_start, panel // BLOCK, 1),
    )
    left_one = masked(
        lax.dynamic_slice_in_dim(x1_rows, start, panel, 1),
        lax.dynamic_slice_in_dim(mask1_rows, block_start, panel // BLOCK, 1),
    )
    right_zero = masked(x0_cols, mask0_cols)
    right_one = masked(x1_cols, mask1_cols)
    left = jnp.stack([left_zero, left_one])
    right = jnp.stack([right_zero, right_one])
    left_offset = row_index // group % n_col
    right_offset = col_index % n_col
    levels = n_col.bit_length() - 1
    for level in range(levels):
        moved_left = passed_along(left, "col", -(1 << level))
        moved_right = passed_along(right, "row", -group * (1 << level))
        left = jnp.where(left_offset // (1 << level) % 2 == 1, moved_left, left)
        right = jnp.where(right_offset // (1 << level) % 2 == 1, moved_right, right)

    def accumulate(left_now, right_now, square, tangent):
        square = square + jnp.dot(left_now[0], right_now[0], preferred_element_type=jnp.float32)
        tangent = tangent + jnp.dot(left_now[0], right_now[1], preferred_element_type=jnp.float32)
        tangent = tangent + jnp.dot(left_now[1], right_now[0], preferred_element_type=jnp.float32)
        return (square, tangent)

    def section_body(section, carry):
        left_now, right_now, square, tangent = carry
        square, tangent = accumulate(left_now, right_now, square, tangent)
        left_now = passed_along(left_now, "col", -1)
        right_now = passed_along(right_now, "row", -group)
        return (left_now, right_now, square, tangent)

    zeros = jnp.zeros((left_zero.shape[0], right_zero.shape[1]), jnp.float32)
    left, right, square, tangent = lax.fori_loop(
        0, n_col - 1, section_body, (left, right, zeros, zeros)
    )
    square, tangent = accumulate(left, right, square, tangent)
    x_square = masked(square, keep_mask).astype(jnp.bfloat16)
    x_tangent = masked(tangent, keep_mask).astype(jnp.bfloat16)
    return (x_square, x_tangent)


def solution(mesh):
    return jax.shard_map(
        per_device,
        mesh=mesh,
        in_specs=(
            P("row", "col"),
            P("row", "col"),
            P("row", "col"),
            P("row", "col"),
            P("row", "col"),
            P("row", "col"),
            P("row", "col"),
            P("row", "col"),
            P("row", "col"),
        ),
        out_specs=(P("row", "col"), P("row", "col")),
        check_vma=False,
    )
```

profile of v0, /device:TPU:0, one launch (start us, length us, event | category | flops | bytes accessed | tf_op | source)
XLA Modules:
  0.0 586.8 jit_solution(3515783852090111300)
XLA Ops:
  0.7 4.8 copy.14
  5.5 3.0 copy.13
  9.5 0.9 copy-done.1
  10.4 1.0 copy-done.2
  11.4 1.5 fusion
  12.8 3.5 pad_maximum_fusion
  16.4 4.0 collective-permute-start.1
  20.5 270.6 %collective-permute-done.1 = bf16[2,2048,768]{1,2,0:T(8,128)(2,1)} collective-permute-done((bf16[2,2048,768]{1,2,0:T(8,128)(2,1)}, bf16[2,2048,768]{1,2,0:T(8,128)(2,1)}, u32[]{:S(2)}, u32[]{:S(2)}) %collective-permute-start.1) | collective-permute-done | bytes 6291488 | tf_op jit(solution)/shard_map/ppermute | solution.py:11
  291.1 5.2 broadcast_select_fusion
  296.6 1.7 fusion.16
  298.6 1.7 fusion.17
  300.3 1.5 pad_maximum_fusion.1
  301.8 3.7 collective-permute-start
  305.5 45.1 %collective-permute-done = bf16[2,256,2048]{2,1,0:T(8,128)(2,1)} collective-permute-done((bf16[2,256,2048]{2,1,0:T(8,128)(2,1)}, bf16[2,256,2048]{2,1,0:T(8,128)(2,1)}, u32[]{:S(2)}, u32[]{:S(2)}) %collective-permute-start) | collective-permute-done | bytes 2097184 | tf_op jit(solution)/shard_map/ppermute | solution.py:11
  350.6 1.6 broadcast_select_fusion.1
  352.2 1.7 collective-permute-start.2
  354.7 3.2 fusion.4
  357.9 40.5 %collective-permute-done.2 = bf16[2,256,2048]{2,1,0:T(8,128)(2,1)} collective-permute-done((bf16[2,256,2048]{2,1,0:T(8,128)(2,1)}, bf16[2,256,2048]{2,1,0:T(8,128)(2,1)}, u32[]{:S(2)}, u32[]{:S(2)}) %collective-permute-start.2) | collective-permute-done | bytes 2097184 | tf_op jit(solution)/shard_map/while/body/eval_jaxpr/ppermute | solution.py:11
  398.4 170.7 %collective-permute-done.3 = bf16[2,2048,768]{1,2,0:T(8,128)(2,1)} collective-permute-done((bf16[2,2048,768]{1,2,0:T(8,128)(2,1)}, bf16[2,2048,768]{1,2,0:T(8,128)(2,1)}, u32[]{:S(2)}, u32[]{:S(2)}) %collective-permute-start.3) | collective-permute-done | bytes 6291488 | tf_op jit(solution)/shard_map/while/body/eval_jaxpr/ppermute | solution.py:11
  569.0 3.2 fusion.7
  572.3 4.0 fusion.15
  576.3 3.2 fusion.6
  579.5 3.2 fusion.2
  582.8 4.0 fusion.14
  (29 shorter events, 2.2 us)
Async XLA Ops:
  0.6 4.9 copy-start.4
  0.6 4.9 copy-start.3
  5.5 3.0 copy-start.5
  8.5 1.9 copy-start.1
  8.5 2.8 copy-start.2
  12.8 3.6 copy-start
  16.4 274.7 %collective-permute-start.1 = (bf16[2,2048,768]{1,2,0:T(8,128)(2,1)}, bf16[2,2048,768]{1,2,0:T(8,128)(2,1)}, u32[]{:S(2)}, u32[]{:S(2)}) collective-permute-start(bf16[2,2048,768]{1,2,0:T(8,128)(2,1)} %pad_maximum_fusion), channel_id=1, source_target_pairs={{0,16},{2,18},{4,20},{6,22},{8,24},{10,26},{12,28},{14,30},{16,0},... | collective-permute-start | bytes 18874376 | tf_op jit(solution)/shard_map/ppermute | solution.py:11
  20.5 275.9 %copy-start.6 = (s32[2,128]{1,0:T(2,128)S(1)}, s32[2,128]{1,0:T(2,128)}, u32[]{:S(2)}) copy-start(s32[2,128]{1,0:T(2,128)} %param.14) | copy-start | bytes 3076
  20.5 275.9 %copy-start.7 = (s32[2,128]{1,0:T(2,128)S(1)}, s32[2,128]{1,0:T(2,128)}, u32[]{:S(2)}) copy-start(s32[2,128]{1,0:T(2,128)} %param.13) | copy-start | bytes 3076
  296.3 272.7 %collective-permute-start.3 = (bf16[2,2048,768]{1,2,0:T(8,128)(2,1)}, bf16[2,2048,768]{1,2,0:T(8,128)(2,1)}, u32[]{:S(2)}, u32[]{:S(2)}) collective-permute-start(bf16[2,2048,768]{1,2,0:T(8,128)(2,1)} %broadcast_select_fusion), channel_id=1, source_target_pairs={{0,16},{2,18},{4,20},{6,22},{8,24},{10,26},{12,28},{14,30},{16,0},... | collective-permute-start | bytes 18874376 | tf_op jit(solution)/shard_map/while/body/eval_jaxpr/ppermute | solution.py:11
  301.8 48.8 %collective-permute-start = (bf16[2,256,2048]{2,1,0:T(8,128)(2,1)}, bf16[2,256,2048]{2,1,0:T(8,128)(2,1)}, u32[]{:S(2)}, u32[]{:S(2)}) collective-permute-start(bf16[2,256,2048]{2,1,0:T(8,128)(2,1)} %pad_maximum_fusion.1), channel_id=1, source_target_pairs={{0,1},{1,0},{2,3},{3,2},{4,5},{5,4},{6,7},{7,6},{8,9},{9,8},{10,11... | collective-permute-start | bytes 6291464 | tf_op jit(solution)/shard_map/ppermute | solution.py:11
  305.5 48.4 %copy-start.8 = (s32[2,6]{1,0:T(2,128)S(1)}, s32[2,6]{1,0:T(2,128)}, u32[]{:S(2)}) copy-start(s32[2,6]{1,0:T(2,128)} %param.17) | copy-start | bytes 148
  352.2 46.2 %collective-permute-start.2 = (bf16[2,256,2048]{2,1,0:T(8,128)(2,1)}, bf16[2,256,2048]{2,1,0:T(8,128)(2,1)}, u32[]{:S(2)}, u32[]{:S(2)}) collective-permute-start(bf16[2,256,2048]{2,1,0:T(8,128)(2,1)} %broadcast_select_fusion.1), channel_id=1, source_target_pairs={{0,1},{1,0},{2,3},{3,2},{4,5},{5,4},{6,7},{7,6},{8,9},{9,8},{10,11... | collective-permute-start | bytes 6291464 | tf_op jit(solution)/shard_map/while/body/eval_jaxpr/ppermute | solution.py:11
where the time goes:
time: 588 us; the launch traced here: 587 us
  waiting for transfers between devices  527 us (90%)
  matrix products  21 us (4%)
  other arithmetic  16.8 us (3%)
  local copies, waits for them, and re-layouts  11.9 us (2%)
  starting transfers between devices  9.48 us (2%)
    ppermute x4, waiting for transfers between devices, passed_along(): lax.ppermute(shard, axis, [(i, (i + by) % devices) for i in range(devices)])  527 us
  transfers between devices with their start and end apart: 4, of which 4 were waited for; matrix products, arithmetic and copies ran while one was open for 2% of the time, Pallas kernels for 0%

commit v1 on v0

--- a/solution.py
+++ b/solution.py
@@ -1,9 +1,323 @@
+import functools
+import math
+
 import jax
 import jax.numpy as jnp
 from jax import lax
+from jax.experimental import pallas as pl
+from jax.experimental.pallas import tpu as pltpu
 from jax.sharding import PartitionSpec as P
 
 BLOCK = 128
+LEVELS = 32000.0
+STEPS = 32.0
+LN2 = math.log(2.0)
+VMEM_BYTES = 48 * 1024 * 1024
+
+VM = functools.partial(pl.BlockSpec, memory_space=pltpu.VMEM)
+SM = functools.partial(pl.BlockSpec, memory_space=pltpu.SMEM)
+HB = functools.partial(pl.BlockSpec, memory_space=pl.ANY)
+
+
+def params():
+    return pltpu.CompilerParams(vmem_limit_bytes=VMEM_BYTES)
+
+
+def cost(flops, moved):
+    return pl.CostEstimate(flops=int(flops), bytes_accessed=int(moved), transcendentals=0)
+
+
+def scaled(values, entry):
+    return (values.astype(jnp.float32) * entry.astype(jnp.float32)).astype(values.dtype)
+
+
+def chunk_kernel(row_block, blocks, place, mask0, mask1, x0, x1, a_out, b_out):
+    first = place[0] * blocks
+    for j in range(blocks):
+        cut = slice(j * BLOCK, (j + 1) * BLOCK)
+        a_out[:, cut] = scaled(x0[:, cut], mask0[row_block, first + j])
+        b_out[:, cut] = scaled(x1[:, cut], mask1[row_block, first + j])
+
+
+def masked_chunk(place, mask0, mask1, x0, x1, step, rows, panel):
+    blocks = panel // BLOCK
+    out = jax.ShapeDtypeStruct((rows, panel), x0.dtype)
+    return pl.pallas_call(
+        functools.partial(chunk_kernel, step * rows // BLOCK, blocks),
+        grid_spec=pltpu.PrefetchScalarGridSpec(
+            num_scalar_prefetch=1,
+            grid=(1,),
+            in_specs=[
+                SM(),
+                SM(),
+                pl.BlockSpec((rows, panel), lambda g, place: (step, place[0])),
+                pl.BlockSpec((rows, panel), lambda g, place: (step, place[0])),
+            ],
+            out_specs=[
+                pl.BlockSpec((rows, panel), lambda g, place: (0, 0)),
+                pl.BlockSpec((rows, panel), lambda g, place: (0, 0)),
+            ],
+        ),
+        out_shape=[out, out],
+        compiler_params=params(),
+        cost_estimate=cost(0, 8 * rows * panel),
+        name="left_chunk",
+    )(place, mask0, mask1, x0, x1)
+
+
+def slab_kernel(blocks, place, mask0, mask1, x0, x1, out):
+    first = place[0] * blocks
+    row_block = pl.program_id(0)
+    for j in range(blocks):
+        cut = slice(j * BLOCK, (j + 1) * BLOCK)
+        out[0, :, cut] = scaled(x0[:, cut], mask0[row_block, first + j])
+        out[1, :, cut] = scaled(x1[:, cut], mask1[row_block, first + j])
+
+
+def masked_slab(place, mask0, mask1, x0, x1, panel):
+    rows = x0.shape[0]
+    return pl.pallas_call(
+        functools.partial(slab_kernel, panel // BLOCK),
+        grid_spec=pltpu.PrefetchScalarGridSpec(
+            num_scalar_prefetch=1,
+            grid=(rows // BLOCK,),
+            in_specs=[
+                SM(),
+                SM(),
+                pl.BlockSpec((BLOCK, panel), lambda g, place: (g, place[0])),
+                pl.BlockSpec((BLOCK, panel), lambda g, place: (g, place[0])),
+            ],
+            out_specs=pl.BlockSpec((2, BLOCK, panel), lambda g, place: (0, g, 0)),
+        ),
+        out_shape=jax.ShapeDtypeStruct((2, rows, panel), x0.dtype),
+        compiler_params=params(),
+        cost_estimate=cost(0, 8 * rows * panel),
+        name="left_slab",
+    )(place, mask0, mask1, x0, x1)
+
+
+def right_kernel(mask0, mask1, x0, x1, out0, out1):
+    step = pl.program_id(0)
+    many = x0.shape[0] // BLOCK
+    for i in range(many):
+        for j in range(x0.shape[1] // BLOCK):
+            at = (slice(i * BLOCK, (i + 1) * BLOCK), slice(j * BLOCK, (j + 1) * BLOCK))
+            out0[at] = scaled(x0[at], mask0[step * many + i, j])
+            out1[at] = scaled(x1[at], mask1[step * many + i, j])
+
+
+def masked_right(mask0, mask1, x0, x1):
+    depth, columns = x0.shape
+    tall = 2 * BLOCK
+    out = jax.ShapeDtypeStruct(x0.shape, x0.dtype)
+    tile = pl.BlockSpec((tall, columns), lambda g: (g, 0))
+    return pl.pallas_call(
+        right_kernel,
+        grid=(depth // tall,),
+        in_specs=[SM(), SM(), tile, tile],
+        out_specs=[tile, tile],
+        out_shape=[out, out],
+        compiler_params=params(),
+        cost_estimate=cost(0, 8 * depth * columns),
+        name="right_panels",
+    )(mask0, mask1, x0, x1)
+
+
+def both_products(held, right0, right1):
+    rows = held.shape[0] // 2
+    first = jnp.dot(held[...], right0[...], preferred_element_type=jnp.float32)
+    second = jnp.dot(held[:rows], right1[...], preferred_element_type=jnp.float32)
+    return first[:rows], first[rows:] + second
+
+
+def local_kernel(diag, own, got, right0, right1, square, tangent, held):
+    rows = own.shape[1]
+
+    @pl.when((pl.program_id(0) == 0) & (diag[0] == 1))
+    def _():
+        held[:rows] = own[0]
+        held[rows:] = own[1]
+
+    @pl.when((pl.program_id(0) == 0) & (diag[0] == 0))
+    def _():
+        held[:rows] = got[0]
+        held[rows:] = got[1]
+
+    square[...], tangent[...] = both_products(held, right0, right1)
+
+
+def local_products(diag, own, got, right0, right1, wide):
+    rows, depth = own.shape[1:]
+    columns = right0.shape[1]
+    out = jax.ShapeDtypeStruct((rows, columns), jnp.float32)
+    whole = pl.BlockSpec((2, rows, depth), lambda g: (0, 0, 0))
+    return pl.pallas_call(
+        local_kernel,
+        grid=(columns // wide,),
+        in_specs=[
+            SM(),
+            whole,
+            whole,
+            pl.BlockSpec((depth, wide), lambda g: (0, g)),
+            pl.BlockSpec((depth, wide), lambda g: (0, g)),
+        ],
+        out_specs=[
+            pl.BlockSpec((rows, wide), lambda g: (0, g)),
+            pl.BlockSpec((rows, wide), lambda g: (0, g)),
+        ],
+        out_shape=[out, out],
+        scratch_shapes=[pltpu.VMEM((2 * rows, depth), own.dtype)],
+        compiler_params=params(),
+        cost_estimate=cost(6 * rows * depth * columns, 8 * rows * depth + 4 * depth * columns),
+        name="own_products",
+    )(diag, own, got, right0, right1)
+
+
+def partial_kernel(diag, near, far, right0, right1, out, held, steps):
+    rows, wide = near.shape[0], right0.shape[1]
+    step = pl.program_id(0)
+    tiles = wide // BLOCK
+    across = pl.num_programs(0) * tiles
+
+    @pl.when((step == 0) & (diag[0] == 1))
+    def _():
+        held[:rows] = near[...]
+        held[rows:] = far[...]
+
+    @pl.when((step == 0) & (diag[0] == 0))
+    def _():
+        held[:rows] = far[...]
+        held[rows:] = near[...]
+
+    for which, values in enumerate(both_products(held, right0, right1)):
+        top = jnp.maximum(jnp.max(jnp.abs(values), axis=0, keepdims=True), 1e-30)
+        level = jnp.ceil(jnp.log(top) * (STEPS / LN2)) + 1.0
+        coded = jnp.round(values * (LEVELS * jnp.exp(level * (-LN2 / STEPS))))
+        coded = jnp.clip(coded, -32767.0, 32767.0).astype(jnp.int32).astype(jnp.int16)
+        for t in range(tiles):
+            at = which * across + step * tiles + t
+            cut = slice(t * BLOCK, (t + 1) * BLOCK)
+            out[pl.ds(pl.multiple_of(at * rows, rows), rows), :] = coded[:, cut]
+            steps[pl.ds(at, 1), :] = level[:, cut]
+
+    @pl.when(step == pl.num_programs(0) - 1)
+    def _():
+        tail = steps.shape[0]
+        out[out.shape[0] - tail :, :] = steps[...].astype(jnp.int32).astype(jnp.int16)
+
+
+def partial_products(diag, near, far, right0, right1, wide):
+    rows, depth = near.shape
+    columns = right0.shape[1]
+    tiles = 2 * columns // BLOCK
+    tail = -(-tiles // 16) * 16
+    whole = pl.BlockSpec((rows, depth), lambda g: (0, 0))
+    return pl.pallas_call(
+        partial_kernel,
+        grid=(columns // wide,),
+        in_specs=[
+            SM(),
+            whole,
+            whole,
+            pl.BlockSpec((depth, wide), lambda g: (0, g)),
+            pl.BlockSpec((depth, wide), lambda g: (0, g)),
+        ],
+        out_specs=pl.BlockSpec((tiles * rows + tail, BLOCK), lambda g: (0, 0)),
+        out_shape=jax.ShapeDtypeStruct((tiles * rows + tail, BLOCK), jnp.int16),
+        scratch_shapes=[
+            pltpu.VMEM((2 * rows, depth), near.dtype),
+            pltpu.VMEM((tail, BLOCK), jnp.float32),
+        ],
+        compiler_params=params(),
+        cost_estimate=cost(6 * rows * depth * columns, 4 * rows * depth + 4 * depth * columns),
+        name="partial_products",
+    )(diag, near, far, right0, right1)
+
+
+def finish_kernel(row_block, keep, square, tangent, coded, *rest):
+    outs = rest[-2:]
+    rows, columns = square.shape
+    across = columns // BLOCK
+    tail = coded.shape[0] - 2 * across * rows
+    levels = coded[coded.shape[0] - tail :, :].astype(jnp.int32).astype(jnp.float32)
+    steps = jnp.exp(levels * (LN2 / STEPS)) * (1.0 / LEVELS)
+    for which, (mine, out) in enumerate(zip((square, tangent), outs)):
+        for j in range(across):
+            at = which * across + j
+            cut = slice(j * BLOCK, (j + 1) * BLOCK)
+            other = coded[at * rows : (at + 1) * rows, :].astype(jnp.int32).astype(jnp.float32)
+            total = mine[:, cut] + other * steps[at : at + 1, :]
+            out[:, cut] = (total * keep[row_block, j].astype(jnp.float32)).astype(out.dtype)
+
+
+def finished(keep, square, tangent, coded, before, step, rows):
+    all_rows, columns = square.shape
+    tile = pl.BlockSpec((rows, columns), lambda g: (step, 0))
+    out = jax.ShapeDtypeStruct((all_rows, columns), jnp.bfloat16)
+    handed = [] if before is None else list(before)
+    return pl.pallas_call(
+        functools.partial(finish_kernel, step * rows // BLOCK),
+        grid=(1,),
+        in_specs=[SM(), tile, tile, pl.BlockSpec(coded.shape, lambda g: (0, 0))]
+        + [HB() for _ in handed],
+        out_specs=[tile, tile],
+        out_shape=[out, out],
+        input_output_aliases={4: 0, 5: 1} if handed else {},
+        compiler_params=params(),
+        cost_estimate=cost(0, 16 * rows * columns),
+        name="finish",
+    )(keep, square, tangent, coded, *handed)
+
+
+def per_device_pair(
+    n_row, x0_rows, x1_rows, x0_cols, x1_cols, mask0_rows, mask1_rows, mask0_cols, mask1_cols, keep
+):
+    n_col = 2
+    group = n_row // n_col
+    panel = x0_cols.shape[0]
+    all_rows = x0_rows.shape[0]
+    row_index = lax.axis_index("row")
+    half = row_index // group
+    is_diag = half == lax.axis_index("col")
+    diag = is_diag.astype(jnp.int32).reshape(1)
+    place = (row_index % group).astype(jnp.int32).reshape(1)
+    rows = 64
+    chunks = all_rows // rows
+    wide = 256
+
+    def device(h, q, c):
+        return (h * group + q) * n_col + c
+
+    spots = [(h, q, c) for h in range(2) for q in range(group) for c in range(2)]
+    over_y = [(device(h, q, c), device(h, q, 1 - c)) for h, q, c in spots]
+    over_z = [(device(h, q, c), device(1 - h, q, c)) for h, q, c in spots]
+    to_diag = [(device(h, q, c), device(h, q, 1 - c)) for h, q, c in spots if h != c]
+    from_diag = [(device(h, q, c), device(h, q, 1 - c)) for h, q, c in spots if h == c]
+
+    def move(values, pairs):
+        return lax.ppermute(values, ("row", "col"), pairs)
+
+    parts = [
+        masked_chunk(place, mask0_rows, mask1_rows, x0_rows, x1_rows, i, rows, panel)
+        for i in range(chunks)
+    ]
+    passed = [move(b, to_diag) for _, b in parts]
+    own = masked_slab(place, mask0_rows, mask1_rows, x0_rows, x1_rows, panel)
+    got = move(own, from_diag)
+    right0, right1 = masked_right(mask0_cols, mask1_cols, x0_cols, x1_cols)
+    near = [
+        move(jnp.where(is_diag, r, a), over_z) for r, (a, _) in zip(passed, parts)
+    ]
+    far = [move(r, over_y) for r in near]
+    coded = [
+        partial_products(diag, n, f, right0, right1, wide) for n, f in zip(near, far)
+    ]
+    back = [move(p, over_z) for p in coded]
+    square, tangent = local_products(diag, own, got, right0, right1, wide)
+    outs = None
+    for i in range(chunks):
+        outs = finished(keep, square, tangent, back[i], outs, i, rows)
+    return tuple(outs)
 
 
 def passed_along(shard, axis, by):
@@ -73,20 +387,14 @@
 
 
 def solution(mesh):
+    if mesh.shape["col"] == 2:
+        body = functools.partial(per_device_pair, mesh.shape["row"])
+    else:
+        body = per_device
     return jax.shard_map(
-        per_device,
+        body,
         mesh=mesh,
-        in_specs=(
-            P("row", "col"),
-            P("row", "col"),
-            P("row", "col"),
-            P("row", "col"),
-            P("row", "col"),
-            P("row", "col"),
-            P("row", "col"),
-            P("row", "col"),
-            P("row", "col"),
-        ),
+        in_specs=(P("row", "col"),) * 9,
         out_specs=(P("row", "col"), P("row", "col")),
         check_vma=False,
     )

time: 588 us -> 131 us (0.22)
  waiting for transfers between devices: 527 us -> 51.2 us
  Pallas kernels: 0 us -> 42.6 us
  matrix products: 21 us -> 0 us
  starting transfers between devices: 9.48 us -> 29.5 us
  other arithmetic: 16.8 us -> 3.93 us
  local copies, waits for them, and re-layouts: 11.9 us -> 1.54 us
    ppermute x4 -> x17, waiting for transfers between devices: 527 us -> 51.2 us  [move(): return lax.ppermute(values, ('row', 'col'), pairs)]
    pallas_call x0 -> x15, Pallas kernels: none -> 42.6 us  [the longest x4 15.9 us: partial_products(): pl.pallas_call(partial_kernel, grid=(columns // wide,), in_specs=[SM(), w...]
    dot_general x6 -> x0, matrix products: 21 us -> none  [the longest x2 7.27 us: accumulate(): jnp.dot(left_now[0], right_now[1], preferred_element_type=jnp.float32)]
    ppermute x4 -> x17, starting transfers between devices: 9.48 us -> 29.5 us  [move(): return lax.ppermute(values, ('row', 'col'), pairs)]
    unnamed x21 -> x14, local copies, waits for them, and re-layouts: 9.89 us -> 1.54 us
  transfers between devices with their start and end apart: 4 -> 17, of which waited for: 4 -> 7; matrix products, arithmetic and copies ran while one was open for 2% -> 3% of each run, Pallas kernels for 0% -> 30%
where the time goes in v1:
time: 131 us; the launch traced here: 130 us
  waiting for transfers between devices  51.2 us (39%)
  Pallas kernels  42.6 us (33%)
  starting transfers between devices  29.5 us (23%)
  other arithmetic  3.93 us (3%)
  local copies, waits for them, and re-layouts  1.54 us (1%)
    ppermute x17, waiting for transfers between devices, move(): return lax.ppermute(values, ('row', 'col'), pairs)  51.2 us
    ppermute x17, starting transfers between devices, move(): return lax.ppermute(values, ('row', 'col'), pairs)  29.5 us
    pallas_call x4, Pallas kernels, partial_products(): pl.pallas_call(partial_kernel, grid=(columns // wide,), in_specs=[SM(), w...  15.9 us
    pallas_call x1, Pallas kernels, masked_right(): pl.pallas_call(right_kernel, grid=(depth // tall,), in_specs=[SM(), SM(),...  6.92 us
    pallas_call x4, Pallas kernels, masked_chunk(): pl.pallas_call(functools.partial(chunk_kernel, step * rows // BLOCK, bloc...  6.62 us
    pallas_call x1, Pallas kernels, local_products(): pl.pallas_call(local_kernel, grid=(columns // wide,), in_specs=[SM(), who...  6.01 us
    pallas_call x4, Pallas kernels, finished(): pl.pallas_call(functools.partial(finish_kernel, step * rows // BLOCK), gr...  5.11 us
    select_n x4, other arithmetic, per_device_pair(): jnp.where(is_diag, r, a)  3.93 us
  transfers between devices with their start and end apart: 17, of which 7 were waited for; matrix products, arithmetic and copies ran while one was open for 3% of the time, Pallas kernels for 30%

profile of v1, /device:TPU:0, one launch (start us, length us, event | category | flops | bytes accessed | tf_op | source)
XLA Modules:
  0.0 129.6 jit_solution(5136270047576780647)
XLA Ops:
  2.0 1.8 %left_chunk.4 = (bf16[64,2048]{1,0:T(8,128)(2,1)S(1)}, bf16[64,2048]{1,0:T(8,128)(2,1)}) custom-call(s32[1]{0:T(128)} %bitcast.1.place, s32[2,128]{1,0:T(2,128)S(1)} %copy-done.1, s32[2,128]{1,0:T(2,128)S(1)} %copy-done.2, bf16[256,16384]{1,0:T(8,128)(2,1)} %x0.11, bf16[256,16384]{1,0:T(8,128)(2,1)} %x1.11), custom_call_target="tpu_custom_call" | custom-call | bytes 1048576 | tf_op jit(solution)/shard_map/left_chunk/pallas_call | solution.py:45
  3.8 1.3 collective-permute-start.1
  5.1 2.1 %left_slab.1.own = bf16[2,256,2048]{2,1,0:T(8,128)(2,1)S(1)} custom-call(s32[1]{0:T(128)} %bitcast.1.place, s32[2,128]{1,0:T(2,128)S(1)} %copy-done.1, s32[2,128]{1,0:T(2,128)S(1)} %copy-done.2, bf16[256,16384]{1,0:T(8,128)(2,1)} %x0.11, bf16[256,16384]{1,0:T(8,128)(2,1)} %x1.11), custom_call_target="tpu_custom_call" | custom-call | bytes 4194304 | tf_op jit(solution)/shard_map/left_slab/pallas_call | solution.py:79
  7.2 7.0 %collective-permute-start = (bf16[2,256,2048]{2,1,0:T(8,128)(2,1)S(1)}, bf16[2,256,2048]{2,1,0:T(8,128)(2,1)}, u32[]{:S(2)}, u32[]{:S(2)}) collective-permute-start(bf16[2,256,2048]{2,1,0:T(8,128)(2,1)S(1)} %left_slab.1.own), channel_id=1, source_target_pairs={{0,1},{2,3},{4,5},{6,7},{8,9},{10,11},{12,13},{14,15},{17,16},{19,... | collective-permute-start | bytes 6291464 | tf_op jit(solution)/shard_map/ppermute | solution.py:298
  14.1 1.8 %left_chunk.5 = (bf16[64,2048]{1,0:T(8,128)(2,1)S(1)}, bf16[64,2048]{1,0:T(8,128)(2,1)}) custom-call(s32[1]{0:T(128)} %bitcast.1.place, s32[2,128]{1,0:T(2,128)S(1)} %copy-done.1, s32[2,128]{1,0:T(2,128)S(1)} %copy-done.2, bf16[256,16384]{1,0:T(8,128)(2,1)} %x0.11, bf16[256,16384]{1,0:T(8,128)(2,1)} %x1.11), custom_call_target="tpu_custom_call" | custom-call | bytes 1048576 | tf_op jit(solution)/shard_map/left_chunk/pallas_call | solution.py:45
  17.2 1.8 %left_chunk.6 = (bf16[64,2048]{1,0:T(8,128)(2,1)S(1)}, bf16[64,2048]{1,0:T(8,128)(2,1)}) custom-call(s32[1]{0:T(128)} %bitcast.1.place, s32[2,128]{1,0:T(2,128)S(1)} %copy-done.1, s32[2,128]{1,0:T(2,128)S(1)} %copy-done.2, bf16[256,16384]{1,0:T(8,128)(2,1)} %x0.11, bf16[256,16384]{1,0:T(8,128)(2,1)} %x1.11), custom_call_target="tpu_custom_call" | custom-call | bytes 1048576 | tf_op jit(solution)/shard_map/left_chunk/pallas_call | solution.py:45
  21.6 1.3 collective-permute-start.13
  23.9 7.0 %collective-permute-start.2 = (bf16[64,2048]{1,0:T(8,128)(2,1)S(1)}, bf16[64,2048]{1,0:T(8,128)(2,1)S(1)}, u32[]{:S(2)}, u32[]{:S(2)}) collective-permute-start(bf16[64,2048]{1,0:T(8,128)(2,1)S(1)} %broadcast_select_fusion.3), channel_id=1, source_target_pairs={{0,16},{1,17},{2,18},{3,19},{4,20},{5,21},{6,22},{7,23},{8,24},{9,... | collective-permute-start | bytes 786440 | tf_op jit(solution)/shard_map/ppermute | solution.py:298
  34.0 1.9 %collective-permute-start.10 = (bf16[64,2048]{1,0:T(8,128)(2,1)S(1)}, bf16[64,2048]{1,0:T(8,128)(2,1)S(1)}, u32[]{:S(2)}, u32[]{:S(2)}) collective-permute-start(bf16[64,2048]{1,0:T(8,128)(2,1)S(1)} %broadcast_select_fusion.1), channel_id=1, source_target_pairs={{0,16},{1,17},{2,18},{3,19},{4,20},{5,21},{6,22},{7,23},{8,24},{9,... | collective-permute-start | bytes 786440 | tf_op jit(solution)/shard_map/ppermute | solution.py:298
  35.9 1.3 %collective-permute-done.13 = bf16[64,2048]{1,0:T(8,128)(2,1)} collective-permute-done((bf16[64,2048]{1,0:T(8,128)(2,1)S(1)}, bf16[64,2048]{1,0:T(8,128)(2,1)}, u32[]{:S(2)}, u32[]{:S(2)}) %collective-permute-start.13) | collective-permute-done | bytes 262176 | tf_op jit(solution)/shard_map/ppermute | solution.py:298
  38.1 1.5 %collective-permute-start.14 = (bf16[64,2048]{1,0:T(8,128)(2,1)S(1)}, bf16[64,2048]{1,0:T(8,128)(2,1)S(1)}, u32[]{:S(2)}, u32[]{:S(2)}) collective-permute-start(bf16[64,2048]{1,0:T(8,128)(2,1)S(1)} %broadcast_select_fusion), channel_id=1, source_target_pairs={{0,16},{1,17},{2,18},{3,19},{4,20},{5,21},{6,22},{7,23},{8,24},{9,... | collective-permute-start | bytes 786440 | tf_op jit(solution)/shard_map/ppermute | solution.py:298
  39.6 20.4 %collective-permute-done.2.near = bf16[64,2048]{1,0:T(8,128)(2,1)S(1)} collective-permute-done((bf16[64,2048]{1,0:T(8,128)(2,1)S(1)}, bf16[64,2048]{1,0:T(8,128)(2,1)S(1)}, u32[]{:S(2)}, u32[]{:S(2)}) %collective-permute-start.2) | collective-permute-done | bytes 262176 | tf_op jit(solution)/shard_map/ppermute | solution.py:298
  60.3 5.3 %collective-permute-done.6.near = bf16[64,2048]{1,0:T(8,128)(2,1)S(1)} collective-permute-done((bf16[64,2048]{1,0:T(8,128)(2,1)S(1)}, bf16[64,2048]{1,0:T(8,128)(2,1)S(1)}, u32[]{:S(2)}, u32[]{:S(2)}) %collective-permute-start.6) | collective-permute-done | bytes 262176 | tf_op jit(solution)/shard_map/ppermute | solution.py:298
  66.0 5.3 %collective-permute-done.10.near = bf16[64,2048]{1,0:T(8,128)(2,1)S(1)} collective-permute-done((bf16[64,2048]{1,0:T(8,128)(2,1)S(1)}, bf16[64,2048]{1,0:T(8,128)(2,1)S(1)}, u32[]{:S(2)}, u32[]{:S(2)}) %collective-permute-start.10) | collective-permute-done | bytes 262176 | tf_op jit(solution)/shard_map/ppermute | solution.py:298
  71.6 4.1 %collective-permute-done.14.near = bf16[64,2048]{1,0:T(8,128)(2,1)S(1)} collective-permute-done((bf16[64,2048]{1,0:T(8,128)(2,1)S(1)}, bf16[64,2048]{1,0:T(8,128)(2,1)S(1)}, u32[]{:S(2)}, u32[]{:S(2)}) %collective-permute-start.14) | collective-permute-done | bytes 262176 | tf_op jit(solution)/shard_map/ppermute | solution.py:298
  75.9 6.9 %right_panels.1 = (bf16[2048,768]{1,0:T(8,128)(2,1)S(1)}, bf16[2048,768]{1,0:T(8,128)(2,1)}) custom-call(s32[16,6]{1,0:T(8,128)S(1)} %copy.17.mask0, s32[16,6]{1,0:T(8,128)S(1)} %copy.18.mask1, bf16[2048,768]{1,0:T(8,128)(2,1)} %x0.7, bf16[2048,768]{1,0:T(8,128)(2,1)} %x1.7), custom_call_target="tpu_custom_call" | custom-call | bytes 12582912 | tf_op jit(solution)/shard_map/right_panels/pallas_call | solution.py:114
  82.8 4.8 %partial_products.4 = s16[784,128]{1,0:T(8,128)(2,1)S(1)} custom-call(s32[1]{0:T(128)} %bitcast.diag, bf16[64,2048]{1,0:T(8,128)(2,1)S(1)} %collective-permute-done.2.near, bf16[64,2048]{1,0:T(8,128)(2,1)} %collective-permute-done.3.far, bf16[2048,768]{1,0:T(8,128)(2,1)S(1)} %get-tuple-element.20.right0, bf16[2048,768]{1,0:T(8,128)(2,1)} %get-tuple-element.21.right1), custom_call_target="tpu_custom_call" | custom-call | flops 603979776 | bytes 6815744 | tf_op jit(solution)/shard_map/partial_products/pallas_call | solution.py:215
  87.7 3.7 %partial_products.5 = s16[784,128]{1,0:T(8,128)(2,1)S(1)} custom-call(s32[1]{0:T(128)} %bitcast.diag, bf16[64,2048]{1,0:T(8,128)(2,1)S(1)} %collective-permute-done.6.near, bf16[64,2048]{1,0:T(8,128)(2,1)} %collective-permute-done.7.far, bf16[2048,768]{1,0:T(8,128)(2,1)S(1)} %get-tuple-element.20.right0, bf16[2048,768]{1,0:T(8,128)(2,1)} %get-tuple-element.21.right1), custom_call_target="tpu_custom_call" | custom-call | flops 603979776 | bytes 6815744 | tf_op jit(solution)/shard_map/partial_products/pallas_call | solution.py:215
  91.4 2.9 %collective-permute-start.8 = (s16[784,128]{1,0:T(8,128)(2,1)S(1)}, s16[784,128]{1,0:T(8,128)(2,1)S(1)}, u32[]{:S(2)}, u32[]{:S(2)}) collective-permute-start(s16[784,128]{1,0:T(8,128)(2,1)S(1)} %partial_products.5), channel_id=1, source_target_pairs={{0,16},{1,17},{2,18},{3,19},{4,20},{5,21},{6,22},{7,23},{8,24},{9,... | collective-permute-start | bytes 602120 | tf_op jit(solution)/shard_map/ppermute | solution.py:298
  94.4 3.7 %partial_products.6 = s16[784,128]{1,0:T(8,128)(2,1)S(1)} custom-call(s32[1]{0:T(128)} %bitcast.diag, bf16[64,2048]{1,0:T(8,128)(2,1)S(1)} %collective-permute-done.10.near, bf16[64,2048]{1,0:T(8,128)(2,1)} %collective-permute-done.11.far, bf16[2048,768]{1,0:T(8,128)(2,1)S(1)} %get-tuple-element.20.right0, bf16[2048,768]{1,0:T(8,128)(2,1)} %get-tuple-element.21.right1), custom_call_target="tpu_custom_call" | custom-call | flops 603979776 | bytes 6815744 | tf_op jit(solution)/shard_map/partial_products/pallas_call | solution.py:215
  98.2 3.6 %partial_products.7 = s16[784,128]{1,0:T(8,128)(2,1)S(1)} custom-call(s32[1]{0:T(128)} %bitcast.diag, bf16[64,2048]{1,0:T(8,128)(2,1)S(1)} %collective-permute-done.14.near, bf16[64,2048]{1,0:T(8,128)(2,1)S(1)} %collective-permute-done.15.far, bf16[2048,768]{1,0:T(8,128)(2,1)S(1)} %get-tuple-element.20.right0, bf16[2048,768]{1,0:T(8,128)(2,1)} %get-tuple-element.21.right1), custom_call_target="tpu_custom_call" | custom-call | flops 603979776 | bytes 6815744 | tf_op jit(solution)/shard_map/partial_products/pallas_call | solution.py:215
  101.9 2.9 %collective-permute-start.16 = (s16[784,128]{1,0:T(8,128)(2,1)S(1)}, s16[784,128]{1,0:T(8,128)(2,1)S(1)}, u32[]{:S(2)}, u32[]{:S(2)}) collective-permute-start(s16[784,128]{1,0:T(8,128)(2,1)S(1)} %partial_products.7), channel_id=1, source_target_pairs={{0,16},{1,17},{2,18},{3,19},{4,20},{5,21},{6,22},{7,23},{8,24},{9,... | collective-permute-start | bytes 602120 | tf_op jit(solution)/shard_map/ppermute | solution.py:298
  104.8 6.0 %own_products.1 = (f32[256,768]{1,0:T(8,128)S(1)}, f32[256,768]{1,0:T(8,128)S(1)}) custom-call(s32[1]{0:T(128)} %bitcast.diag, bf16[2,256,2048]{2,1,0:T(8,128)(2,1)S(1)} %left_slab.1.own, bf16[2,256,2048]{2,1,0:T(8,128)(2,1)} %collective-permute-done.got, bf16[2048,768]{1,0:T(8,128)(2,1)} %copy-done, bf16[2048,768]{1,0:T(8,128)(2,1)} %get-tuple-element.21.right1), custom_call_target="tpu_custom_call" | custom-call | flops 2415919104 | bytes 10485760 | tf_op jit(solution)/shard_map/own_products/pallas_call | solution.py:154
  110.8 13.6 %collective-permute-done.16.coded = s16[784,128]{1,0:T(8,128)(2,1)S(1)} collective-permute-done((s16[784,128]{1,0:T(8,128)(2,1)S(1)}, s16[784,128]{1,0:T(8,128)(2,1)S(1)}, u32[]{:S(2)}, u32[]{:S(2)}) %collective-permute-start.16) | collective-permute-done | bytes 200736 | tf_op jit(solution)/shard_map/ppermute | solution.py:298
  (43 shorter events, 16.5 us)
Async XLA Ops:
  0.6 0.7 copy-start.1
  1.3 0.7 copy-start.2
  3.8 19.1 %collective-permute-start.1 = (bf16[64,2048]{1,0:T(8,128)(2,1)}, bf16[64,2048]{1,0:T(8,128)(2,1)}, u32[]{:S(2)}, u32[]{:S(2)}) collective-permute-start(bf16[64,2048]{1,0:T(8,128)(2,1)} %get-tuple-element.24), channel_id=1, source_target_pairs={{1,0},{3,2},{5,4},{7,6},{9,8},{11,10},{13,12},{15,14},{16,17},{18,... | collective-permute-start | bytes 786440 | tf_op jit(solution)/shard_map/ppermute | solution.py:298
  7.2 97.6 %collective-permute-start = (bf16[2,256,2048]{2,1,0:T(8,128)(2,1)S(1)}, bf16[2,256,2048]{2,1,0:T(8,128)(2,1)}, u32[]{:S(2)}, u32[]{:S(2)}) collective-permute-start(bf16[2,256,2048]{2,1,0:T(8,128)(2,1)S(1)} %left_slab.1.own), channel_id=1, source_target_pairs={{0,1},{2,3},{4,5},{6,7},{8,9},{10,11},{12,13},{14,15},{17,16},{19,... | collective-permute-start | bytes 6291464 | tf_op jit(solution)/shard_map/ppermute | solution.py:298
  15.9 15.0 %collective-permute-start.5 = (bf16[64,2048]{1,0:T(8,128)(2,1)}, bf16[64,2048]{1,0:T(8,128)(2,1)}, u32[]{:S(2)}, u32[]{:S(2)}) collective-permute-start(bf16[64,2048]{1,0:T(8,128)(2,1)} %get-tuple-element.26), channel_id=1, source_target_pairs={{1,0},{3,2},{5,4},{7,6},{9,8},{11,10},{13,12},{15,14},{16,17},{18,... | collective-permute-start | bytes 786440 | tf_op jit(solution)/shard_map/ppermute | solution.py:298
  19.1 13.9 %collective-permute-start.9 = (bf16[64,2048]{1,0:T(8,128)(2,1)}, bf16[64,2048]{1,0:T(8,128)(2,1)}, u32[]{:S(2)}, u32[]{:S(2)}) collective-permute-start(bf16[64,2048]{1,0:T(8,128)(2,1)} %get-tuple-element.28), channel_id=1, source_target_pairs={{1,0},{3,2},{5,4},{7,6},{9,8},{11,10},{13,12},{15,14},{16,17},{18,... | collective-permute-start | bytes 786440 | tf_op jit(solution)/shard_map/ppermute | solution.py:298
  21.5 54.2 %copy-start.4 = (s32[16,6]{0,1:T(8,128)S(1)}, s32[16,6]{0,1:T(8,128)}, u32[]{:S(2)}) copy-start(s32[16,6]{0,1:T(8,128)} %param.15) | copy-start | bytes 1156
  21.6 54.3 %copy-start.5 = (s32[16,6]{0,1:T(8,128)S(1)}, s32[16,6]{0,1:T(8,128)}, u32[]{:S(2)}) copy-start(s32[16,6]{0,1:T(8,128)} %param.16) | copy-start | bytes 1156
  21.6 15.6 %collective-permute-start.13 = (bf16[64,2048]{1,0:T(8,128)(2,1)S(1)}, bf16[64,2048]{1,0:T(8,128)(2,1)}, u32[]{:S(2)}, u32[]{:S(2)}) collective-permute-start(bf16[64,2048]{1,0:T(8,128)(2,1)S(1)} %get-tuple-element.30), channel_id=1, source_target_pairs={{1,0},{3,2},{5,4},{7,6},{9,8},{11,10},{13,12},{15,14},{16,17},{18,... | collective-permute-start | bytes 786440 | tf_op jit(solution)/shard_map/ppermute | solution.py:298
  23.9 36.2 %collective-permute-start.2 = (bf16[64,2048]{1,0:T(8,128)(2,1)S(1)}, bf16[64,2048]{1,0:T(8,128)(2,1)S(1)}, u32[]{:S(2)}, u32[]{:S(2)}) collective-permute-start(bf16[64,2048]{1,0:T(8,128)(2,1)S(1)} %broadcast_select_fusion.3), channel_id=1, source_target_pairs={{0,16},{1,17},{2,18},{3,19},{4,20},{5,21},{6,22},{7,23},{8,24},{9,... | collective-permute-start | bytes 786440 | tf_op jit(solution)/shard_map/ppermute | solution.py:298
  31.9 33.7 %collective-permute-start.6 = (bf16[64,2048]{1,0:T(8,128)(2,1)S(1)}, bf16[64,2048]{1,0:T(8,128)(2,1)S(1)}, u32[]{:S(2)}, u32[]{:S(2)}) collective-permute-start(bf16[64,2048]{1,0:T(8,128)(2,1)S(1)} %broadcast_select_fusion.2), channel_id=1, source_target_pairs={{0,16},{1,17},{2,18},{3,19},{4,20},{5,21},{6,22},{7,23},{8,24},{9,... | collective-permute-start | bytes 786440 | tf_op jit(solution)/shard_map/ppermute | solution.py:298
  34.0 37.3 %collective-permute-start.10 = (bf16[64,2048]{1,0:T(8,128)(2,1)S(1)}, bf16[64,2048]{1,0:T(8,128)(2,1)S(1)}, u32[]{:S(2)}, u32[]{:S(2)}) collective-permute-start(bf16[64,2048]{1,0:T(8,128)(2,1)S(1)} %broadcast_select_fusion.1), channel_id=1, source_target_pairs={{0,16},{1,17},{2,18},{3,19},{4,20},{5,21},{6,22},{7,23},{8,24},{9,... | collective-permute-start | bytes 786440 | tf_op jit(solution)/shard_map/ppermute | solution.py:298
  38.1 37.6 %collective-permute-start.14 = (bf16[64,2048]{1,0:T(8,128)(2,1)S(1)}, bf16[64,2048]{1,0:T(8,128)(2,1)S(1)}, u32[]{:S(2)}, u32[]{:S(2)}) collective-permute-start(bf16[64,2048]{1,0:T(8,128)(2,1)S(1)} %broadcast_select_fusion), channel_id=1, source_target_pairs={{0,16},{1,17},{2,18},{3,19},{4,20},{5,21},{6,22},{7,23},{8,24},{9,... | collective-permute-start | bytes 786440 | tf_op jit(solution)/shard_map/ppermute | solution.py:298
  60.0 22.8 %collective-permute-start.3 = (bf16[64,2048]{1,0:T(8,128)(2,1)S(1)}, bf16[64,2048]{1,0:T(8,128)(2,1)}, u32[]{:S(2)}, u32[]{:S(2)}) collective-permute-start(bf16[64,2048]{1,0:T(8,128)(2,1)S(1)} %collective-permute-done.2.near), channel_id=1, source_target_pairs={{0,1},{1,0},{2,3},{3,2},{4,5},{5,4},{6,7},{7,6},{8,9},{9,8},{10,11... | collective-permute-start | bytes 786440 | tf_op jit(solution)/shard_map/ppermute | solution.py:298
  65.7 22.0 %collective-permute-start.7 = (bf16[64,2048]{1,0:T(8,128)(2,1)S(1)}, bf16[64,2048]{1,0:T(8,128)(2,1)}, u32[]{:S(2)}, u32[]{:S(2)}) collective-permute-start(bf16[64,2048]{1,0:T(8,128)(2,1)S(1)} %collective-permute-done.6.near), channel_id=1, source_target_pairs={{0,1},{1,0},{2,3},{3,2},{4,5},{5,4},{6,7},{7,6},{8,9},{9,8},{10,11... | collective-permute-start | bytes 786440 | tf_op jit(solution)/shard_map/ppermute | solution.py:298
  71.3 23.1 %collective-permute-start.11 = (bf16[64,2048]{1,0:T(8,128)(2,1)S(1)}, bf16[64,2048]{1,0:T(8,128)(2,1)}, u32[]{:S(2)}, u32[]{:S(2)}) collective-permute-start(bf16[64,2048]{1,0:T(8,128)(2,1)S(1)} %collective-permute-done.10.near), channel_id=1, source_target_pairs={{0,1},{1,0},{2,3},{3,2},{4,5},{5,4},{6,7},{7,6},{8,9},{9,8},{10,11... | collective-permute-start | bytes 786440 | tf_op jit(solution)/shard_map/ppermute | solution.py:298
  75.7 22.5 %collective-permute-start.15 = (bf16[64,2048]{1,0:T(8,128)(2,1)S(1)}, bf16[64,2048]{1,0:T(8,128)(2,1)S(1)}, u32[]{:S(2)}, u32[]{:S(2)}) collective-permute-start(bf16[64,2048]{1,0:T(8,128)(2,1)S(1)} %collective-permute-done.14.near), channel_id=1, source_target_pairs={{0,1},{1,0},{2,3},{3,2},{4,5},{5,4},{6,7},{7,6},{8,9},{9,8},{10,11... | collective-permute-start | bytes 786440 | tf_op jit(solution)/shard_map/ppermute | solution.py:298
  82.8 15.4 %copy-start = (bf16[2048,768]{1,0:T(8,128)(2,1)}, bf16[2048,768]{1,0:T(8,128)(2,1)S(1)}, u32[]{:S(2)}) copy-start(bf16[2048,768]{1,0:T(8,128)(2,1)S(1)} %get-tuple-element.20.right0) | copy-start | bytes 9437188
  87.6 40.7 %collective-permute-start.4 = (s16[784,128]{1,0:T(8,128)(2,1)S(1)}, s16[784,128]{1,0:T(8,128)(2,1)S(1)}, u32[]{:S(2)}, u32[]{:S(2)}) collective-permute-start(s16[784,128]{1,0:T(8,128)(2,1)S(1)} %partial_products.4), channel_id=1, source_target_pairs={{0,16},{1,17},{2,18},{3,19},{4,20},{5,21},{6,22},{7,23},{8,24},{9,... | collective-permute-start | bytes 602120 | tf_op jit(solution)/shard_map/ppermute | solution.py:298
  91.4 35.6 %collective-permute-start.8 = (s16[784,128]{1,0:T(8,128)(2,1)S(1)}, s16[784,128]{1,0:T(8,128)(2,1)S(1)}, u32[]{:S(2)}, u32[]{:S(2)}) collective-permute-start(s16[784,128]{1,0:T(8,128)(2,1)S(1)} %partial_products.5), channel_id=1, source_target_pairs={{0,16},{1,17},{2,18},{3,19},{4,20},{5,21},{6,22},{7,23},{8,24},{9,... | collective-permute-start | bytes 602120 | tf_op jit(solution)/shard_map/ppermute | solution.py:298
  98.1 27.7 %collective-permute-start.12 = (s16[784,128]{1,0:T(8,128)(2,1)S(1)}, s16[784,128]{1,0:T(8,128)(2,1)S(1)}, u32[]{:S(2)}, u32[]{:S(2)}) collective-permute-start(s16[784,128]{1,0:T(8,128)(2,1)S(1)} %partial_products.6), channel_id=1, source_target_pairs={{0,16},{1,17},{2,18},{3,19},{4,20},{5,21},{6,22},{7,23},{8,24},{9,... | collective-permute-start | bytes 602120 | tf_op jit(solution)/shard_map/ppermute | solution.py:298
  101.9 22.6 %copy-start.3 = (s32[2,6]{1,0:T(2,128)S(1)}, s32[2,6]{1,0:T(2,128)}, u32[]{:S(2)}) copy-start(s32[2,6]{1,0:T(2,128)} %keep.7) | copy-start | bytes 148
  101.9 22.6 %collective-permute-start.16 = (s16[784,128]{1,0:T(8,128)(2,1)S(1)}, s16[784,128]{1,0:T(8,128)(2,1)S(1)}, u32[]{:S(2)}, u32[]{:S(2)}) collective-permute-start(s16[784,128]{1,0:T(8,128)(2,1)S(1)} %partial_products.7), channel_id=1, source_target_pairs={{0,16},{1,17},{2,18},{3,19},{4,20},{5,21},{6,22},{7,23},{8,24},{9,... | collective-permute-start | bytes 602120 | tf_op jit(solution)/shard_map/ppermute | solution.py:298

commit v2 on v1

v2 whole, which is shorter than its diff:
```python
import functools
import math

import jax
import jax.numpy as jnp
from jax import lax
from jax.experimental import pallas as pl
from jax.experimental.pallas import tpu as pltpu
from jax.sharding import PartitionSpec as P

BLOCK = 128
LEVELS = 32000.0
STEPS = 32.0
LN2 = math.log(2.0)
VMEM_BYTES = 48 * 1024 * 1024

VM = functools.partial(pl.BlockSpec, memory_space=pltpu.VMEM)
SM = functools.partial(pl.BlockSpec, memory_space=pltpu.SMEM)
HB = functools.partial(pl.BlockSpec, memory_space=pl.ANY)


def params():
    return pltpu.CompilerParams(vmem_limit_bytes=VMEM_BYTES)


def cost(flops, moved):
    return pl.CostEstimate(flops=int(flops) // 64, bytes_accessed=int(moved) // 64, transcendentals=0)


def scaled(values, entry):
    return (values.astype(jnp.float32) * entry.astype(jnp.float32)).astype(values.dtype)


def row_pieces(start, rows):
    edges = sorted({start, start + rows} | {e for e in range(0, start + rows, BLOCK) if e > start})
    return [(lo // BLOCK, slice(lo - start, hi - start)) for lo, hi in zip(edges, edges[1:])]


def chunk_kernel(spans, panel, with_slab, *refs):
    place, diag, mask0, mask1, x0, x1 = refs[:6]
    held, sems = refs[-2:]
    many = 2 * len(spans) + with_slab
    outs = refs[-2 - many : -2]
    slab = outs[-1] if with_slab else None
    blocks = panel // BLOCK
    first = place[0] * blocks
    at = pl.ds(pl.multiple_of(place[0] * panel, BLOCK), panel)
    origin = 0 if with_slab else spans[0][0]
    copies = []
    for n, (lo, hi) in enumerate(spans):
        lo = origin if n == 0 else lo
        for i, x in enumerate((x0, x1)):
            here = pl.ds(lo - origin, hi - lo)
            copies.append(
                pltpu.make_async_copy(x.at[pl.ds(lo, hi - lo), at], held.at[i, here], sems.at[n, i])
            )
    for copy in copies:
        copy.start()
    for n, (lo, hi) in enumerate(spans):
        a_out, swap = outs[2 * n], outs[2 * n + 1]
        copies[2 * n].wait()
        copies[2 * n + 1].wait()
        if with_slab:
            top = origin if n == 0 else lo
            for row_block, piece in row_pieces(top, hi - top):
                rows = slice(piece.start + top, piece.stop + top)
                for j in range(blocks):
                    cut = slice(j * BLOCK, (j + 1) * BLOCK)
                    slab[rows, cut] = scaled(held[1, rows, cut], mask1[row_block, first + j])
        for row_block, piece in row_pieces(lo, hi - lo):
            rows = slice(piece.start + lo - origin, piece.stop + lo - origin)
            for j in range(blocks):
                cut = slice(j * BLOCK, (j + 1) * BLOCK)
                a_out[piece, cut] = scaled(held[0, rows, cut], mask0[row_block, first + j])
            if not with_slab:
                for j in range(blocks):
                    cut = slice(j * BLOCK, (j + 1) * BLOCK)
                    swap[piece, cut] = scaled(held[1, rows, cut], mask1[row_block, first + j])

        @pl.when(diag[0] == 1)
        def _():
            swap[...] = a_out[...]

        if with_slab:

            @pl.when(diag[0] == 0)
            def _():
                swap[...] = slab[lo:hi]


def masked_chunks(place, diag, mask0, mask1, x0, x1, spans, panel, with_slab, after=()):
    outs = []
    for lo, hi in spans:
        outs += [jax.ShapeDtypeStruct((hi - lo, panel), x0.dtype)] * 2
    high = spans[-1][1] - (0 if with_slab else spans[0][0])
    if with_slab:
        outs.append(jax.ShapeDtypeStruct((spans[-1][1], panel), x0.dtype))
    return pl.pallas_call(
        functools.partial(chunk_kernel, spans, panel, with_slab),
        in_specs=[SM(), SM(), SM(), SM(), HB(), HB()] + [HB() for _ in after],
        out_specs=[VM() for _ in outs],
        out_shape=outs,
        scratch_shapes=[
            pltpu.VMEM((2, high, panel), x0.dtype),
            pltpu.SemaphoreType.DMA((len(spans), 2)),
        ],
        compiler_params=params(),
        cost_estimate=cost(0, 8 * high * panel),
        name="left_chunks",
    )(place, diag, mask0, mask1, x0, x1, *after)


def choose_kernel(many, diag, one, other, *refs):
    held, outs, sems = refs[:many], refs[-many - 2 : -1], refs[-1]
    others = [
        pltpu.make_async_copy(x, out, sems.at[1 + i])
        for i, (x, out) in enumerate(zip(held, outs[1:]))
    ]
    for copy in others:
        copy.start()

    @pl.when(diag[0] == 1)
    def _():
        copy = pltpu.make_async_copy(one, outs[0], sems.at[0])
        copy.start()
        copy.wait()

    @pl.when(diag[0] == 0)
    def _():
        copy = pltpu.make_async_copy(other, outs[0], sems.at[0])
        copy.start()
        copy.wait()

    for copy in others:
        copy.wait()


def chosen(diag, one, other, held=(), after=()):
    outs = [jax.ShapeDtypeStruct(x.shape, x.dtype) for x in (one, *held)]
    return pl.pallas_call(
        functools.partial(choose_kernel, len(held)),
        in_specs=[SM(), HB(), HB()] + [HB() for _ in (*held, *after)],
        out_specs=[HB() for _ in outs],
        out_shape=outs,
        scratch_shapes=[pltpu.SemaphoreType.DMA((len(outs),))],
        compiler_params=params(),
        cost_estimate=cost(0, 4 * one.size),
        name="to_send",
    )(diag, one, other, *held, *after)


def right_kernel(mask0, mask1, x0, x1, *rest):
    out0, out1 = rest[-2:]
    step = pl.program_id(0)
    many = x0.shape[0] // BLOCK
    for i in range(many):
        for j in range(x0.shape[1] // BLOCK):
            at = (slice(i * BLOCK, (i + 1) * BLOCK), slice(j * BLOCK, (j + 1) * BLOCK))
            out0[at] = scaled(x0[at], mask0[step * many + i, j])
            out1[at] = scaled(x1[at], mask1[step * many + i, j])


def masked_right(mask0, mask1, x0, x1, after=()):
    depth, columns = x0.shape
    tall = 2 * BLOCK
    out = jax.ShapeDtypeStruct(x0.shape, x0.dtype)
    tile = pl.BlockSpec((tall, columns), lambda g: (g, 0))
    return pl.pallas_call(
        right_kernel,
        grid=(depth // tall,),
        in_specs=[SM(), SM(), tile, tile] + [HB() for _ in after],
        out_specs=[tile, tile],
        out_shape=[out, out],
        compiler_params=params(),
        cost_estimate=cost(0, 8 * depth * columns),
        name="right_panels",
    )(mask0, mask1, x0, x1, *after)


def both_products(held, right0, right1):
    rows = held.shape[0] // 2
    first = jnp.dot(held[...], right0[...], preferred_element_type=jnp.float32)
    second = jnp.dot(held[:rows], right1[...], preferred_element_type=jnp.float32)
    return first[:rows], first[rows:] + second


def fetched(pieces, held, sems):
    copies = []
    top = 0
    for i, piece in enumerate(pieces):
        rows = piece.shape[0]
        copies.append(pltpu.make_async_copy(piece, held.at[pl.ds(top, rows)], sems.at[i]))
        top += rows
    for copy in copies:
        copy.start()
    for copy in copies:
        copy.wait()


def fetch_left(diag, one, other, held, sems):
    first = pl.program_id(0) == 0

    @pl.when(first & (diag[0] == 1))
    def _():
        fetched(one, held, sems)

    @pl.when(first & (diag[0] == 0))
    def _():
        fetched(other, held, sems)


def local_kernel(many, diag, right0, right1, *refs):
    own, got = refs[: many + 1], refs[many + 1 : 2 * many + 2]
    square, tangent, held, sems = refs[-4:]
    fetch_left(diag, own, got, held, sems)
    square[...], tangent[...] = both_products(held, right0, right1)


def local_products(diag, own, got, right0, right1, wide, after=()):
    rows, depth = own[-1].shape
    columns = right0.shape[1]
    many = len(own) - 1
    out = jax.ShapeDtypeStruct((rows, columns), jnp.float32)
    tile = pl.BlockSpec((rows, wide), lambda g: (0, g))
    return pl.pallas_call(
        functools.partial(local_kernel, many),
        grid=(columns // wide,),
        in_specs=[
            SM(),
            pl.BlockSpec((depth, wide), lambda g: (0, g)),
            pl.BlockSpec((depth, wide), lambda g: (0, g)),
        ]
        + [HB() for _ in (*own, *got, *after)],
        out_specs=[tile, tile],
        out_shape=[out, out],
        scratch_shapes=[
            pltpu.VMEM((2 * rows, depth), own[-1].dtype),
            pltpu.SemaphoreType.DMA((many + 1,)),
        ],
        compiler_params=params(),
        cost_estimate=cost(6 * rows * depth * columns, 8 * rows * depth + 4 * depth * columns),
        name="own_products",
    )(diag, right0, right1, *own, *got, *after)


def partial_kernel(diag, right0, right1, near, far, *refs):
    out, held, steps, sems = refs[-4:]
    rows, wide = near.shape[0], right0.shape[1]
    step = pl.program_id(0)
    tiles = wide // BLOCK
    across = pl.num_programs(0) * tiles
    fetch_left(diag, (near, far), (far, near), held, sems)
    for which, values in enumerate(both_products(held, right0, right1)):
        top = jnp.maximum(jnp.max(jnp.abs(values), axis=0, keepdims=True), 1e-30)
        level = jnp.ceil(jnp.log(top) * (STEPS / LN2)) + 1.0
        coded = jnp.round(values * (LEVELS * jnp.exp(level * (-LN2 / STEPS))))
        coded = jnp.clip(coded, -32767.0, 32767.0).astype(jnp.int32).astype(jnp.int16)
        for t in range(tiles):
            at = which * across + step * tiles + t
            cut = slice(t * BLOCK, (t + 1) * BLOCK)
            out[pl.ds(pl.multiple_of(at * rows, rows), rows), :] = coded[:, cut]
            steps[pl.ds(at, 1), :] = level[:, cut]

    @pl.when(step == pl.num_programs(0) - 1)
    def _():
        tail = steps.shape[0]
        out[out.shape[0] - tail :, :] = steps[...].astype(jnp.int32).astype(jnp.int16)


def partial_products(diag, near, far, right0, right1, wide, after=()):
    rows, depth = near.shape
    columns = right0.shape[1]
    tiles = 2 * columns // BLOCK
    tail = -(-tiles // 16) * 16
    return pl.pallas_call(
        partial_kernel,
        grid=(columns // wide,),
        in_specs=[
            SM(),
            pl.BlockSpec((depth, wide), lambda g: (0, g)),
            pl.BlockSpec((depth, wide), lambda g: (0, g)),
            HB(),
            HB(),
        ]
        + [HB() for _ in after],
        out_specs=pl.BlockSpec((tiles * rows + tail, BLOCK), lambda g: (0, 0)),
        out_shape=jax.ShapeDtypeStruct((tiles * rows + tail, BLOCK), jnp.int16),
        scratch_shapes=[
            pltpu.VMEM((2 * rows, depth), near.dtype),
            pltpu.VMEM((tail, BLOCK), jnp.float32),
            pltpu.SemaphoreType.DMA((2,)),
        ],
        compiler_params=params(),
        cost_estimate=cost(6 * rows * depth * columns, 4 * rows * depth + 4 * depth * columns),
        name="partial_products",
    )(diag, right0, right1, near, far, *after)


def finish_kernel(start, keep, coded, square, tangent, *rest):
    out0, out1, mine, made, in_sems, out_sems = rest[-6:]
    rows, columns = mine.shape[1:]
    across = columns // BLOCK
    at = pl.ds(start, rows)
    arrivals = [
        pltpu.make_async_copy(x.at[at], mine.at[i], in_sems.at[i])
        for i, x in enumerate((square, tangent))
    ]
    results = [
        pltpu.make_async_copy(made.at[i], x.at[at], out_sems.at[i])
        for i, x in enumerate((out0, out1))
    ]
    for copy in arrivals:
        copy.start()
    tail = coded.shape[0] - 2 * across * rows
    levels = coded[coded.shape[0] - tail :, :].astype(jnp.int32).astype(jnp.float32)
    steps = jnp.exp(levels * (LN2 / STEPS)) * (1.0 / LEVELS)
    for which in range(2):
        arrivals[which].wait()
        for j in range(across):
            tile = which * across + j
            cut = slice(j * BLOCK, (j + 1) * BLOCK)
            other = coded[tile * rows : (tile + 1) * rows, :].astype(jnp.int32).astype(jnp.float32)
            total = mine[which, :, cut] + other * steps[tile : tile + 1, :]
            for row_block, piece in row_pieces(start, rows):
                kept = total[piece] * keep[row_block, j].astype(jnp.float32)
                made[which, piece, cut] = kept.astype(made.dtype)
        results[which].start()
    for copy in results:
        copy.wait()


def finished(keep, square, tangent, coded, before, start, stop):
    rows = stop - start
    columns = square.shape[1]
    out = jax.ShapeDtypeStruct(square.shape, jnp.bfloat16)
    handed = [] if before is None else list(before)
    return pl.pallas_call(
        functools.partial(finish_kernel, start),
        in_specs=[SM(), VM(), HB(), HB()] + [HB() for _ in handed],
        out_specs=[HB(), HB()],
        out_shape=[out, out],
        input_output_aliases={4: 0, 5: 1} if handed else {},
        scratch_shapes=[
            pltpu.VMEM((2, rows, columns), jnp.float32),
            pltpu.VMEM((2, rows, columns), jnp.bfloat16),
            pltpu.SemaphoreType.DMA((2,)),
            pltpu.SemaphoreType.DMA((2,)),
        ],
        compiler_params=params(),
        cost_estimate=cost(0, 16 * rows * columns),
        name="finish",
    )(keep, coded, square, tangent, *handed)


def per_device_pair(
    n_row, x0_rows, x1_rows, x0_cols, x1_cols, mask0_rows, mask1_rows, mask0_cols, mask1_cols, keep
):
    n_col = 2
    group = n_row // n_col
    panel = x0_cols.shape[0]
    all_rows = x0_rows.shape[0]
    row_index = lax.axis_index("row")
    half = row_index // group
    diag = (half == lax.axis_index("col")).astype(jnp.int32).reshape(1)
    place = (row_index % group).astype(jnp.int32).reshape(1)
    edges = [all_rows * e // 8 for e in (0, 2, 4, 6, 8)]
    spans = list(zip(edges, edges[1:]))
    wide = 256

    def device(h, q, c):
        return (h * group + q) * n_col + c

    spots = [(h, q, c) for h in range(2) for q in range(group) for c in range(2)]
    over_y = [(device(h, q, c), device(h, q, 1 - c)) for h, q, c in spots]
    over_z = [(device(h, q, c), device(1 - h, q, c)) for h, q, c in spots]

    def move(values, pairs):
        return lax.ppermute(values, ("row", "col"), pairs)

    def chunks(spans, with_slab, after=()):
        return masked_chunks(
            place, diag, mask0_rows, mask1_rows, x0_rows, x1_rows, spans, panel, with_slab, after
        )

    def product(i, after=()):
        return partial_products(diag, near[i], far[i], right0, right1, wide, after)

    many = len(spans)
    a, swap, passed, near, far, coded, back = ([None] * many for _ in range(7))
    a[0], swap[0] = chunks(spans[:1], False)
    *rest, own_b = chunks(spans[1:], True, (swap[0],))
    a[1:], swap[1:] = rest[0::2], rest[1::2]
    right0 = right1 = square = tangent = got_b = outs = None
    for i in range(many):
        passed[i] = move(swap[i], over_y)
        gate = [near[i - 1]] if i else []
        if i == 1:
            gate.append(right0)
        if i >= 2:
            gate.append(coded[i - 2])
        if i == many - 1:
            square, tangent = local_products(
                diag, (*a, own_b), (*passed, got_b), right0, right1, wide, (coded[0],)
            )
            outs = finished(keep, square, tangent, back[0], None, *spans[0])
            gate.append(outs[0])
        held = swap[i + 1 : i + 2] + ([own_b] if i == 1 else [])
        send, *held = chosen(diag, passed[i], a[i], held, gate)
        if i < many - 1:
            swap[i + 1] = held[0]
        near[i] = move(send, over_z)
        if i == 0:
            right0, right1 = masked_right(mask0_cols, mask1_cols, x0_cols, x1_cols, (send,))
        if i == 1:
            own_b = held[1]
            got_b = move(own_b, over_y)
        if i >= 1:
            far[i - 1] = move(near[i - 1], over_y)
            coded[i - 1] = product(i - 1)
            back[i - 1] = move(coded[i - 1], over_z)
    outs = finished(keep, square, tangent, back[1], outs, *spans[1])
    far[many - 1] = move(near[many - 1], over_y)
    coded[many - 1] = product(many - 1, (coded[many - 2], outs[0]))
    back[many - 1] = move(coded[many - 1], over_z)
    for i in range(2, many):
        outs = finished(keep, square, tangent, back[i], outs, *spans[i])
    return tuple(outs)


def passed_along(shard, axis, by):
    devices = lax.axis_size(axis)
    return lax.ppermute(shard, axis, [(i, (i + by) % devices) for i in range(devices)])


def masked(values, mask):
    rows_b, cols_b = mask.shape
    tiles = values.reshape(rows_b, BLOCK, cols_b, BLOCK)
    return (tiles * mask.astype(values.dtype)[:, None, :, None]).reshape(values.shape)


def per_device(
    x0_rows, x1_rows, x0_cols, x1_cols, mask0_rows, mask1_rows, mask0_cols, mask1_cols, keep_mask
):
    n_row = lax.axis_size("row")
    n_col = lax.axis_size("col")
    group = n_row // n_col
    row_index = lax.axis_index("row")
    col_index = lax.axis_index("col")
    panel = x0_cols.shape[0]
    start = row_index % group * panel
    block_start = row_index % group * (panel // BLOCK)
    left_zero = masked(
        lax.dynamic_slice_in_dim(x0_rows, start, panel, 1),
        lax.dynamic_slice_in_dim(mask0_rows, block_start, panel // BLOCK, 1),
    )
    left_one = masked(
        lax.dynamic_slice_in_dim(x1_rows, start, panel, 1),
        lax.dynamic_slice_in_dim(mask1_rows, block_start, panel // BLOCK, 1),
    )
    right_zero = masked(x0_cols, mask0_cols)
    right_one = masked(x1_cols, mask1_cols)
    left = jnp.stack([left_zero, left_one])
    right = jnp.stack([right_zero, right_one])
    left_offset = row_index // group % n_col
    right_offset = col_index % n_col
    levels = n_col.bit_length() - 1
    for level in range(levels):
        moved_left = passed_along(left, "col", -(1 << level))
        moved_right = passed_along(right, "row", -group * (1 << level))
        left = jnp.where(left_offset // (1 << level) % 2 == 1, moved_left, left)
        right = jnp.where(right_offset // (1 << level) % 2 == 1, moved_right, right)

    def accumulate(left_now, right_now, square, tangent):
        square = square + jnp.dot(left_now[0], right_now[0], preferred_element_type=jnp.float32)
        tangent = tangent + jnp.dot(left_now[0], right_now[1], preferred_element_type=jnp.float32)
        tangent = tangent + jnp.dot(left_now[1], right_now[0], preferred_element_type=jnp.float32)
        return (square, tangent)

    def section_body(section, carry):
        left_now, right_now, square, tangent = carry
        square, tangent = accumulate(left_now, right_now, square, tangent)
        left_now = passed_along(left_now, "col", -1)
        right_now = passed_along(right_now, "row", -group)
        return (left_now, right_now, square, tangent)

    zeros = jnp.zeros((left_zero.shape[0], right_zero.shape[1]), jnp.float32)
    left, right, square, tangent = lax.fori_loop(
        0, n_col - 1, section_body, (left, right, zeros, zeros)
    )
    square, tangent = accumulate(left, right, square, tangent)
    x_square = masked(square, keep_mask).astype(jnp.bfloat16)
    x_tangent = masked(tangent, keep_mask).astype(jnp.bfloat16)
    return (x_square, x_tangent)


def solution(mesh):
    if mesh.shape["col"] == 2:
        body = functools.partial(per_device_pair, mesh.shape["row"])
    else:
        body = per_device
    return jax.shard_map(
        body,
        mesh=mesh,
        in_specs=(P("row", "col"),) * 9,
        out_specs=(P("row", "col"), P("row", "col")),
        check_vma=False,
    )
```

time: 131 us -> 136 us (1.038)
  waiting for transfers between devices: 51.2 us -> 68.5 us
  starting transfers between devices: 29.5 us -> 21 us
  other arithmetic: 3.93 us -> 0 us
  local copies, waits for them, and re-layouts: 1.54 us -> 5.22 us
  Pallas kernels: 42.6 us -> 39.4 us
    ppermute x17, waiting for transfers between devices: 51.2 us -> 68.5 us  [move(): return lax.ppermute(values, ('row', 'col'), pairs)]
    ppermute x17, starting transfers between devices: 29.5 us -> 21 us  [move(): return lax.ppermute(values, ('row', 'col'), pairs)]
    select_n x4 -> x0, other arithmetic: 3.93 us -> none  [per_device_pair(): jnp.where(is_diag, r, a)]
    unnamed x14 -> x26, local copies, waits for them, and re-layouts: 1.54 us -> 5.22 us
    pallas_call x14 -> x15, Pallas kernels: 35.7 us -> 32.4 us  [the longest x4 14.7 us: partial_products(): pl.pallas_call(partial_kernel, grid=(columns // wide,), in_specs=[SM(), p...]
  transfers between devices with their start and end apart: 17 -> 17, of which waited for: 7 -> 10; matrix products, arithmetic and copies ran while one was open for 3% -> 0% of each run, Pallas kernels for 30% -> 26%
where the time goes in v2:
time: 136 us; the launch traced here: 135 us
  waiting for transfers between devices  68.5 us (50%)
  Pallas kernels  39.4 us (29%)
  starting transfers between devices  21 us (15%)
  local copies, waits for them, and re-layouts  5.22 us (4%)
    ppermute x17, waiting for transfers between devices, move(): return lax.ppermute(values, ('row', 'col'), pairs)  68.5 us
    ppermute x17, starting transfers between devices, move(): return lax.ppermute(values, ('row', 'col'), pairs)  21 us
    pallas_call x4, Pallas kernels, partial_products(): pl.pallas_call(partial_kernel, grid=(columns // wide,), in_specs=[SM(), p...  14.7 us
    pallas_call x4, Pallas kernels, finished(): pl.pallas_call(functools.partial(finish_kernel, start), in_specs=[SM(), V...  7.32 us
    pallas_call x1, Pallas kernels, masked_right(): pl.pallas_call(right_kernel, grid=(depth // tall,), in_specs=[SM(), SM(),...  6.97 us
    pallas_call x1, Pallas kernels, local_products(): pl.pallas_call(functools.partial(local_kernel, many), grid=(columns // wi...  5.37 us
    unnamed x26, local copies, waits for them, and re-layouts  5.22 us
    pallas_call x2, Pallas kernels, masked_chunks(): pl.pallas_call(functools.partial(chunk_kernel, spans, panel, with_slab),...  4.07 us
  transfers between devices with their start and end apart: 17, of which 10 were waited for; matrix products, arithmetic and copies ran while one was open for 0% of the time, Pallas kernels for 26%

profile of v2, /device:TPU:0, one launch (start us, length us, event | category | flops | bytes accessed | tf_op | source)
XLA Modules:
  0.0 135.1 jit_solution(16095052218434125133)
XLA Ops:
  2.0 1.7 %left_chunks.2 = (bf16[64,2048]{1,0:T(8,128)(2,1)S(1)}, bf16[64,2048]{1,0:T(8,128)(2,1)S(1)}) custom-call(s32[1]{0:T(128)} %bitcast.1.refs_0_, s32[1]{0:T(128)} %bitcast.refs_1_.diag, s32[2,128]{1,0:T(2,128)S(1)} %copy-done.8, s32[2,128]{1,0:T(2,128)S(1)} %copy-done.9, bf16[256,16384]{1,0:T(8,128)(2,1)} %refs_4_.3, bf16[256,16384]{1,0:T(8,128)(2,1)} %refs_5_.3), custom_call_target="tpu_custom_call" | custom-call | bytes 16384 | tf_op jit(solution)/shard_map/left_chunks/pallas_call | solution.py:98
  3.8 3.0 %collective-permute-start = (bf16[64,2048]{1,0:T(8,128)(2,1)S(1)}, bf16[64,2048]{1,0:T(8,128)(2,1)S(1)}, u32[]{:S(2)}, u32[]{:S(2)}) collective-permute-start(bf16[64,2048]{1,0:T(8,128)(2,1)S(1)} %get-tuple-element.28.refs_6_), channel_id=1, source_target_pairs={{0,1},{1,0},{2,3},{3,2},{4,5},{5,4},{6,7},{7,6},{8,9},{9,8},{10,11... | collective-permute-start | bytes 786440 | tf_op jit(solution)/shard_map/ppermute | solution.py:378
  6.8 2.3 %left_chunks.3 = (bf16[64,2048]{1,0:T(8,128)(2,1)S(1)}, bf16[64,2048]{1,0:T(8,128)(2,1)S(1)}, bf16[64,2048]{1,0:T(8,128)(2,1)S(1)}, bf16[64,2048]{1,0:T(8,128)(2...) custom-call(s32[1]{0:T(128)} %bitcast.1.refs_0_, ...), custom_call_target="tpu_custom_call" | custom-call | bytes 65536 | tf_op jit(solution)/shard_map/left_chunks/pallas_call | solution.py:98
  9.2 4.0 %collective-permute-done.one.refs_5_ = bf16[64,2048]{1,0:T(8,128)(2,1)S(1)} collective-permute-done((bf16[64,2048]{1,0:T(8,128)(2,1)S(1)}, bf16[64,2048]{1,0:T(8,128)(2,1)S(1)}, u32[]{:S(2)}, u32[]{:S(2)}) %collective-permute-start) | collective-permute-done | bytes 262176 | tf_op jit(solution)/shard_map/ppermute | solution.py:378
  13.8 2.9 %collective-permute-start.2 = (bf16[64,2048]{1,0:T(8,128)(2,1)S(1)}, bf16[64,2048]{1,0:T(8,128)(2,1)S(1)}, u32[]{:S(2)}, u32[]{:S(2)}) collective-permute-start(bf16[64,2048]{1,0:T(8,128)(2,1)S(1)} %get-tuple-element.31.rest_0_), channel_id=1, source_target_pairs={{0,16},{1,17},{2,18},{3,19},{4,20},{5,21},{6,22},{7,23},{8,24},{9,... | collective-permute-start | bytes 786440 | tf_op jit(solution)/shard_map/ppermute | solution.py:378
  18.4 7.0 %right_panels.1 = (bf16[2048,768]{1,0:T(8,128)(2,1)S(1)}, bf16[2048,768]{1,0:T(8,128)(2,1)}) custom-call(s32[16,6]{1,0:T(8,128)S(1)} %copy.17.mask0, s32[16,6]{1,0:T(8,128)S(1)} %copy.18.mask1, bf16[2048,768]{1,0:T(8,128)(2,1)} %x0.1, bf16[2048,768]{1,0:T(8,128)(2,1)} %x1.1, bf16[64,2048]{1,0:T(8,128)(2,1)S(1)} %get-tuple-element.31.rest_0_), custom_call_target="tpu_custom_call" | custom-call | bytes 196608 | tf_op jit(solution)/shard_map/right_panels/pallas_call | solution.py:168
  31.6 11.4 %collective-permute-done.4.refs_1_.near = bf16[64,2048]{1,0:T(8,128)(2,1)S(1)} collective-permute-done((bf16[64,2048]{1,0:T(8,128)(2,1)S(1)}, bf16[64,2048]{1,0:T(8,128)(2,1)S(1)}, u32[]{:S(2)}, u32[]{:S(2)}) %collective-permute-start.4) | collective-permute-done | bytes 262176 | tf_op jit(solution)/shard_map/ppermute | solution.py:378
  43.6 16.2 %collective-permute-done.5.far = bf16[64,2048]{1,0:T(8,128)(2,1)S(1)} collective-permute-done((bf16[64,2048]{1,0:T(8,128)(2,1)S(1)}, bf16[64,2048]{1,0:T(8,128)(2,1)S(1)}, u32[]{:S(2)}, u32[]{:S(2)}) %collective-permute-start.5) | collective-permute-done | bytes 262176 | tf_op jit(solution)/shard_map/ppermute | solution.py:378
  59.9 3.7 %partial_products.4.refs_2_.refs_10_ = s16[784,128]{1,0:T(8,128)(2,1)S(1)} custom-call(s32[1]{0:T(128)} %bitcast.refs_1_.diag, bf16[2048,768]{1,0:T(8,128)(2,1)S(1)} %copy-done.1, bf16[2048,768]{1,0:T(8,128)(2,1)} %get-tuple-element.33.right1, bf16[64,2048]{1,0:T(8,128)(2,1)S(1)} %collective-permute-done.2.refs_2_.near, ...), custom_call_target="tpu_custom_call" | custom-call | flops 9437184 | bytes 106496 | tf_op jit(solution)/shard_map/partial_products/pallas_call | solution.py:275
  63.5 1.9 %collective-permute-done.3.one.refs_7_ = bf16[64,2048]{1,0:T(8,128)(2,1)S(1)} collective-permute-done((bf16[64,2048]{1,0:T(8,128)(2,1)S(1)}, bf16[64,2048]{1,0:T(8,128)(2,1)S(1)}, u32[]{:S(2)}, u32[]{:S(2)}) %collective-permute-start.3) | collective-permute-done | bytes 262176 | tf_op jit(solution)/shard_map/ppermute | solution.py:378
  67.1 2.9 %collective-permute-start.9 = (s16[784,128]{1,0:T(8,128)(2,1)S(1)}, s16[784,128]{1,0:T(8,128)(2,1)S(1)}, u32[]{:S(2)}, u32[]{:S(2)}) collective-permute-start(s16[784,128]{1,0:T(8,128)(2,1)S(1)} %partial_products.4.refs_2_.refs_10_), channel_id=1, source_target_pairs={{0,16},{1,17},{2,18},{3,19},{4,20},{5,21},{6,22},{7,23},{8,24},{9,... | collective-permute-start | bytes 602120 | tf_op jit(solution)/shard_map/ppermute | solution.py:378
  71.1 3.7 %partial_products.5.refs_1_ = s16[784,128]{1,0:T(8,128)(2,1)S(1)} custom-call(s32[1]{0:T(128)} %bitcast.refs_1_.diag, bf16[2048,768]{1,0:T(8,128)(2,1)S(1)} %copy-done.1, bf16[2048,768]{1,0:T(8,128)(2,1)} %get-tuple-element.33.right1, bf16[64,2048]{1,0:T(8,128)(2,1)S(1)} %collective-permute-done.4.refs_1_.near, bf16[64,2048]{1,0:T(8,128)(2,1)S(1)} %collective-permute-done.8.far), custom_call_target="tpu_custom_call" | custom-call | flops 9437184 | bytes 106496 | tf_op jit(solution)/shard_map/partial_products/pallas_call | solution.py:275
  74.8 5.4 %own_products.1 = (f32[256,768]{1,0:T(8,128)S(1)}, f32[256,768]{1,0:T(8,128)S(1)}) custom-call(s32[1]{0:T(128)} %bitcast.refs_1_.diag, bf16[2048,768]{1,0:T(8,128)(2,1)} %copy-done, bf16[2048,768]{1,0:T(8,128)(2,1)} %get-tuple-element.33.right1, bf16[64,2048]{1,0:T(8,128)(2,1)S(1)} %get-tuple-element.29.other.refs_0_, ...), custom_call_target="tpu_custom_call" | custom-call | flops 37748736 | bytes 163840 | tf_op jit(solution)/shard_map/own_products/pallas_call | solution.py:225
  80.2 5.8 %collective-permute-done.9.coded = s16[784,128]{1,0:T(8,128)(2,1)S(1)} collective-permute-done((s16[784,128]{1,0:T(8,128)(2,1)S(1)}, s16[784,128]{1,0:T(8,128)(2,1)S(1)}, u32[]{:S(2)}, u32[]{:S(2)}) %collective-permute-start.9) | collective-permute-done | bytes 200736 | tf_op jit(solution)/shard_map/ppermute | solution.py:378
  86.0 1.8 %finish.4 = (bf16[256,768]{1,0:T(8,128)(2,1)}, bf16[256,768]{1,0:T(8,128)(2,1)}) custom-call(s32[2,6]{1,0:T(2,128)S(1)} %copy-done.7, s16[784,128]{1,0:T(8,128)(2,1)S(1)} %collective-permute-done.9.coded, f32[256,768]{1,0:T(8,128)S(1)} %get-tuple-element.46.square, f32[256,768]{1,0:T(8,128)S(1)} %get-tuple-element.47.tangent), custom_call_target="tpu_custom_call" | custom-call | bytes 12288 | tf_op jit(solution)/shard_map/finish/pallas_call | solution.py:337
  89.8 10.7 %collective-permute-done.11.near = bf16[64,2048]{1,0:T(8,128)(2,1)S(1)} collective-permute-done((bf16[64,2048]{1,0:T(8,128)(2,1)S(1)}, bf16[64,2048]{1,0:T(8,128)(2,1)S(1)}, u32[]{:S(2)}, u32[]{:S(2)}) %collective-permute-start.11) | collective-permute-done | bytes 262176 | tf_op jit(solution)/shard_map/ppermute | solution.py:378
  101.6 3.7 %partial_products.6.refs_0_ = s16[784,128]{1,0:T(8,128)(2,1)S(1)} custom-call(s32[1]{0:T(128)} %bitcast.refs_1_.diag, bf16[2048,768]{1,0:T(8,128)(2,1)S(1)} %copy-done.2, bf16[2048,768]{1,0:T(8,128)(2,1)} %get-tuple-element.33.right1, bf16[64,2048]{1,0:T(8,128)(2,1)S(1)} %collective-permute-done.7.refs_0_.near, bf16[64,2048]{1,0:T(8,128)(2,1)S(1)} %collective-permute-done.13.far), custom_call_target="tpu_custom_call" | custom-call | flops 9437184 | bytes 106496 | tf_op jit(solution)/shard_map/partial_products/pallas_call | solution.py:275
  105.3 3.0 %collective-permute-start.16 = (s16[784,128]{1,0:T(8,128)(2,1)S(1)}, s16[784,128]{1,0:T(8,128)(2,1)S(1)}, u32[]{:S(2)}, u32[]{:S(2)}) collective-permute-start(s16[784,128]{1,0:T(8,128)(2,1)S(1)} %partial_products.6.refs_0_), channel_id=1, source_target_pairs={{0,16},{1,17},{2,18},{3,19},{4,20},{5,21},{6,22},{7,23},{8,24},{9,... | collective-permute-start | bytes 602120 | tf_op jit(solution)/shard_map/ppermute | solution.py:378
  108.3 7.5 %collective-permute-done.14.coded = s16[784,128]{1,0:T(8,128)(2,1)S(1)} collective-permute-done((s16[784,128]{1,0:T(8,128)(2,1)S(1)}, s16[784,128]{1,0:T(8,128)(2,1)S(1)}, u32[]{:S(2)}, u32[]{:S(2)}) %collective-permute-start.14) | collective-permute-done | bytes 200736 | tf_op jit(solution)/shard_map/ppermute | solution.py:378
  115.8 1.8 %finish.5 = (bf16[256,768]{1,0:T(8,128)(2,1)}, bf16[256,768]{1,0:T(8,128)(2,1)}) custom-call(s32[2,6]{1,0:T(2,128)S(1)} %copy-done.7, s16[784,128]{1,0:T(8,128)(2,1)S(1)} %collective-permute-done.14.coded, f32[256,768]{1,0:T(8,128)S(1)} %get-tuple-element.46.square, ...), custom_call_target="tpu_custom_call", output_to_operand_aliasing={{0}: (4, {}), {1}: (5, {})} | custom-call | bytes 12288 | tf_op jit(solution)/shard_map/finish/pallas_call | solution.py:337
  118.6 3.7 %partial_products.7 = s16[784,128]{1,0:T(8,128)(2,1)S(1)} custom-call(s32[1]{0:T(128)} %bitcast.refs_1_.diag, bf16[2048,768]{1,0:T(8,128)(2,1)S(1)} %copy-done.2, bf16[2048,768]{1,0:T(8,128)(2,1)} %get-tuple-element.33.right1, bf16[64,2048]{1,0:T(8,128)(2,1)S(1)} %collective-permute-done.11.near, bf16[64,2048]{1,0:T(8,128)(2,1)S(1)} %collective-permute-done.12.far, ...), custom_call_target="tpu_custom_call" | custom-call | flops 9437184 | bytes 106496 | tf_op jit(solution)/shard_map/partial_products/pallas_call | solution.py:275
  122.4 1.8 %finish.6 = (bf16[256,768]{1,0:T(8,128)(2,1)}, bf16[256,768]{1,0:T(8,128)(2,1)}) custom-call(s32[2,6]{1,0:T(2,128)S(1)} %copy-done.7, s16[784,128]{1,0:T(8,128)(2,1)S(1)} %collective-permute-done.16.coded, f32[256,768]{1,0:T(8,128)S(1)} %get-tuple-element.46.square, ...), custom_call_target="tpu_custom_call", output_to_operand_aliasing={{0}: (4, {}), {1}: (5, {})} | custom-call | bytes 12288 | tf_op jit(solution)/shard_map/finish/pallas_call | solution.py:337
  124.2 9.0 %collective-permute-done.15.coded = s16[784,128]{1,0:T(8,128)(2,1)S(1)} collective-permute-done((s16[784,128]{1,0:T(8,128)(2,1)S(1)}, s16[784,128]{1,0:T(8,128)(2,1)S(1)}, u32[]{:S(2)}, u32[]{:S(2)}) %collective-permute-start.15) | collective-permute-done | bytes 200736 | tf_op jit(solution)/shard_map/ppermute | solution.py:378
  133.2 1.8 %finish.7 = (bf16[256,768]{1,0:T(8,128)(2,1)}, bf16[256,768]{1,0:T(8,128)(2,1)}) custom-call(s32[2,6]{1,0:T(2,128)S(1)} %copy-done.7, s16[784,128]{1,0:T(8,128)(2,1)S(1)} %collective-permute-done.15.coded, f32[256,768]{1,0:T(8,128)S(1)} %get-tuple-element.46.square, ...), custom_call_target="tpu_custom_call", output_to_operand_aliasing={{0}: (4, {}), {1}: (5, {})} | custom-call | bytes 12288 | tf_op jit(solution)/shard_map/finish/pallas_call | solution.py:337
  (52 shorter events, 17.4 us)
Async XLA Ops:
  3.8 14.5 %copy-start.10 = (s32[16,6]{0,1:T(8,128)S(1)}, s32[16,6]{0,1:T(8,128)}, u32[]{:S(2)}) copy-start(s32[16,6]{0,1:T(8,128)} %param.15) | copy-start | bytes 1156
  3.8 14.6 %copy-start.11 = (s32[16,6]{0,1:T(8,128)S(1)}, s32[16,6]{0,1:T(8,128)}, u32[]{:S(2)}) copy-start(s32[16,6]{0,1:T(8,128)} %param.16) | copy-start | bytes 1156
  3.8 9.3 %collective-permute-start = (bf16[64,2048]{1,0:T(8,128)(2,1)S(1)}, bf16[64,2048]{1,0:T(8,128)(2,1)S(1)}, u32[]{:S(2)}, u32[]{:S(2)}) collective-permute-start(bf16[64,2048]{1,0:T(8,128)(2,1)S(1)} %get-tuple-element.28.refs_6_), channel_id=1, source_target_pairs={{0,1},{1,0},{2,3},{3,2},{4,5},{5,4},{6,7},{7,6},{8,9},{9,8},{10,11... | collective-permute-start | bytes 786440 | tf_op jit(solution)/shard_map/ppermute | solution.py:378
  9.1 7.6 %copy-start.5 = (bf16[64,2048]{1,0:T(8,128)(2,1)}, bf16[64,2048]{1,0:T(8,128)(2,1)S(1)}, u32[]{:S(2)}) copy-start(bf16[64,2048]{1,0:T(8,128)(2,1)S(1)} %get-tuple-element.36.refs_0_) | copy-start | bytes 786436
  13.8 14.1 %collective-permute-start.2 = (bf16[64,2048]{1,0:T(8,128)(2,1)S(1)}, bf16[64,2048]{1,0:T(8,128)(2,1)S(1)}, u32[]{:S(2)}, u32[]{:S(2)}) collective-permute-start(bf16[64,2048]{1,0:T(8,128)(2,1)S(1)} %get-tuple-element.31.rest_0_), channel_id=1, source_target_pairs={{0,16},{1,17},{2,18},{3,19},{4,20},{5,21},{6,22},{7,23},{8,24},{9,... | collective-permute-start | bytes 786440 | tf_op jit(solution)/shard_map/ppermute | solution.py:378
  16.7 11.2 %collective-permute-start.1 = (bf16[64,2048]{1,0:T(8,128)(2,1)}, bf16[64,2048]{1,0:T(8,128)(2,1)S(1)}, u32[]{:S(2)}, u32[]{:S(2)}) collective-permute-start(bf16[64,2048]{1,0:T(8,128)(2,1)} %get-tuple-element.34), channel_id=1, source_target_pairs={{0,1},{1,0},{2,3},{3,2},{4,5},{5,4},{6,7},{7,6},{8,9},{9,8},{10,11... | collective-permute-start | bytes 786440 | tf_op jit(solution)/shard_map/ppermute | solution.py:378
  18.4 9.5 %copy-start.6 = (bf16[64,2048]{1,0:T(8,128)(2,1)S(1)}, bf16[64,2048]{1,0:T(8,128)(2,1)}, u32[]{:S(2)}) copy-start(bf16[64,2048]{1,0:T(8,128)(2,1)} %copy-done.5) | copy-start | bytes 786436
  27.9 32.0 %copy-start.1 = (bf16[2048,768]{1,0:T(8,128)(2,1)S(1)}, bf16[2048,768]{1,0:T(8,128)(2,1)}, u32[]{:S(2)}) copy-start(bf16[2048,768]{1,0:T(8,128)(2,1)} %copy-done) | copy-start | bytes 9437188
  28.1 46.7 %collective-permute-start.10 = (bf16[256,2048]{1,0:T(8,128)(2,1)S(1)}, bf16[256,2048]{1,0:T(8,128)(2,1)S(1)}, u32[]{:S(2)}, u32[]{:S(2)}) collective-permute-start(bf16[256,2048]{1,0:T(8,128)(2,1)S(1)} %get-tuple-element.45.refs_4_), channel_id=1, source_target_pairs={{0,1},{1,0},{2,3},{3,2},{4,5},{5,4},{6,7},{7,6},{8,9},{9,8},{10,11... | collective-permute-start | bytes 3145736 | tf_op jit(solution)/shard_map/ppermute | solution.py:378
  29.6 13.4 %collective-permute-start.4 = (bf16[64,2048]{1,0:T(8,128)(2,1)S(1)}, bf16[64,2048]{1,0:T(8,128)(2,1)S(1)}, u32[]{:S(2)}, u32[]{:S(2)}) collective-permute-start(bf16[64,2048]{1,0:T(8,128)(2,1)S(1)} %get-tuple-element.41), channel_id=1, source_target_pairs={{0,16},{1,17},{2,18},{3,19},{4,20},{5,21},{6,22},{7,23},{8,24},{9,... | collective-permute-start | bytes 786440 | tf_op jit(solution)/shard_map/ppermute | solution.py:378
  29.6 30.3 %collective-permute-start.5 = (bf16[64,2048]{1,0:T(8,128)(2,1)S(1)}, bf16[64,2048]{1,0:T(8,128)(2,1)S(1)}, u32[]{:S(2)}, u32[]{:S(2)}) collective-permute-start(bf16[64,2048]{1,0:T(8,128)(2,1)S(1)} %collective-permute-done.2.refs_2_.near), channel_id=1, source_target_pairs={{0,1},{1,0},{2,3},{3,2},{4,5},{5,4},{6,7},{7,6},{8,9},{9,8},{10,11... | collective-permute-start | bytes 786440 | tf_op jit(solution)/shard_map/ppermute | solution.py:378
  30.2 35.3 %collective-permute-start.3 = (bf16[64,2048]{1,0:T(8,128)(2,1)S(1)}, bf16[64,2048]{1,0:T(8,128)(2,1)S(1)}, u32[]{:S(2)}, u32[]{:S(2)}) collective-permute-start(bf16[64,2048]{1,0:T(8,128)(2,1)S(1)} %get-tuple-element.38), channel_id=1, source_target_pairs={{0,1},{1,0},{2,3},{3,2},{4,5},{5,4},{6,7},{7,6},{8,9},{9,8},{10,11... | collective-permute-start | bytes 786440 | tf_op jit(solution)/shard_map/ppermute | solution.py:378
  43.0 28.1 %collective-permute-start.8 = (bf16[64,2048]{1,0:T(8,128)(2,1)S(1)}, bf16[64,2048]{1,0:T(8,128)(2,1)S(1)}, u32[]{:S(2)}, u32[]{:S(2)}) collective-permute-start(bf16[64,2048]{1,0:T(8,128)(2,1)S(1)} %collective-permute-done.4.refs_1_.near), channel_id=1, source_target_pairs={{0,1},{1,0},{2,3},{3,2},{4,5},{5,4},{6,7},{7,6},{8,9},{9,8},{10,11... | collective-permute-start | bytes 786440 | tf_op jit(solution)/shard_map/ppermute | solution.py:378
  65.6 9.2 %collective-permute-start.6 = (bf16[64,2048]{1,0:T(8,128)(2,1)S(1)}, bf16[64,2048]{1,0:T(8,128)(2,1)S(1)}, u32[]{:S(2)}, u32[]{:S(2)}) collective-permute-start(bf16[64,2048]{1,0:T(8,128)(2,1)S(1)} %get-tuple-element.42), channel_id=1, source_target_pairs={{0,1},{1,0},{2,3},{3,2},{4,5},{5,4},{6,7},{7,6},{8,9},{9,8},{10,11... | collective-permute-start | bytes 786440 | tf_op jit(solution)/shard_map/ppermute | solution.py:378
  67.0 20.8 %collective-permute-start.7 = (bf16[64,2048]{1,0:T(8,128)(2,1)S(1)}, bf16[64,2048]{1,0:T(8,128)(2,1)S(1)}, u32[]{:S(2)}, u32[]{:S(2)}) collective-permute-start(bf16[64,2048]{1,0:T(8,128)(2,1)S(1)} %get-tuple-element.44), channel_id=1, source_target_pairs={{0,16},{1,17},{2,18},{3,19},{4,20},{5,21},{6,22},{7,23},{8,24},{9,... | collective-permute-start | bytes 786440 | tf_op jit(solution)/shard_map/ppermute | solution.py:378
  67.1 19.0 %collective-permute-start.9 = (s16[784,128]{1,0:T(8,128)(2,1)S(1)}, s16[784,128]{1,0:T(8,128)(2,1)S(1)}, u32[]{:S(2)}, u32[]{:S(2)}) collective-permute-start(s16[784,128]{1,0:T(8,128)(2,1)S(1)} %partial_products.4.refs_2_.refs_10_), channel_id=1, source_target_pairs={{0,16},{1,17},{2,18},{3,19},{4,20},{5,21},{6,22},{7,23},{8,24},{9,... | collective-permute-start | bytes 602120 | tf_op jit(solution)/shard_map/ppermute | solution.py:378
  74.8 11.2 %copy-start.7 = (s32[2,6]{1,0:T(2,128)S(1)}, s32[2,6]{1,0:T(2,128)}, u32[]{:S(2)}) copy-start(s32[2,6]{1,0:T(2,128)} %keep.7) | copy-start | bytes 148
  80.2 21.4 %copy-start.2 = (bf16[2048,768]{1,0:T(8,128)(2,1)S(1)}, bf16[2048,768]{1,0:T(8,128)(2,1)}, u32[]{:S(2)}) copy-start(bf16[2048,768]{1,0:T(8,128)(2,1)} %copy-done) | copy-start | bytes 9437188
  88.9 11.6 %collective-permute-start.11 = (bf16[64,2048]{1,0:T(8,128)(2,1)S(1)}, bf16[64,2048]{1,0:T(8,128)(2,1)S(1)}, u32[]{:S(2)}, u32[]{:S(2)}) collective-permute-start(bf16[64,2048]{1,0:T(8,128)(2,1)S(1)} %to_send.7), channel_id=1, source_target_pairs={{0,16},{1,17},{2,18},{3,19},{4,20},{5,21},{6,22},{7,23},{8,24},{9,... | collective-permute-start | bytes 786440 | tf_op jit(solution)/shard_map/ppermute | solution.py:378
  89.0 12.6 %collective-permute-start.13 = (bf16[64,2048]{1,0:T(8,128)(2,1)S(1)}, bf16[64,2048]{1,0:T(8,128)(2,1)S(1)}, u32[]{:S(2)}, u32[]{:S(2)}) collective-permute-start(bf16[64,2048]{1,0:T(8,128)(2,1)S(1)} %collective-permute-done.7.refs_0_.near), channel_id=1, source_target_pairs={{0,1},{1,0},{2,3},{3,2},{4,5},{5,4},{6,7},{7,6},{8,9},{9,8},{10,11... | collective-permute-start | bytes 786440 | tf_op jit(solution)/shard_map/ppermute | solution.py:378
  100.6 17.1 %collective-permute-start.12 = (bf16[64,2048]{1,0:T(8,128)(2,1)S(1)}, bf16[64,2048]{1,0:T(8,128)(2,1)S(1)}, u32[]{:S(2)}, u32[]{:S(2)}) collective-permute-start(bf16[64,2048]{1,0:T(8,128)(2,1)S(1)} %collective-permute-done.11.near), channel_id=1, source_target_pairs={{0,1},{1,0},{2,3},{3,2},{4,5},{5,4},{6,7},{7,6},{8,9},{9,8},{10,11... | collective-permute-start | bytes 786440 | tf_op jit(solution)/shard_map/ppermute | solution.py:378
  101.6 14.2 %collective-permute-start.14 = (s16[784,128]{1,0:T(8,128)(2,1)S(1)}, s16[784,128]{1,0:T(8,128)(2,1)S(1)}, u32[]{:S(2)}, u32[]{:S(2)}) collective-permute-start(s16[784,128]{1,0:T(8,128)(2,1)S(1)} %partial_products.5.refs_1_), channel_id=1, source_target_pairs={{0,16},{1,17},{2,18},{3,19},{4,20},{5,21},{6,22},{7,23},{8,24},{9,... | collective-permute-start | bytes 602120 | tf_op jit(solution)/shard_map/ppermute | solution.py:378
  105.3 17.1 %collective-permute-start.16 = (s16[784,128]{1,0:T(8,128)(2,1)S(1)}, s16[784,128]{1,0:T(8,128)(2,1)S(1)}, u32[]{:S(2)}, u32[]{:S(2)}) collective-permute-start(s16[784,128]{1,0:T(8,128)(2,1)S(1)} %partial_products.6.refs_0_), channel_id=1, source_target_pairs={{0,16},{1,17},{2,18},{3,19},{4,20},{5,21},{6,22},{7,23},{8,24},{9,... | collective-permute-start | bytes 602120 | tf_op jit(solution)/shard_map/ppermute | solution.py:378
  122.3 10.9 %collective-permute-start.15 = (s16[784,128]{1,0:T(8,128)(2,1)S(1)}, s16[784,128]{1,0:T(8,128)(2,1)S(1)}, u32[]{:S(2)}, u32[]{:S(2)}) collective-permute-start(s16[784,128]{1,0:T(8,128)(2,1)S(1)} %partial_products.7), channel_id=1, source_target_pairs={{0,16},{1,17},{2,18},{3,19},{4,20},{5,21},{6,22},{7,23},{8,24},{9,... | collective-permute-start | bytes 602120 | tf_op jit(solution)/shard_map/ppermute | solution.py:378
  (5 other events, 5.0 us)

commit v3 on v2

--- a/solution.py
+++ b/solution.py
@@ -36,12 +36,12 @@
     return [(lo // BLOCK, slice(lo - start, hi - start)) for lo, hi in zip(edges, edges[1:])]
 
 
-def chunk_kernel(spans, panel, with_slab, *refs):
+def chunk_kernel(spans, slabs, panel, *refs):
     place, diag, mask0, mask1, x0, x1 = refs[:6]
     held, sems = refs[-2:]
-    many = 2 * len(spans) + with_slab
+    many = 2 * len(spans) + len(slabs)
     outs = refs[-2 - many : -2]
-    slab = outs[-1] if with_slab else None
+    with_slab = len(slabs) > 0
     blocks = panel // BLOCK
     first = place[0] * blocks
     at = pl.ds(pl.multiple_of(place[0] * panel, BLOCK), panel)
@@ -56,47 +56,45 @@
             )
     for copy in copies:
         copy.start()
+    for copy in copies:
+        copy.wait()
+    for n, (lo, hi) in enumerate(slabs):
+        for row_block, piece in row_pieces(lo, hi - lo):
+            rows = slice(piece.start + lo, piece.stop + lo)
+            for j in range(blocks):
+                cut = slice(j * BLOCK, (j + 1) * BLOCK)
+                product = scaled(held[1, rows, cut], mask1[row_block, first + j])
+                outs[2 * len(spans) + n][piece, cut] = product
     for n, (lo, hi) in enumerate(spans):
         a_out, swap = outs[2 * n], outs[2 * n + 1]
-        copies[2 * n].wait()
-        copies[2 * n + 1].wait()
-        if with_slab:
-            top = origin if n == 0 else lo
-            for row_block, piece in row_pieces(top, hi - top):
-                rows = slice(piece.start + top, piece.stop + top)
-                for j in range(blocks):
-                    cut = slice(j * BLOCK, (j + 1) * BLOCK)
-                    slab[rows, cut] = scaled(held[1, rows, cut], mask1[row_block, first + j])
         for row_block, piece in row_pieces(lo, hi - lo):
             rows = slice(piece.start + lo - origin, piece.stop + lo - origin)
             for j in range(blocks):
                 cut = slice(j * BLOCK, (j + 1) * BLOCK)
                 a_out[piece, cut] = scaled(held[0, rows, cut], mask0[row_block, first + j])
-            if not with_slab:
+
+        @pl.when(diag[0] == 1)
+        def _():
+            swap[...] = a_out[...]
+
+        @pl.when(diag[0] == 0)
+        def _():
+            for row_block, piece in row_pieces(lo, hi - lo):
+                rows = slice(piece.start + lo - origin, piece.stop + lo - origin)
                 for j in range(blocks):
                     cut = slice(j * BLOCK, (j + 1) * BLOCK)
                     swap[piece, cut] = scaled(held[1, rows, cut], mask1[row_block, first + j])
 
-        @pl.when(diag[0] == 1)
-        def _():
-            swap[...] = a_out[...]
-
-        if with_slab:
-
-            @pl.when(diag[0] == 0)
-            def _():
-                swap[...] = slab[lo:hi]
-
-
-def masked_chunks(place, diag, mask0, mask1, x0, x1, spans, panel, with_slab, after=()):
+
+def masked_chunks(place, diag, mask0, mask1, x0, x1, spans, slabs, panel, after=()):
     outs = []
     for lo, hi in spans:
         outs += [jax.ShapeDtypeStruct((hi - lo, panel), x0.dtype)] * 2
-    high = spans[-1][1] - (0 if with_slab else spans[0][0])
-    if with_slab:
-        outs.append(jax.ShapeDtypeStruct((spans[-1][1], panel), x0.dtype))
-    return pl.pallas_call(
-        functools.partial(chunk_kernel, spans, panel, with_slab),
+    for lo, hi in slabs:
+        outs.append(jax.ShapeDtypeStruct((hi - lo, panel), x0.dtype))
+    high = spans[-1][1] - (0 if slabs else spans[0][0])
+    return pl.pallas_call(
+        functools.partial(chunk_kernel, spans, slabs, panel),
         in_specs=[SM(), SM(), SM(), SM(), HB(), HB()] + [HB() for _ in after],
         out_specs=[VM() for _ in outs],
         out_shape=outs,
@@ -210,16 +208,16 @@
 
 
 def local_kernel(many, diag, right0, right1, *refs):
-    own, got = refs[: many + 1], refs[many + 1 : 2 * many + 2]
+    own, got = refs[:many], refs[many : 2 * many]
     square, tangent, held, sems = refs[-4:]
     fetch_left(diag, own, got, held, sems)
     square[...], tangent[...] = both_products(held, right0, right1)
 
 
 def local_products(diag, own, got, right0, right1, wide, after=()):
-    rows, depth = own[-1].shape
-    columns = right0.shape[1]
-    many = len(own) - 1
+    rows = sum(piece.shape[0] for piece in own) // 2
+    depth, columns = right0.shape
+    many = len(own)
     out = jax.ShapeDtypeStruct((rows, columns), jnp.float32)
     tile = pl.BlockSpec((rows, wide), lambda g: (0, g))
     return pl.pallas_call(
@@ -235,7 +233,7 @@
         out_shape=[out, out],
         scratch_shapes=[
             pltpu.VMEM((2 * rows, depth), own[-1].dtype),
-            pltpu.SemaphoreType.DMA((many + 1,)),
+            pltpu.SemaphoreType.DMA((many,)),
         ],
         compiler_params=params(),
         cost_estimate=cost(6 * rows * depth * columns, 8 * rows * depth + 4 * depth * columns),
@@ -243,13 +241,14 @@
     )(diag, right0, right1, *own, *got, *after)
 
 
-def partial_kernel(diag, right0, right1, near, far, *refs):
+def partial_kernel(many, diag, right0, right1, *refs):
+    near, far = refs[:many], refs[many : 2 * many]
     out, held, steps, sems = refs[-4:]
-    rows, wide = near.shape[0], right0.shape[1]
+    rows, wide = held.shape[0] // 2, right0.shape[1]
     step = pl.program_id(0)
     tiles = wide // BLOCK
     across = pl.num_programs(0) * tiles
-    fetch_left(diag, (near, far), (far, near), held, sems)
+    fetch_left(diag, near + far, far + near, held, sems)
     for which, values in enumerate(both_products(held, right0, right1)):
         top = jnp.maximum(jnp.max(jnp.abs(values), axis=0, keepdims=True), 1e-30)
         level = jnp.ceil(jnp.log(top) * (STEPS / LN2)) + 1.0
@@ -268,88 +267,84 @@
 
 
 def partial_products(diag, near, far, right0, right1, wide, after=()):
-    rows, depth = near.shape
-    columns = right0.shape[1]
+    rows = sum(piece.shape[0] for piece in near)
+    depth, columns = right0.shape
     tiles = 2 * columns // BLOCK
     tail = -(-tiles // 16) * 16
     return pl.pallas_call(
-        partial_kernel,
+        functools.partial(partial_kernel, len(near)),
         grid=(columns // wide,),
         in_specs=[
             SM(),
             pl.BlockSpec((depth, wide), lambda g: (0, g)),
             pl.BlockSpec((depth, wide), lambda g: (0, g)),
-            HB(),
-            HB(),
         ]
-        + [HB() for _ in after],
+        + [HB() for _ in (*near, *far, *after)],
         out_specs=pl.BlockSpec((tiles * rows + tail, BLOCK), lambda g: (0, 0)),
         out_shape=jax.ShapeDtypeStruct((tiles * rows + tail, BLOCK), jnp.int16),
         scratch_shapes=[
-            pltpu.VMEM((2 * rows, depth), near.dtype),
+            pltpu.VMEM((2 * rows, depth), near[0].dtype),
             pltpu.VMEM((tail, BLOCK), jnp.float32),
-            pltpu.SemaphoreType.DMA((2,)),
+            pltpu.SemaphoreType.DMA((2 * len(near),)),
         ],
         compiler_params=params(),
         cost_estimate=cost(6 * rows * depth * columns, 4 * rows * depth + 4 * depth * columns),
         name="partial_products",
-    )(diag, right0, right1, near, far, *after)
-
-
-def finish_kernel(start, keep, coded, square, tangent, *rest):
-    out0, out1, mine, made, in_sems, out_sems = rest[-6:]
-    rows, columns = mine.shape[1:]
+    )(diag, right0, right1, *near, *far, *after)
+
+
+def finish_kernel(start, many, keep, coded, square, tangent, *rest):
+    given, outs, passed = rest[:many], rest[-5 - many : -3 - many], rest[-3 - many : -3]
+    made, out_sems, sems = rest[-3:]
+    rows, columns = square.shape
     across = columns // BLOCK
-    at = pl.ds(start, rows)
-    arrivals = [
-        pltpu.make_async_copy(x.at[at], mine.at[i], in_sems.at[i])
-        for i, x in enumerate((square, tangent))
+    others = [
+        pltpu.make_async_copy(x, y, sems.at[i]) for i, (x, y) in enumerate(zip(given, passed))
     ]
     results = [
-        pltpu.make_async_copy(made.at[i], x.at[at], out_sems.at[i])
-        for i, x in enumerate((out0, out1))
+        pltpu.make_async_copy(made.at[i], x.at[pl.ds(start, rows)], out_sems.at[i])
+        for i, x in enumerate(outs)
     ]
-    for copy in arrivals:
+    for copy in others:
         copy.start()
     tail = coded.shape[0] - 2 * across * rows
     levels = coded[coded.shape[0] - tail :, :].astype(jnp.int32).astype(jnp.float32)
     steps = jnp.exp(levels * (LN2 / STEPS)) * (1.0 / LEVELS)
-    for which in range(2):
-        arrivals[which].wait()
+    for which, mine in enumerate((square, tangent)):
         for j in range(across):
             tile = which * across + j
             cut = slice(j * BLOCK, (j + 1) * BLOCK)
             other = coded[tile * rows : (tile + 1) * rows, :].astype(jnp.int32).astype(jnp.float32)
-            total = mine[which, :, cut] + other * steps[tile : tile + 1, :]
+            total = mine[:, cut] + other * steps[tile : tile + 1, :]
             for row_block, piece in row_pieces(start, rows):
                 kept = total[piece] * keep[row_block, j].astype(jnp.float32)
                 made[which, piece, cut] = kept.astype(made.dtype)
         results[which].start()
-    for copy in results:
-        copy.wait()
-
-
-def finished(keep, square, tangent, coded, before, start, stop):
-    rows = stop - start
-    columns = square.shape[1]
-    out = jax.ShapeDtypeStruct(square.shape, jnp.bfloat16)
-    handed = [] if before is None else list(before)
-    return pl.pallas_call(
-        functools.partial(finish_kernel, start),
-        in_specs=[SM(), VM(), HB(), HB()] + [HB() for _ in handed],
-        out_specs=[HB(), HB()],
-        out_shape=[out, out],
-        input_output_aliases={4: 0, 5: 1} if handed else {},
+    for copy in results + others:
+        copy.wait()
+
+
+def finished(keep, square, tangent, coded, before, start, all_rows, held=(), after=()):
+    rows, columns = square.shape
+    out = jax.ShapeDtypeStruct((all_rows, columns), jnp.bfloat16)
+    held, before = list(held), list(before)
+    passed = [jax.ShapeDtypeStruct(x.shape, x.dtype) for x in held]
+    many = len(held)
+    return pl.pallas_call(
+        functools.partial(finish_kernel, start, many),
+        in_specs=[SM(), VM(), VM(), VM()] + [HB() for _ in (*held, *before, *after)],
+        out_specs=[HB() for _ in range(2 + many)],
+        out_shape=[out, out] + passed,
+        input_output_aliases={4 + many: 0, 5 + many: 1} if before else {},
         scratch_shapes=[
-            pltpu.VMEM((2, rows, columns), jnp.float32),
             pltpu.VMEM((2, rows, columns), jnp.bfloat16),
             pltpu.SemaphoreType.DMA((2,)),
-            pltpu.SemaphoreType.DMA((2,)),
+            pltpu.SemaphoreType.DMA((max(many, 1),)),
         ],
         compiler_params=params(),
         cost_estimate=cost(0, 16 * rows * columns),
         name="finish",
-    )(keep, coded, square, tangent, *handed)
+    )(keep, coded, square, tangent, *held, *before, *after)
 
 
 def per_device_pair(
@@ -363,8 +358,10 @@
     half = row_index // group
     diag = (half == lax.axis_index("col")).astype(jnp.int32).reshape(1)
     place = (row_index % group).astype(jnp.int32).reshape(1)
-    edges = [all_rows * e // 8 for e in (0, 2, 4, 6, 8)]
+    edges = [all_rows * e // 8 for e in (0, 1, 3, 5, 8)]
     spans = list(zip(edges, edges[1:]))
+    many = len(spans)
+    split = edges[-2]
     wide = 256
 
     def device(h, q, c):
@@ -377,54 +374,45 @@
     def move(values, pairs):
         return lax.ppermute(values, ("row", "col"), pairs)
 
-    def chunks(spans, with_slab, after=()):
+    def chunks(spans, slabs, after=()):
         return masked_chunks(
-            place, diag, mask0_rows, mask1_rows, x0_rows, x1_rows, spans, panel, with_slab, after
+            place, diag, mask0_rows, mask1_rows, x0_rows, x1_rows, spans, slabs, panel, after
         )
 
-    def product(i, after=()):
-        return partial_products(diag, near[i], far[i], right0, right1, wide, after)
-
-    many = len(spans)
-    a, swap, passed, near, far, coded, back = ([None] * many for _ in range(7))
-    a[0], swap[0] = chunks(spans[:1], False)
-    *rest, own_b = chunks(spans[1:], True, (swap[0],))
+    def partials(which, after=()):
+        return partial_products(diag, near[which], far[which], right0, right1, wide, after)
+
+    def own(which, b, got, after=()):
+        mine, other = (*a[which], b), (*passed[which], got)
+        return local_products(diag, mine, other, right0, right1, wide, after)
+
+    a, swap, passed, near, far = ([None] * many for _ in range(5))
+    a[0], swap[0] = chunks(spans[:1], ())
+    *rest, top_b, low_b = chunks(spans[1:], ((0, split), (split, all_rows)), (swap[0],))
     a[1:], swap[1:] = rest[0::2], rest[1::2]
-    right0 = right1 = square = tangent = got_b = outs = None
+    right0 = right1 = None
     for i in range(many):
         passed[i] = move(swap[i], over_y)
-        gate = [near[i - 1]] if i else []
+        last = i == many - 1
+        held = (top_b,) if last else (swap[i + 1],)
+        gate = {1: (near[0],), 2: (right0,), 3: (far[0], far[1])}.get(i, ())
+        send, later = chosen(diag, passed[i], a[i], held, gate)
+        if last:
+            top_b = later
+        else:
+            swap[i + 1] = later
+        near[i] = move(send, over_z)
+        far[i] = move(near[i], over_y)
         if i == 1:
-            gate.append(right0)
-        if i >= 2:
-            gate.append(coded[i - 2])
-        if i == many - 1:
-            square, tangent = local_products(
-                diag, (*a, own_b), (*passed, got_b), right0, right1, wide, (coded[0],)
-            )
-            outs = finished(keep, square, tangent, back[0], None, *spans[0])
-            gate.append(outs[0])
-        held = swap[i + 1 : i + 2] + ([own_b] if i == 1 else [])
-        send, *held = chosen(diag, passed[i], a[i], held, gate)
-        if i < many - 1:
-            swap[i + 1] = held[0]
-        near[i] = move(send, over_z)
-        if i == 0:
             right0, right1 = masked_right(mask0_cols, mask1_cols, x0_cols, x1_cols, (send,))
-        if i == 1:
-            own_b = held[1]
-            got_b = move(own_b, over_y)
-        if i >= 1:
-            far[i - 1] = move(near[i - 1], over_y)
-            coded[i - 1] = product(i - 1)
-            back[i - 1] = move(coded[i - 1], over_z)
-    outs = finished(keep, square, tangent, back[1], outs, *spans[1])
-    far[many - 1] = move(near[many - 1], over_y)
-    coded[many - 1] = product(many - 1, (coded[many - 2], outs[0]))
-    back[many - 1] = move(coded[many - 1], over_z)
-    for i in range(2, many):
-        outs = finished(keep, square, tangent, back[i], outs, *spans[i])
-    return tuple(outs)
+    early, late = slice(0, many - 1), slice(many - 1, many)
+    back = move(partials(early), over_z)
+    square, tangent = own(early, top_b, move(top_b, over_y))
+    coded = partials(late)
+    *outs, low_b = finished(keep, square, tangent, back, (), 0, all_rows, (low_b,), (coded,))
+    back = move(coded, over_z)
+    square, tangent = own(late, low_b, move(low_b, over_y))
+    return tuple(finished(keep, square, tangent, back, outs, split, all_rows))
 
 
 def passed_along(shard, axis, by):

time: 136 us -> 109 us (0.80)
  waiting for transfers between devices: 68.5 us -> 52.8 us
  Pallas kernels: 39.4 us -> 34.2 us
  starting transfers between devices: 21 us -> 18 us
  local copies, waits for them, and re-layouts: 5.22 us -> 2.22 us
    ppermute x17 -> x16, waiting for transfers between devices: 68.5 us -> 52.8 us  [move(): return lax.ppermute(values, ('row', 'col'), pairs)]
    pallas_call x10 -> x6, Pallas kernels: 26.1 us -> 16.7 us  [the longest x2 9.41 us: partial_products(): pl.pallas_call(functools.partial(partial_kernel, len(near)), grid=(column...]
    pallas_call x1 -> x2, Pallas kernels: 5.37 us -> 9 us  [local_products(): pl.pallas_call(functools.partial(local_kernel, many), grid=(columns // wi...]
    ppermute x17 -> x16, starting transfers between devices: 21 us -> 18 us  [move(): return lax.ppermute(values, ('row', 'col'), pairs)]
    unnamed x26 -> x16, local copies, waits for them, and re-layouts: 5.22 us -> 2.22 us
  transfers between devices with their start and end apart: 17 -> 16, of which waited for: 10 -> 8; matrix products, arithmetic and copies ran while one was open for 0% -> 1% of each run, Pallas kernels for 26% -> 27%
where the time goes in v3:
time: 109 us; the launch traced here: 108 us
  waiting for transfers between devices  52.8 us (48%)
  Pallas kernels  34.2 us (31%)
  starting transfers between devices  18 us (17%)
  local copies, waits for them, and re-layouts  2.22 us (2%)
    ppermute x16, waiting for transfers between devices, move(): return lax.ppermute(values, ('row', 'col'), pairs)  52.8 us
    ppermute x16, starting transfers between devices, move(): return lax.ppermute(values, ('row', 'col'), pairs)  18 us
    pallas_call x2, Pallas kernels, partial_products(): pl.pallas_call(functools.partial(partial_kernel, len(near)), grid=(column...  9.41 us
    pallas_call x2, Pallas kernels, local_products(): pl.pallas_call(functools.partial(local_kernel, many), grid=(columns // wi...  9 us
    pallas_call x1, Pallas kernels, masked_right(): pl.pallas_call(right_kernel, grid=(depth // tall,), in_specs=[SM(), SM(),...  6.91 us
    pallas_call x2, Pallas kernels, masked_chunks(): pl.pallas_call(functools.partial(chunk_kernel, spans, slabs, panel), in_s...  4.28 us
    pallas_call x2, Pallas kernels, finished(): pl.pallas_call(functools.partial(finish_kernel, start, many), in_specs=[S...  3.03 us
    unnamed x16, local copies, waits for them, and re-layouts  2.22 us
  transfers between devices with their start and end apart: 16, of which 8 were waited for; matrix products, arithmetic and copies ran while one was open for 1% of the time, Pallas kernels for 27%

profile of v3, /device:TPU:0, one launch (start us, length us, event | category | flops | bytes accessed | tf_op | source)
XLA Modules:
  0.0 108.1 jit_solution(1933294899455806640)
XLA Ops:
  2.0 1.6 %left_chunks.2 = (bf16[32,2048]{1,0:T(8,128)(2,1)S(1)}, bf16[32,2048]{1,0:T(8,128)(2,1)S(1)}) custom-call(s32[1]{0:T(128)} %bitcast.1.refs_0_, s32[1]{0:T(128)} %bitcast.refs_1_.diag, s32[2,128]{1,0:T(2,128)S(1)} %copy-done.2, s32[2,128]{1,0:T(2,128)S(1)} %copy-done.3, bf16[256,16384]{1,0:T(8,128)(2,1)} %refs_4_.3, bf16[256,16384]{1,0:T(8,128)(2,1)} %refs_5_.3), custom_call_target="tpu_custom_call" | custom-call | bytes 8192 | tf_op jit(solution)/shard_map/left_chunks/pallas_call | solution.py:96
  3.6 3.0 %collective-permute-start = (bf16[32,2048]{1,0:T(8,128)(2,1)S(1)}, bf16[32,2048]{1,0:T(8,128)(2,1)S(1)}, u32[]{:S(2)}, u32[]{:S(2)}) collective-permute-start(bf16[32,2048]{1,0:T(8,128)(2,1)S(1)} %get-tuple-element.29.refs_6_), channel_id=1, source_target_pairs={{0,1},{1,0},{2,3},{3,2},{4,5},{5,4},{6,7},{7,6},{8,9},{9,8},{10,11... | collective-permute-start | bytes 393224 | tf_op jit(solution)/shard_map/ppermute | solution.py:375
  6.7 2.7 %left_chunks.3 = (bf16[64,2048]{1,0:T(8,128)(2,1)S(1)}, bf16[64,2048]{1,0:T(8,128)(2,1)S(1)}, bf16[64,2048]{1,0:T(8,128)(2,1)S(1)}, bf16[64,2048]{1,0:T(8,128)(2...) custom-call(s32[1]{0:T(128)} %bitcast.1.refs_0_, ...), custom_call_target="tpu_custom_call" | custom-call | bytes 65536 | tf_op jit(solution)/shard_map/left_chunks/pallas_call | solution.py:96
  10.4 1.8 %collective-permute-start.1 = (bf16[64,2048]{1,0:T(8,128)(2,1)S(1)}, bf16[64,2048]{1,0:T(8,128)(2,1)S(1)}, u32[]{:S(2)}, u32[]{:S(2)}) collective-permute-start(bf16[64,2048]{1,0:T(8,128)(2,1)S(1)} %get-tuple-element.32), channel_id=1, source_target_pairs={{0,1},{1,0},{2,3},{3,2},{4,5},{5,4},{6,7},{7,6},{8,9},{9,8},{10,11... | collective-permute-start | bytes 786440 | tf_op jit(solution)/shard_map/ppermute | solution.py:375
  12.2 2.6 %collective-permute-start.2 = (bf16[32,2048]{1,0:T(8,128)(2,1)S(1)}, bf16[32,2048]{1,0:T(8,128)(2,1)S(1)}, u32[]{:S(2)}, u32[]{:S(2)}) collective-permute-start(bf16[32,2048]{1,0:T(8,128)(2,1)S(1)} %get-tuple-element.35), channel_id=1, source_target_pairs={{0,16},{1,17},{2,18},{3,19},{4,20},{5,21},{6,22},{7,23},{8,24},{9,... | collective-permute-start | bytes 393224 | tf_op jit(solution)/shard_map/ppermute | solution.py:375
  14.8 5.2 %collective-permute-done.2.refs_1_.refs_0_ = bf16[32,2048]{1,0:T(8,128)(2,1)S(1)} collective-permute-done((bf16[32,2048]{1,0:T(8,128)(2,1)S(1)}, bf16[32,2048]{1,0:T(8,128)(2,1)S(1)}, u32[]{:S(2)}, u32[]{:S(2)}) %collective-permute-start.2) | collective-permute-done | bytes 131104 | tf_op jit(solution)/shard_map/ppermute | solution.py:375
  21.4 1.3 %collective-permute-start.6 = (bf16[64,2048]{1,0:T(8,128)(2,1)S(1)}, bf16[64,2048]{1,0:T(8,128)(2,1)}, u32[]{:S(2)}, u32[]{:S(2)}) collective-permute-start(bf16[64,2048]{1,0:T(8,128)(2,1)S(1)} %get-tuple-element.36.rest_0_), channel_id=1, source_target_pairs={{0,16},{1,17},{2,18},{3,19},{4,20},{5,21},{6,22},{7,23},{8,24},{9,... | collective-permute-start | bytes 786440 | tf_op jit(solution)/shard_map/ppermute | solution.py:375
  23.6 6.9 %right_panels.1 = (bf16[2048,768]{1,0:T(8,128)(2,1)S(1)}, bf16[2048,768]{1,0:T(8,128)(2,1)}) custom-call(s32[16,6]{1,0:T(8,128)S(1)} %copy.13.mask0, s32[16,6]{1,0:T(8,128)S(1)} %copy.14.mask1, bf16[2048,768]{1,0:T(8,128)(2,1)} %x0.1, bf16[2048,768]{1,0:T(8,128)(2,1)} %x1.1, bf16[64,2048]{1,0:T(8,128)(2,1)S(1)} %get-tuple-element.36.rest_0_), custom_call_target="tpu_custom_call" | custom-call | bytes 196608 | tf_op jit(solution)/shard_map/right_panels/pallas_call | solution.py:166
  31.7 1.9 %collective-permute-done.6.refs_1_ = bf16[64,2048]{1,0:T(8,128)(2,1)} collective-permute-done((bf16[64,2048]{1,0:T(8,128)(2,1)S(1)}, bf16[64,2048]{1,0:T(8,128)(2,1)}, u32[]{:S(2)}, u32[]{:S(2)}) %collective-permute-start.6) | collective-permute-done | bytes 262176 | tf_op jit(solution)/shard_map/ppermute | solution.py:375
  33.6 1.3 %collective-permute-start.7 = (bf16[64,2048]{1,0:T(8,128)(2,1)}, bf16[64,2048]{1,0:T(8,128)(2,1)S(1)}, u32[]{:S(2)}, u32[]{:S(2)}) collective-permute-start(bf16[64,2048]{1,0:T(8,128)(2,1)} %collective-permute-done.6.refs_1_), channel_id=1, source_target_pairs={{0,1},{1,0},{2,3},{3,2},{4,5},{5,4},{6,7},{7,6},{8,9},{9,8},{10,11... | collective-permute-start | bytes 786440 | tf_op jit(solution)/shard_map/ppermute | solution.py:375
  35.9 11.9 %collective-permute-done.5.refs_1_.refs_3_ = bf16[32,2048]{1,0:T(8,128)(2,1)S(1)} collective-permute-done((bf16[32,2048]{1,0:T(8,128)(2,1)S(1)}, bf16[32,2048]{1,0:T(8,128)(2,1)S(1)}, u32[]{:S(2)}, u32[]{:S(2)}) %collective-permute-start.5) | collective-permute-done | bytes 131104 | tf_op jit(solution)/shard_map/ppermute | solution.py:375
  48.2 1.3 %collective-permute-start.8 = (bf16[96,2048]{1,0:T(8,128)(2,1)S(1)}, bf16[96,2048]{1,0:T(8,128)(2,1)S(1)}, u32[]{:S(2)}, u32[]{:S(2)}) collective-permute-start(bf16[96,2048]{1,0:T(8,128)(2,1)S(1)} %get-tuple-element.45), channel_id=1, source_target_pairs={{0,16},{1,17},{2,18},{3,19},{4,20},{5,21},{6,22},{7,23},{8,24},{9,... | collective-permute-start | bytes 1179656 | tf_op jit(solution)/shard_map/ppermute | solution.py:375
  49.5 1.3 %collective-permute-start.12 = (bf16[64,2048]{1,0:T(8,128)(2,1)S(1)}, bf16[64,2048]{1,0:T(8,128)(2,1)S(1)}, u32[]{:S(2)}, u32[]{:S(2)}) collective-permute-start(bf16[64,2048]{1,0:T(8,128)(2,1)S(1)} %collective-permute-done.11.refs_2_), channel_id=1, source_target_pairs={{0,1},{1,0},{2,3},{3,2},{4,5},{5,4},{6,7},{7,6},{8,9},{9,8},{10,11... | collective-permute-start | bytes 786440 | tf_op jit(solution)/shard_map/ppermute | solution.py:375
  51.5 7.2 %collective-permute-done.12.refs_5_ = bf16[64,2048]{1,0:T(8,128)(2,1)S(1)} collective-permute-done((bf16[64,2048]{1,0:T(8,128)(2,1)S(1)}, bf16[64,2048]{1,0:T(8,128)(2,1)S(1)}, u32[]{:S(2)}, u32[]{:S(2)}) %collective-permute-start.12) | collective-permute-done | bytes 262176 | tf_op jit(solution)/shard_map/ppermute | solution.py:375
  58.7 5.3 %partial_products.3 = s16[1936,128]{1,0:T(8,128)(2,1)S(1)} custom-call(s32[1]{0:T(128)} %bitcast.refs_1_.diag, bf16[2048,768]{1,0:T(8,128)(2,1)S(1)} %get-tuple-element.37.refs_1_.right0, bf16[2048,768]{1,0:T(8,128)(2,1)} %get-tuple-element.38.right1, bf16[32,2048]{1,0:T(8,128)(2,1)S(1)} %collective-permute-done.2.refs_1_.refs_0_, ...), custom_call_target="tpu_custom_call" | custom-call | flops 23592960 | bytes 118784 | tf_op jit(solution)/shard_map/partial_products/pallas_call | solution.py:274
  64.0 2.0 %collective-permute-start.13 = (s16[1936,128]{1,0:T(8,128)(2,1)S(1)}, s16[1936,128]{1,0:T(8,128)(2,1)S(1)}, u32[]{:S(2)}, u32[]{:S(2)}) collective-permute-start(s16[1936,128]{1,0:T(8,128)(2,1)S(1)} %partial_products.3), channel_id=1, source_target_pairs={{0,16},{1,17},{2,18},{3,19},{4,20},{5,21},{6,22},{7,23},{8,24},{9,... | collective-permute-start | bytes 1486856 | tf_op jit(solution)/shard_map/ppermute | solution.py:375
  66.0 14.1 %collective-permute-done.8.refs_0_ = bf16[96,2048]{1,0:T(8,128)(2,1)S(1)} collective-permute-done((bf16[96,2048]{1,0:T(8,128)(2,1)S(1)}, bf16[96,2048]{1,0:T(8,128)(2,1)S(1)}, u32[]{:S(2)}, u32[]{:S(2)}) %collective-permute-start.8) | collective-permute-done | bytes 393248 | tf_op jit(solution)/shard_map/ppermute | solution.py:375
  80.1 5.0 %own_products.2 = (f32[160,768]{1,0:T(8,128)S(1)}, f32[160,768]{1,0:T(8,128)S(1)}) custom-call(s32[1]{0:T(128)} %bitcast.refs_1_.diag, bf16[2048,768]{1,0:T(8,128)(2,1)} %copy-done, bf16[2048,768]{1,0:T(8,128)(2,1)} %get-tuple-element.38.right1, bf16[32,2048]{1,0:T(8,128)(2,1)S(1)} %get-tuple-element.30.other.refs_0_, ...), custom_call_target="tpu_custom_call" | custom-call | flops 23592960 | bytes 139264 | tf_op jit(solution)/shard_map/own_products/pallas_call | solution.py:223
  85.0 4.0 %collective-permute-done.9.refs_1_ = bf16[96,2048]{1,0:T(8,128)(2,1)S(1)} collective-permute-done((bf16[96,2048]{1,0:T(8,128)(2,1)S(1)}, bf16[96,2048]{1,0:T(8,128)(2,1)S(1)}, u32[]{:S(2)}, u32[]{:S(2)}) %collective-permute-start.9) | collective-permute-done | bytes 393248 | tf_op jit(solution)/shard_map/ppermute | solution.py:375
  89.0 4.1 %partial_products.2.rest_1_ = s16[1168,128]{1,0:T(8,128)(2,1)S(1)} custom-call(s32[1]{0:T(128)} %bitcast.refs_1_.diag, bf16[2048,768]{1,0:T(8,128)(2,1)S(1)} %copy-done.1, bf16[2048,768]{1,0:T(8,128)(2,1)} %get-tuple-element.38.right1, bf16[96,2048]{1,0:T(8,128)(2,1)S(1)} %collective-permute-done.8.refs_0_, bf16[96,2048]{1,0:T(8,128)(2,1)S(1)} %collective-permute-done.9.refs_1_), custom_call_target="tpu_custom_call" | custom-call | flops 14155776 | bytes 110592 | tf_op jit(solution)/shard_map/partial_products/pallas_call | solution.py:274
  93.1 1.7 %finish.2 = (bf16[256,768]{1,0:T(8,128)(2,1)}, bf16[256,768]{1,0:T(8,128)(2,1)}, bf16[96,2048]{1,0:T(8,128)(2,1)S(1)}) custom-call(s32[2,6]{1,0:T(2,128)S(1)} %copy-done.5, s16[1936,128]{1,0:T(8,128)(2,1)S(1)} %collective-permute-done.13.coded, f32[160,768]{1,0:T(8,128)S(1)} %get-tuple-element.48.square, f32[160,768]{1,0:T(8,128)S(1)} %get-tuple-element.49.tangent, ...), custom_call_target="tpu_custom_call" | custom-call | bytes 30720 | tf_op jit(solution)/shard_map/finish/pallas_call | solution.py:333
  95.0 7.7 %collective-permute-done.15.refs_3_ = bf16[96,2048]{1,0:T(8,128)(2,1)S(1)} collective-permute-done((bf16[96,2048]{1,0:T(8,128)(2,1)S(1)}, bf16[96,2048]{1,0:T(8,128)(2,1)S(1)}, u32[]{:S(2)}, u32[]{:S(2)}) %collective-permute-start.15) | collective-permute-done | bytes 393248 | tf_op jit(solution)/shard_map/ppermute | solution.py:375
  102.7 4.0 %own_products.3 = (f32[96,768]{1,0:T(8,128)S(1)}, f32[96,768]{1,0:T(8,128)S(1)}) custom-call(s32[1]{0:T(128)} %bitcast.refs_1_.diag, bf16[2048,768]{1,0:T(8,128)(2,1)S(1)} %copy-done.1, bf16[2048,768]{1,0:T(8,128)(2,1)} %get-tuple-element.38.right1, bf16[96,2048]{1,0:T(8,128)(2,1)S(1)} %get-tuple-element.43.other.refs_0_, ...), custom_call_target="tpu_custom_call" | custom-call | flops 14155776 | bytes 122880 | tf_op jit(solution)/shard_map/own_products/pallas_call | solution.py:223
  106.7 1.4 %finish.3 = (bf16[256,768]{1,0:T(8,128)(2,1)}, bf16[256,768]{1,0:T(8,128)(2,1)}) custom-call(s32[2,6]{1,0:T(2,128)S(1)} %copy-done.5, s16[1168,128]{1,0:T(8,128)(2,1)S(1)} %collective-permute-done.10.coded, f32[96,768]{1,0:T(8,128)S(1)} %get-tuple-element.52.square, ...), custom_call_target="tpu_custom_call", output_to_operand_aliasing={{0}: (4, {}), {1}: (5, {})} | custom-call | bytes 18432 | tf_op jit(solution)/shard_map/finish/pallas_call | solution.py:333
  (37 shorter events, 8.0 us)
Async XLA Ops:
  0.7 0.7 copy-start.2
  1.3 0.7 copy-start.3
  2.0 4.7 %copy-start.4 = (s32[2,128]{1,0:T(2,128)S(1)}, s32[2,128]{1,0:T(2,128)}, u32[]{:S(2)}) copy-start(s32[2,128]{1,0:T(2,128)} %refs_3_.3) | copy-start | bytes 3076
  3.6 19.1 %copy-start.6 = (s32[16,6]{0,1:T(8,128)S(1)}, s32[16,6]{0,1:T(8,128)}, u32[]{:S(2)}) copy-start(s32[16,6]{0,1:T(8,128)} %param.15) | copy-start | bytes 1156
  3.6 6.5 %collective-permute-start = (bf16[32,2048]{1,0:T(8,128)(2,1)S(1)}, bf16[32,2048]{1,0:T(8,128)(2,1)S(1)}, u32[]{:S(2)}, u32[]{:S(2)}) collective-permute-start(bf16[32,2048]{1,0:T(8,128)(2,1)S(1)} %get-tuple-element.29.refs_6_), channel_id=1, source_target_pairs={{0,1},{1,0},{2,3},{3,2},{4,5},{5,4},{6,7},{7,6},{8,9},{9,8},{10,11... | collective-permute-start | bytes 393224 | tf_op jit(solution)/shard_map/ppermute | solution.py:375
  10.4 9.6 %collective-permute-start.1 = (bf16[64,2048]{1,0:T(8,128)(2,1)S(1)}, bf16[64,2048]{1,0:T(8,128)(2,1)S(1)}, u32[]{:S(2)}, u32[]{:S(2)}) collective-permute-start(bf16[64,2048]{1,0:T(8,128)(2,1)S(1)} %get-tuple-element.32), channel_id=1, source_target_pairs={{0,1},{1,0},{2,3},{3,2},{4,5},{5,4},{6,7},{7,6},{8,9},{9,8},{10,11... | collective-permute-start | bytes 786440 | tf_op jit(solution)/shard_map/ppermute | solution.py:375
  12.2 7.8 %collective-permute-start.2 = (bf16[32,2048]{1,0:T(8,128)(2,1)S(1)}, bf16[32,2048]{1,0:T(8,128)(2,1)S(1)}, u32[]{:S(2)}, u32[]{:S(2)}) collective-permute-start(bf16[32,2048]{1,0:T(8,128)(2,1)S(1)} %get-tuple-element.35), channel_id=1, source_target_pairs={{0,16},{1,17},{2,18},{3,19},{4,20},{5,21},{6,22},{7,23},{8,24},{9,... | collective-permute-start | bytes 393224 | tf_op jit(solution)/shard_map/ppermute | solution.py:375
  20.7 9.8 %collective-permute-start.3 = (bf16[64,2048]{1,0:T(8,128)(2,1)}, bf16[64,2048]{1,0:T(8,128)(2,1)S(1)}, u32[]{:S(2)}, u32[]{:S(2)}) collective-permute-start(bf16[64,2048]{1,0:T(8,128)(2,1)} %get-tuple-element.39), channel_id=1, source_target_pairs={{0,1},{1,0},{2,3},{3,2},{4,5},{5,4},{6,7},{7,6},{8,9},{9,8},{10,11... | collective-permute-start | bytes 786440 | tf_op jit(solution)/shard_map/ppermute | solution.py:375
  21.4 12.2 %collective-permute-start.6 = (bf16[64,2048]{1,0:T(8,128)(2,1)S(1)}, bf16[64,2048]{1,0:T(8,128)(2,1)}, u32[]{:S(2)}, u32[]{:S(2)}) collective-permute-start(bf16[64,2048]{1,0:T(8,128)(2,1)S(1)} %get-tuple-element.36.rest_0_), channel_id=1, source_target_pairs={{0,16},{1,17},{2,18},{3,19},{4,20},{5,21},{6,22},{7,23},{8,24},{9,... | collective-permute-start | bytes 786440 | tf_op jit(solution)/shard_map/ppermute | solution.py:375
  30.5 33.5 %copy-start = (bf16[2048,768]{1,0:T(8,128)(2,1)}, bf16[2048,768]{1,0:T(8,128)(2,1)S(1)}, u32[]{:S(2)}) copy-start(bf16[2048,768]{1,0:T(8,128)(2,1)S(1)} %get-tuple-element.37.refs_1_.right0) | copy-start | bytes 9437188
  30.8 17.0 %collective-permute-start.4 = (bf16[96,2048]{1,0:T(8,128)(2,1)S(1)}, bf16[96,2048]{1,0:T(8,128)(2,1)S(1)}, u32[]{:S(2)}, u32[]{:S(2)}) collective-permute-start(bf16[96,2048]{1,0:T(8,128)(2,1)S(1)} %get-tuple-element.42), channel_id=1, source_target_pairs={{0,1},{1,0},{2,3},{3,2},{4,5},{5,4},{6,7},{7,6},{8,9},{9,8},{10,11... | collective-permute-start | bytes 1179656 | tf_op jit(solution)/shard_map/ppermute | solution.py:375
  33.6 14.2 %collective-permute-start.7 = (bf16[64,2048]{1,0:T(8,128)(2,1)}, bf16[64,2048]{1,0:T(8,128)(2,1)S(1)}, u32[]{:S(2)}, u32[]{:S(2)}) collective-permute-start(bf16[64,2048]{1,0:T(8,128)(2,1)} %collective-permute-done.6.refs_1_), channel_id=1, source_target_pairs={{0,1},{1,0},{2,3},{3,2},{4,5},{5,4},{6,7},{7,6},{8,9},{9,8},{10,11... | collective-permute-start | bytes 786440 | tf_op jit(solution)/shard_map/ppermute | solution.py:375
  34.9 14.5 %collective-permute-start.11 = (bf16[64,2048]{1,0:T(8,128)(2,1)S(1)}, bf16[64,2048]{1,0:T(8,128)(2,1)S(1)}, u32[]{:S(2)}, u32[]{:S(2)}) collective-permute-start(bf16[64,2048]{1,0:T(8,128)(2,1)S(1)} %get-tuple-element.46), channel_id=1, source_target_pairs={{0,16},{1,17},{2,18},{3,19},{4,20},{5,21},{6,22},{7,23},{8,24},{9,... | collective-permute-start | bytes 786440 | tf_op jit(solution)/shard_map/ppermute | solution.py:375
  34.9 12.9 %collective-permute-start.5 = (bf16[32,2048]{1,0:T(8,128)(2,1)S(1)}, bf16[32,2048]{1,0:T(8,128)(2,1)S(1)}, u32[]{:S(2)}, u32[]{:S(2)}) collective-permute-start(bf16[32,2048]{1,0:T(8,128)(2,1)S(1)} %collective-permute-done.2.refs_1_.refs_0_), channel_id=1, source_target_pairs={{0,1},{1,0},{2,3},{3,2},{4,5},{5,4},{6,7},{7,6},{8,9},{9,8},{10,11... | collective-permute-start | bytes 393224 | tf_op jit(solution)/shard_map/ppermute | solution.py:375
  48.2 31.9 %collective-permute-start.8 = (bf16[96,2048]{1,0:T(8,128)(2,1)S(1)}, bf16[96,2048]{1,0:T(8,128)(2,1)S(1)}, u32[]{:S(2)}, u32[]{:S(2)}) collective-permute-start(bf16[96,2048]{1,0:T(8,128)(2,1)S(1)} %get-tuple-element.45), channel_id=1, source_target_pairs={{0,16},{1,17},{2,18},{3,19},{4,20},{5,21},{6,22},{7,23},{8,24},{9,... | collective-permute-start | bytes 1179656 | tf_op jit(solution)/shard_map/ppermute | solution.py:375
  49.5 9.2 %collective-permute-start.12 = (bf16[64,2048]{1,0:T(8,128)(2,1)S(1)}, bf16[64,2048]{1,0:T(8,128)(2,1)S(1)}, u32[]{:S(2)}, u32[]{:S(2)}) collective-permute-start(bf16[64,2048]{1,0:T(8,128)(2,1)S(1)} %collective-permute-done.11.refs_2_), channel_id=1, source_target_pairs={{0,1},{1,0},{2,3},{3,2},{4,5},{5,4},{6,7},{7,6},{8,9},{9,8},{10,11... | collective-permute-start | bytes 786440 | tf_op jit(solution)/shard_map/ppermute | solution.py:375
  50.8 29.3 %collective-permute-start.14 = (bf16[160,2048]{1,0:T(8,128)(2,1)S(1)}, bf16[160,2048]{1,0:T(8,128)(2,1)S(1)}, u32[]{:S(2)}, u32[]{:S(2)}) collective-permute-start(bf16[160,2048]{1,0:T(8,128)(2,1)S(1)} %get-tuple-element.47.refs_3_), channel_id=1, source_target_pairs={{0,1},{1,0},{2,3},{3,2},{4,5},{5,4},{6,7},{7,6},{8,9},{9,8},{10,11... | collective-permute-start | bytes 1966088 | tf_op jit(solution)/shard_map/ppermute | solution.py:375
  64.0 29.1 %collective-permute-start.13 = (s16[1936,128]{1,0:T(8,128)(2,1)S(1)}, s16[1936,128]{1,0:T(8,128)(2,1)S(1)}, u32[]{:S(2)}, u32[]{:S(2)}) collective-permute-start(s16[1936,128]{1,0:T(8,128)(2,1)S(1)} %partial_products.3), channel_id=1, source_target_pairs={{0,16},{1,17},{2,18},{3,19},{4,20},{5,21},{6,22},{7,23},{8,24},{9,... | collective-permute-start | bytes 1486856 | tf_op jit(solution)/shard_map/ppermute | solution.py:375
  66.0 23.0 %copy-start.1 = (bf16[2048,768]{1,0:T(8,128)(2,1)S(1)}, bf16[2048,768]{1,0:T(8,128)(2,1)}, u32[]{:S(2)}) copy-start(bf16[2048,768]{1,0:T(8,128)(2,1)} %copy-done) | copy-start | bytes 9437188
  80.0 8.9 %collective-permute-start.9 = (bf16[96,2048]{1,0:T(8,128)(2,1)S(1)}, bf16[96,2048]{1,0:T(8,128)(2,1)S(1)}, u32[]{:S(2)}, u32[]{:S(2)}) collective-permute-start(bf16[96,2048]{1,0:T(8,128)(2,1)S(1)} %collective-permute-done.8.refs_0_), channel_id=1, source_target_pairs={{0,1},{1,0},{2,3},{3,2},{4,5},{5,4},{6,7},{7,6},{8,9},{9,8},{10,11... | collective-permute-start | bytes 1179656 | tf_op jit(solution)/shard_map/ppermute | solution.py:375
  85.0 8.1 %copy-start.5 = (s32[2,6]{1,0:T(2,128)S(1)}, s32[2,6]{1,0:T(2,128)}, u32[]{:S(2)}) copy-start(s32[2,6]{1,0:T(2,128)} %keep.3) | copy-start | bytes 148
  94.8 7.8 %collective-permute-start.15 = (bf16[96,2048]{1,0:T(8,128)(2,1)S(1)}, bf16[96,2048]{1,0:T(8,128)(2,1)S(1)}, u32[]{:S(2)}, u32[]{:S(2)}) collective-permute-start(bf16[96,2048]{1,0:T(8,128)(2,1)S(1)} %get-tuple-element.51.refs_1_), channel_id=1, source_target_pairs={{0,1},{1,0},{2,3},{3,2},{4,5},{5,4},{6,7},{7,6},{8,9},{9,8},{10,11... | collective-permute-start | bytes 1179656 | tf_op jit(solution)/shard_map/ppermute | solution.py:375
  94.9 11.8 %collective-permute-start.10 = (s16[1168,128]{1,0:T(8,128)(2,1)S(1)}, s16[1168,128]{1,0:T(8,128)(2,1)S(1)}, u32[]{:S(2)}, u32[]{:S(2)}) collective-permute-start(s16[1168,128]{1,0:T(8,128)(2,1)S(1)} %partial_products.2.rest_1_), channel_id=1, source_target_pairs={{0,16},{1,17},{2,18},{3,19},{4,20},{5,21},{6,22},{7,23},{8,24},{9,... | collective-permute-start | bytes 897032 | tf_op jit(solution)/shard_map/ppermute | solution.py:375

commit v4 on v3

--- a/solution.py
+++ b/solution.py
@@ -23,8 +23,10 @@
     return pltpu.CompilerParams(vmem_limit_bytes=VMEM_BYTES)
 
 
-def cost(flops, moved):
-    return pl.CostEstimate(flops=int(flops) // 64, bytes_accessed=int(moved) // 64, transcendentals=0)
+def cost(flops, moved, weight=1 / 64):
+    return pl.CostEstimate(
+        flops=int(flops * weight), bytes_accessed=int(moved * weight), transcendentals=0
+    )
 
 
 def scaled(values, entry):
@@ -37,10 +39,16 @@
 
 
 def chunk_kernel(spans, slabs, panel, *refs):
-    place, diag, mask0, mask1, x0, x1 = refs[:6]
-    held, sems = refs[-2:]
+    place, diag, mask0_far, mask1_far, x0, x1 = refs[:6]
+    held, mask0, mask1, mask_sems, sems = refs[-5:]
     many = 2 * len(spans) + len(slabs)
-    outs = refs[-2 - many : -2]
+    outs = refs[-5 - many : -5]
+    masks = [
+        pltpu.make_async_copy(mask0_far, mask0, mask_sems.at[0]),
+        pltpu.make_async_copy(mask1_far, mask1, mask_sems.at[1]),
+    ]
+    for copy in masks:
+        copy.start()
     with_slab = len(slabs) > 0
     blocks = panel // BLOCK
     first = place[0] * blocks
@@ -56,7 +64,7 @@
             )
     for copy in copies:
         copy.start()
-    for copy in copies:
+    for copy in masks + copies:
         copy.wait()
     for n, (lo, hi) in enumerate(slabs):
         for row_block, piece in row_pieces(lo, hi - lo):
@@ -95,11 +103,14 @@
     high = spans[-1][1] - (0 if slabs else spans[0][0])
     return pl.pallas_call(
         functools.partial(chunk_kernel, spans, slabs, panel),
-        in_specs=[SM(), SM(), SM(), SM(), HB(), HB()] + [HB() for _ in after],
+        in_specs=[SM(), SM()] + [HB() for _ in range(4 + len(after))],
         out_specs=[VM() for _ in outs],
         out_shape=outs,
         scratch_shapes=[
             pltpu.VMEM((2, high, panel), x0.dtype),
+            pltpu.SMEM(mask0.shape, mask0.dtype),
+            pltpu.SMEM(mask1.shape, mask1.dtype),
+            pltpu.SemaphoreType.DMA((2,)),
             pltpu.SemaphoreType.DMA((len(spans), 2)),
         ],
         compiler_params=params(),
@@ -108,8 +119,9 @@
     )(place, diag, mask0, mask1, x0, x1, *after)
 
 
-def choose_kernel(many, diag, one, other, *refs):
-    held, outs, sems = refs[:many], refs[-many - 2 : -1], refs[-1]
+def choose_kernel(gates, many, diag, *refs):
+    one, other = refs[gates : gates + 2]
+    held, outs, sems = refs[gates + 2 : gates + 2 + many], refs[-many - 2 : -1], refs[-1]
     others = [
         pltpu.make_async_copy(x, out, sems.at[1 + i])
         for i, (x, out) in enumerate(zip(held, outs[1:]))
@@ -136,15 +148,34 @@
 def chosen(diag, one, other, held=(), after=()):
     outs = [jax.ShapeDtypeStruct(x.shape, x.dtype) for x in (one, *held)]
     return pl.pallas_call(
-        functools.partial(choose_kernel, len(held)),
-        in_specs=[SM(), HB(), HB()] + [HB() for _ in (*held, *after)],
+        functools.partial(choose_kernel, len(after), len(held)),
+        in_specs=[SM()] + [HB() for _ in (*after, one, other, *held)],
         out_specs=[HB() for _ in outs],
         out_shape=outs,
         scratch_shapes=[pltpu.SemaphoreType.DMA((len(outs),))],
         compiler_params=params(),
         cost_estimate=cost(0, 4 * one.size),
         name="to_send",
-    )(diag, one, other, *held, *after)
+    )(diag, *after, one, other, *held)
+
+
+def hand_kernel(one, gate, out, sem):
+    copy = pltpu.make_async_copy(one, out, sem)
+    copy.start()
+    copy.wait()
+
+
+def handed_on(one, gate):
+    return pl.pallas_call(
+        hand_kernel,
+        in_specs=[HB(), HB()],
+        out_specs=HB(),
+        out_shape=jax.ShapeDtypeStruct(one.shape, one.dtype),
+        scratch_shapes=[pltpu.SemaphoreType.DMA],
+        compiler_params=params(),
+        cost_estimate=cost(0, 4 * one.size),
+        name="handed_on",
+    )(one, gate)
 
 
 def right_kernel(mask0, mask1, x0, x1, *rest):
@@ -241,9 +272,20 @@
     )(diag, right0, right1, *own, *got, *after)
 
 
-def partial_kernel(many, diag, right0, right1, *refs):
+def partial_kernel(many, given, diag, right0, right1, *refs):
     near, far = refs[:many], refs[many : 2 * many]
-    out, held, steps, sems = refs[-4:]
+    out, passed = refs[-5 - given], refs[-4 - given : -4]
+    held, steps, sems, hand_sems = refs[-4:]
+    others = [
+        pltpu.make_async_copy(x, y, hand_sems.at[i])
+        for i, (x, y) in enumerate(zip(refs[2 * many : 2 * many + given], passed))
+    ]
+
+    @pl.when(pl.program_id(0) == 0)
+    def _():
+        for copy in others:
+            copy.start()
+
     rows, wide = held.shape[0] // 2, right0.shape[1]
     step = pl.program_id(0)
     tiles = wide // BLOCK
@@ -264,33 +306,40 @@
     def _():
         tail = steps.shape[0]
         out[out.shape[0] - tail :, :] = steps[...].astype(jnp.int32).astype(jnp.int16)
-
-
-def partial_products(diag, near, far, right0, right1, wide, after=()):
+        for copy in others:
+            copy.wait()
+
+
+def partial_products(diag, near, far, right0, right1, wide, given=(), weight=1 / 64):
     rows = sum(piece.shape[0] for piece in near)
     depth, columns = right0.shape
     tiles = 2 * columns // BLOCK
     tail = -(-tiles // 16) * 16
     return pl.pallas_call(
-        functools.partial(partial_kernel, len(near)),
+        functools.partial(partial_kernel, len(near), len(given)),
         grid=(columns // wide,),
         in_specs=[
             SM(),
             pl.BlockSpec((depth, wide), lambda g: (0, g)),
             pl.BlockSpec((depth, wide), lambda g: (0, g)),
         ]
-        + [HB() for _ in (*near, *far, *after)],
-        out_specs=pl.BlockSpec((tiles * rows + tail, BLOCK), lambda g: (0, 0)),
-        out_shape=jax.ShapeDtypeStruct((tiles * rows + tail, BLOCK), jnp.int16),
+        + [HB() for _ in (*near, *far, *given)],
+        out_specs=[pl.BlockSpec((tiles * rows + tail, BLOCK), lambda g: (0, 0))]
+        + [HB() for _ in given],
+        out_shape=[jax.ShapeDtypeStruct((tiles * rows + tail, BLOCK), jnp.int16)]
+        + [jax.ShapeDtypeStruct(x.shape, x.dtype) for x in given],
         scratch_shapes=[
             pltpu.VMEM((2 * rows, depth), near[0].dtype),
             pltpu.VMEM((tail, BLOCK), jnp.float32),
             pltpu.SemaphoreType.DMA((2 * len(near),)),
+            pltpu.SemaphoreType.DMA((max(len(given), 1),)),
         ],
         compiler_params=params(),
-        cost_estimate=cost(6 * rows * depth * columns, 4 * rows * depth + 4 * depth * columns),
+        cost_estimate=cost(
+            6 * rows * depth * columns, 4 * rows * depth + 4 * depth * columns, weight
+        ),
         name="partial_products",
-    )(diag, right0, right1, *near, *far, *after)
+    )(diag, right0, right1, *near, *far, *given)
 
 
 def finish_kernel(start, many, keep, coded, square, tangent, *rest):
@@ -324,7 +373,9 @@
         copy.wait()
 
 
-def finished(keep, square, tangent, coded, before, start, all_rows, held=(), after=()):
+def finished(
+    keep, square, tangent, coded, before, start, all_rows, held=(), after=(), weight=1 / 64
+):
     rows, columns = square.shape
     out = jax.ShapeDtypeStruct((all_rows, columns), jnp.bfloat16)
     held, before = list(held), list(before)
@@ -342,7 +393,7 @@
             pltpu.SemaphoreType.DMA((max(many, 1),)),
         ],
         compiler_params=params(),
-        cost_estimate=cost(0, 16 * rows * columns),
+        cost_estimate=cost(0, 16 * rows * columns, weight),
         name="finish",
     )(keep, coded, square, tangent, *held, *before, *after)
 
@@ -358,10 +409,11 @@
     half = row_index // group
     diag = (half == lax.axis_index("col")).astype(jnp.int32).reshape(1)
     place = (row_index % group).astype(jnp.int32).reshape(1)
-    edges = [all_rows * e // 8 for e in (0, 1, 3, 5, 8)]
+    edges = [all_rows * e // 16 for e in (0, 3, 7, 13, 16)]
     spans = list(zip(edges, edges[1:]))
     many = len(spans)
-    split = edges[-2]
+    split = edges[2]
+    final = all_rows * 10 // 16
     wide = 256
 
     def device(h, q, c):
@@ -379,39 +431,43 @@
             place, diag, mask0_rows, mask1_rows, x0_rows, x1_rows, spans, slabs, panel, after
         )
 
-    def partials(which, after=()):
-        return partial_products(diag, near[which], far[which], right0, right1, wide, after)
-
-    def own(which, b, got, after=()):
-        mine, other = (*a[which], b), (*passed[which], got)
-        return local_products(diag, mine, other, right0, right1, wide, after)
+    def partials(which, given=(), **more):
+        return partial_products(diag, near[which], far[which], right0, right1, wide, given, **more)
+
+    def own(which, b, got):
+        mine, other = (*a[which], *b), (*passed[which], *got)
+        return local_products(diag, mine, other, right0, right1, wide)
 
     a, swap, passed, near, far = ([None] * many for _ in range(5))
     a[0], swap[0] = chunks(spans[:1], ())
-    *rest, top_b, low_b = chunks(spans[1:], ((0, split), (split, all_rows)), (swap[0],))
-    a[1:], swap[1:] = rest[0::2], rest[1::2]
-    right0 = right1 = None
+    slabs = ((0, split), (split, final), (final, all_rows))
+    *rest, b0, b1, b2 = chunks(spans[1:], slabs, (swap[0],))
+    a[1:], swap[1:] = rest[0:-1:2], rest[1::2]
+    early, late = slice(0, 2), slice(2, many)
+    right0 = right1 = coded = None
     for i in range(many):
         passed[i] = move(swap[i], over_y)
         last = i == many - 1
-        held = (top_b,) if last else (swap[i + 1],)
-        gate = {1: (near[0],), 2: (right0,), 3: (far[0], far[1])}.get(i, ())
-        send, later = chosen(diag, passed[i], a[i], held, gate)
         if last:
-            top_b = later
+            (coded,) = partials(early)
+        gate = {1: (near[0],), 2: (right0,), 3: (coded,)}.get(i, ())
+        send, later = chosen(diag, passed[i], a[i], (b0 if last else swap[i + 1],), gate)
+        if last:
+            b0 = later
         else:
             swap[i + 1] = later
         near[i] = move(send, over_z)
         far[i] = move(near[i], over_y)
         if i == 1:
             right0, right1 = masked_right(mask0_cols, mask1_cols, x0_cols, x1_cols, (send,))
-    early, late = slice(0, many - 1), slice(many - 1, many)
-    back = move(partials(early), over_z)
-    square, tangent = own(early, top_b, move(top_b, over_y))
-    coded = partials(late)
-    *outs, low_b = finished(keep, square, tangent, back, (), 0, all_rows, (low_b,), (coded,))
+    back = move(handed_on(coded, near[-1]), over_z)
+    square, tangent = own(early, (b0,), (move(b0, over_y),))
+    coded, b1 = partials(late, (b1,), weight=16)
+    *outs, b2 = finished(
+        keep, square, tangent, back, (), 0, all_rows, (b2,), (coded,), weight=1024
+    )
     back = move(coded, over_z)
-    square, tangent = own(late, low_b, move(low_b, over_y))
+    square, tangent = own(late, (b1, b2), (move(b1, over_y), move(b2, over_y)))
     return tuple(finished(keep, square, tangent, back, outs, split, all_rows))
 
 

time: 109 us -> 119 us (1.092)
  waiting for transfers between devices: 52.8 us -> 62.1 us
    ppermute x16 -> x17, waiting for transfers between devices: 52.8 us -> 62.1 us  [move(): return lax.ppermute(values, ('row', 'col'), pairs)]
    pallas_call x6 -> x7, Pallas kernels: 11 us -> 11.8 us  [the longest x2 9.55 us: partial_products(): pl.pallas_call(functools.partial(partial_kernel, len(near), len(given)),...]
    ppermute x16 -> x17, starting transfers between devices: 18 us -> 18.5 us  [move(): return lax.ppermute(values, ('row', 'col'), pairs)]
  transfers between devices with their start and end apart: 16 -> 17, of which waited for: 8 -> 9; matrix products, arithmetic and copies ran while one was open for 1% -> 0% of each run, Pallas kernels for 27% -> 26%
where the time goes in v4:
time: 119 us; the launch traced here: 118 us
  waiting for transfers between devices  62.1 us (52%)
  Pallas kernels  34.7 us (29%)
  starting transfers between devices  18.5 us (16%)
  local copies, waits for them, and re-layouts  2.22 us (2%)
    ppermute x17, waiting for transfers between devices, move(): return lax.ppermute(values, ('row', 'col'), pairs)  62.1 us
    ppermute x17, starting transfers between devices, move(): return lax.ppermute(values, ('row', 'col'), pairs)  18.5 us
    pallas_call x2, Pallas kernels, local_products(): pl.pallas_call(functools.partial(local_kernel, many), grid=(columns // wi...  9.69 us
    pallas_call x2, Pallas kernels, partial_products(): pl.pallas_call(functools.partial(partial_kernel, len(near), len(given)),...  9.55 us
    pallas_call x1, Pallas kernels, masked_right(): pl.pallas_call(right_kernel, grid=(depth // tall,), in_specs=[SM(), SM(),...  6.97 us
    pallas_call x2, Pallas kernels, masked_chunks(): pl.pallas_call(functools.partial(chunk_kernel, spans, slabs, panel), in_s...  3.24 us
    pallas_call x2, Pallas kernels, finished(): pl.pallas_call(functools.partial(finish_kernel, start, many), in_specs=[S...  3.03 us
  transfers between devices with their start and end apart: 17, of which 9 were waited for; matrix products, arithmetic and copies ran while one was open for 0% of the time, Pallas kernels for 26%

profile of v4, /device:TPU:0, one launch (start us, length us, event | category | flops | bytes accessed | tf_op | source)
XLA Modules:
  0.0 118.4 jit_solution(5472915662247091651)
XLA Ops:
  3.2 3.1 %collective-permute-start = (bf16[48,2048]{1,0:T(8,128)(2,1)S(1)}, bf16[48,2048]{1,0:T(8,128)(2,1)S(1)}, u32[]{:S(2)}, u32[]{:S(2)}) collective-permute-start(bf16[48,2048]{1,0:T(8,128)(2,1)S(1)} %get-tuple-element.32.refs_6_), channel_id=1, source_target_pairs={{0,1},{1,0},{2,3},{3,2},{4,5},{5,4},{6,7},{7,6},{8,9},{9,8},{10,11... | collective-permute-start | bytes 589832 | tf_op jit(solution)/shard_map/ppermute | solution.py:427
  6.2 2.1 %left_chunks.3 = (bf16[64,2048]{1,0:T(8,128)(2,1)S(1)}, bf16[64,2048]{1,0:T(8,128)(2,1)S(1)}, bf16[96,2048]{1,0:T(8,128)(2,1)S(1)}, bf16[96,2048]{1,0:T(8,128)(2...) custom-call(s32[1]{0:T(128)} %bitcast.1.refs_0_, ...), custom_call_target="tpu_custom_call" | custom-call | bytes 65536 | tf_op jit(solution)/shard_map/left_chunks/pallas_call | solution.py:104
  9.0 2.1 %collective-permute-done.refs_0_.refs_3_ = bf16[48,2048]{1,0:T(8,128)(2,1)S(1)} collective-permute-done((bf16[48,2048]{1,0:T(8,128)(2,1)S(1)}, bf16[48,2048]{1,0:T(8,128)(2,1)S(1)}, u32[]{:S(2)}, u32[]{:S(2)}) %collective-permute-start) | collective-permute-done | bytes 196640 | tf_op jit(solution)/shard_map/ppermute | solution.py:427
  11.4 1.8 %collective-permute-start.2 = (bf16[64,2048]{1,0:T(8,128)(2,1)S(1)}, bf16[64,2048]{1,0:T(8,128)(2,1)S(1)}, u32[]{:S(2)}, u32[]{:S(2)}) collective-permute-start(bf16[64,2048]{1,0:T(8,128)(2,1)S(1)} %get-tuple-element.36), channel_id=1, source_target_pairs={{0,1},{1,0},{2,3},{3,2},{4,5},{5,4},{6,7},{7,6},{8,9},{9,8},{10,11... | collective-permute-start | bytes 786440 | tf_op jit(solution)/shard_map/ppermute | solution.py:427
  13.3 2.6 %collective-permute-start.1 = (bf16[48,2048]{1,0:T(8,128)(2,1)S(1)}, bf16[48,2048]{1,0:T(8,128)(2,1)S(1)}, u32[]{:S(2)}, u32[]{:S(2)}) collective-permute-start(bf16[48,2048]{1,0:T(8,128)(2,1)S(1)} %get-tuple-element.35), channel_id=1, source_target_pairs={{0,16},{1,17},{2,18},{3,19},{4,20},{5,21},{6,22},{7,23},{8,24},{9,... | collective-permute-start | bytes 589832 | tf_op jit(solution)/shard_map/ppermute | solution.py:427
  15.8 8.0 %collective-permute-done.1.refs_0_ = bf16[48,2048]{1,0:T(8,128)(2,1)S(1)} collective-permute-done((bf16[48,2048]{1,0:T(8,128)(2,1)S(1)}, bf16[48,2048]{1,0:T(8,128)(2,1)S(1)}, u32[]{:S(2)}, u32[]{:S(2)}) %collective-permute-start.1) | collective-permute-done | bytes 196640 | tf_op jit(solution)/shard_map/ppermute | solution.py:427
  25.5 7.0 %right_panels.1 = (bf16[2048,768]{1,0:T(8,128)(2,1)S(1)}, bf16[2048,768]{1,0:T(8,128)(2,1)}) custom-call(s32[16,6]{1,0:T(8,128)S(1)} %copy.13.mask0, s32[16,6]{1,0:T(8,128)S(1)} %copy.14.mask1, bf16[2048,768]{1,0:T(8,128)(2,1)} %x0.1, bf16[2048,768]{1,0:T(8,128)(2,1)} %x1.1, bf16[64,2048]{1,0:T(8,128)(2,1)S(1)} %get-tuple-element.39.rest_0_), custom_call_target="tpu_custom_call" | custom-call | bytes 196608 | tf_op jit(solution)/shard_map/right_panels/pallas_call | solution.py:197
  32.4 2.4 %collective-permute-done.3.refs_1_.refs_4_ = bf16[96,2048]{1,0:T(8,128)(2,1)S(1)} collective-permute-done((bf16[96,2048]{1,0:T(8,128)(2,1)}, bf16[96,2048]{1,0:T(8,128)(2,1)S(1)}, u32[]{:S(2)}, u32[]{:S(2)}) %collective-permute-start.3) | collective-permute-done | bytes 393248 | tf_op jit(solution)/shard_map/ppermute | solution.py:427
  35.9 13.1 %collective-permute-done.5.refs_1_ = bf16[64,2048]{1,0:T(8,128)(2,1)S(1)} collective-permute-done((bf16[64,2048]{1,0:T(8,128)(2,1)S(1)}, bf16[64,2048]{1,0:T(8,128)(2,1)S(1)}, u32[]{:S(2)}, u32[]{:S(2)}) %collective-permute-start.5) | collective-permute-done | bytes 262176 | tf_op jit(solution)/shard_map/ppermute | solution.py:427
  49.0 1.5 %collective-permute-start.7 = (bf16[64,2048]{1,0:T(8,128)(2,1)S(1)}, bf16[64,2048]{1,0:T(8,128)(2,1)S(1)}, u32[]{:S(2)}, u32[]{:S(2)}) collective-permute-start(bf16[64,2048]{1,0:T(8,128)(2,1)S(1)} %collective-permute-done.5.refs_1_), channel_id=1, source_target_pairs={{0,1},{1,0},{2,3},{3,2},{4,5},{5,4},{6,7},{7,6},{8,9},{9,8},{10,11... | collective-permute-start | bytes 786440 | tf_op jit(solution)/shard_map/ppermute | solution.py:427
  51.0 1.5 %collective-permute-start.8 = (bf16[48,2048]{1,0:T(8,128)(2,1)S(1)}, bf16[48,2048]{1,0:T(8,128)(2,1)S(1)}, u32[]{:S(2)}, u32[]{:S(2)}) collective-permute-start(bf16[48,2048]{1,0:T(8,128)(2,1)S(1)} %get-tuple-element.46), channel_id=1, source_target_pairs={{0,1},{1,0},{2,3},{3,2},{4,5},{5,4},{6,7},{7,6},{8,9},{9,8},{10,11... | collective-permute-start | bytes 589832 | tf_op jit(solution)/shard_map/ppermute | solution.py:427
  52.5 5.8 %collective-permute-done.6.refs_2_ = bf16[48,2048]{1,0:T(8,128)(2,1)S(1)} collective-permute-done((bf16[48,2048]{1,0:T(8,128)(2,1)S(1)}, bf16[48,2048]{1,0:T(8,128)(2,1)S(1)}, u32[]{:S(2)}, u32[]{:S(2)}) %collective-permute-start.6) | collective-permute-done | bytes 196640 | tf_op jit(solution)/shard_map/ppermute | solution.py:427
  58.4 4.4 %partial_products.2.refs_0_.one = s16[1360,128]{1,0:T(8,128)(2,1)S(1)} custom-call(s32[1]{0:T(128)} %bitcast.refs_1_.diag, bf16[2048,768]{1,0:T(8,128)(2,1)S(1)} %get-tuple-element.40.refs_0_.right0, bf16[2048,768]{1,0:T(8,128)(2,1)} %get-tuple-element.41.right1, bf16[48,2048]{1,0:T(8,128)(2,1)S(1)} %collective-permute-done.1.refs_0_, ...), custom_call_target="tpu_custom_call" | custom-call | flops 16515072 | bytes 112640 | tf_op jit(solution)/shard_map/partial_products/pallas_call | solution.py:318
  63.4 1.9 %collective-permute-start.10 = (bf16[96,2048]{1,0:T(8,128)(2,1)S(1)}, bf16[96,2048]{1,0:T(8,128)(2,1)S(1)}, u32[]{:S(2)}, u32[]{:S(2)}) collective-permute-start(bf16[96,2048]{1,0:T(8,128)(2,1)S(1)} %collective-permute-done.4.refs_0_), channel_id=1, source_target_pairs={{0,1},{1,0},{2,3},{3,2},{4,5},{5,4},{6,7},{7,6},{8,9},{9,8},{10,11... | collective-permute-start | bytes 1179656 | tf_op jit(solution)/shard_map/ppermute | solution.py:427
  65.4 7.4 %collective-permute-done.9.refs_1_.gate = bf16[48,2048]{1,0:T(8,128)(2,1)S(1)} collective-permute-done((bf16[48,2048]{1,0:T(8,128)(2,1)S(1)}, bf16[48,2048]{1,0:T(8,128)(2,1)S(1)}, u32[]{:S(2)}, u32[]{:S(2)}) %collective-permute-start.9) | collective-permute-done | bytes 196640 | tf_op jit(solution)/shard_map/ppermute | solution.py:427
  72.8 1.5 %collective-permute-start.11 = (bf16[48,2048]{1,0:T(8,128)(2,1)S(1)}, bf16[48,2048]{1,0:T(8,128)(2,1)S(1)}, u32[]{:S(2)}, u32[]{:S(2)}) collective-permute-start(bf16[48,2048]{1,0:T(8,128)(2,1)S(1)} %collective-permute-done.9.refs_1_.gate), channel_id=1, source_target_pairs={{0,1},{1,0},{2,3},{3,2},{4,5},{5,4},{6,7},{7,6},{8,9},{9,8},{10,11... | collective-permute-start | bytes 589832 | tf_op jit(solution)/shard_map/ppermute | solution.py:427
  75.0 3.4 %collective-permute-done.11.refs_3_ = bf16[48,2048]{1,0:T(8,128)(2,1)S(1)} collective-permute-done((bf16[48,2048]{1,0:T(8,128)(2,1)S(1)}, bf16[48,2048]{1,0:T(8,128)(2,1)S(1)}, u32[]{:S(2)}, u32[]{:S(2)}) %collective-permute-start.11) | collective-permute-done | bytes 196640 | tf_op jit(solution)/shard_map/ppermute | solution.py:427
  78.5 5.2 %partial_products.3 = (s16[1744,128]{1,0:T(8,128)(2,1)S(1)}, bf16[48,2048]{1,0:T(8,128)(2,1)S(1)}) custom-call(s32[1]{0:T(128)} %bitcast.refs_1_.diag, bf16[2048,768]{1,0:T(8,128)(2,1)S(1)} %get-tuple-element.40.refs_0_.right0, bf16[2048,768]{1,0:T(8,128)(2,1)} %get-tuple-element.41.right1, bf16[96,2048]{1,0:T(8,128)(2,1)S(1)} %collective-permute-done.4.refs_0_, ...), custom_call_target="tpu_custom_call" | custom-call | flops 21743271936 | bytes 119537664 | tf_op jit(solution)/shard_map/partial_products/pallas_call | solution.py:318
  83.7 4.3 %own_products.2 = (f32[112,768]{1,0:T(8,128)S(1)}, f32[112,768]{1,0:T(8,128)S(1)}) custom-call(s32[1]{0:T(128)} %bitcast.refs_1_.diag, bf16[2048,768]{1,0:T(8,128)(2,1)S(1)} %get-tuple-element.40.refs_0_.right0, bf16[2048,768]{1,0:T(8,128)(2,1)} %get-tuple-element.41.right1, bf16[48,2048]{1,0:T(8,128)(2,1)S(1)} %get-tuple-element.33.refs_1_.refs_0_, ...), custom_call_target="tpu_custom_call" | custom-call | flops 16515072 | bytes 126976 | tf_op jit(solution)/shard_map/own_products/pallas_call | solution.py:254
  88.1 11.9 %collective-permute-done.13.coded = s16[1360,128]{1,0:T(8,128)(2,1)S(1)} collective-permute-done((s16[1360,128]{1,0:T(8,128)(2,1)S(1)}, s16[1360,128]{1,0:T(8,128)(2,1)S(1)}, u32[]{:S(2)}, u32[]{:S(2)}) %collective-permute-start.13) | collective-permute-done | bytes 348192 | tf_op jit(solution)/shard_map/ppermute | solution.py:427
  100.0 1.6 %finish.2 = (bf16[256,768]{1,0:T(8,128)(2,1)}, bf16[256,768]{1,0:T(8,128)(2,1)}, bf16[96,2048]{1,0:T(8,128)(2,1)S(1)}) custom-call(s32[2,6]{1,0:T(2,128)S(1)} %copy-done.6, s16[1360,128]{1,0:T(8,128)(2,1)S(1)} %collective-permute-done.13.coded, f32[112,768]{1,0:T(8,128)S(1)} %get-tuple-element.54.square, f32[112,768]{1,0:T(8,128)S(1)} %get-tuple-element.55.tangent, ...), custom_call_target="tpu_custom_call" | custom-call | bytes 1409286144 | tf_op jit(solution)/shard_map/finish/pallas_call | solution.py:384
  101.6 1.6 %collective-permute-start.16 = (bf16[96,2048]{1,0:T(8,128)(2,1)S(1)}, bf16[96,2048]{1,0:T(8,128)(2,1)S(1)}, u32[]{:S(2)}, u32[]{:S(2)}) collective-permute-start(bf16[96,2048]{1,0:T(8,128)(2,1)S(1)} %get-tuple-element.57.refs_3_), channel_id=1, source_target_pairs={{0,1},{1,0},{2,3},{3,2},{4,5},{5,4},{6,7},{7,6},{8,9},{9,8},{10,11... | collective-permute-start | bytes 1179656 | tf_op jit(solution)/shard_map/ppermute | solution.py:427
  103.7 7.9 %collective-permute-done.15.refs_6_ = bf16[48,2048]{1,0:T(8,128)(2,1)S(1)} collective-permute-done((bf16[48,2048]{1,0:T(8,128)(2,1)S(1)}, bf16[48,2048]{1,0:T(8,128)(2,1)S(1)}, u32[]{:S(2)}, u32[]{:S(2)}) %collective-permute-start.15) | collective-permute-done | bytes 196640 | tf_op jit(solution)/shard_map/ppermute | solution.py:427
  111.6 5.4 %own_products.3 = (f32[144,768]{1,0:T(8,128)S(1)}, f32[144,768]{1,0:T(8,128)S(1)}) custom-call(s32[1]{0:T(128)} %bitcast.refs_1_.diag, bf16[2048,768]{1,0:T(8,128)(2,1)} %copy-done, bf16[2048,768]{1,0:T(8,128)(2,1)} %get-tuple-element.41.right1, bf16[96,2048]{1,0:T(8,128)(2,1)S(1)} %get-tuple-element.43.refs_2_.refs_0_, ...), custom_call_target="tpu_custom_call" | custom-call | flops 21233664 | bytes 135168 | tf_op jit(solution)/shard_map/own_products/pallas_call | solution.py:254
  (48 shorter events, 10.1 us)
Async XLA Ops:
  3.2 22.2 %copy-start.9 = (s32[16,6]{0,1:T(8,128)S(1)}, s32[16,6]{0,1:T(8,128)}, u32[]{:S(2)}) copy-start(s32[16,6]{0,1:T(8,128)} %param.15) | copy-start | bytes 1156
  3.2 22.2 %copy-start.10 = (s32[16,6]{0,1:T(8,128)S(1)}, s32[16,6]{0,1:T(8,128)}, u32[]{:S(2)}) copy-start(s32[16,6]{0,1:T(8,128)} %param.16) | copy-start | bytes 1156
  3.2 8.0 %collective-permute-start = (bf16[48,2048]{1,0:T(8,128)(2,1)S(1)}, bf16[48,2048]{1,0:T(8,128)(2,1)S(1)}, u32[]{:S(2)}, u32[]{:S(2)}) collective-permute-start(bf16[48,2048]{1,0:T(8,128)(2,1)S(1)} %get-tuple-element.32.refs_6_), channel_id=1, source_target_pairs={{0,1},{1,0},{2,3},{3,2},{4,5},{5,4},{6,7},{7,6},{8,9},{9,8},{10,11... | collective-permute-start | bytes 589832 | tf_op jit(solution)/shard_map/ppermute | solution.py:427
  9.0 16.3 %copy-start.1 = (bf16[48,2048]{1,0:T(8,128)(2,1)}, bf16[48,2048]{1,0:T(8,128)(2,1)S(1)}, u32[]{:S(2)}) copy-start(bf16[48,2048]{1,0:T(8,128)(2,1)S(1)} %get-tuple-element.44.refs_3_) | copy-start | bytes 589828
  11.4 12.4 %collective-permute-start.2 = (bf16[64,2048]{1,0:T(8,128)(2,1)S(1)}, bf16[64,2048]{1,0:T(8,128)(2,1)S(1)}, u32[]{:S(2)}, u32[]{:S(2)}) collective-permute-start(bf16[64,2048]{1,0:T(8,128)(2,1)S(1)} %get-tuple-element.36), channel_id=1, source_target_pairs={{0,1},{1,0},{2,3},{3,2},{4,5},{5,4},{6,7},{7,6},{8,9},{9,8},{10,11... | collective-permute-start | bytes 786440 | tf_op jit(solution)/shard_map/ppermute | solution.py:427
  13.3 10.6 %collective-permute-start.1 = (bf16[48,2048]{1,0:T(8,128)(2,1)S(1)}, bf16[48,2048]{1,0:T(8,128)(2,1)S(1)}, u32[]{:S(2)}, u32[]{:S(2)}) collective-permute-start(bf16[48,2048]{1,0:T(8,128)(2,1)S(1)} %get-tuple-element.35), channel_id=1, source_target_pairs={{0,16},{1,17},{2,18},{3,19},{4,20},{5,21},{6,22},{7,23},{8,24},{9,... | collective-permute-start | bytes 589832 | tf_op jit(solution)/shard_map/ppermute | solution.py:427
  24.6 10.2 %collective-permute-start.3 = (bf16[96,2048]{1,0:T(8,128)(2,1)}, bf16[96,2048]{1,0:T(8,128)(2,1)S(1)}, u32[]{:S(2)}, u32[]{:S(2)}) collective-permute-start(bf16[96,2048]{1,0:T(8,128)(2,1)} %get-tuple-element.42), channel_id=1, source_target_pairs={{0,1},{1,0},{2,3},{3,2},{4,5},{5,4},{6,7},{7,6},{8,9},{9,8},{10,11... | collective-permute-start | bytes 1179656 | tf_op jit(solution)/shard_map/ppermute | solution.py:427
  25.3 23.7 %collective-permute-start.5 = (bf16[64,2048]{1,0:T(8,128)(2,1)S(1)}, bf16[64,2048]{1,0:T(8,128)(2,1)S(1)}, u32[]{:S(2)}, u32[]{:S(2)}) collective-permute-start(bf16[64,2048]{1,0:T(8,128)(2,1)S(1)} %get-tuple-element.39.rest_0_), channel_id=1, source_target_pairs={{0,16},{1,17},{2,18},{3,19},{4,20},{5,21},{6,22},{7,23},{8,24},{9,... | collective-permute-start | bytes 786440 | tf_op jit(solution)/shard_map/ppermute | solution.py:427
  25.5 9.4 %copy-start.2 = (bf16[48,2048]{1,0:T(8,128)(2,1)S(1)}, bf16[48,2048]{1,0:T(8,128)(2,1)}, u32[]{:S(2)}) copy-start(bf16[48,2048]{1,0:T(8,128)(2,1)} %copy-done.1) | copy-start | bytes 589828
  32.4 51.3 %copy-start = (bf16[2048,768]{1,0:T(8,128)(2,1)}, bf16[2048,768]{1,0:T(8,128)(2,1)S(1)}, u32[]{:S(2)}) copy-start(bf16[2048,768]{1,0:T(8,128)(2,1)S(1)} %get-tuple-element.40.refs_0_.right0) | copy-start | bytes 9437188
  35.3 28.1 %collective-permute-start.4 = (bf16[96,2048]{1,0:T(8,128)(2,1)S(1)}, bf16[96,2048]{1,0:T(8,128)(2,1)S(1)}, u32[]{:S(2)}, u32[]{:S(2)}) collective-permute-start(bf16[96,2048]{1,0:T(8,128)(2,1)S(1)} %get-tuple-element.45), channel_id=1, source_target_pairs={{0,16},{1,17},{2,18},{3,19},{4,20},{5,21},{6,22},{7,23},{8,24},{9,... | collective-permute-start | bytes 1179656 | tf_op jit(solution)/shard_map/ppermute | solution.py:427
  49.0 9.3 %collective-permute-start.7 = (bf16[64,2048]{1,0:T(8,128)(2,1)S(1)}, bf16[64,2048]{1,0:T(8,128)(2,1)S(1)}, u32[]{:S(2)}, u32[]{:S(2)}) collective-permute-start(bf16[64,2048]{1,0:T(8,128)(2,1)S(1)} %collective-permute-done.5.refs_1_), channel_id=1, source_target_pairs={{0,1},{1,0},{2,3},{3,2},{4,5},{5,4},{6,7},{7,6},{8,9},{9,8},{10,11... | collective-permute-start | bytes 786440 | tf_op jit(solution)/shard_map/ppermute | solution.py:427
  50.5 7.8 %collective-permute-start.6 = (bf16[48,2048]{1,0:T(8,128)(2,1)S(1)}, bf16[48,2048]{1,0:T(8,128)(2,1)S(1)}, u32[]{:S(2)}, u32[]{:S(2)}) collective-permute-start(bf16[48,2048]{1,0:T(8,128)(2,1)S(1)} %collective-permute-done.1.refs_0_), channel_id=1, source_target_pairs={{0,1},{1,0},{2,3},{3,2},{4,5},{5,4},{6,7},{7,6},{8,9},{9,8},{10,11... | collective-permute-start | bytes 589832 | tf_op jit(solution)/shard_map/ppermute | solution.py:427
  51.0 11.7 %collective-permute-start.8 = (bf16[48,2048]{1,0:T(8,128)(2,1)S(1)}, bf16[48,2048]{1,0:T(8,128)(2,1)S(1)}, u32[]{:S(2)}, u32[]{:S(2)}) collective-permute-start(bf16[48,2048]{1,0:T(8,128)(2,1)S(1)} %get-tuple-element.46), channel_id=1, source_target_pairs={{0,1},{1,0},{2,3},{3,2},{4,5},{5,4},{6,7},{7,6},{8,9},{9,8},{10,11... | collective-permute-start | bytes 589832 | tf_op jit(solution)/shard_map/ppermute | solution.py:427
  58.4 20.1 %copy-start.8 = (bf16[48,2048]{1,0:T(8,128)(2,1)S(1)}, bf16[48,2048]{1,0:T(8,128)(2,1)}, u32[]{:S(2)}) copy-start(bf16[48,2048]{1,0:T(8,128)(2,1)} %copy-done.7) | copy-start | bytes 589828
  63.3 9.5 %collective-permute-start.9 = (bf16[48,2048]{1,0:T(8,128)(2,1)S(1)}, bf16[48,2048]{1,0:T(8,128)(2,1)S(1)}, u32[]{:S(2)}, u32[]{:S(2)}) collective-permute-start(bf16[48,2048]{1,0:T(8,128)(2,1)S(1)} %get-tuple-element.49), channel_id=1, source_target_pairs={{0,16},{1,17},{2,18},{3,19},{4,20},{5,21},{6,22},{7,23},{8,24},{9,... | collective-permute-start | bytes 589832 | tf_op jit(solution)/shard_map/ppermute | solution.py:427
  63.4 15.0 %collective-permute-start.10 = (bf16[96,2048]{1,0:T(8,128)(2,1)S(1)}, bf16[96,2048]{1,0:T(8,128)(2,1)S(1)}, u32[]{:S(2)}, u32[]{:S(2)}) collective-permute-start(bf16[96,2048]{1,0:T(8,128)(2,1)S(1)} %collective-permute-done.4.refs_0_), channel_id=1, source_target_pairs={{0,1},{1,0},{2,3},{3,2},{4,5},{5,4},{6,7},{7,6},{8,9},{9,8},{10,11... | collective-permute-start | bytes 1179656 | tf_op jit(solution)/shard_map/ppermute | solution.py:427
  72.8 5.7 %collective-permute-start.11 = (bf16[48,2048]{1,0:T(8,128)(2,1)S(1)}, bf16[48,2048]{1,0:T(8,128)(2,1)S(1)}, u32[]{:S(2)}, u32[]{:S(2)}) collective-permute-start(bf16[48,2048]{1,0:T(8,128)(2,1)S(1)} %collective-permute-done.9.refs_1_.gate), channel_id=1, source_target_pairs={{0,1},{1,0},{2,3},{3,2},{4,5},{5,4},{6,7},{7,6},{8,9},{9,8},{10,11... | collective-permute-start | bytes 589832 | tf_op jit(solution)/shard_map/ppermute | solution.py:427
  74.3 9.5 %collective-permute-start.14 = (bf16[112,2048]{1,0:T(8,128)(2,1)S(1)}, bf16[112,2048]{1,0:T(8,128)(2,1)S(1)}, u32[]{:S(2)}, u32[]{:S(2)}) collective-permute-start(bf16[112,2048]{1,0:T(8,128)(2,1)S(1)} %get-tuple-element.53.refs_2_), channel_id=1, source_target_pairs={{0,1},{1,0},{2,3},{3,2},{4,5},{5,4},{6,7},{7,6},{8,9},{9,8},{10,11... | collective-permute-start | bytes 1376264 | tf_op jit(solution)/shard_map/ppermute | solution.py:427
  75.0 25.1 %collective-permute-start.13 = (s16[1360,128]{1,0:T(8,128)(2,1)S(1)}, s16[1360,128]{1,0:T(8,128)(2,1)S(1)}, u32[]{:S(2)}, u32[]{:S(2)}) collective-permute-start(s16[1360,128]{1,0:T(8,128)(2,1)S(1)} %handed_on.1), channel_id=1, source_target_pairs={{0,16},{1,17},{2,18},{3,19},{4,20},{5,21},{6,22},{7,23},{8,24},{9,... | collective-permute-start | bytes 1044488 | tf_op jit(solution)/shard_map/ppermute | solution.py:427
  83.6 16.4 %copy-start.6 = (s32[2,6]{1,0:T(2,128)S(1)}, s32[2,6]{1,0:T(2,128)}, u32[]{:S(2)}) copy-start(s32[2,6]{1,0:T(2,128)} %keep.3) | copy-start | bytes 148
  83.6 33.3 %collective-permute-start.12 = (s16[1744,128]{1,0:T(8,128)(2,1)S(1)}, s16[1744,128]{1,0:T(8,128)(2,1)S(1)}, u32[]{:S(2)}, u32[]{:S(2)}) collective-permute-start(s16[1744,128]{1,0:T(8,128)(2,1)S(1)} %get-tuple-element.51.rest_1_), channel_id=1, source_target_pairs={{0,16},{1,17},{2,18},{3,19},{4,20},{5,21},{6,22},{7,23},{8,24},{9,... | collective-permute-start | bytes 1339400 | tf_op jit(solution)/shard_map/ppermute | solution.py:427
  101.6 10.0 %collective-permute-start.16 = (bf16[96,2048]{1,0:T(8,128)(2,1)S(1)}, bf16[96,2048]{1,0:T(8,128)(2,1)S(1)}, u32[]{:S(2)}, u32[]{:S(2)}) collective-permute-start(bf16[96,2048]{1,0:T(8,128)(2,1)S(1)} %get-tuple-element.57.refs_3_), channel_id=1, source_target_pairs={{0,1},{1,0},{2,3},{3,2},{4,5},{5,4},{6,7},{7,6},{8,9},{9,8},{10,11... | collective-permute-start | bytes 1179656 | tf_op jit(solution)/shard_map/ppermute | solution.py:427
  103.2 8.4 %collective-permute-start.15 = (bf16[48,2048]{1,0:T(8,128)(2,1)S(1)}, bf16[48,2048]{1,0:T(8,128)(2,1)S(1)}, u32[]{:S(2)}, u32[]{:S(2)}) collective-permute-start(bf16[48,2048]{1,0:T(8,128)(2,1)S(1)} %get-tuple-element.52.refs_2_), channel_id=1, source_target_pairs={{0,1},{1,0},{2,3},{3,2},{4,5},{5,4},{6,7},{7,6},{8,9},{9,8},{10,11... | collective-permute-start | bytes 589832 | tf_op jit(solution)/shard_map/ppermute | solution.py:427
  (4 other events, 6.3 us)

commit v5 on v4

--- a/solution.py
+++ b/solution.py
@@ -23,10 +23,8 @@
     return pltpu.CompilerParams(vmem_limit_bytes=VMEM_BYTES)
 
 
-def cost(flops, moved, weight=1 / 64):
-    return pl.CostEstimate(
-        flops=int(flops * weight), bytes_accessed=int(moved * weight), transcendentals=0
-    )
+def cost(flops, moved):
+    return pl.CostEstimate(flops=int(flops) // 64, bytes_accessed=int(moved) // 64, transcendentals=0)
 
 
 def scaled(values, entry):
@@ -159,23 +157,29 @@
     )(diag, *after, one, other, *held)
 
 
-def hand_kernel(one, gate, out, sem):
-    copy = pltpu.make_async_copy(one, out, sem)
-    copy.start()
-    copy.wait()
-
-
-def handed_on(one, gate):
-    return pl.pallas_call(
-        hand_kernel,
-        in_specs=[HB(), HB()],
-        out_specs=HB(),
-        out_shape=jax.ShapeDtypeStruct(one.shape, one.dtype),
-        scratch_shapes=[pltpu.SemaphoreType.DMA],
-        compiler_params=params(),
-        cost_estimate=cost(0, 4 * one.size),
+def hand_kernel(many, *refs):
+    sems = refs[-1]
+    copies = [
+        pltpu.make_async_copy(refs[i], refs[i - many - 1], sems.at[i]) for i in range(many)
+    ]
+    for copy in copies:
+        copy.start()
+    for copy in copies:
+        copy.wait()
+
+
+def handed_on(values, gates):
+    outs = [jax.ShapeDtypeStruct(x.shape, x.dtype) for x in values]
+    return pl.pallas_call(
+        functools.partial(hand_kernel, len(values)),
+        in_specs=[HB() for _ in (*values, *gates)],
+        out_specs=[HB() for _ in outs],
+        out_shape=outs,
+        scratch_shapes=[pltpu.SemaphoreType.DMA((len(outs),))],
+        compiler_params=params(),
+        cost_estimate=cost(0, 4 * sum(x.size for x in values)),
         name="handed_on",
-    )(one, gate)
+    )(*values, *gates)
 
 
 def right_kernel(mask0, mask1, x0, x1, *rest):
@@ -310,7 +314,7 @@
             copy.wait()
 
 
-def partial_products(diag, near, far, right0, right1, wide, given=(), weight=1 / 64):
+def partial_products(diag, near, far, right0, right1, wide, given=(), gates=()):
     rows = sum(piece.shape[0] for piece in near)
     depth, columns = right0.shape
     tiles = 2 * columns // BLOCK
@@ -323,7 +327,7 @@
             pl.BlockSpec((depth, wide), lambda g: (0, g)),
             pl.BlockSpec((depth, wide), lambda g: (0, g)),
         ]
-        + [HB() for _ in (*near, *far, *given)],
+        + [HB() for _ in (*near, *far, *given, *gates)],
         out_specs=[pl.BlockSpec((tiles * rows + tail, BLOCK), lambda g: (0, 0))]
         + [HB() for _ in given],
         out_shape=[jax.ShapeDtypeStruct((tiles * rows + tail, BLOCK), jnp.int16)]
@@ -335,11 +339,9 @@
             pltpu.SemaphoreType.DMA((max(len(given), 1),)),
         ],
         compiler_params=params(),
-        cost_estimate=cost(
-            6 * rows * depth * columns, 4 * rows * depth + 4 * depth * columns, weight
-        ),
+        cost_estimate=cost(6 * rows * depth * columns, 4 * rows * depth + 4 * depth * columns),
         name="partial_products",
-    )(diag, right0, right1, *near, *far, *given)
+    )(diag, right0, right1, *near, *far, *given, *gates)
 
 
 def finish_kernel(start, many, keep, coded, square, tangent, *rest):
@@ -373,9 +375,7 @@
         copy.wait()
 
 
-def finished(
-    keep, square, tangent, coded, before, start, all_rows, held=(), after=(), weight=1 / 64
-):
+def finished(keep, square, tangent, coded, before, start, all_rows, held=(), after=()):
     rows, columns = square.shape
     out = jax.ShapeDtypeStruct((all_rows, columns), jnp.bfloat16)
     held, before = list(held), list(before)
@@ -393,7 +393,7 @@
             pltpu.SemaphoreType.DMA((max(many, 1),)),
         ],
         compiler_params=params(),
-        cost_estimate=cost(0, 16 * rows * columns, weight),
+        cost_estimate=cost(0, 16 * rows * columns),
         name="finish",
     )(keep, coded, square, tangent, *held, *before, *after)
 
@@ -413,7 +413,6 @@
     spans = list(zip(edges, edges[1:]))
     many = len(spans)
     split = edges[2]
-    final = all_rows * 10 // 16
     wide = 256
 
     def device(h, q, c):
@@ -439,36 +438,35 @@
         return local_products(diag, mine, other, right0, right1, wide)
 
     a, swap, passed, near, far = ([None] * many for _ in range(5))
+    early, late = slice(0, 2), slice(2, many)
     a[0], swap[0] = chunks(spans[:1], ())
-    slabs = ((0, split), (split, final), (final, all_rows))
-    *rest, b0, b1, b2 = chunks(spans[1:], slabs, (swap[0],))
-    a[1:], swap[1:] = rest[0:-1:2], rest[1::2]
-    early, late = slice(0, 2), slice(2, many)
-    right0 = right1 = coded = None
+    *rest, b0, b1 = chunks(spans[1:], ((0, split), (split, all_rows)), (swap[0],))
+    a[1:], swap[1:] = rest[0::2], rest[1::2]
+    right0 = right1 = None
     for i in range(many):
         passed[i] = move(swap[i], over_y)
         last = i == many - 1
-        if last:
-            (coded,) = partials(early)
-        gate = {1: (near[0],), 2: (right0,), 3: (coded,)}.get(i, ())
+        gate = {1: (near[0],), 2: (right0,)}.get(i, ())
         send, later = chosen(diag, passed[i], a[i], (b0 if last else swap[i + 1],), gate)
         if last:
             b0 = later
         else:
             swap[i + 1] = later
         near[i] = move(send, over_z)
-        far[i] = move(near[i], over_y)
         if i == 1:
             right0, right1 = masked_right(mask0_cols, mask1_cols, x0_cols, x1_cols, (send,))
-    back = move(handed_on(coded, near[-1]), over_z)
-    square, tangent = own(early, (b0,), (move(b0, over_y),))
-    coded, b1 = partials(late, (b1,), weight=16)
-    *outs, b2 = finished(
-        keep, square, tangent, back, (), 0, all_rows, (b2,), (coded,), weight=1024
-    )
+    far[0], far[1], far[3] = (move(near[i], over_y) for i in (0, 1, 3))
+    (coded,) = partials(early)
+    coded, last_near = handed_on((coded, near[2]), (near[3],))
     back = move(coded, over_z)
-    square, tangent = own(late, (b1, b2), (move(b1, over_y), move(b2, over_y)))
-    return tuple(finished(keep, square, tangent, back, outs, split, all_rows))
+    far[2] = move(last_near, over_y)
+    mine = own(early, (b0,), (move(b0, over_y),))
+    coded, b1 = partials(late, given=(b1,), gates=mine[:1])
+    (coded,) = handed_on((coded,), (back,))
+    outs = finished(keep, *mine, back, (), 0, all_rows)
+    back = move(coded, over_z)
+    mine = own(late, (b1,), (move(b1, over_y),))
+    return tuple(finished(keep, *mine, back, outs, split, all_rows))
 
 
 def passed_along(shard, axis, by):

time: 119 us -> 108 us (0.908)
  waiting for transfers between devices: 62.1 us -> 44.1 us
  starting transfers between devices: 18.5 us -> 25.7 us
    ppermute x17 -> x16, waiting for transfers between devices: 62.1 us -> 44.1 us  [move(): return lax.ppermute(values, ('row', 'col'), pairs)]
    ppermute x17 -> x16, starting transfers between devices: 18.5 us -> 25.7 us  [move(): return lax.ppermute(values, ('row', 'col'), pairs)]
  transfers between devices with their start and end apart: 17 -> 16, of which waited for: 9 -> 9; matrix products, arithmetic and copies ran while one was open for 0% -> 0% of each run, Pallas kernels for 26% -> 29%
where the time goes in v5:
time: 108 us; the launch traced here: 107 us
  waiting for transfers between devices  44.1 us (41%)
  Pallas kernels  35.1 us (32%)
  starting transfers between devices  25.7 us (24%)
  local copies, waits for them, and re-layouts  1.55 us (1%)
    ppermute x16, waiting for transfers between devices, move(): return lax.ppermute(values, ('row', 'col'), pairs)  44.1 us
    ppermute x16, starting transfers between devices, move(): return lax.ppermute(values, ('row', 'col'), pairs)  25.7 us
    pallas_call x2, Pallas kernels, partial_products(): pl.pallas_call(functools.partial(partial_kernel, len(near), len(given)),...  9.96 us
    pallas_call x2, Pallas kernels, local_products(): pl.pallas_call(functools.partial(local_kernel, many), grid=(columns // wi...  9.34 us
    pallas_call x1, Pallas kernels, masked_right(): pl.pallas_call(right_kernel, grid=(depth // tall,), in_specs=[SM(), SM(),...  6.96 us
    pallas_call x2, Pallas kernels, masked_chunks(): pl.pallas_call(functools.partial(chunk_kernel, spans, slabs, panel), in_s...  3.24 us
    pallas_call x2, Pallas kernels, finished(): pl.pallas_call(functools.partial(finish_kernel, start, many), in_specs=[S...  2.84 us
  transfers between devices with their start and end apart: 16, of which 9 were waited for; matrix products, arithmetic and copies ran while one was open for 0% of the time, Pallas kernels for 29%

profile of v5, /device:TPU:0, one launch (start us, length us, event | category | flops | bytes accessed | tf_op | source)
XLA Modules:
  0.0 107.2 jit_solution(4686121451136088934)
XLA Ops:
  3.2 3.1 %collective-permute-start = (bf16[48,2048]{1,0:T(8,128)(2,1)S(1)}, bf16[48,2048]{1,0:T(8,128)(2,1)S(1)}, u32[]{:S(2)}, u32[]{:S(2)}) collective-permute-start(bf16[48,2048]{1,0:T(8,128)(2,1)S(1)} %get-tuple-element.32.refs_6_), channel_id=1, source_target_pairs={{0,1},{1,0},{2,3},{3,2},{4,5},{5,4},{6,7},{7,6},{8,9},{9,8},{10,11... | collective-permute-start | bytes 589832 | tf_op jit(solution)/shard_map/ppermute | solution.py:426
  6.2 2.1 %left_chunks.3 = (bf16[64,2048]{1,0:T(8,128)(2,1)S(1)}, bf16[64,2048]{1,0:T(8,128)(2,1)S(1)}, bf16[96,2048]{1,0:T(8,128)(2,1)S(1)}, bf16[96,2048]{1,0:T(8,128)(2...) custom-call(s32[1]{0:T(128)} %bitcast.1.refs_0_, ...), custom_call_target="tpu_custom_call" | custom-call | bytes 65536 | tf_op jit(solution)/shard_map/left_chunks/pallas_call | solution.py:102
  8.4 2.8 %collective-permute-done.refs_0_.refs_3_ = bf16[48,2048]{1,0:T(8,128)(2,1)S(1)} collective-permute-done((bf16[48,2048]{1,0:T(8,128)(2,1)S(1)}, bf16[48,2048]{1,0:T(8,128)(2,1)S(1)}, u32[]{:S(2)}, u32[]{:S(2)}) %collective-permute-start) | collective-permute-done | bytes 196640 | tf_op jit(solution)/shard_map/ppermute | solution.py:426
  11.4 1.8 %collective-permute-start.2 = (bf16[64,2048]{1,0:T(8,128)(2,1)S(1)}, bf16[64,2048]{1,0:T(8,128)(2,1)S(1)}, u32[]{:S(2)}, u32[]{:S(2)}) collective-permute-start(bf16[64,2048]{1,0:T(8,128)(2,1)S(1)} %get-tuple-element.36), channel_id=1, source_target_pairs={{0,1},{1,0},{2,3},{3,2},{4,5},{5,4},{6,7},{7,6},{8,9},{9,8},{10,11... | collective-permute-start | bytes 786440 | tf_op jit(solution)/shard_map/ppermute | solution.py:426
  13.3 2.6 %collective-permute-start.1 = (bf16[48,2048]{1,0:T(8,128)(2,1)S(1)}, bf16[48,2048]{1,0:T(8,128)(2,1)S(1)}, u32[]{:S(2)}, u32[]{:S(2)}) collective-permute-start(bf16[48,2048]{1,0:T(8,128)(2,1)S(1)} %get-tuple-element.35), channel_id=1, source_target_pairs={{0,16},{1,17},{2,18},{3,19},{4,20},{5,21},{6,22},{7,23},{8,24},{9,... | collective-permute-start | bytes 589832 | tf_op jit(solution)/shard_map/ppermute | solution.py:426
  15.8 8.0 %collective-permute-done.1.refs_0_ = bf16[48,2048]{1,0:T(8,128)(2,1)S(1)} collective-permute-done((bf16[48,2048]{1,0:T(8,128)(2,1)S(1)}, bf16[48,2048]{1,0:T(8,128)(2,1)S(1)}, u32[]{:S(2)}, u32[]{:S(2)}) %collective-permute-start.1) | collective-permute-done | bytes 196640 | tf_op jit(solution)/shard_map/ppermute | solution.py:426
  25.6 7.0 %right_panels.1 = (bf16[2048,768]{1,0:T(8,128)(2,1)S(1)}, bf16[2048,768]{1,0:T(8,128)(2,1)}) custom-call(s32[16,6]{1,0:T(8,128)S(1)} %copy.13.mask0, s32[16,6]{1,0:T(8,128)S(1)} %copy.14.mask1, bf16[2048,768]{1,0:T(8,128)(2,1)} %x0.1, bf16[2048,768]{1,0:T(8,128)(2,1)} %x1.1, bf16[64,2048]{1,0:T(8,128)(2,1)} %get-tuple-element.39.rest_0_), custom_call_target="tpu_custom_call" | custom-call | bytes 196608 | tf_op jit(solution)/shard_map/right_panels/pallas_call | solution.py:201
  32.5 2.4 %collective-permute-done.3.refs_1_.refs_3_ = bf16[96,2048]{1,0:T(8,128)(2,1)S(1)} collective-permute-done((bf16[96,2048]{1,0:T(8,128)(2,1)}, bf16[96,2048]{1,0:T(8,128)(2,1)S(1)}, u32[]{:S(2)}, u32[]{:S(2)}) %collective-permute-start.3) | collective-permute-done | bytes 393248 | tf_op jit(solution)/shard_map/ppermute | solution.py:426
  37.4 3.2 %collective-permute-done.7.refs_1_ = bf16[64,2048]{1,0:T(8,128)(2,1)S(1)} collective-permute-done((bf16[64,2048]{1,0:T(8,128)(2,1)}, bf16[64,2048]{1,0:T(8,128)(2,1)S(1)}, u32[]{:S(2)}, u32[]{:S(2)}) %collective-permute-start.7) | collective-permute-done | bytes 262176 | tf_op jit(solution)/shard_map/ppermute | solution.py:426
  40.6 9.8 %collective-permute-start.9 = (bf16[64,2048]{1,0:T(8,128)(2,1)S(1)}, bf16[64,2048]{1,0:T(8,128)(2,1)S(1)}, u32[]{:S(2)}, u32[]{:S(2)}) collective-permute-start(bf16[64,2048]{1,0:T(8,128)(2,1)S(1)} %collective-permute-done.7.refs_1_), channel_id=1, source_target_pairs={{0,1},{1,0},{2,3},{3,2},{4,5},{5,4},{6,7},{7,6},{8,9},{9,8},{10,11... | collective-permute-start | bytes 786440 | tf_op jit(solution)/shard_map/ppermute | solution.py:426
  51.1 2.1 %collective-permute-start.12 = (bf16[112,2048]{1,0:T(8,128)(2,1)S(1)}, bf16[112,2048]{1,0:T(8,128)(2,1)S(1)}, u32[]{:S(2)}, u32[]{:S(2)}) collective-permute-start(bf16[112,2048]{1,0:T(8,128)(2,1)S(1)} %get-tuple-element.52.refs_2_), channel_id=1, source_target_pairs={{0,1},{1,0},{2,3},{3,2},{4,5},{5,4},{6,7},{7,6},{8,9},{9,8},{10,11... | collective-permute-start | bytes 1376264 | tf_op jit(solution)/shard_map/ppermute | solution.py:426
  53.2 3.7 %collective-permute-done.8.refs_2_ = bf16[48,2048]{1,0:T(8,128)(2,1)S(1)} collective-permute-done((bf16[48,2048]{1,0:T(8,128)(2,1)S(1)}, bf16[48,2048]{1,0:T(8,128)(2,1)S(1)}, u32[]{:S(2)}, u32[]{:S(2)}) %collective-permute-start.8) | collective-permute-done | bytes 196640 | tf_op jit(solution)/shard_map/ppermute | solution.py:426
  56.9 4.4 %partial_products.2.refs_0_ = s16[1360,128]{1,0:T(8,128)(2,1)S(1)} custom-call(s32[1]{0:T(128)} %bitcast.refs_1_.diag, bf16[2048,768]{1,0:T(8,128)(2,1)S(1)} %get-tuple-element.40.refs_0_.right0, bf16[2048,768]{1,0:T(8,128)(2,1)} %get-tuple-element.41.right1, bf16[48,2048]{1,0:T(8,128)(2,1)S(1)} %collective-permute-done.1.refs_0_, ...), custom_call_target="tpu_custom_call" | custom-call | flops 16515072 | bytes 112640 | tf_op jit(solution)/shard_map/partial_products/pallas_call | solution.py:322
  61.3 3.1 %collective-permute-done.6.refs_2_.refs_1_ = bf16[48,2048]{1,0:T(8,128)(2,1)S(1)} collective-permute-done((bf16[48,2048]{1,0:T(8,128)(2,1)S(1)}, bf16[48,2048]{1,0:T(8,128)(2,1)S(1)}, u32[]{:S(2)}, u32[]{:S(2)}) %collective-permute-start.6) | collective-permute-done | bytes 196640 | tf_op jit(solution)/shard_map/ppermute | solution.py:426
  64.7 1.4 %collective-permute-start.10 = (bf16[96,2048]{1,0:T(8,128)(2,1)S(1)}, bf16[96,2048]{1,0:T(8,128)(2,1)S(1)}, u32[]{:S(2)}, u32[]{:S(2)}) collective-permute-start(bf16[96,2048]{1,0:T(8,128)(2,1)S(1)} %get-tuple-element.50), channel_id=1, source_target_pairs={{0,1},{1,0},{2,3},{3,2},{4,5},{5,4},{6,7},{7,6},{8,9},{9,8},{10,11... | collective-permute-start | bytes 1179656 | tf_op jit(solution)/shard_map/ppermute | solution.py:426
  66.8 4.3 %own_products.2 = (f32[112,768]{1,0:T(8,128)S(1)}, f32[112,768]{1,0:T(8,128)S(1)}) custom-call(s32[1]{0:T(128)} %bitcast.refs_1_.diag, bf16[2048,768]{1,0:T(8,128)(2,1)S(1)} %get-tuple-element.40.refs_0_.right0, bf16[2048,768]{1,0:T(8,128)(2,1)} %get-tuple-element.41.right1, bf16[48,2048]{1,0:T(8,128)(2,1)S(1)} %get-tuple-element.33.refs_1_.refs_0_, ...), custom_call_target="tpu_custom_call" | custom-call | flops 16515072 | bytes 126976 | tf_op jit(solution)/shard_map/own_products/pallas_call | solution.py:258
  71.1 7.4 %collective-permute-done.11.refs_3_ = bf16[48,2048]{1,0:T(8,128)(2,1)S(1)} collective-permute-done((bf16[48,2048]{1,0:T(8,128)(2,1)S(1)}, bf16[48,2048]{1,0:T(8,128)(2,1)S(1)}, u32[]{:S(2)}, u32[]{:S(2)}) %collective-permute-start.11) | collective-permute-done | bytes 196640 | tf_op jit(solution)/shard_map/ppermute | solution.py:426
  78.5 5.6 %partial_products.3 = (s16[1744,128]{1,0:T(8,128)(2,1)S(1)}, bf16[144,2048]{1,0:T(8,128)(2,1)S(1)}) custom-call(s32[1]{0:T(128)} %bitcast.refs_1_.diag, bf16[2048,768]{1,0:T(8,128)(2,1)} %copy-done, bf16[2048,768]{1,0:T(8,128)(2,1)} %get-tuple-element.41.right1, bf16[96,2048]{1,0:T(8,128)(2,1)S(1)} %collective-permute-done.4.refs_1_.refs_0_, ...), custom_call_target="tpu_custom_call" | custom-call | flops 21233664 | bytes 116736 | tf_op jit(solution)/shard_map/partial_products/pallas_call | solution.py:322
  84.1 1.4 %collective-permute-start.15 = (bf16[144,2048]{1,0:T(8,128)(2,1)S(1)}, bf16[144,2048]{1,0:T(8,128)(2,1)S(1)}, u32[]{:S(2)}, u32[]{:S(2)}) collective-permute-start(bf16[144,2048]{1,0:T(8,128)(2,1)S(1)} %get-tuple-element.56.refs_2_), channel_id=1, source_target_pairs={{0,1},{1,0},{2,3},{3,2},{4,5},{5,4},{6,7},{7,6},{8,9},{9,8},{10,11... | collective-permute-start | bytes 1769480 | tf_op jit(solution)/shard_map/ppermute | solution.py:426
  85.9 1.4 %finish.2 = (bf16[256,768]{1,0:T(8,128)(2,1)}, bf16[256,768]{1,0:T(8,128)(2,1)}) custom-call(s32[2,6]{1,0:T(2,128)S(1)} %copy-done.6, s16[1360,128]{1,0:T(8,128)(2,1)S(1)} %collective-permute-done.13.refs_1_.coded, f32[112,768]{1,0:T(8,128)S(1)} %get-tuple-element.53.refs_5_.square, f32[112,768]{1,0:T(8,128)S(1)} %get-tuple-element.59.tangent), custom_call_target="tpu_custom_call" | custom-call | bytes 21504 | tf_op jit(solution)/shard_map/finish/pallas_call | solution.py:384
  87.3 9.7 %collective-permute-done.15.refs_5_ = bf16[144,2048]{1,0:T(8,128)(2,1)S(1)} collective-permute-done((bf16[144,2048]{1,0:T(8,128)(2,1)S(1)}, bf16[144,2048]{1,0:T(8,128)(2,1)S(1)}, u32[]{:S(2)}, u32[]{:S(2)}) %collective-permute-start.15) | collective-permute-done | bytes 589856 | tf_op jit(solution)/shard_map/ppermute | solution.py:426
  97.0 5.0 %own_products.3 = (f32[144,768]{1,0:T(8,128)S(1)}, f32[144,768]{1,0:T(8,128)S(1)}) custom-call(s32[1]{0:T(128)} %bitcast.refs_1_.diag, bf16[2048,768]{1,0:T(8,128)(2,1)} %copy-done, bf16[2048,768]{1,0:T(8,128)(2,1)} %get-tuple-element.41.right1, bf16[96,2048]{1,0:T(8,128)(2,1)S(1)} %get-tuple-element.43.refs_2_.refs_0_, ...), custom_call_target="tpu_custom_call" | custom-call | flops 21233664 | bytes 135168 | tf_op jit(solution)/shard_map/own_products/pallas_call | solution.py:258
  102.0 3.7 %collective-permute-done.14.coded = s16[1744,128]{1,0:T(8,128)(2,1)S(1)} collective-permute-done((s16[1744,128]{1,0:T(8,128)(2,1)S(1)}, s16[1744,128]{1,0:T(8,128)(2,1)S(1)}, u32[]{:S(2)}, u32[]{:S(2)}) %collective-permute-start.14) | collective-permute-done | bytes 446496 | tf_op jit(solution)/shard_map/ppermute | solution.py:426
  105.8 1.4 %finish.3 = (bf16[256,768]{1,0:T(8,128)(2,1)}, bf16[256,768]{1,0:T(8,128)(2,1)}) custom-call(s32[2,6]{1,0:T(2,128)S(1)} %copy-done.6, s16[1744,128]{1,0:T(8,128)(2,1)S(1)} %collective-permute-done.14.coded, f32[144,768]{1,0:T(8,128)S(1)} %get-tuple-element.57.square, ...), custom_call_target="tpu_custom_call", output_to_operand_aliasing={{0}: (4, {}), {1}: (5, {})} | custom-call | bytes 27648 | tf_op jit(solution)/shard_map/finish/pallas_call | solution.py:384
  (43 shorter events, 9.0 us)
Async XLA Ops:
  0.7 0.7 copy-start.3
  2.0 4.2 %copy-start.5 = (s32[2,128]{1,0:T(2,128)S(1)}, s32[2,128]{1,0:T(2,128)}, u32[]{:S(2)}) copy-start(s32[2,128]{1,0:T(2,128)} %refs_3_.3) | copy-start | bytes 3076
  3.2 22.2 %copy-start.7 = (s32[16,6]{0,1:T(8,128)S(1)}, s32[16,6]{0,1:T(8,128)}, u32[]{:S(2)}) copy-start(s32[16,6]{0,1:T(8,128)} %param.15) | copy-start | bytes 1156
  3.2 22.3 %copy-start.8 = (s32[16,6]{0,1:T(8,128)S(1)}, s32[16,6]{0,1:T(8,128)}, u32[]{:S(2)}) copy-start(s32[16,6]{0,1:T(8,128)} %param.16) | copy-start | bytes 1156
  3.2 8.0 %collective-permute-start = (bf16[48,2048]{1,0:T(8,128)(2,1)S(1)}, bf16[48,2048]{1,0:T(8,128)(2,1)S(1)}, u32[]{:S(2)}, u32[]{:S(2)}) collective-permute-start(bf16[48,2048]{1,0:T(8,128)(2,1)S(1)} %get-tuple-element.32.refs_6_), channel_id=1, source_target_pairs={{0,1},{1,0},{2,3},{3,2},{4,5},{5,4},{6,7},{7,6},{8,9},{9,8},{10,11... | collective-permute-start | bytes 589832 | tf_op jit(solution)/shard_map/ppermute | solution.py:426
  8.4 17.0 %copy-start.1 = (bf16[48,2048]{1,0:T(8,128)(2,1)}, bf16[48,2048]{1,0:T(8,128)(2,1)S(1)}, u32[]{:S(2)}) copy-start(bf16[48,2048]{1,0:T(8,128)(2,1)S(1)} %get-tuple-element.44.refs_3_) | copy-start | bytes 589828
  11.4 12.4 %collective-permute-start.2 = (bf16[64,2048]{1,0:T(8,128)(2,1)S(1)}, bf16[64,2048]{1,0:T(8,128)(2,1)S(1)}, u32[]{:S(2)}, u32[]{:S(2)}) collective-permute-start(bf16[64,2048]{1,0:T(8,128)(2,1)S(1)} %get-tuple-element.36), channel_id=1, source_target_pairs={{0,1},{1,0},{2,3},{3,2},{4,5},{5,4},{6,7},{7,6},{8,9},{9,8},{10,11... | collective-permute-start | bytes 786440 | tf_op jit(solution)/shard_map/ppermute | solution.py:426
  13.3 10.6 %collective-permute-start.1 = (bf16[48,2048]{1,0:T(8,128)(2,1)S(1)}, bf16[48,2048]{1,0:T(8,128)(2,1)S(1)}, u32[]{:S(2)}, u32[]{:S(2)}) collective-permute-start(bf16[48,2048]{1,0:T(8,128)(2,1)S(1)} %get-tuple-element.35), channel_id=1, source_target_pairs={{0,16},{1,17},{2,18},{3,19},{4,20},{5,21},{6,22},{7,23},{8,24},{9,... | collective-permute-start | bytes 589832 | tf_op jit(solution)/shard_map/ppermute | solution.py:426
  24.7 10.2 %collective-permute-start.3 = (bf16[96,2048]{1,0:T(8,128)(2,1)}, bf16[96,2048]{1,0:T(8,128)(2,1)S(1)}, u32[]{:S(2)}, u32[]{:S(2)}) collective-permute-start(bf16[96,2048]{1,0:T(8,128)(2,1)} %get-tuple-element.42), channel_id=1, source_target_pairs={{0,1},{1,0},{2,3},{3,2},{4,5},{5,4},{6,7},{7,6},{8,9},{9,8},{10,11... | collective-permute-start | bytes 1179656 | tf_op jit(solution)/shard_map/ppermute | solution.py:426
  25.4 15.2 %collective-permute-start.7 = (bf16[64,2048]{1,0:T(8,128)(2,1)}, bf16[64,2048]{1,0:T(8,128)(2,1)S(1)}, u32[]{:S(2)}, u32[]{:S(2)}) collective-permute-start(bf16[64,2048]{1,0:T(8,128)(2,1)} %get-tuple-element.39.rest_0_), channel_id=1, source_target_pairs={{0,16},{1,17},{2,18},{3,19},{4,20},{5,21},{6,22},{7,23},{8,24},{9,... | collective-permute-start | bytes 786440 | tf_op jit(solution)/shard_map/ppermute | solution.py:426
  25.6 9.4 %copy-start.2 = (bf16[48,2048]{1,0:T(8,128)(2,1)S(1)}, bf16[48,2048]{1,0:T(8,128)(2,1)}, u32[]{:S(2)}) copy-start(bf16[48,2048]{1,0:T(8,128)(2,1)} %copy-done.1) | copy-start | bytes 589828
  32.5 34.3 %copy-start = (bf16[2048,768]{1,0:T(8,128)(2,1)}, bf16[2048,768]{1,0:T(8,128)(2,1)S(1)}, u32[]{:S(2)}) copy-start(bf16[2048,768]{1,0:T(8,128)(2,1)S(1)} %get-tuple-element.40.refs_0_.right0) | copy-start | bytes 9437188
  35.4 15.1 %collective-permute-start.5 = (bf16[48,2048]{1,0:T(8,128)(2,1)S(1)}, bf16[48,2048]{1,0:T(8,128)(2,1)S(1)}, u32[]{:S(2)}, u32[]{:S(2)}) collective-permute-start(bf16[48,2048]{1,0:T(8,128)(2,1)S(1)} %get-tuple-element.46), channel_id=1, source_target_pairs={{0,1},{1,0},{2,3},{3,2},{4,5},{5,4},{6,7},{7,6},{8,9},{9,8},{10,11... | collective-permute-start | bytes 589832 | tf_op jit(solution)/shard_map/ppermute | solution.py:426
  36.2 28.2 %collective-permute-start.4 = (bf16[96,2048]{1,0:T(8,128)(2,1)S(1)}, bf16[96,2048]{1,0:T(8,128)(2,1)S(1)}, u32[]{:S(2)}, u32[]{:S(2)}) collective-permute-start(bf16[96,2048]{1,0:T(8,128)(2,1)S(1)} %get-tuple-element.45), channel_id=1, source_target_pairs={{0,16},{1,17},{2,18},{3,19},{4,20},{5,21},{6,22},{7,23},{8,24},{9,... | collective-permute-start | bytes 1179656 | tf_op jit(solution)/shard_map/ppermute | solution.py:426
  40.6 16.3 %collective-permute-start.9 = (bf16[64,2048]{1,0:T(8,128)(2,1)S(1)}, bf16[64,2048]{1,0:T(8,128)(2,1)S(1)}, u32[]{:S(2)}, u32[]{:S(2)}) collective-permute-start(bf16[64,2048]{1,0:T(8,128)(2,1)S(1)} %collective-permute-done.7.refs_1_), channel_id=1, source_target_pairs={{0,1},{1,0},{2,3},{3,2},{4,5},{5,4},{6,7},{7,6},{8,9},{9,8},{10,11... | collective-permute-start | bytes 786440 | tf_op jit(solution)/shard_map/ppermute | solution.py:426
  50.4 6.5 %collective-permute-start.8 = (bf16[48,2048]{1,0:T(8,128)(2,1)S(1)}, bf16[48,2048]{1,0:T(8,128)(2,1)S(1)}, u32[]{:S(2)}, u32[]{:S(2)}) collective-permute-start(bf16[48,2048]{1,0:T(8,128)(2,1)S(1)} %collective-permute-done.1.refs_0_), channel_id=1, source_target_pairs={{0,1},{1,0},{2,3},{3,2},{4,5},{5,4},{6,7},{7,6},{8,9},{9,8},{10,11... | collective-permute-start | bytes 589832 | tf_op jit(solution)/shard_map/ppermute | solution.py:426
  51.0 13.3 %collective-permute-start.6 = (bf16[48,2048]{1,0:T(8,128)(2,1)S(1)}, bf16[48,2048]{1,0:T(8,128)(2,1)S(1)}, u32[]{:S(2)}, u32[]{:S(2)}) collective-permute-start(bf16[48,2048]{1,0:T(8,128)(2,1)S(1)} %get-tuple-element.49), channel_id=1, source_target_pairs={{0,16},{1,17},{2,18},{3,19},{4,20},{5,21},{6,22},{7,23},{8,24},{9,... | collective-permute-start | bytes 589832 | tf_op jit(solution)/shard_map/ppermute | solution.py:426
  51.1 15.7 %collective-permute-start.12 = (bf16[112,2048]{1,0:T(8,128)(2,1)S(1)}, bf16[112,2048]{1,0:T(8,128)(2,1)S(1)}, u32[]{:S(2)}, u32[]{:S(2)}) collective-permute-start(bf16[112,2048]{1,0:T(8,128)(2,1)S(1)} %get-tuple-element.52.refs_2_), channel_id=1, source_target_pairs={{0,1},{1,0},{2,3},{3,2},{4,5},{5,4},{6,7},{7,6},{8,9},{9,8},{10,11... | collective-permute-start | bytes 1376264 | tf_op jit(solution)/shard_map/ppermute | solution.py:426
  64.7 13.8 %collective-permute-start.10 = (bf16[96,2048]{1,0:T(8,128)(2,1)S(1)}, bf16[96,2048]{1,0:T(8,128)(2,1)S(1)}, u32[]{:S(2)}, u32[]{:S(2)}) collective-permute-start(bf16[96,2048]{1,0:T(8,128)(2,1)S(1)} %get-tuple-element.50), channel_id=1, source_target_pairs={{0,1},{1,0},{2,3},{3,2},{4,5},{5,4},{6,7},{7,6},{8,9},{9,8},{10,11... | collective-permute-start | bytes 1179656 | tf_op jit(solution)/shard_map/ppermute | solution.py:426
  66.1 19.4 %collective-permute-start.13 = (s16[1360,128]{1,0:T(8,128)(2,1)S(1)}, s16[1360,128]{1,0:T(8,128)(2,1)S(1)}, u32[]{:S(2)}, u32[]{:S(2)}) collective-permute-start(s16[1360,128]{1,0:T(8,128)(2,1)S(1)} %get-tuple-element.55), channel_id=1, source_target_pairs={{0,16},{1,17},{2,18},{3,19},{4,20},{5,21},{6,22},{7,23},{8,24},{9,... | collective-permute-start | bytes 1044488 | tf_op jit(solution)/shard_map/ppermute | solution.py:426
  66.1 12.4 %collective-permute-start.11 = (bf16[48,2048]{1,0:T(8,128)(2,1)S(1)}, bf16[48,2048]{1,0:T(8,128)(2,1)S(1)}, u32[]{:S(2)}, u32[]{:S(2)}) collective-permute-start(bf16[48,2048]{1,0:T(8,128)(2,1)S(1)} %collective-permute-done.6.refs_2_.refs_1_), channel_id=1, source_target_pairs={{0,1},{1,0},{2,3},{3,2},{4,5},{5,4},{6,7},{7,6},{8,9},{9,8},{10,11... | collective-permute-start | bytes 589832 | tf_op jit(solution)/shard_map/ppermute | solution.py:426
  78.5 7.3 %copy-start.6 = (s32[2,6]{1,0:T(2,128)S(1)}, s32[2,6]{1,0:T(2,128)}, u32[]{:S(2)}) copy-start(s32[2,6]{1,0:T(2,128)} %keep.3) | copy-start | bytes 148
  84.1 12.9 %collective-permute-start.15 = (bf16[144,2048]{1,0:T(8,128)(2,1)S(1)}, bf16[144,2048]{1,0:T(8,128)(2,1)S(1)}, u32[]{:S(2)}, u32[]{:S(2)}) collective-permute-start(bf16[144,2048]{1,0:T(8,128)(2,1)S(1)} %get-tuple-element.56.refs_2_), channel_id=1, source_target_pairs={{0,1},{1,0},{2,3},{3,2},{4,5},{5,4},{6,7},{7,6},{8,9},{9,8},{10,11... | collective-permute-start | bytes 1769480 | tf_op jit(solution)/shard_map/ppermute | solution.py:426
  85.8 20.0 %collective-permute-start.14 = (s16[1744,128]{1,0:T(8,128)(2,1)S(1)}, s16[1744,128]{1,0:T(8,128)(2,1)S(1)}, u32[]{:S(2)}, u32[]{:S(2)}) collective-permute-start(s16[1744,128]{1,0:T(8,128)(2,1)S(1)} %handed_on.3), channel_id=1, source_target_pairs={{0,16},{1,17},{2,18},{3,19},{4,20},{5,21},{6,22},{7,23},{8,24},{9,... | collective-permute-start | bytes 1339400 | tf_op jit(solution)/shard_map/ppermute | solution.py:426
  (1 other events, 0.7 us)

commit v6 on v5

--- a/solution.py
+++ b/solution.py
@@ -13,14 +13,15 @@
 STEPS = 32.0
 LN2 = math.log(2.0)
 VMEM_BYTES = 48 * 1024 * 1024
+ALL_VMEM_BYTES = 62 * 1024 * 1024
 
 VM = functools.partial(pl.BlockSpec, memory_space=pltpu.VMEM)
 SM = functools.partial(pl.BlockSpec, memory_space=pltpu.SMEM)
 HB = functools.partial(pl.BlockSpec, memory_space=pl.ANY)
 
 
-def params():
-    return pltpu.CompilerParams(vmem_limit_bytes=VMEM_BYTES)
+def params(limit=VMEM_BYTES):
+    return pltpu.CompilerParams(vmem_limit_bytes=limit)
 
 
 def cost(flops, moved):
@@ -111,7 +112,7 @@
             pltpu.SemaphoreType.DMA((2,)),
             pltpu.SemaphoreType.DMA((len(spans), 2)),
         ],
-        compiler_params=params(),
+        compiler_params=params(VMEM_BYTES if slabs else ALL_VMEM_BYTES),
         cost_estimate=cost(0, 8 * high * panel),
         name="left_chunks",
     )(place, diag, mask0, mask1, x0, x1, *after)
@@ -409,7 +410,7 @@
     half = row_index // group
     diag = (half == lax.axis_index("col")).astype(jnp.int32).reshape(1)
     place = (row_index % group).astype(jnp.int32).reshape(1)
-    edges = [all_rows * e // 16 for e in (0, 3, 7, 13, 16)]
+    edges = [all_rows * e // 16 for e in (0, 3, 8, 13, 16)]
     spans = list(zip(edges, edges[1:]))
     many = len(spans)
     split = edges[2]

time: 108 us -> 109 us (level)
  waiting for transfers between devices: 44.1 us -> 54.2 us
  starting transfers between devices: 25.7 us -> 18.6 us
  Pallas kernels: 35.1 us -> 34 us
    ppermute x16, waiting for transfers between devices: 44.1 us -> 54.2 us  [move(): return lax.ppermute(values, ('row', 'col'), pairs)]
    ppermute x16, starting transfers between devices: 25.7 us -> 18.6 us  [move(): return lax.ppermute(values, ('row', 'col'), pairs)]
  transfers between devices with their start and end apart: 16 -> 16, of which waited for: 9 -> 11; matrix products, arithmetic and copies ran while one was open for 0% -> 0% of each run, Pallas kernels for 29% -> 27%
where the time goes in v6:
time: 109 us
  waiting for transfers between devices  54.2 us (50%)
  Pallas kernels  34 us (31%)
  starting transfers between devices  18.6 us (17%)
  local copies, waits for them, and re-layouts  1.15 us (1%)
    ppermute x16, waiting for transfers between devices, move(): return lax.ppermute(values, ('row', 'col'), pairs)  54.2 us
    ppermute x16, starting transfers between devices, move(): return lax.ppermute(values, ('row', 'col'), pairs)  18.6 us
    pallas_call x2, Pallas kernels, partial_products(): pl.pallas_call(functools.partial(partial_kernel, len(near), len(given)),...  9.31 us
    pallas_call x2, Pallas kernels, local_products(): pl.pallas_call(functools.partial(local_kernel, many), grid=(columns // wi...  8.44 us
    pallas_call x1, Pallas kernels, masked_right(): pl.pallas_call(right_kernel, grid=(depth // tall,), in_specs=[SM(), SM(),...  6.96 us
    pallas_call x2, Pallas kernels, masked_chunks(): pl.pallas_call(functools.partial(chunk_kernel, spans, slabs, panel), in_s...  4.01 us
    pallas_call x2, Pallas kernels, finished(): pl.pallas_call(functools.partial(finish_kernel, start, many), in_specs=[S...  2.84 us
  transfers between devices with their start and end apart: 16, of which 11 were waited for; matrix products, arithmetic and copies ran while one was open for 0% of the time, Pallas kernels for 27%

profile of v6, /device:TPU:0, one launch (start us, length us, event | category | flops | bytes accessed | tf_op | source)
XLA Modules:
  0.0 108.8 jit_solution(9863215084590967680)
XLA Ops:
  0.7 1.9 %left_chunks.2 = (bf16[48,2048]{1,0:T(8,128)(2,1)}, bf16[48,2048]{1,0:T(8,128)(2,1)}) custom-call(s32[1]{0:T(128)} %bitcast.1.refs_0_, s32[1]{0:T(128)} %bitcast.refs_1_.diag, s32[2,128]{1,0:T(2,128)} %refs_2_.3, s32[2,128]{1,0:T(2,128)} %refs_3_.3, bf16[256,16384]{1,0:T(8,128)(2,1)} %refs_4_.3, bf16[256,16384]{1,0:T(8,128)(2,1)} %refs_5_.3), custom_call_target="tpu_custom_call" | custom-call | bytes 12288 | tf_op jit(solution)/shard_map/left_chunks/pallas_call | solution.py:103
  2.6 3.1 %collective-permute-start = (bf16[48,2048]{1,0:T(8,128)(2,1)}, bf16[48,2048]{1,0:T(8,128)(2,1)S(1)}, u32[]{:S(2)}, u32[]{:S(2)}) collective-permute-start(bf16[48,2048]{1,0:T(8,128)(2,1)} %get-tuple-element.32.refs_6_), channel_id=1, source_target_pairs={{0,1},{1,0},{2,3},{3,2},{4,5},{5,4},{6,7},{7,6},{8,9},{9,8},{10,11... | collective-permute-start | bytes 589832 | tf_op jit(solution)/shard_map/ppermute | solution.py:427
  6.6 2.1 %left_chunks.3 = (bf16[80,2048]{1,0:T(8,128)(2,1)S(1)}, bf16[80,2048]{1,0:T(8,128)(2,1)S(1)}, bf16[80,2048]{1,0:T(8,128)(2,1)S(1)}, bf16[80,2048]{1,0:T(8,128)(2...) custom-call(s32[1]{0:T(128)} %bitcast.1.refs_0_, ...), custom_call_target="tpu_custom_call" | custom-call | bytes 65536 | tf_op jit(solution)/shard_map/left_chunks/pallas_call | solution.py:103
  8.7 2.0 %collective-permute-done.refs_0_.refs_3_ = bf16[48,2048]{1,0:T(8,128)(2,1)S(1)} collective-permute-done((bf16[48,2048]{1,0:T(8,128)(2,1)}, bf16[48,2048]{1,0:T(8,128)(2,1)S(1)}, u32[]{:S(2)}, u32[]{:S(2)}) %collective-permute-start) | collective-permute-done | bytes 196640 | tf_op jit(solution)/shard_map/ppermute | solution.py:427
  11.1 1.8 %collective-permute-start.2 = (bf16[80,2048]{1,0:T(8,128)(2,1)S(1)}, bf16[80,2048]{1,0:T(8,128)(2,1)S(1)}, u32[]{:S(2)}, u32[]{:S(2)}) collective-permute-start(bf16[80,2048]{1,0:T(8,128)(2,1)S(1)} %get-tuple-element.36), channel_id=1, source_target_pairs={{0,1},{1,0},{2,3},{3,2},{4,5},{5,4},{6,7},{7,6},{8,9},{9,8},{10,11... | collective-permute-start | bytes 983048 | tf_op jit(solution)/shard_map/ppermute | solution.py:427
  12.9 2.6 %collective-permute-start.1 = (bf16[48,2048]{1,0:T(8,128)(2,1)S(1)}, bf16[48,2048]{1,0:T(8,128)(2,1)S(1)}, u32[]{:S(2)}, u32[]{:S(2)}) collective-permute-start(bf16[48,2048]{1,0:T(8,128)(2,1)S(1)} %get-tuple-element.35), channel_id=1, source_target_pairs={{0,16},{1,17},{2,18},{3,19},{4,20},{5,21},{6,22},{7,23},{8,24},{9,... | collective-permute-start | bytes 589832 | tf_op jit(solution)/shard_map/ppermute | solution.py:427
  15.5 8.0 %collective-permute-done.1.refs_0_ = bf16[48,2048]{1,0:T(8,128)(2,1)S(1)} collective-permute-done((bf16[48,2048]{1,0:T(8,128)(2,1)S(1)}, bf16[48,2048]{1,0:T(8,128)(2,1)S(1)}, u32[]{:S(2)}, u32[]{:S(2)}) %collective-permute-start.1) | collective-permute-done | bytes 196640 | tf_op jit(solution)/shard_map/ppermute | solution.py:427
  25.2 7.0 %right_panels.1 = (bf16[2048,768]{1,0:T(8,128)(2,1)S(1)}, bf16[2048,768]{1,0:T(8,128)(2,1)}) custom-call(s32[16,6]{1,0:T(8,128)S(1)} %copy.13.mask0, s32[16,6]{1,0:T(8,128)S(1)} %copy.14.mask1, bf16[2048,768]{1,0:T(8,128)(2,1)} %x0.1, bf16[2048,768]{1,0:T(8,128)(2,1)} %x1.1, bf16[80,2048]{1,0:T(8,128)(2,1)} %get-tuple-element.39.rest_0_), custom_call_target="tpu_custom_call" | custom-call | bytes 196608 | tf_op jit(solution)/shard_map/right_panels/pallas_call | solution.py:202
  34.4 7.2 %collective-permute-done.7.refs_1_ = bf16[80,2048]{1,0:T(8,128)(2,1)S(1)} collective-permute-done((bf16[80,2048]{1,0:T(8,128)(2,1)}, bf16[80,2048]{1,0:T(8,128)(2,1)S(1)}, u32[]{:S(2)}, u32[]{:S(2)}) %collective-permute-start.7) | collective-permute-done | bytes 327712 | tf_op jit(solution)/shard_map/ppermute | solution.py:427
  41.6 1.3 %collective-permute-start.9 = (bf16[80,2048]{1,0:T(8,128)(2,1)S(1)}, bf16[80,2048]{1,0:T(8,128)(2,1)S(1)}, u32[]{:S(2)}, u32[]{:S(2)}) collective-permute-start(bf16[80,2048]{1,0:T(8,128)(2,1)S(1)} %collective-permute-done.7.refs_1_), channel_id=1, source_target_pairs={{0,1},{1,0},{2,3},{3,2},{4,5},{5,4},{6,7},{7,6},{8,9},{9,8},{10,11... | collective-permute-start | bytes 983048 | tf_op jit(solution)/shard_map/ppermute | solution.py:427
  44.0 1.4 %collective-permute-start.12 = (bf16[128,2048]{1,0:T(8,128)(2,1)S(1)}, bf16[128,2048]{1,0:T(8,128)(2,1)S(1)}, u32[]{:S(2)}, u32[]{:S(2)}) collective-permute-start(bf16[128,2048]{1,0:T(8,128)(2,1)S(1)} %get-tuple-element.52.refs_2_), channel_id=1, source_target_pairs={{0,1},{1,0},{2,3},{3,2},{4,5},{5,4},{6,7},{7,6},{8,9},{9,8},{10,11... | collective-permute-start | bytes 1572872 | tf_op jit(solution)/shard_map/ppermute | solution.py:427
  45.3 2.9 %collective-permute-start.6 = (bf16[48,2048]{1,0:T(8,128)(2,1)S(1)}, bf16[48,2048]{1,0:T(8,128)(2,1)S(1)}, u32[]{:S(2)}, u32[]{:S(2)}) collective-permute-start(bf16[48,2048]{1,0:T(8,128)(2,1)S(1)} %get-tuple-element.49), channel_id=1, source_target_pairs={{0,16},{1,17},{2,18},{3,19},{4,20},{5,21},{6,22},{7,23},{8,24},{9,... | collective-permute-start | bytes 589832 | tf_op jit(solution)/shard_map/ppermute | solution.py:427
  48.2 8.2 %collective-permute-done.8.refs_2_ = bf16[48,2048]{1,0:T(8,128)(2,1)S(1)} collective-permute-done((bf16[48,2048]{1,0:T(8,128)(2,1)S(1)}, bf16[48,2048]{1,0:T(8,128)(2,1)S(1)}, u32[]{:S(2)}, u32[]{:S(2)}) %collective-permute-start.8) | collective-permute-done | bytes 196640 | tf_op jit(solution)/shard_map/ppermute | solution.py:427
  56.5 4.6 %partial_products.2.refs_0_ = s16[1552,128]{1,0:T(8,128)(2,1)S(1)} custom-call(s32[1]{0:T(128)} %bitcast.refs_1_.diag, bf16[2048,768]{1,0:T(8,128)(2,1)S(1)} %get-tuple-element.40.refs_0_.right0, bf16[2048,768]{1,0:T(8,128)(2,1)} %get-tuple-element.41.right1, bf16[48,2048]{1,0:T(8,128)(2,1)S(1)} %collective-permute-done.1.refs_0_, ...), custom_call_target="tpu_custom_call" | custom-call | flops 18874368 | bytes 114688 | tf_op jit(solution)/shard_map/partial_products/pallas_call | solution.py:323
  61.1 2.0 %collective-permute-done.4.refs_1_.refs_0_ = bf16[80,2048]{1,0:T(8,128)(2,1)S(1)} collective-permute-done((bf16[80,2048]{1,0:T(8,128)(2,1)S(1)}, bf16[80,2048]{1,0:T(8,128)(2,1)S(1)}, u32[]{:S(2)}, u32[]{:S(2)}) %collective-permute-start.4) | collective-permute-done | bytes 327712 | tf_op jit(solution)/shard_map/ppermute | solution.py:427
  63.1 3.6 %collective-permute-done.6.refs_2_.refs_1_ = bf16[48,2048]{1,0:T(8,128)(2,1)S(1)} collective-permute-done((bf16[48,2048]{1,0:T(8,128)(2,1)S(1)}, bf16[48,2048]{1,0:T(8,128)(2,1)S(1)}, u32[]{:S(2)}, u32[]{:S(2)}) %collective-permute-start.6) | collective-permute-done | bytes 196640 | tf_op jit(solution)/shard_map/ppermute | solution.py:427
  69.1 4.2 %own_products.2 = (f32[128,768]{1,0:T(8,128)S(1)}, f32[128,768]{1,0:T(8,128)S(1)}) custom-call(s32[1]{0:T(128)} %bitcast.refs_1_.diag, bf16[2048,768]{1,0:T(8,128)(2,1)S(1)} %get-tuple-element.40.refs_0_.right0, bf16[2048,768]{1,0:T(8,128)(2,1)} %get-tuple-element.41.right1, bf16[48,2048]{1,0:T(8,128)(2,1)S(1)} %copy-done, ...), custom_call_target="tpu_custom_call" | custom-call | flops 18874368 | bytes 131072 | tf_op jit(solution)/shard_map/own_products/pallas_call | solution.py:259
  73.4 7.1 %collective-permute-done.11.refs_3_ = bf16[48,2048]{1,0:T(8,128)(2,1)S(1)} collective-permute-done((bf16[48,2048]{1,0:T(8,128)(2,1)S(1)}, bf16[48,2048]{1,0:T(8,128)(2,1)S(1)}, u32[]{:S(2)}, u32[]{:S(2)}) %collective-permute-start.11) | collective-permute-done | bytes 196640 | tf_op jit(solution)/shard_map/ppermute | solution.py:427
  80.5 4.7 %partial_products.3 = (s16[1552,128]{1,0:T(8,128)(2,1)S(1)}, bf16[128,2048]{1,0:T(8,128)(2,1)S(1)}) custom-call(s32[1]{0:T(128)} %bitcast.refs_1_.diag, bf16[2048,768]{1,0:T(8,128)(2,1)S(1)} %get-tuple-element.40.refs_0_.right0, bf16[2048,768]{1,0:T(8,128)(2,1)} %get-tuple-element.41.right1, bf16[80,2048]{1,0:T(8,128)(2,1)S(1)} %collective-permute-done.4.refs_1_.refs_0_, ...), custom_call_target="tpu_custom_call" | custom-call | flops 18874368 | bytes 114688 | tf_op jit(solution)/shard_map/partial_products/pallas_call | solution.py:323
  87.1 1.4 %finish.2 = (bf16[256,768]{1,0:T(8,128)(2,1)}, bf16[256,768]{1,0:T(8,128)(2,1)}) custom-call(s32[2,6]{1,0:T(2,128)S(1)} %copy-done.4, s16[1552,128]{1,0:T(8,128)(2,1)S(1)} %collective-permute-done.13.refs_1_.coded, f32[128,768]{1,0:T(8,128)S(1)} %get-tuple-element.53.refs_5_.square, f32[128,768]{1,0:T(8,128)S(1)} %get-tuple-element.59.tangent), custom_call_target="tpu_custom_call" | custom-call | bytes 24576 | tf_op jit(solution)/shard_map/finish/pallas_call | solution.py:385
  88.5 9.1 %collective-permute-done.15.refs_5_ = bf16[128,2048]{1,0:T(8,128)(2,1)S(1)} collective-permute-done((bf16[128,2048]{1,0:T(8,128)(2,1)S(1)}, bf16[128,2048]{1,0:T(8,128)(2,1)S(1)}, u32[]{:S(2)}, u32[]{:S(2)}) %collective-permute-start.15) | collective-permute-done | bytes 524320 | tf_op jit(solution)/shard_map/ppermute | solution.py:427
  97.7 4.2 %own_products.3 = (f32[128,768]{1,0:T(8,128)S(1)}, f32[128,768]{1,0:T(8,128)S(1)}) custom-call(s32[1]{0:T(128)} %bitcast.refs_1_.diag, bf16[2048,768]{1,0:T(8,128)(2,1)S(1)} %get-tuple-element.40.refs_0_.right0, bf16[2048,768]{1,0:T(8,128)(2,1)} %get-tuple-element.41.right1, bf16[80,2048]{1,0:T(8,128)(2,1)S(1)} %get-tuple-element.43.refs_2_.refs_0_, ...), custom_call_target="tpu_custom_call" | custom-call | flops 18874368 | bytes 131072 | tf_op jit(solution)/shard_map/own_products/pallas_call | solution.py:259
  101.9 5.5 %collective-permute-done.14.coded = s16[1552,128]{1,0:T(8,128)(2,1)S(1)} collective-permute-done((s16[1552,128]{1,0:T(8,128)(2,1)S(1)}, s16[1552,128]{1,0:T(8,128)(2,1)S(1)}, u32[]{:S(2)}, u32[]{:S(2)}) %collective-permute-start.14) | collective-permute-done | bytes 397344 | tf_op jit(solution)/shard_map/ppermute | solution.py:427
  107.4 1.4 %finish.3 = (bf16[256,768]{1,0:T(8,128)(2,1)}, bf16[256,768]{1,0:T(8,128)(2,1)}) custom-call(s32[2,6]{1,0:T(2,128)S(1)} %copy-done.4, s16[1552,128]{1,0:T(8,128)(2,1)S(1)} %collective-permute-done.14.coded, f32[128,768]{1,0:T(8,128)S(1)} %get-tuple-element.57.square, ...), custom_call_target="tpu_custom_call", output_to_operand_aliasing={{0}: (4, {}), {1}: (5, {})} | custom-call | bytes 24576 | tf_op jit(solution)/shard_map/finish/pallas_call | solution.py:385
  (43 shorter events, 10.6 us)
Async XLA Ops:
  0.7 5.0 %copy-start.5 = (s32[2,128]{1,0:T(2,128)S(1)}, s32[2,128]{1,0:T(2,128)}, u32[]{:S(2)}) copy-start(s32[2,128]{1,0:T(2,128)} %refs_2_.3) | copy-start | bytes 3076
  0.7 5.0 %copy-start.6 = (s32[2,128]{1,0:T(2,128)S(1)}, s32[2,128]{1,0:T(2,128)}, u32[]{:S(2)}) copy-start(s32[2,128]{1,0:T(2,128)} %refs_3_.3) | copy-start | bytes 3076
  2.6 8.2 %copy-start = (bf16[48,2048]{1,0:T(8,128)(2,1)S(1)}, bf16[48,2048]{1,0:T(8,128)(2,1)}, u32[]{:S(2)}) copy-start(bf16[48,2048]{1,0:T(8,128)(2,1)} %get-tuple-element.33.refs_1_.refs_0_) | copy-start | bytes 589828
  2.6 8.2 %collective-permute-start = (bf16[48,2048]{1,0:T(8,128)(2,1)}, bf16[48,2048]{1,0:T(8,128)(2,1)S(1)}, u32[]{:S(2)}, u32[]{:S(2)}) collective-permute-start(bf16[48,2048]{1,0:T(8,128)(2,1)} %get-tuple-element.32.refs_6_), channel_id=1, source_target_pairs={{0,1},{1,0},{2,3},{3,2},{4,5},{5,4},{6,7},{7,6},{8,9},{9,8},{10,11... | collective-permute-start | bytes 589832 | tf_op jit(solution)/shard_map/ppermute | solution.py:427
  6.6 18.5 %copy-start.7 = (s32[16,6]{0,1:T(8,128)S(1)}, s32[16,6]{0,1:T(8,128)}, u32[]{:S(2)}) copy-start(s32[16,6]{0,1:T(8,128)} %param.15) | copy-start | bytes 1156
  6.6 18.6 %copy-start.8 = (s32[16,6]{0,1:T(8,128)S(1)}, s32[16,6]{0,1:T(8,128)}, u32[]{:S(2)}) copy-start(s32[16,6]{0,1:T(8,128)} %param.16) | copy-start | bytes 1156
  8.7 4.2 %copy-start.2 = (bf16[48,2048]{1,0:T(8,128)(2,1)}, bf16[48,2048]{1,0:T(8,128)(2,1)S(1)}, u32[]{:S(2)}) copy-start(bf16[48,2048]{1,0:T(8,128)(2,1)S(1)} %get-tuple-element.44.refs_3_) | copy-start | bytes 589828
  11.1 12.4 %collective-permute-start.2 = (bf16[80,2048]{1,0:T(8,128)(2,1)S(1)}, bf16[80,2048]{1,0:T(8,128)(2,1)S(1)}, u32[]{:S(2)}, u32[]{:S(2)}) collective-permute-start(bf16[80,2048]{1,0:T(8,128)(2,1)S(1)} %get-tuple-element.36), channel_id=1, source_target_pairs={{0,1},{1,0},{2,3},{3,2},{4,5},{5,4},{6,7},{7,6},{8,9},{9,8},{10,11... | collective-permute-start | bytes 983048 | tf_op jit(solution)/shard_map/ppermute | solution.py:427
  12.9 10.6 %collective-permute-start.1 = (bf16[48,2048]{1,0:T(8,128)(2,1)S(1)}, bf16[48,2048]{1,0:T(8,128)(2,1)S(1)}, u32[]{:S(2)}, u32[]{:S(2)}) collective-permute-start(bf16[48,2048]{1,0:T(8,128)(2,1)S(1)} %get-tuple-element.35), channel_id=1, source_target_pairs={{0,16},{1,17},{2,18},{3,19},{4,20},{5,21},{6,22},{7,23},{8,24},{9,... | collective-permute-start | bytes 589832 | tf_op jit(solution)/shard_map/ppermute | solution.py:427
  24.4 8.8 %collective-permute-start.3 = (bf16[80,2048]{1,0:T(8,128)(2,1)}, bf16[80,2048]{1,0:T(8,128)(2,1)S(1)}, u32[]{:S(2)}, u32[]{:S(2)}) collective-permute-start(bf16[80,2048]{1,0:T(8,128)(2,1)} %get-tuple-element.42), channel_id=1, source_target_pairs={{0,1},{1,0},{2,3},{3,2},{4,5},{5,4},{6,7},{7,6},{8,9},{9,8},{10,11... | collective-permute-start | bytes 983048 | tf_op jit(solution)/shard_map/ppermute | solution.py:427
  25.1 16.5 %collective-permute-start.7 = (bf16[80,2048]{1,0:T(8,128)(2,1)}, bf16[80,2048]{1,0:T(8,128)(2,1)S(1)}, u32[]{:S(2)}, u32[]{:S(2)}) collective-permute-start(bf16[80,2048]{1,0:T(8,128)(2,1)} %get-tuple-element.39.rest_0_), channel_id=1, source_target_pairs={{0,16},{1,17},{2,18},{3,19},{4,20},{5,21},{6,22},{7,23},{8,24},{9,... | collective-permute-start | bytes 983048 | tf_op jit(solution)/shard_map/ppermute | solution.py:427
  25.2 8.0 %copy-start.3 = (bf16[48,2048]{1,0:T(8,128)(2,1)S(1)}, bf16[48,2048]{1,0:T(8,128)(2,1)}, u32[]{:S(2)}) copy-start(bf16[48,2048]{1,0:T(8,128)(2,1)} %copy-done.2) | copy-start | bytes 589828
  33.6 10.0 %collective-permute-start.5 = (bf16[48,2048]{1,0:T(8,128)(2,1)S(1)}, bf16[48,2048]{1,0:T(8,128)(2,1)S(1)}, u32[]{:S(2)}, u32[]{:S(2)}) collective-permute-start(bf16[48,2048]{1,0:T(8,128)(2,1)S(1)} %get-tuple-element.46), channel_id=1, source_target_pairs={{0,1},{1,0},{2,3},{3,2},{4,5},{5,4},{6,7},{7,6},{8,9},{9,8},{10,11... | collective-permute-start | bytes 589832 | tf_op jit(solution)/shard_map/ppermute | solution.py:427
  41.6 14.9 %collective-permute-start.9 = (bf16[80,2048]{1,0:T(8,128)(2,1)S(1)}, bf16[80,2048]{1,0:T(8,128)(2,1)S(1)}, u32[]{:S(2)}, u32[]{:S(2)}) collective-permute-start(bf16[80,2048]{1,0:T(8,128)(2,1)S(1)} %collective-permute-done.7.refs_1_), channel_id=1, source_target_pairs={{0,1},{1,0},{2,3},{3,2},{4,5},{5,4},{6,7},{7,6},{8,9},{9,8},{10,11... | collective-permute-start | bytes 983048 | tf_op jit(solution)/shard_map/ppermute | solution.py:427
  42.9 20.2 %collective-permute-start.4 = (bf16[80,2048]{1,0:T(8,128)(2,1)S(1)}, bf16[80,2048]{1,0:T(8,128)(2,1)S(1)}, u32[]{:S(2)}, u32[]{:S(2)}) collective-permute-start(bf16[80,2048]{1,0:T(8,128)(2,1)S(1)} %get-tuple-element.45), channel_id=1, source_target_pairs={{0,16},{1,17},{2,18},{3,19},{4,20},{5,21},{6,22},{7,23},{8,24},{9,... | collective-permute-start | bytes 983048 | tf_op jit(solution)/shard_map/ppermute | solution.py:427
  42.9 13.6 %collective-permute-start.8 = (bf16[48,2048]{1,0:T(8,128)(2,1)S(1)}, bf16[48,2048]{1,0:T(8,128)(2,1)S(1)}, u32[]{:S(2)}, u32[]{:S(2)}) collective-permute-start(bf16[48,2048]{1,0:T(8,128)(2,1)S(1)} %collective-permute-done.1.refs_0_), channel_id=1, source_target_pairs={{0,1},{1,0},{2,3},{3,2},{4,5},{5,4},{6,7},{7,6},{8,9},{9,8},{10,11... | collective-permute-start | bytes 589832 | tf_op jit(solution)/shard_map/ppermute | solution.py:427
  44.0 25.2 %collective-permute-start.12 = (bf16[128,2048]{1,0:T(8,128)(2,1)S(1)}, bf16[128,2048]{1,0:T(8,128)(2,1)S(1)}, u32[]{:S(2)}, u32[]{:S(2)}) collective-permute-start(bf16[128,2048]{1,0:T(8,128)(2,1)S(1)} %get-tuple-element.52.refs_2_), channel_id=1, source_target_pairs={{0,1},{1,0},{2,3},{3,2},{4,5},{5,4},{6,7},{7,6},{8,9},{9,8},{10,11... | collective-permute-start | bytes 1572872 | tf_op jit(solution)/shard_map/ppermute | solution.py:427
  45.3 21.4 %collective-permute-start.6 = (bf16[48,2048]{1,0:T(8,128)(2,1)S(1)}, bf16[48,2048]{1,0:T(8,128)(2,1)S(1)}, u32[]{:S(2)}, u32[]{:S(2)}) collective-permute-start(bf16[48,2048]{1,0:T(8,128)(2,1)S(1)} %get-tuple-element.49), channel_id=1, source_target_pairs={{0,16},{1,17},{2,18},{3,19},{4,20},{5,21},{6,22},{7,23},{8,24},{9,... | collective-permute-start | bytes 589832 | tf_op jit(solution)/shard_map/ppermute | solution.py:427
  67.0 13.4 %collective-permute-start.10 = (bf16[80,2048]{1,0:T(8,128)(2,1)S(1)}, bf16[80,2048]{1,0:T(8,128)(2,1)S(1)}, u32[]{:S(2)}, u32[]{:S(2)}) collective-permute-start(bf16[80,2048]{1,0:T(8,128)(2,1)S(1)} %get-tuple-element.50), channel_id=1, source_target_pairs={{0,1},{1,0},{2,3},{3,2},{4,5},{5,4},{6,7},{7,6},{8,9},{9,8},{10,11... | collective-permute-start | bytes 983048 | tf_op jit(solution)/shard_map/ppermute | solution.py:427
  68.0 18.8 %collective-permute-start.13 = (s16[1552,128]{1,0:T(8,128)(2,1)S(1)}, s16[1552,128]{1,0:T(8,128)(2,1)S(1)}, u32[]{:S(2)}, u32[]{:S(2)}) collective-permute-start(s16[1552,128]{1,0:T(8,128)(2,1)S(1)} %get-tuple-element.55), channel_id=1, source_target_pairs={{0,16},{1,17},{2,18},{3,19},{4,20},{5,21},{6,22},{7,23},{8,24},{9,... | collective-permute-start | bytes 1191944 | tf_op jit(solution)/shard_map/ppermute | solution.py:427
  68.0 12.4 %collective-permute-start.11 = (bf16[48,2048]{1,0:T(8,128)(2,1)S(1)}, bf16[48,2048]{1,0:T(8,128)(2,1)S(1)}, u32[]{:S(2)}, u32[]{:S(2)}) collective-permute-start(bf16[48,2048]{1,0:T(8,128)(2,1)S(1)} %collective-permute-done.6.refs_2_.refs_1_), channel_id=1, source_target_pairs={{0,1},{1,0},{2,3},{3,2},{4,5},{5,4},{6,7},{7,6},{8,9},{9,8},{10,11... | collective-permute-start | bytes 589832 | tf_op jit(solution)/shard_map/ppermute | solution.py:427
  80.4 6.6 %copy-start.4 = (s32[2,6]{1,0:T(2,128)S(1)}, s32[2,6]{1,0:T(2,128)}, u32[]{:S(2)}) copy-start(s32[2,6]{1,0:T(2,128)} %keep.3) | copy-start | bytes 148
  85.2 12.5 %collective-permute-start.15 = (bf16[128,2048]{1,0:T(8,128)(2,1)S(1)}, bf16[128,2048]{1,0:T(8,128)(2,1)S(1)}, u32[]{:S(2)}, u32[]{:S(2)}) collective-permute-start(bf16[128,2048]{1,0:T(8,128)(2,1)S(1)} %get-tuple-element.56.refs_2_), channel_id=1, source_target_pairs={{0,1},{1,0},{2,3},{3,2},{4,5},{5,4},{6,7},{7,6},{8,9},{9,8},{10,11... | collective-permute-start | bytes 1572872 | tf_op jit(solution)/shard_map/ppermute | solution.py:427
  87.0 20.4 %collective-permute-start.14 = (s16[1552,128]{1,0:T(8,128)(2,1)S(1)}, s16[1552,128]{1,0:T(8,128)(2,1)S(1)}, u32[]{:S(2)}, u32[]{:S(2)}) collective-permute-start(s16[1552,128]{1,0:T(8,128)(2,1)S(1)} %handed_on.3), channel_id=1, source_target_pairs={{0,16},{1,17},{2,18},{3,19},{4,20},{5,21},{6,22},{7,23},{8,24},{9,... | collective-permute-start | bytes 1191944 | tf_op jit(solution)/shard_map/ppermute | solution.py:427
  (1 other events, 1.0 us)

commit v7 on v6

--- a/solution.py
+++ b/solution.py
@@ -37,85 +37,49 @@
     return [(lo // BLOCK, slice(lo - start, hi - start)) for lo, hi in zip(edges, edges[1:])]
 
 
-def chunk_kernel(spans, slabs, panel, *refs):
-    place, diag, mask0_far, mask1_far, x0, x1 = refs[:6]
-    held, mask0, mask1, mask_sems, sems = refs[-5:]
-    many = 2 * len(spans) + len(slabs)
-    outs = refs[-5 - many : -5]
-    masks = [
-        pltpu.make_async_copy(mask0_far, mask0, mask_sems.at[0]),
-        pltpu.make_async_copy(mask1_far, mask1, mask_sems.at[1]),
-    ]
-    for copy in masks:
-        copy.start()
-    with_slab = len(slabs) > 0
+def chunk_kernel(start, panel, *refs):
+    place, mask0_far, mask1_far, x0, x1 = refs[:5]
+    a_out, b_out, held, mask0, mask1, mask_sems, sems = refs[-7:]
+    rows = a_out.shape[0]
     blocks = panel // BLOCK
     first = place[0] * blocks
     at = pl.ds(pl.multiple_of(place[0] * panel, BLOCK), panel)
-    origin = 0 if with_slab else spans[0][0]
-    copies = []
-    for n, (lo, hi) in enumerate(spans):
-        lo = origin if n == 0 else lo
-        for i, x in enumerate((x0, x1)):
-            here = pl.ds(lo - origin, hi - lo)
-            copies.append(
-                pltpu.make_async_copy(x.at[pl.ds(lo, hi - lo), at], held.at[i, here], sems.at[n, i])
-            )
+    copies = [
+        pltpu.make_async_copy(mask0_far, mask0, mask_sems.at[0]),
+        pltpu.make_async_copy(mask1_far, mask1, mask_sems.at[1]),
+        pltpu.make_async_copy(x0.at[pl.ds(start, rows), at], held.at[0], sems.at[0]),
+        pltpu.make_async_copy(x1.at[pl.ds(start, rows), at], held.at[1], sems.at[1]),
+    ]
     for copy in copies:
         copy.start()
-    for copy in masks + copies:
-        copy.wait()
-    for n, (lo, hi) in enumerate(slabs):
-        for row_block, piece in row_pieces(lo, hi - lo):
-            rows = slice(piece.start + lo, piece.stop + lo)
+    for copy in copies:
+        copy.wait()
+    for which, (mask, out) in enumerate(((mask0, a_out), (mask1, b_out))):
+        for row_block, piece in row_pieces(start, rows):
             for j in range(blocks):
                 cut = slice(j * BLOCK, (j + 1) * BLOCK)
-                product = scaled(held[1, rows, cut], mask1[row_block, first + j])
-                outs[2 * len(spans) + n][piece, cut] = product
-    for n, (lo, hi) in enumerate(spans):
-        a_out, swap = outs[2 * n], outs[2 * n + 1]
-        for row_block, piece in row_pieces(lo, hi - lo):
-            rows = slice(piece.start + lo - origin, piece.stop + lo - origin)
-            for j in range(blocks):
-                cut = slice(j * BLOCK, (j + 1) * BLOCK)
-                a_out[piece, cut] = scaled(held[0, rows, cut], mask0[row_block, first + j])
-
-        @pl.when(diag[0] == 1)
-        def _():
-            swap[...] = a_out[...]
-
-        @pl.when(diag[0] == 0)
-        def _():
-            for row_block, piece in row_pieces(lo, hi - lo):
-                rows = slice(piece.start + lo - origin, piece.stop + lo - origin)
-                for j in range(blocks):
-                    cut = slice(j * BLOCK, (j + 1) * BLOCK)
-                    swap[piece, cut] = scaled(held[1, rows, cut], mask1[row_block, first + j])
-
-
-def masked_chunks(place, diag, mask0, mask1, x0, x1, spans, slabs, panel, after=()):
-    outs = []
-    for lo, hi in spans:
-        outs += [jax.ShapeDtypeStruct((hi - lo, panel), x0.dtype)] * 2
-    for lo, hi in slabs:
-        outs.append(jax.ShapeDtypeStruct((hi - lo, panel), x0.dtype))
-    high = spans[-1][1] - (0 if slabs else spans[0][0])
-    return pl.pallas_call(
-        functools.partial(chunk_kernel, spans, slabs, panel),
-        in_specs=[SM(), SM()] + [HB() for _ in range(4 + len(after))],
-        out_specs=[VM() for _ in outs],
-        out_shape=outs,
+                out[piece, cut] = scaled(held[which, piece, cut], mask[row_block, first + j])
+
+
+def masked_chunk(place, mask0, mask1, x0, x1, span, panel, limit, after=()):
+    rows = span[1] - span[0]
+    out = jax.ShapeDtypeStruct((rows, panel), x0.dtype)
+    return pl.pallas_call(
+        functools.partial(chunk_kernel, span[0], panel),
+        in_specs=[SM()] + [HB() for _ in range(4 + len(after))],
+        out_specs=[VM(), VM()],
+        out_shape=[out, out],
         scratch_shapes=[
-            pltpu.VMEM((2, high, panel), x0.dtype),
+            pltpu.VMEM((2, rows, panel), x0.dtype),
             pltpu.SMEM(mask0.shape, mask0.dtype),
             pltpu.SMEM(mask1.shape, mask1.dtype),
             pltpu.SemaphoreType.DMA((2,)),
-            pltpu.SemaphoreType.DMA((len(spans), 2)),
+            pltpu.SemaphoreType.DMA((2,)),
         ],
-        compiler_params=params(VMEM_BYTES if slabs else ALL_VMEM_BYTES),
-        cost_estimate=cost(0, 8 * high * panel),
-        name="left_chunks",
-    )(place, diag, mask0, mask1, x0, x1, *after)
+        compiler_params=params(limit),
+        cost_estimate=cost(0, 8 * rows * panel),
+        name="left_chunk",
+    )(place, mask0, mask1, x0, x1, *after)
 
 
 def choose_kernel(gates, many, diag, *refs):
@@ -410,10 +374,8 @@
     half = row_index // group
     diag = (half == lax.axis_index("col")).astype(jnp.int32).reshape(1)
     place = (row_index % group).astype(jnp.int32).reshape(1)
-    edges = [all_rows * e // 16 for e in (0, 3, 8, 13, 16)]
-    spans = list(zip(edges, edges[1:]))
-    many = len(spans)
-    split = edges[2]
+    split = all_rows * 7 // 16
+    spans = ((0, split), (split, all_rows))
     wide = 256
 
     def device(h, q, c):
@@ -422,52 +384,47 @@
     spots = [(h, q, c) for h in range(2) for q in range(group) for c in range(2)]
     over_y = [(device(h, q, c), device(h, q, 1 - c)) for h, q, c in spots]
     over_z = [(device(h, q, c), device(1 - h, q, c)) for h, q, c in spots]
+    ring = [
+        (device(h, q, c), device(h, q, 1 - c) if h == c else device(1 - h, q, c))
+        for h, q, c in spots
+    ]
+    across = [
+        (device(h, q, c), device(h, q, c) if h == c else device(1 - h, q, 1 - c))
+        for h, q, c in spots
+    ]
 
     def move(values, pairs):
         return lax.ppermute(values, ("row", "col"), pairs)
 
-    def chunks(spans, slabs, after=()):
-        return masked_chunks(
-            place, diag, mask0_rows, mask1_rows, x0_rows, x1_rows, spans, slabs, panel, after
+    def chunk(i, limit, after=()):
+        return masked_chunk(
+            place, mask0_rows, mask1_rows, x0_rows, x1_rows, spans[i], panel, limit, after
         )
 
-    def partials(which, given=(), **more):
-        return partial_products(diag, near[which], far[which], right0, right1, wide, given, **more)
-
-    def own(which, b, got):
-        mine, other = (*a[which], *b), (*passed[which], *got)
+    def partials(near, far, **more):
+        return partial_products(diag, (near,), (far,), right0, right1, wide, **more)
+
+    def own(mine, other):
         return local_products(diag, mine, other, right0, right1, wide)
 
-    a, swap, passed, near, far = ([None] * many for _ in range(5))
-    early, late = slice(0, 2), slice(2, many)
-    a[0], swap[0] = chunks(spans[:1], ())
-    *rest, b0, b1 = chunks(spans[1:], ((0, split), (split, all_rows)), (swap[0],))
-    a[1:], swap[1:] = rest[0::2], rest[1::2]
-    right0 = right1 = None
-    for i in range(many):
-        passed[i] = move(swap[i], over_y)
-        last = i == many - 1
-        gate = {1: (near[0],), 2: (right0,)}.get(i, ())
-        send, later = chosen(diag, passed[i], a[i], (b0 if last else swap[i + 1],), gate)
-        if last:
-            b0 = later
-        else:
-            swap[i + 1] = later
-        near[i] = move(send, over_z)
-        if i == 1:
-            right0, right1 = masked_right(mask0_cols, mask1_cols, x0_cols, x1_cols, (send,))
-    far[0], far[1], far[3] = (move(near[i], over_y) for i in (0, 1, 3))
-    (coded,) = partials(early)
-    coded, last_near = handed_on((coded, near[2]), (near[3],))
+    a0, b0 = chunk(0, ALL_VMEM_BYTES)
+    from_ring, from_across, got_b = move(a0, ring), move(b0, across), move(b0, over_y)
+    a1, b1 = chunk(1, VMEM_BYTES, (a0,))
+    right0, right1 = masked_right(mask0_cols, mask1_cols, x0_cols, x1_cols, (a1,))
+    near, a1, b1 = chosen(diag, from_ring, from_across, (a1, b1), (right0, got_b))
+    mine0, other0 = (a0, b0), (from_ring, got_b)
+    from_ring, from_across = move(a1, ring), move(b1, across)
+    coded, *_ = partials(near, move(near, over_y))
+    near, coded = chosen(diag, from_ring, from_across, (coded,))
     back = move(coded, over_z)
-    far[2] = move(last_near, over_y)
-    mine = own(early, (b0,), (move(b0, over_y),))
-    coded, b1 = partials(late, given=(b1,), gates=mine[:1])
+    far = move(near, over_y)
+    sums = own(mine0, other0)
+    coded, b1 = partials(near, far, given=(b1,), gates=sums[:1])
     (coded,) = handed_on((coded,), (back,))
-    outs = finished(keep, *mine, back, (), 0, all_rows)
+    outs = finished(keep, *sums, back, (), 0, all_rows)
     back = move(coded, over_z)
-    mine = own(late, (b1,), (move(b1, over_y),))
-    return tuple(finished(keep, *mine, back, outs, split, all_rows))
+    sums = own((a1, b1), (from_ring, move(b1, over_y)))
+    return tuple(finished(keep, *sums, back, outs, split, all_rows))
 
 
 def passed_along(shard, axis, by):

time: 109 us -> 148 us (1.36)
  the two profiles are of different devices: /device:TPU:0 before, /device:TPU:24 now
where the time goes in v7:
time: 148 us; the launch traced here: 147 us
  waiting for transfers between devices  101 us (68%)
  Pallas kernels  33.2 us (22%)
  starting transfers between devices  9.34 us (6%)
  local copies, waits for them, and re-layouts  2.87 us (2%)
    ppermute x10, waiting for transfers between devices, move(): return lax.ppermute(values, ('row', 'col'), pairs)  101 us
    pallas_call x2, Pallas kernels, partial_products(): pl.pallas_call(functools.partial(partial_kernel, len(near), len(given)),...  9.49 us
    ppermute x10, starting transfers between devices, move(): return lax.ppermute(values, ('row', 'col'), pairs)  9.34 us
    pallas_call x2, Pallas kernels, local_products(): pl.pallas_call(functools.partial(local_kernel, many), grid=(columns // wi...  8.96 us
    pallas_call x1, Pallas kernels, masked_right(): pl.pallas_call(right_kernel, grid=(depth // tall,), in_specs=[SM(), SM(),...  6.95 us
    pallas_call x2, Pallas kernels, masked_chunk(): pl.pallas_call(functools.partial(chunk_kernel, span[0], panel), in_specs=...  3.86 us
  transfers between devices with their start and end apart: 10, of which 6 were waited for; matrix products, arithmetic and copies ran while one was open for 0% of the time, Pallas kernels for 20%

profile of v7, /device:TPU:24, one launch (start us, length us, event | category | flops | bytes accessed | tf_op | source)
XLA Modules:
  0.0 146.9 jit_solution(6803553903015636822)
XLA Ops:
  0.7 2.2 %left_chunk.2 = (bf16[112,2048]{1,0:T(8,128)(2,1)}, bf16[112,2048]{1,0:T(8,128)(2,1)}) custom-call(s32[1]{0:T(128)} %bitcast.1.refs_0_, s32[2,128]{1,0:T(2,128)} %refs_1_.3, s32[2,128]{1,0:T(2,128)} %refs_2_.3, bf16[256,16384]{1,0:T(8,128)(2,1)} %refs_3_.3, bf16[256,16384]{1,0:T(8,128)(2,1)} %refs_4_.3), custom_call_target="tpu_custom_call" | custom-call | bytes 28672 | tf_op jit(solution)/shard_map/left_chunk/pallas_call | solution.py:67
  2.9 0.4 collective-permute-start.1
  3.3 5.4 %collective-permute-start.2 = (bf16[112,2048]{1,0:T(8,128)(2,1)}, bf16[112,2048]{1,0:T(8,128)(2,1)S(1)}, u32[]{:S(2)}, u32[]{:S(2)}) collective-permute-start(bf16[112,2048]{1,0:T(8,128)(2,1)} %get-tuple-element.25.refs_1_), channel_id=1, source_target_pairs={{0,0},{1,16},{2,2},{3,18},{4,4},{5,20},{6,6},{7,22},{8,8},{9,24},{... | collective-permute-start | bytes 1376264 | tf_op jit(solution)/shard_map/ppermute | solution.py:397
  8.9 1.0 copy-done.2
  9.9 1.6 %left_chunk.3 = (bf16[144,2048]{1,0:T(8,128)(2,1)S(1)}, bf16[144,2048]{1,0:T(8,128)(2,1)S(1)}) custom-call(s32[1]{0:T(128)} %bitcast.1.refs_0_, s32[2,128]{1,0:T(2,128)S(1)} %copy-done.6, s32[2,128]{1,0:T(2,128)S(1)} %copy-done.7, bf16[256,16384]{1,0:T(8,128)(2,1)} %refs_3_.3, bf16[256,16384]{1,0:T(8,128)(2,1)} %refs_4_.3, bf16[112,2048]{1,0:T(8,128)(2,1)S(1)} %copy-done.2), custom_call_target="tpu_custom_call" | custom-call | bytes 36864 | tf_op jit(solution)/shard_map/left_chunk/pallas_call | solution.py:67
  11.7 6.9 %right_panels.1 = (bf16[2048,768]{1,0:T(8,128)(2,1)S(1)}, bf16[2048,768]{1,0:T(8,128)(2,1)}) custom-call(s32[16,6]{1,0:T(8,128)S(1)} %copy.13.mask0, s32[16,6]{1,0:T(8,128)S(1)} %copy.14.mask1, bf16[2048,768]{1,0:T(8,128)(2,1)} %x0.1, bf16[2048,768]{1,0:T(8,128)(2,1)} %x1.1, bf16[144,2048]{1,0:T(8,128)(2,1)S(1)} %get-tuple-element.22.rest_0_.refs_4_), custom_call_target="tpu_custom_call" | custom-call | bytes 196608 | tf_op jit(solution)/shard_map/right_panels/pallas_call | solution.py:166
  18.7 1.7 %copy-done = bf16[2048,768]{1,0:T(8,128)(2,1)} copy-done((bf16[2048,768]{1,0:T(8,128)(2,1)}, bf16[2048,768]{1,0:T(8,128)(2,1)S(1)}, u32[]{:S(2)}) %copy-start) | copy-done | bytes 3145752
  20.3 26.4 %collective-permute-done.2.refs_3_ = bf16[112,2048]{1,0:T(8,128)(2,1)S(1)} collective-permute-done((bf16[112,2048]{1,0:T(8,128)(2,1)}, bf16[112,2048]{1,0:T(8,128)(2,1)S(1)}, u32[]{:S(2)}, u32[]{:S(2)}) %collective-permute-start.2) | collective-permute-done | bytes 458784 | tf_op jit(solution)/shard_map/ppermute | solution.py:397
  46.7 0.6 to_send.2
  47.3 1.9 %collective-permute-start.4 = (bf16[144,2048]{1,0:T(8,128)(2,1)S(1)}, bf16[144,2048]{1,0:T(8,128)(2,1)S(1)}, u32[]{:S(2)}, u32[]{:S(2)}) collective-permute-start(bf16[144,2048]{1,0:T(8,128)(2,1)S(1)} %get-tuple-element.28.refs_2_), channel_id=1, source_target_pairs={{0,0},{1,16},{2,2},{3,18},{4,4},{5,20},{6,6},{7,22},{8,8},{9,24},{... | collective-permute-start | bytes 1769480 | tf_op jit(solution)/shard_map/ppermute | solution.py:397
  49.2 0.8 collective-permute-start.5
  50.1 22.3 %collective-permute-done.5.refs_1_ = bf16[112,2048]{1,0:T(8,128)(2,1)S(1)} collective-permute-done((bf16[112,2048]{1,0:T(8,128)(2,1)S(1)}, bf16[112,2048]{1,0:T(8,128)(2,1)S(1)}, u32[]{:S(2)}, u32[]{:S(2)}) %collective-permute-start.5) | collective-permute-done | bytes 458784 | tf_op jit(solution)/shard_map/ppermute | solution.py:397
  72.4 4.5 %partial_products.2.refs_2_ = s16[1360,128]{1,0:T(8,128)(2,1)S(1)} custom-call(s32[1]{0:T(128)} %bitcast.diag, bf16[2048,768]{1,0:T(8,128)(2,1)S(1)} %copy-done.1, bf16[2048,768]{1,0:T(8,128)(2,1)} %get-tuple-element.24.right1, bf16[112,2048]{1,0:T(8,128)(2,1)S(1)} %get-tuple-element.29.refs_0_, bf16[112,2048]{1,0:T(8,128)(2,1)S(1)} %collective-permute-done.5.refs_1_), custom_call_target="tpu_custom_call" | custom-call | flops 16515072 | bytes 112640 | tf_op jit(solution)/shard_map/partial_products/pallas_call | solution.py:287
  76.9 28.7 %collective-permute-done.4.refs_1_ = bf16[144,2048]{1,0:T(8,128)(2,1)S(1)} collective-permute-done((bf16[144,2048]{1,0:T(8,128)(2,1)S(1)}, bf16[144,2048]{1,0:T(8,128)(2,1)S(1)}, u32[]{:S(2)}, u32[]{:S(2)}) %collective-permute-start.4) | collective-permute-done | bytes 589856 | tf_op jit(solution)/shard_map/ppermute | solution.py:397
  105.7 0.3 to_send.3
  106.2 4.3 %own_products.2 = (f32[112,768]{1,0:T(8,128)S(1)}, f32[112,768]{1,0:T(8,128)S(1)}) custom-call(s32[1]{0:T(128)} %bitcast.diag, bf16[2048,768]{1,0:T(8,128)(2,1)S(1)} %copy-done.1, bf16[2048,768]{1,0:T(8,128)(2,1)} %get-tuple-element.24.right1, bf16[112,2048]{1,0:T(8,128)(2,1)S(1)} %copy-done.3, bf16[112,2048]{1,0:T(8,128)(2,1)S(1)} %copy-done.4, ...), custom_call_target="tpu_custom_call" | custom-call | flops 16515072 | bytes 126976 | tf_op jit(solution)/shard_map/own_products/pallas_call | solution.py:223
  110.5 10.8 %collective-permute-done.6.refs_1_ = bf16[144,2048]{1,0:T(8,128)(2,1)S(1)} collective-permute-done((bf16[144,2048]{1,0:T(8,128)(2,1)S(1)}, bf16[144,2048]{1,0:T(8,128)(2,1)S(1)}, u32[]{:S(2)}, u32[]{:S(2)}) %collective-permute-start.6) | collective-permute-done | bytes 589856 | tf_op jit(solution)/shard_map/ppermute | solution.py:397
  121.3 4.9 %partial_products.3 = (s16[1744,128]{1,0:T(8,128)(2,1)S(1)}, bf16[144,2048]{1,0:T(8,128)(2,1)S(1)}) custom-call(s32[1]{0:T(128)} %bitcast.diag, bf16[2048,768]{1,0:T(8,128)(2,1)} %copy-done, bf16[2048,768]{1,0:T(8,128)(2,1)} %get-tuple-element.24.right1, bf16[144,2048]{1,0:T(8,128)(2,1)S(1)} %get-tuple-element.30.refs_0_, ...), custom_call_target="tpu_custom_call" | custom-call | flops 21233664 | bytes 116736 | tf_op jit(solution)/shard_map/partial_products/pallas_call | solution.py:287
  126.3 0.3 collective-permute-start.9
  126.7 0.3 handed_on.1
  127.0 1.4 finish.2
  128.4 12.3 %collective-permute-done.9.refs_3_ = bf16[144,2048]{1,0:T(8,128)(2,1)S(1)} collective-permute-done((bf16[144,2048]{1,0:T(8,128)(2,1)S(1)}, bf16[144,2048]{1,0:T(8,128)(2,1)S(1)}, u32[]{:S(2)}, u32[]{:S(2)}) %collective-permute-start.9) | collective-permute-done | bytes 589856 | tf_op jit(solution)/shard_map/ppermute | solution.py:397
  140.8 4.7 %own_products.3 = (f32[144,768]{1,0:T(8,128)S(1)}, f32[144,768]{1,0:T(8,128)S(1)}) custom-call(s32[1]{0:T(128)} %bitcast.diag, bf16[2048,768]{1,0:T(8,128)(2,1)} %copy-done, bf16[2048,768]{1,0:T(8,128)(2,1)} %get-tuple-element.24.right1, bf16[144,2048]{1,0:T(8,128)(2,1)S(1)} %get-tuple-element.27.refs_0_, bf16[144,2048]{1,0:T(8,128)(2,1)S(1)} %get-tuple-element.34.refs_1_, ...), custom_call_target="tpu_custom_call" | custom-call | flops 21233664 | bytes 135168 | tf_op jit(solution)/shard_map/own_products/pallas_call | solution.py:223
  145.5 1.5 finish.3
  (30 shorter events, 0.7 us)
Async XLA Ops:
  0.6 8.2 %copy-start.6 = (s32[2,128]{1,0:T(2,128)S(1)}, s32[2,128]{1,0:T(2,128)}, u32[]{:S(2)}) copy-start(s32[2,128]{1,0:T(2,128)} %refs_1_.3) | copy-start | bytes 3076
  0.7 8.2 %copy-start.7 = (s32[2,128]{1,0:T(2,128)S(1)}, s32[2,128]{1,0:T(2,128)}, u32[]{:S(2)}) copy-start(s32[2,128]{1,0:T(2,128)} %refs_2_.3) | copy-start | bytes 3076
  2.9 17.4 %collective-permute-start.1 = (bf16[112,2048]{1,0:T(8,128)(2,1)}, bf16[112,2048]{1,0:T(8,128)(2,1)S(1)}, u32[]{:S(2)}, u32[]{:S(2)}) collective-permute-start(bf16[112,2048]{1,0:T(8,128)(2,1)} %get-tuple-element.21.refs_5_.refs_0_), channel_id=1, source_target_pairs={{0,1},{1,17},{2,3},{3,19},{4,5},{5,21},{6,7},{7,23},{8,9},{9,25},{... | collective-permute-start | bytes 1376264 | tf_op jit(solution)/shard_map/ppermute | solution.py:397
  3.3 43.4 %collective-permute-start.2 = (bf16[112,2048]{1,0:T(8,128)(2,1)}, bf16[112,2048]{1,0:T(8,128)(2,1)S(1)}, u32[]{:S(2)}, u32[]{:S(2)}) collective-permute-start(bf16[112,2048]{1,0:T(8,128)(2,1)} %get-tuple-element.25.refs_1_), channel_id=1, source_target_pairs={{0,0},{1,16},{2,2},{3,18},{4,4},{5,20},{6,6},{7,22},{8,8},{9,24},{... | collective-permute-start | bytes 1376264 | tf_op jit(solution)/shard_map/ppermute | solution.py:397
  8.8 37.9 %collective-permute-start = (bf16[112,2048]{1,0:T(8,128)(2,1)}, bf16[112,2048]{1,0:T(8,128)(2,1)S(1)}, u32[]{:S(2)}, u32[]{:S(2)}) collective-permute-start(bf16[112,2048]{1,0:T(8,128)(2,1)} %get-tuple-element.25.refs_1_), channel_id=1, source_target_pairs={{0,1},{1,0},{2,3},{3,2},{4,5},{5,4},{6,7},{7,6},{8,9},{9,8},{10,11... | collective-permute-start | bytes 1376264 | tf_op jit(solution)/shard_map/ppermute | solution.py:397
  8.9 1.0 copy-start.2
  9.9 1.6 %copy-start.8 = (s32[16,6]{0,1:T(8,128)S(1)}, s32[16,6]{0,1:T(8,128)}, u32[]{:S(2)}) copy-start(s32[16,6]{0,1:T(8,128)} %param.15) | copy-start | bytes 1156
  9.9 1.7 %copy-start.9 = (s32[16,6]{0,1:T(8,128)S(1)}, s32[16,6]{0,1:T(8,128)}, u32[]{:S(2)}) copy-start(s32[16,6]{0,1:T(8,128)} %param.16) | copy-start | bytes 1156
  18.7 1.7 %copy-start = (bf16[2048,768]{1,0:T(8,128)(2,1)}, bf16[2048,768]{1,0:T(8,128)(2,1)S(1)}, u32[]{:S(2)}) copy-start(bf16[2048,768]{1,0:T(8,128)(2,1)S(1)} %get-tuple-element.23.refs_0_.right0) | copy-start | bytes 9437188
  20.3 52.1 %copy-start.1 = (bf16[2048,768]{1,0:T(8,128)(2,1)S(1)}, bf16[2048,768]{1,0:T(8,128)(2,1)}, u32[]{:S(2)}) copy-start(bf16[2048,768]{1,0:T(8,128)(2,1)} %copy-done) | copy-start | bytes 9437188
  47.2 29.7 %collective-permute-start.3 = (bf16[144,2048]{1,0:T(8,128)(2,1)S(1)}, bf16[144,2048]{1,0:T(8,128)(2,1)S(1)}, u32[]{:S(2)}, u32[]{:S(2)}) collective-permute-start(bf16[144,2048]{1,0:T(8,128)(2,1)S(1)} %get-tuple-element.27.refs_0_), channel_id=1, source_target_pairs={{0,1},{1,17},{2,3},{3,19},{4,5},{5,21},{6,7},{7,23},{8,9},{9,25},{... | collective-permute-start | bytes 1769480 | tf_op jit(solution)/shard_map/ppermute | solution.py:397
  47.3 58.4 %collective-permute-start.4 = (bf16[144,2048]{1,0:T(8,128)(2,1)S(1)}, bf16[144,2048]{1,0:T(8,128)(2,1)S(1)}, u32[]{:S(2)}, u32[]{:S(2)}) collective-permute-start(bf16[144,2048]{1,0:T(8,128)(2,1)S(1)} %get-tuple-element.28.refs_2_), channel_id=1, source_target_pairs={{0,0},{1,16},{2,2},{3,18},{4,4},{5,20},{6,6},{7,22},{8,8},{9,24},{... | collective-permute-start | bytes 1769480 | tf_op jit(solution)/shard_map/ppermute | solution.py:397
  49.2 23.1 %collective-permute-start.5 = (bf16[112,2048]{1,0:T(8,128)(2,1)S(1)}, bf16[112,2048]{1,0:T(8,128)(2,1)S(1)}, u32[]{:S(2)}, u32[]{:S(2)}) collective-permute-start(bf16[112,2048]{1,0:T(8,128)(2,1)S(1)} %get-tuple-element.29.refs_0_), channel_id=1, source_target_pairs={{0,1},{1,0},{2,3},{3,2},{4,5},{5,4},{6,7},{7,6},{8,9},{9,8},{10,11... | collective-permute-start | bytes 1376264 | tf_op jit(solution)/shard_map/ppermute | solution.py:397
  72.4 33.8 %copy-start.3 = (bf16[112,2048]{1,0:T(8,128)(2,1)S(1)}, bf16[112,2048]{1,0:T(8,128)(2,1)}, u32[]{:S(2)}) copy-start(bf16[112,2048]{1,0:T(8,128)(2,1)} %get-tuple-element.21.refs_5_.refs_0_) | copy-start | bytes 1376260
  72.4 33.8 %copy-start.4 = (bf16[112,2048]{1,0:T(8,128)(2,1)S(1)}, bf16[112,2048]{1,0:T(8,128)(2,1)}, u32[]{:S(2)}) copy-start(bf16[112,2048]{1,0:T(8,128)(2,1)} %get-tuple-element.25.refs_1_) | copy-start | bytes 1376260
  106.0 15.3 %collective-permute-start.6 = (bf16[144,2048]{1,0:T(8,128)(2,1)S(1)}, bf16[144,2048]{1,0:T(8,128)(2,1)S(1)}, u32[]{:S(2)}, u32[]{:S(2)}) collective-permute-start(bf16[144,2048]{1,0:T(8,128)(2,1)S(1)} %get-tuple-element.30.refs_0_), channel_id=1, source_target_pairs={{0,1},{1,0},{2,3},{3,2},{4,5},{5,4},{6,7},{7,6},{8,9},{9,8},{10,11... | collective-permute-start | bytes 1769480 | tf_op jit(solution)/shard_map/ppermute | solution.py:397
  106.0 20.6 %collective-permute-start.7 = (s16[1360,128]{1,0:T(8,128)(2,1)S(1)}, s16[1360,128]{1,0:T(8,128)(2,1)S(1)}, u32[]{:S(2)}, u32[]{:S(2)}) collective-permute-start(s16[1360,128]{1,0:T(8,128)(2,1)S(1)} %get-tuple-element.33), channel_id=1, source_target_pairs={{0,16},{1,17},{2,18},{3,19},{4,20},{5,21},{6,22},{7,23},{8,24},{9,... | collective-permute-start | bytes 1044488 | tf_op jit(solution)/shard_map/ppermute | solution.py:397
  121.3 5.7 %copy-start.5 = (s32[2,6]{1,0:T(2,128)S(1)}, s32[2,6]{1,0:T(2,128)}, u32[]{:S(2)}) copy-start(s32[2,6]{1,0:T(2,128)} %keep.3) | copy-start | bytes 148
  126.3 14.5 %collective-permute-start.9 = (bf16[144,2048]{1,0:T(8,128)(2,1)S(1)}, bf16[144,2048]{1,0:T(8,128)(2,1)S(1)}, u32[]{:S(2)}, u32[]{:S(2)}) collective-permute-start(bf16[144,2048]{1,0:T(8,128)(2,1)S(1)} %get-tuple-element.34.refs_1_), channel_id=1, source_target_pairs={{0,1},{1,0},{2,3},{3,2},{4,5},{5,4},{6,7},{7,6},{8,9},{9,8},{10,11... | collective-permute-start | bytes 1769480 | tf_op jit(solution)/shard_map/ppermute | solution.py:397
  126.9 18.5 %collective-permute-start.8 = (s16[1744,128]{1,0:T(8,128)(2,1)S(1)}, s16[1744,128]{1,0:T(8,128)(2,1)S(1)}, u32[]{:S(2)}, u32[]{:S(2)}) collective-permute-start(s16[1744,128]{1,0:T(8,128)(2,1)S(1)} %handed_on.1), channel_id=1, source_target_pairs={{0,16},{1,17},{2,18},{3,19},{4,20},{5,21},{6,22},{7,23},{8,24},{9,... | collective-permute-start | bytes 1339400 | tf_op jit(solution)/shard_map/ppermute | solution.py:397

commit v8 on v7

--- a/solution.py
+++ b/solution.py
@@ -37,10 +37,11 @@
     return [(lo // BLOCK, slice(lo - start, hi - start)) for lo, hi in zip(edges, edges[1:])]
 
 
-def chunk_kernel(start, panel, *refs):
+def chunk_kernel(spans, stacked, panel, *refs):
     place, mask0_far, mask1_far, x0, x1 = refs[:5]
-    a_out, b_out, held, mask0, mask1, mask_sems, sems = refs[-7:]
-    rows = a_out.shape[0]
+    outs = refs[-5 - 2 * len(spans) + stacked : -5]
+    held, mask0, mask1, mask_sems, sems = refs[-5:]
+    start, rows = spans[0][0], held.shape[1]
     blocks = panel // BLOCK
     first = place[0] * blocks
     at = pl.ds(pl.multiple_of(place[0] * panel, BLOCK), panel)
@@ -54,21 +55,33 @@
         copy.start()
     for copy in copies:
         copy.wait()
-    for which, (mask, out) in enumerate(((mask0, a_out), (mask1, b_out))):
-        for row_block, piece in row_pieces(start, rows):
-            for j in range(blocks):
-                cut = slice(j * BLOCK, (j + 1) * BLOCK)
-                out[piece, cut] = scaled(held[which, piece, cut], mask[row_block, first + j])
-
-
-def masked_chunk(place, mask0, mask1, x0, x1, span, panel, limit, after=()):
-    rows = span[1] - span[0]
-    out = jax.ShapeDtypeStruct((rows, panel), x0.dtype)
-    return pl.pallas_call(
-        functools.partial(chunk_kernel, span[0], panel),
+    for n, (lo, hi) in enumerate(spans):
+        for which, mask in enumerate((mask0, mask1)):
+            joint = stacked and n == 0
+            out = outs[0] if joint else outs[2 * n - stacked + which]
+            down = which * (hi - lo) if joint else 0
+            for row_block, part in row_pieces(lo, hi - lo):
+                source = slice(part.start + lo - start, part.stop + lo - start)
+                target = slice(part.start + down, part.stop + down)
+                for j in range(blocks):
+                    cut = slice(j * BLOCK, (j + 1) * BLOCK)
+                    values = scaled(held[which, source, cut], mask[row_block, first + j])
+                    out[target, cut] = values
+
+
+def masked_chunks(place, mask0, mask1, x0, x1, spans, stacked, panel, limit, after=()):
+    rows = spans[-1][1] - spans[0][0]
+    outs = []
+    for n, (lo, hi) in enumerate(spans):
+        if stacked and n == 0:
+            outs.append(jax.ShapeDtypeStruct((2 * (hi - lo), panel), x0.dtype))
+        else:
+            outs += [jax.ShapeDtypeStruct((hi - lo, panel), x0.dtype)] * 2
+    return pl.pallas_call(
+        functools.partial(chunk_kernel, spans, int(stacked), panel),
         in_specs=[SM()] + [HB() for _ in range(4 + len(after))],
-        out_specs=[VM(), VM()],
-        out_shape=[out, out],
+        out_specs=[VM() for _ in outs],
+        out_shape=outs,
         scratch_shapes=[
             pltpu.VMEM((2, rows, panel), x0.dtype),
             pltpu.SMEM(mask0.shape, mask0.dtype),
@@ -78,7 +91,7 @@
         ],
         compiler_params=params(limit),
         cost_estimate=cost(0, 8 * rows * panel),
-        name="left_chunk",
+        name="left_chunks",
     )(place, mask0, mask1, x0, x1, *after)
 
 
@@ -182,72 +195,85 @@
     return first[:rows], first[rows:] + second
 
 
-def fetched(pieces, held, sems):
+def piece(array, lo=0, hi=None):
+    return (array, lo, array.shape[0] if hi is None else hi)
+
+
+def numbered(one, other):
+    arrays = []
+    for array, _, _ in (*one, *other):
+        if all(array is not known for known in arrays):
+            arrays.append(array)
+    number = {id(array): i for i, array in enumerate(arrays)}
+    return arrays, *(
+        tuple((number[id(array)], lo, hi) for array, lo, hi in pieces) for pieces in (one, other)
+    )
+
+
+def fetched(pieces, refs, held, sems):
     copies = []
     top = 0
-    for i, piece in enumerate(pieces):
-        rows = piece.shape[0]
-        copies.append(pltpu.make_async_copy(piece, held.at[pl.ds(top, rows)], sems.at[i]))
-        top += rows
+    for i, (which, lo, hi) in enumerate(pieces):
+        source = refs[which].at[pl.ds(lo, hi - lo)]
+        copies.append(pltpu.make_async_copy(source, held.at[pl.ds(top, hi - lo)], sems.at[i]))
+        top += hi - lo
     for copy in copies:
         copy.start()
     for copy in copies:
         copy.wait()
 
 
-def fetch_left(diag, one, other, held, sems):
+def fetch_left(diag, one, other, refs, held, sems):
     first = pl.program_id(0) == 0
 
     @pl.when(first & (diag[0] == 1))
     def _():
-        fetched(one, held, sems)
+        fetched(one, refs, held, sems)
 
     @pl.when(first & (diag[0] == 0))
     def _():
-        fetched(other, held, sems)
-
-
-def local_kernel(many, diag, right0, right1, *refs):
-    own, got = refs[:many], refs[many : 2 * many]
+        fetched(other, refs, held, sems)
+
+
+def local_kernel(one, other, diag, right0, right1, *refs):
     square, tangent, held, sems = refs[-4:]
-    fetch_left(diag, own, got, held, sems)
+    fetch_left(diag, one, other, refs, held, sems)
     square[...], tangent[...] = both_products(held, right0, right1)
 
 
-def local_products(diag, own, got, right0, right1, wide, after=()):
-    rows = sum(piece.shape[0] for piece in own) // 2
+def local_products(diag, one, other, right0, right1, wide):
+    arrays, one, other = numbered(one, other)
+    rows = sum(hi - lo for _, lo, hi in one) // 2
     depth, columns = right0.shape
-    many = len(own)
     out = jax.ShapeDtypeStruct((rows, columns), jnp.float32)
     tile = pl.BlockSpec((rows, wide), lambda g: (0, g))
     return pl.pallas_call(
-        functools.partial(local_kernel, many),
+        functools.partial(local_kernel, one, other),
         grid=(columns // wide,),
         in_specs=[
             SM(),
             pl.BlockSpec((depth, wide), lambda g: (0, g)),
             pl.BlockSpec((depth, wide), lambda g: (0, g)),
         ]
-        + [HB() for _ in (*own, *got, *after)],
+        + [HB() for _ in arrays],
         out_specs=[tile, tile],
         out_shape=[out, out],
         scratch_shapes=[
-            pltpu.VMEM((2 * rows, depth), own[-1].dtype),
-            pltpu.SemaphoreType.DMA((many,)),
+            pltpu.VMEM((2 * rows, depth), right0.dtype),
+            pltpu.SemaphoreType.DMA((len(one),)),
         ],
         compiler_params=params(),
         cost_estimate=cost(6 * rows * depth * columns, 8 * rows * depth + 4 * depth * columns),
         name="own_products",
-    )(diag, right0, right1, *own, *got, *after)
-
-
-def partial_kernel(many, given, diag, right0, right1, *refs):
-    near, far = refs[:many], refs[many : 2 * many]
+    )(diag, right0, right1, *arrays)
+
+
+def partial_kernel(one, other, many, given, diag, right0, right1, *refs):
     out, passed = refs[-5 - given], refs[-4 - given : -4]
     held, steps, sems, hand_sems = refs[-4:]
     others = [
         pltpu.make_async_copy(x, y, hand_sems.at[i])
-        for i, (x, y) in enumerate(zip(refs[2 * many : 2 * many + given], passed))
+        for i, (x, y) in enumerate(zip(refs[many : many + given], passed))
     ]
 
     @pl.when(pl.program_id(0) == 0)
@@ -259,7 +285,7 @@
     step = pl.program_id(0)
     tiles = wide // BLOCK
     across = pl.num_programs(0) * tiles
-    fetch_left(diag, near + far, far + near, held, sems)
+    fetch_left(diag, one, other, refs, held, sems)
     for which, values in enumerate(both_products(held, right0, right1)):
         top = jnp.maximum(jnp.max(jnp.abs(values), axis=0, keepdims=True), 1e-30)
         level = jnp.ceil(jnp.log(top) * (STEPS / LN2)) + 1.0
@@ -279,34 +305,35 @@
             copy.wait()
 
 
-def partial_products(diag, near, far, right0, right1, wide, given=(), gates=()):
-    rows = sum(piece.shape[0] for piece in near)
+def partial_products(diag, one, other, right0, right1, wide, given=(), gates=()):
+    arrays, one, other = numbered(one, other)
+    rows = sum(hi - lo for _, lo, hi in one) // 2
     depth, columns = right0.shape
     tiles = 2 * columns // BLOCK
     tail = -(-tiles // 16) * 16
     return pl.pallas_call(
-        functools.partial(partial_kernel, len(near), len(given)),
+        functools.partial(partial_kernel, one, other, len(arrays), len(given)),
         grid=(columns // wide,),
         in_specs=[
             SM(),
             pl.BlockSpec((depth, wide), lambda g: (0, g)),
             pl.BlockSpec((depth, wide), lambda g: (0, g)),
         ]
-        + [HB() for _ in (*near, *far, *given, *gates)],
+        + [HB() for _ in (*arrays, *given, *gates)],
         out_specs=[pl.BlockSpec((tiles * rows + tail, BLOCK), lambda g: (0, 0))]
         + [HB() for _ in given],
         out_shape=[jax.ShapeDtypeStruct((tiles * rows + tail, BLOCK), jnp.int16)]
         + [jax.ShapeDtypeStruct(x.shape, x.dtype) for x in given],
         scratch_shapes=[
-            pltpu.VMEM((2 * rows, depth), near[0].dtype),
+            pltpu.VMEM((2 * rows, depth), right0.dtype),
             pltpu.VMEM((tail, BLOCK), jnp.float32),
-            pltpu.SemaphoreType.DMA((2 * len(near),)),
+            pltpu.SemaphoreType.DMA((len(one),)),
             pltpu.SemaphoreType.DMA((max(len(given), 1),)),
         ],
         compiler_params=params(),
         cost_estimate=cost(6 * rows * depth * columns, 4 * rows * depth + 4 * depth * columns),
         name="partial_products",
-    )(diag, right0, right1, *near, *far, *given, *gates)
+    )(diag, right0, right1, *arrays, *given, *gates)
 
 
 def finish_kernel(start, many, keep, coded, square, tangent, *rest):
@@ -332,9 +359,9 @@
             cut = slice(j * BLOCK, (j + 1) * BLOCK)
             other = coded[tile * rows : (tile + 1) * rows, :].astype(jnp.int32).astype(jnp.float32)
             total = mine[:, cut] + other * steps[tile : tile + 1, :]
-            for row_block, piece in row_pieces(start, rows):
-                kept = total[piece] * keep[row_block, j].astype(jnp.float32)
-                made[which, piece, cut] = kept.astype(made.dtype)
+            for row_block, part in row_pieces(start, rows):
+                kept = total[part] * keep[row_block, j].astype(jnp.float32)
+                made[which, part, cut] = kept.astype(made.dtype)
         results[which].start()
     for copy in results + others:
         copy.wait()
@@ -374,8 +401,8 @@
     half = row_index // group
     diag = (half == lax.axis_index("col")).astype(jnp.int32).reshape(1)
     place = (row_index % group).astype(jnp.int32).reshape(1)
-    split = all_rows * 7 // 16
-    spans = ((0, split), (split, all_rows))
+    direct = all_rows // 8
+    split = all_rows // 2
     wide = 256
 
     def device(h, q, c):
@@ -388,42 +415,49 @@
         (device(h, q, c), device(h, q, 1 - c) if h == c else device(1 - h, q, c))
         for h, q, c in spots
     ]
-    across = [
-        (device(h, q, c), device(h, q, c) if h == c else device(1 - h, q, 1 - c))
-        for h, q, c in spots
-    ]
-
     def move(values, pairs):
         return lax.ppermute(values, ("row", "col"), pairs)
 
-    def chunk(i, limit, after=()):
-        return masked_chunk(
-            place, mask0_rows, mask1_rows, x0_rows, x1_rows, spans[i], panel, limit, after
-        )
-
-    def partials(near, far, **more):
-        return partial_products(diag, (near,), (far,), right0, right1, wide, **more)
-
-    def own(mine, other):
-        return local_products(diag, mine, other, right0, right1, wide)
-
-    a0, b0 = chunk(0, ALL_VMEM_BYTES)
-    from_ring, from_across, got_b = move(a0, ring), move(b0, across), move(b0, over_y)
-    a1, b1 = chunk(1, VMEM_BYTES, (a0,))
-    right0, right1 = masked_right(mask0_cols, mask1_cols, x0_cols, x1_cols, (a1,))
-    near, a1, b1 = chosen(diag, from_ring, from_across, (a1, b1), (right0, got_b))
-    mine0, other0 = (a0, b0), (from_ring, got_b)
-    from_ring, from_across = move(a1, ring), move(b1, across)
-    coded, *_ = partials(near, move(near, over_y))
-    near, coded = chosen(diag, from_ring, from_across, (coded,))
+    def chunks(spans, stacked, limit, after=()):
+        inputs = (place, mask0_rows, mask1_rows, x0_rows, x1_rows)
+        return masked_chunks(*inputs, spans, stacked, panel, limit, after)
+
+    def partials(one, other, **more):
+        return partial_products(diag, one, other, right0, right1, wide, **more)
+
+    def own(one, other):
+        return local_products(diag, one, other, right0, right1, wide)
+
+    def parts(joint, a, b):
+        top, low = piece(joint, 0, direct), piece(joint, direct)
+        return (top, piece(a), low, piece(b))
+
+    joint, a1, b1 = chunks(((0, direct), (direct, split)), True, ALL_VMEM_BYTES)
+    passed1 = move(b1, over_y)
+    near0 = move(joint, ring)
+    a2, b2 = chunks(((split, all_rows),), False, VMEM_BYTES, (a1,))
+    right0, right1 = masked_right(mask0_cols, mask1_cols, x0_cols, x1_cols, (a2,))
+    send, b2 = chosen(diag, passed1, a1, (b2,), (near0, right0))
+    near1 = move(send, over_z)
+    passed2 = move(b2, over_y)
+    far0 = move(near0, over_y)
+    send, a1 = chosen(diag, passed2, a2, (a1,), (far0,))
+    near2 = move(send, over_z)
+    got1 = move(a1, over_y)
+    far1 = move(near1, over_y)
+    (coded,) = partials(parts(near0, near1, far1), parts(far0, far1, near1))
+    coded, near2 = handed_on((coded, near2), (got1,))
     back = move(coded, over_z)
-    far = move(near, over_y)
-    sums = own(mine0, other0)
-    coded, b1 = partials(near, far, given=(b1,), gates=sums[:1])
+    far2 = move(near2, over_y)
+    sums = own(parts(joint, a1, b1), parts(near0, got1, passed1))
+    coded, a2 = partials(
+        (piece(near2), piece(far2)), (piece(far2), piece(near2)), given=(a2,), gates=sums[:1]
+    )
     (coded,) = handed_on((coded,), (back,))
     outs = finished(keep, *sums, back, (), 0, all_rows)
     back = move(coded, over_z)
-    sums = own((a1, b1), (from_ring, move(b1, over_y)))
+    got2 = move(a2, over_y)
+    sums = own((piece(a2), piece(b2)), (piece(got2), piece(passed2)))
     return tuple(finished(keep, *sums, back, outs, split, all_rows))
 
 

time: 148 us -> 106 us (0.72)
  waiting for transfers between devices: 101 us -> 50.8 us
  starting transfers between devices: 9.34 us -> 20.6 us
  local copies, waits for them, and re-layouts: 2.87 us -> 1.2 us
    ppermute x10 -> x12, waiting for transfers between devices: 101 us -> 50.8 us  [move(): return lax.ppermute(values, ('row', 'col'), pairs)]
    ppermute x10 -> x12, starting transfers between devices: 9.34 us -> 20.6 us  [move(): return lax.ppermute(values, ('row', 'col'), pairs)]
    unnamed x22 -> x20, local copies, waits for them, and re-layouts: 2.87 us -> 1.2 us
  transfers between devices with their start and end apart: 10 -> 12, of which waited for: 6 -> 8; matrix products, arithmetic and copies ran while one was open for 0% -> 0% of each run, Pallas kernels for 20% -> 26%
where the time goes in v8:
time: 106 us; the launch traced here: 105 us
  waiting for transfers between devices  50.8 us (48%)
  Pallas kernels  31.8 us (30%)
  starting transfers between devices  20.6 us (19%)
  local copies, waits for them, and re-layouts  1.2 us (1%)
    ppermute x12, waiting for transfers between devices, move(): return lax.ppermute(values, ('row', 'col'), pairs)  50.8 us
    ppermute x12, starting transfers between devices, move(): return lax.ppermute(values, ('row', 'col'), pairs)  20.6 us
    pallas_call x2, Pallas kernels, partial_products(): pl.pallas_call(functools.partial(partial_kernel, one, other, len(arrays),...  8.77 us
    pallas_call x2, Pallas kernels, local_products(): pl.pallas_call(functools.partial(local_kernel, one, other), grid=(columns...  8.4 us
    pallas_call x1, Pallas kernels, masked_right(): pl.pallas_call(right_kernel, grid=(depth // tall,), in_specs=[SM(), SM(),...  6.99 us
    pallas_call x2, Pallas kernels, masked_chunks(): pl.pallas_call(functools.partial(chunk_kernel, spans, int(stacked), panel...  3.9 us
    pallas_call x2, Pallas kernels, finished(): pl.pallas_call(functools.partial(finish_kernel, start, many), in_specs=[S...  2.84 us
  transfers between devices with their start and end apart: 12, of which 8 were waited for; matrix products, arithmetic and copies ran while one was open for 0% of the time, Pallas kernels for 26%

profile of v8, /device:TPU:24, one launch (start us, length us, event | category | flops | bytes accessed | tf_op | source)
XLA Modules:
  0.0 105.3 jit_solution(17332135507814185511)
XLA Ops:
  0.7 2.4 %left_chunks.2 = (bf16[64,2048]{1,0:T(8,128)(2,1)}, bf16[96,2048]{1,0:T(8,128)(2,1)}, bf16[96,2048]{1,0:T(8,128)(2,1)}) custom-call(s32[1]{0:T(128)} %bitcast.1.refs_0_, s32[2,128]{1,0:T(2,128)} %refs_1_.3, s32[2,128]{1,0:T(2,128)} %refs_2_.3, bf16[256,16384]{1,0:T(8,128)(2,1)} %refs_3_.3, bf16[256,16384]{1,0:T(8,128)(2,1)} %refs_4_.3), custom_call_target="tpu_custom_call" | custom-call | bytes 32768 | tf_op jit(solution)/shard_map/left_chunks/pallas_call | solution.py:80
  3.1 1.6 %collective-permute-start.1 = (bf16[96,2048]{1,0:T(8,128)(2,1)}, bf16[96,2048]{1,0:T(8,128)(2,1)S(1)}, u32[]{:S(2)}, u32[]{:S(2)}) collective-permute-start(bf16[96,2048]{1,0:T(8,128)(2,1)} %get-tuple-element.28.refs_2_), channel_id=1, source_target_pairs={{0,1},{1,0},{2,3},{3,2},{4,5},{5,4},{6,7},{7,6},{8,9},{9,8},{10,11... | collective-permute-start | bytes 1179656 | tf_op jit(solution)/shard_map/ppermute | solution.py:419
  4.6 0.3 collective-permute-start
  5.2 1.0 copy-done
  6.2 1.5 %left_chunks.3 = (bf16[128,2048]{1,0:T(8,128)(2,1)S(1)}, bf16[128,2048]{1,0:T(8,128)(2,1)S(1)}) custom-call(s32[1]{0:T(128)} %bitcast.1.refs_0_, s32[2,128]{1,0:T(2,128)S(1)} %copy-done.5, s32[2,128]{1,0:T(2,128)S(1)} %copy-done.6, bf16[256,16384]{1,0:T(8,128)(2,1)} %refs_3_.3, bf16[256,16384]{1,0:T(8,128)(2,1)} %refs_4_.3, bf16[96,2048]{1,0:T(8,128)(2,1)S(1)} %copy-done), custom_call_target="tpu_custom_call" | custom-call | bytes 32768 | tf_op jit(solution)/shard_map/left_chunks/pallas_call | solution.py:80
  7.7 7.0 %right_panels.1 = (bf16[2048,768]{1,0:T(8,128)(2,1)S(1)}, bf16[2048,768]{1,0:T(8,128)(2,1)}) custom-call(s32[16,6]{1,0:T(8,128)S(1)} %copy.13.mask0, s32[16,6]{1,0:T(8,128)S(1)} %copy.14.mask1, bf16[2048,768]{1,0:T(8,128)(2,1)} %x0.1, bf16[2048,768]{1,0:T(8,128)(2,1)} %x1.1, bf16[128,2048]{1,0:T(8,128)(2,1)S(1)} %get-tuple-element.24.rest_0_.refs_2_), custom_call_target="tpu_custom_call" | custom-call | bytes 196608 | tf_op jit(solution)/shard_map/right_panels/pallas_call | solution.py:179
  14.7 5.1 %collective-permute-done.refs_0_.refs_3_ = bf16[64,2048]{1,0:T(8,128)(2,1)S(1)} collective-permute-done((bf16[64,2048]{1,0:T(8,128)(2,1)}, bf16[64,2048]{1,0:T(8,128)(2,1)S(1)}, u32[]{:S(2)}, u32[]{:S(2)}) %collective-permute-start) | collective-permute-done | bytes 262176 | tf_op jit(solution)/shard_map/ppermute | solution.py:419
  20.2 1.8 %collective-permute-start.2 = (bf16[96,2048]{1,0:T(8,128)(2,1)S(1)}, bf16[96,2048]{1,0:T(8,128)(2,1)S(1)}, u32[]{:S(2)}, u32[]{:S(2)}) collective-permute-start(bf16[96,2048]{1,0:T(8,128)(2,1)S(1)} %get-tuple-element.30), channel_id=1, source_target_pairs={{0,16},{1,17},{2,18},{3,19},{4,20},{5,21},{6,22},{7,23},{8,24},{9,... | collective-permute-start | bytes 1179656 | tf_op jit(solution)/shard_map/ppermute | solution.py:419
  22.2 16.4 %collective-permute-done.4.refs_3_.refs_0_ = bf16[64,2048]{1,0:T(8,128)(2,1)S(1)} collective-permute-done((bf16[64,2048]{1,0:T(8,128)(2,1)S(1)}, bf16[64,2048]{1,0:T(8,128)(2,1)S(1)}, u32[]{:S(2)}, u32[]{:S(2)}) %collective-permute-start.4) | collective-permute-done | bytes 262176 | tf_op jit(solution)/shard_map/ppermute | solution.py:419
  39.0 0.4 collective-permute-done.2.refs_1_
  39.4 13.0 %collective-permute-start.3 = (bf16[96,2048]{1,0:T(8,128)(2,1)S(1)}, bf16[96,2048]{1,0:T(8,128)(2,1)S(1)}, u32[]{:S(2)}, u32[]{:S(2)}) collective-permute-start(bf16[96,2048]{1,0:T(8,128)(2,1)S(1)} %collective-permute-done.2.refs_1_), channel_id=1, source_target_pairs={{0,1},{1,0},{2,3},{3,2},{4,5},{5,4},{6,7},{7,6},{8,9},{9,8},{10,11... | collective-permute-start | bytes 1179656 | tf_op jit(solution)/shard_map/ppermute | solution.py:419
  52.4 9.9 %collective-permute-done.3.refs_2_ = bf16[96,2048]{1,0:T(8,128)(2,1)S(1)} collective-permute-done((bf16[96,2048]{1,0:T(8,128)(2,1)S(1)}, bf16[96,2048]{1,0:T(8,128)(2,1)S(1)}, u32[]{:S(2)}, u32[]{:S(2)}) %collective-permute-start.3) | collective-permute-done | bytes 393248 | tf_op jit(solution)/shard_map/ppermute | solution.py:419
  62.3 4.7 %partial_products.2.refs_0_ = s16[1552,128]{1,0:T(8,128)(2,1)S(1)} custom-call(s32[1]{0:T(128)} %bitcast.diag, bf16[2048,768]{1,0:T(8,128)(2,1)S(1)} %get-tuple-element.25.refs_1_.right0, bf16[2048,768]{1,0:T(8,128)(2,1)} %get-tuple-element.26.right1, bf16[64,2048]{1,0:T(8,128)(2,1)S(1)} %collective-permute-done.refs_0_.refs_3_, ...), custom_call_target="tpu_custom_call" | custom-call | flops 18874368 | bytes 114688 | tf_op jit(solution)/shard_map/partial_products/pallas_call | solution.py:314
  67.1 3.0 %collective-permute-done.7.refs_2_.refs_4_ = bf16[96,2048]{1,0:T(8,128)(2,1)S(1)} collective-permute-done((bf16[96,2048]{1,0:T(8,128)(2,1)S(1)}, bf16[96,2048]{1,0:T(8,128)(2,1)S(1)}, u32[]{:S(2)}, u32[]{:S(2)}) %collective-permute-start.7) | collective-permute-done | bytes 393248 | tf_op jit(solution)/shard_map/ppermute | solution.py:419
  70.3 1.8 %collective-permute-start.8 = (bf16[128,2048]{1,0:T(8,128)(2,1)S(1)}, bf16[128,2048]{1,0:T(8,128)(2,1)S(1)}, u32[]{:S(2)}, u32[]{:S(2)}) collective-permute-start(bf16[128,2048]{1,0:T(8,128)(2,1)S(1)} %get-tuple-element.34.refs_0_), channel_id=1, source_target_pairs={{0,1},{1,0},{2,3},{3,2},{4,5},{5,4},{6,7},{7,6},{8,9},{9,8},{10,11... | collective-permute-start | bytes 1572872 | tf_op jit(solution)/shard_map/ppermute | solution.py:419
  72.1 4.5 %own_products.2 = (f32[128,768]{1,0:T(8,128)S(1)}, f32[128,768]{1,0:T(8,128)S(1)}) custom-call(s32[1]{0:T(128)} %bitcast.diag, bf16[2048,768]{1,0:T(8,128)(2,1)S(1)} %get-tuple-element.25.refs_1_.right0, bf16[2048,768]{1,0:T(8,128)(2,1)} %get-tuple-element.26.right1, bf16[64,2048]{1,0:T(8,128)(2,1)S(1)} %copy-done.3, ...), custom_call_target="tpu_custom_call" | custom-call | flops 18874368 | bytes 131072 | tf_op jit(solution)/shard_map/own_products/pallas_call | solution.py:250
  76.6 6.9 %collective-permute-done.8.refs_1_ = bf16[128,2048]{1,0:T(8,128)(2,1)S(1)} collective-permute-done((bf16[128,2048]{1,0:T(8,128)(2,1)S(1)}, bf16[128,2048]{1,0:T(8,128)(2,1)S(1)}, u32[]{:S(2)}, u32[]{:S(2)}) %collective-permute-start.8) | collective-permute-done | bytes 524320 | tf_op jit(solution)/shard_map/ppermute | solution.py:419
  83.6 4.0 %partial_products.3 = (s16[1552,128]{1,0:T(8,128)(2,1)S(1)}, bf16[128,2048]{1,0:T(8,128)(2,1)S(1)}) custom-call(s32[1]{0:T(128)} %bitcast.diag, bf16[2048,768]{1,0:T(8,128)(2,1)S(1)} %get-tuple-element.25.refs_1_.right0, bf16[2048,768]{1,0:T(8,128)(2,1)} %get-tuple-element.26.right1, bf16[128,2048]{1,0:T(8,128)(2,1)S(1)} %get-tuple-element.34.refs_0_, ...), custom_call_target="tpu_custom_call" | custom-call | flops 18874368 | bytes 114688 | tf_op jit(solution)/shard_map/partial_products/pallas_call | solution.py:314
  87.6 1.5 %collective-permute-start.11 = (bf16[128,2048]{1,0:T(8,128)(2,1)S(1)}, bf16[128,2048]{1,0:T(8,128)(2,1)S(1)}, u32[]{:S(2)}, u32[]{:S(2)}) collective-permute-start(bf16[128,2048]{1,0:T(8,128)(2,1)S(1)} %get-tuple-element.38.refs_0_), channel_id=1, source_target_pairs={{0,1},{1,0},{2,3},{3,2},{4,5},{5,4},{6,7},{7,6},{8,9},{9,8},{10,11... | collective-permute-start | bytes 1572872 | tf_op jit(solution)/shard_map/ppermute | solution.py:419
  89.1 2.9 %collective-permute-done.9.refs_1_.coded = s16[1552,128]{1,0:T(8,128)(2,1)S(1)} collective-permute-done((s16[1552,128]{1,0:T(8,128)(2,1)S(1)}, s16[1552,128]{1,0:T(8,128)(2,1)S(1)}, u32[]{:S(2)}, u32[]{:S(2)}) %collective-permute-start.9) | collective-permute-done | bytes 397344 | tf_op jit(solution)/shard_map/ppermute | solution.py:419
  92.3 1.4 %finish.2 = (bf16[256,768]{1,0:T(8,128)(2,1)}, bf16[256,768]{1,0:T(8,128)(2,1)}) custom-call(s32[2,6]{1,0:T(2,128)S(1)} %copy-done.4, s16[1552,128]{1,0:T(8,128)(2,1)S(1)} %collective-permute-done.9.refs_1_.coded, f32[128,768]{1,0:T(8,128)S(1)} %get-tuple-element.35.refs_3_.square, f32[128,768]{1,0:T(8,128)S(1)} %get-tuple-element.41.tangent), custom_call_target="tpu_custom_call" | custom-call | bytes 24576 | tf_op jit(solution)/shard_map/finish/pallas_call | solution.py:376
  93.7 6.2 %collective-permute-done.11.refs_2_ = bf16[128,2048]{1,0:T(8,128)(2,1)S(1)} collective-permute-done((bf16[128,2048]{1,0:T(8,128)(2,1)S(1)}, bf16[128,2048]{1,0:T(8,128)(2,1)S(1)}, u32[]{:S(2)}, u32[]{:S(2)}) %collective-permute-start.11) | collective-permute-done | bytes 524320 | tf_op jit(solution)/shard_map/ppermute | solution.py:419
  100.0 3.9 %own_products.3 = (f32[128,768]{1,0:T(8,128)S(1)}, f32[128,768]{1,0:T(8,128)S(1)}) custom-call(s32[1]{0:T(128)} %bitcast.diag, bf16[2048,768]{1,0:T(8,128)(2,1)S(1)} %get-tuple-element.25.refs_1_.right0, bf16[2048,768]{1,0:T(8,128)(2,1)} %get-tuple-element.26.right1, bf16[128,2048]{1,0:T(8,128)(2,1)S(1)} %get-tuple-element.38.refs_0_, ...), custom_call_target="tpu_custom_call" | custom-call | flops 18874368 | bytes 131072 | tf_op jit(solution)/shard_map/own_products/pallas_call | solution.py:250
  103.9 1.4 %finish.3 = (bf16[256,768]{1,0:T(8,128)(2,1)}, bf16[256,768]{1,0:T(8,128)(2,1)}) custom-call(s32[2,6]{1,0:T(2,128)S(1)} %copy-done.4, s16[1552,128]{1,0:T(8,128)(2,1)S(1)} %collective-permute-done.10.coded, f32[128,768]{1,0:T(8,128)S(1)} %get-tuple-element.39.square, ...), custom_call_target="tpu_custom_call", output_to_operand_aliasing={{0}: (4, {}), {1}: (5, {})} | custom-call | bytes 24576 | tf_op jit(solution)/shard_map/finish/pallas_call | solution.py:376
  (33 shorter events, 1.7 us)
Async XLA Ops:
  0.6 4.3 %copy-start.7 = (s32[16,6]{0,1:T(8,128)S(1)}, s32[16,6]{0,1:T(8,128)}, u32[]{:S(2)}) copy-start(s32[16,6]{0,1:T(8,128)} %param.15) | copy-start | bytes 1156
  0.7 4.4 %copy-start.8 = (s32[16,6]{0,1:T(8,128)S(1)}, s32[16,6]{0,1:T(8,128)}, u32[]{:S(2)}) copy-start(s32[16,6]{0,1:T(8,128)} %param.16) | copy-start | bytes 1156
  0.7 4.5 %copy-start.5 = (s32[2,128]{1,0:T(2,128)S(1)}, s32[2,128]{1,0:T(2,128)}, u32[]{:S(2)}) copy-start(s32[2,128]{1,0:T(2,128)} %refs_1_.3) | copy-start | bytes 3076
  0.7 4.5 %copy-start.6 = (s32[2,128]{1,0:T(2,128)S(1)}, s32[2,128]{1,0:T(2,128)}, u32[]{:S(2)}) copy-start(s32[2,128]{1,0:T(2,128)} %refs_2_.3) | copy-start | bytes 3076
  3.1 16.8 %collective-permute-start.1 = (bf16[96,2048]{1,0:T(8,128)(2,1)}, bf16[96,2048]{1,0:T(8,128)(2,1)S(1)}, u32[]{:S(2)}, u32[]{:S(2)}) collective-permute-start(bf16[96,2048]{1,0:T(8,128)(2,1)} %get-tuple-element.28.refs_2_), channel_id=1, source_target_pairs={{0,1},{1,0},{2,3},{3,2},{4,5},{5,4},{6,7},{7,6},{8,9},{9,8},{10,11... | collective-permute-start | bytes 1179656 | tf_op jit(solution)/shard_map/ppermute | solution.py:419
  4.6 15.2 %collective-permute-start = (bf16[64,2048]{1,0:T(8,128)(2,1)}, bf16[64,2048]{1,0:T(8,128)(2,1)S(1)}, u32[]{:S(2)}, u32[]{:S(2)}) collective-permute-start(bf16[64,2048]{1,0:T(8,128)(2,1)} %get-tuple-element.27.refs_0_), channel_id=1, source_target_pairs={{0,1},{1,17},{2,3},{3,19},{4,5},{5,21},{6,7},{7,23},{8,9},{9,25},{... | collective-permute-start | bytes 786440 | tf_op jit(solution)/shard_map/ppermute | solution.py:419
  5.2 1.0 copy-start
  7.7 12.1 %copy-start.1 = (bf16[96,2048]{1,0:T(8,128)(2,1)S(1)}, bf16[96,2048]{1,0:T(8,128)(2,1)}, u32[]{:S(2)}) copy-start(bf16[96,2048]{1,0:T(8,128)(2,1)} %get-tuple-element.23.refs_5_.refs_3_) | copy-start | bytes 1179652
  20.1 18.5 %collective-permute-start.5 = (bf16[128,2048]{1,0:T(8,128)(2,1)S(1)}, bf16[128,2048]{1,0:T(8,128)(2,1)S(1)}, u32[]{:S(2)}, u32[]{:S(2)}) collective-permute-start(bf16[128,2048]{1,0:T(8,128)(2,1)S(1)} %get-tuple-element.31.refs_1_), channel_id=1, source_target_pairs={{0,1},{1,0},{2,3},{3,2},{4,5},{5,4},{6,7},{7,6},{8,9},{9,8},{10,11... | collective-permute-start | bytes 1572872 | tf_op jit(solution)/shard_map/ppermute | solution.py:419
  20.2 19.3 %collective-permute-start.2 = (bf16[96,2048]{1,0:T(8,128)(2,1)S(1)}, bf16[96,2048]{1,0:T(8,128)(2,1)S(1)}, u32[]{:S(2)}, u32[]{:S(2)}) collective-permute-start(bf16[96,2048]{1,0:T(8,128)(2,1)S(1)} %get-tuple-element.30), channel_id=1, source_target_pairs={{0,16},{1,17},{2,18},{3,19},{4,20},{5,21},{6,22},{7,23},{8,24},{9,... | collective-permute-start | bytes 1179656 | tf_op jit(solution)/shard_map/ppermute | solution.py:419
  22.0 16.6 %collective-permute-start.4 = (bf16[64,2048]{1,0:T(8,128)(2,1)S(1)}, bf16[64,2048]{1,0:T(8,128)(2,1)S(1)}, u32[]{:S(2)}, u32[]{:S(2)}) collective-permute-start(bf16[64,2048]{1,0:T(8,128)(2,1)S(1)} %collective-permute-done.refs_0_.refs_3_), channel_id=1, source_target_pairs={{0,1},{1,0},{2,3},{3,2},{4,5},{5,4},{6,7},{7,6},{8,9},{9,8},{10,11... | collective-permute-start | bytes 786440 | tf_op jit(solution)/shard_map/ppermute | solution.py:419
  38.8 31.2 %collective-permute-start.6 = (bf16[128,2048]{1,0:T(8,128)(2,1)S(1)}, bf16[128,2048]{1,0:T(8,128)(2,1)S(1)}, u32[]{:S(2)}, u32[]{:S(2)}) collective-permute-start(bf16[128,2048]{1,0:T(8,128)(2,1)S(1)} %get-tuple-element.32), channel_id=1, source_target_pairs={{0,16},{1,17},{2,18},{3,19},{4,20},{5,21},{6,22},{7,23},{8,24},{9,... | collective-permute-start | bytes 1572872 | tf_op jit(solution)/shard_map/ppermute | solution.py:419
  39.4 22.9 %collective-permute-start.3 = (bf16[96,2048]{1,0:T(8,128)(2,1)S(1)}, bf16[96,2048]{1,0:T(8,128)(2,1)S(1)}, u32[]{:S(2)}, u32[]{:S(2)}) collective-permute-start(bf16[96,2048]{1,0:T(8,128)(2,1)S(1)} %collective-permute-done.2.refs_1_), channel_id=1, source_target_pairs={{0,1},{1,0},{2,3},{3,2},{4,5},{5,4},{6,7},{7,6},{8,9},{9,8},{10,11... | collective-permute-start | bytes 1179656 | tf_op jit(solution)/shard_map/ppermute | solution.py:419
  52.4 17.6 %collective-permute-start.7 = (bf16[96,2048]{1,0:T(8,128)(2,1)S(1)}, bf16[96,2048]{1,0:T(8,128)(2,1)S(1)}, u32[]{:S(2)}, u32[]{:S(2)}) collective-permute-start(bf16[96,2048]{1,0:T(8,128)(2,1)S(1)} %get-tuple-element.33.refs_1_), channel_id=1, source_target_pairs={{0,1},{1,0},{2,3},{3,2},{4,5},{5,4},{6,7},{7,6},{8,9},{9,8},{10,11... | collective-permute-start | bytes 1179656 | tf_op jit(solution)/shard_map/ppermute | solution.py:419
  62.3 9.8 %copy-start.2 = (bf16[96,2048]{1,0:T(8,128)(2,1)S(1)}, bf16[96,2048]{1,0:T(8,128)(2,1)}, u32[]{:S(2)}) copy-start(bf16[96,2048]{1,0:T(8,128)(2,1)} %get-tuple-element.28.refs_2_) | copy-start | bytes 1179652
  62.3 9.8 %copy-start.3 = (bf16[64,2048]{1,0:T(8,128)(2,1)S(1)}, bf16[64,2048]{1,0:T(8,128)(2,1)}, u32[]{:S(2)}) copy-start(bf16[64,2048]{1,0:T(8,128)(2,1)} %get-tuple-element.27.refs_0_) | copy-start | bytes 786436
  70.3 13.3 %collective-permute-start.8 = (bf16[128,2048]{1,0:T(8,128)(2,1)S(1)}, bf16[128,2048]{1,0:T(8,128)(2,1)S(1)}, u32[]{:S(2)}, u32[]{:S(2)}) collective-permute-start(bf16[128,2048]{1,0:T(8,128)(2,1)S(1)} %get-tuple-element.34.refs_0_), channel_id=1, source_target_pairs={{0,1},{1,0},{2,3},{3,2},{4,5},{5,4},{6,7},{7,6},{8,9},{9,8},{10,11... | collective-permute-start | bytes 1572872 | tf_op jit(solution)/shard_map/ppermute | solution.py:419
  72.1 19.9 %collective-permute-start.9 = (s16[1552,128]{1,0:T(8,128)(2,1)S(1)}, s16[1552,128]{1,0:T(8,128)(2,1)S(1)}, u32[]{:S(2)}, u32[]{:S(2)}) collective-permute-start(s16[1552,128]{1,0:T(8,128)(2,1)S(1)} %get-tuple-element.37), channel_id=1, source_target_pairs={{0,16},{1,17},{2,18},{3,19},{4,20},{5,21},{6,22},{7,23},{8,24},{9,... | collective-permute-start | bytes 1191944 | tf_op jit(solution)/shard_map/ppermute | solution.py:419
  83.6 8.7 %copy-start.4 = (s32[2,6]{1,0:T(2,128)S(1)}, s32[2,6]{1,0:T(2,128)}, u32[]{:S(2)}) copy-start(s32[2,6]{1,0:T(2,128)} %keep.3) | copy-start | bytes 148
  87.6 12.4 %collective-permute-start.11 = (bf16[128,2048]{1,0:T(8,128)(2,1)S(1)}, bf16[128,2048]{1,0:T(8,128)(2,1)S(1)}, u32[]{:S(2)}, u32[]{:S(2)}) collective-permute-start(bf16[128,2048]{1,0:T(8,128)(2,1)S(1)} %get-tuple-element.38.refs_0_), channel_id=1, source_target_pairs={{0,1},{1,0},{2,3},{3,2},{4,5},{5,4},{6,7},{7,6},{8,9},{9,8},{10,11... | collective-permute-start | bytes 1572872 | tf_op jit(solution)/shard_map/ppermute | solution.py:419
  92.2 11.6 %collective-permute-start.10 = (s16[1552,128]{1,0:T(8,128)(2,1)S(1)}, s16[1552,128]{1,0:T(8,128)(2,1)S(1)}, u32[]{:S(2)}, u32[]{:S(2)}) collective-permute-start(s16[1552,128]{1,0:T(8,128)(2,1)S(1)} %handed_on.3), channel_id=1, source_target_pairs={{0,16},{1,17},{2,18},{3,19},{4,20},{5,21},{6,22},{7,23},{8,24},{9,... | collective-permute-start | bytes 1191944 | tf_op jit(solution)/shard_map/ppermute | solution.py:419

commit v9 on v8

--- a/solution.py
+++ b/solution.py
@@ -260,7 +260,7 @@
         out_shape=[out, out],
         scratch_shapes=[
             pltpu.VMEM((2 * rows, depth), right0.dtype),
-            pltpu.SemaphoreType.DMA((len(one),)),
+            pltpu.SemaphoreType.DMA((max(len(one), len(other)),)),
         ],
         compiler_params=params(),
         cost_estimate=cost(6 * rows * depth * columns, 8 * rows * depth + 4 * depth * columns),
@@ -268,12 +268,13 @@
     )(diag, right0, right1, *arrays)
 
 
-def partial_kernel(one, other, many, given, diag, right0, right1, *refs):
+def partial_kernel(one, other, many, cuts, diag, right0, right1, *refs):
+    given = len(cuts)
     out, passed = refs[-5 - given], refs[-4 - given : -4]
     held, steps, sems, hand_sems = refs[-4:]
     others = [
-        pltpu.make_async_copy(x, y, hand_sems.at[i])
-        for i, (x, y) in enumerate(zip(refs[many : many + given], passed))
+        pltpu.make_async_copy(x.at[pl.ds(lo, hi - lo)], y, hand_sems.at[i])
+        for i, (x, y, (lo, hi)) in enumerate(zip(refs[many : many + given], passed, cuts))
     ]
 
     @pl.when(pl.program_id(0) == 0)
@@ -312,7 +313,7 @@
     tiles = 2 * columns // BLOCK
     tail = -(-tiles // 16) * 16
     return pl.pallas_call(
-        functools.partial(partial_kernel, one, other, len(arrays), len(given)),
+        functools.partial(partial_kernel, one, other, len(arrays), [cut for _, *cut in given]),
         grid=(columns // wide,),
         in_specs=[
             SM(),
@@ -323,26 +324,28 @@
         out_specs=[pl.BlockSpec((tiles * rows + tail, BLOCK), lambda g: (0, 0))]
         + [HB() for _ in given],
         out_shape=[jax.ShapeDtypeStruct((tiles * rows + tail, BLOCK), jnp.int16)]
-        + [jax.ShapeDtypeStruct(x.shape, x.dtype) for x in given],
+        + [jax.ShapeDtypeStruct((hi - lo, x.shape[1]), x.dtype) for x, lo, hi in given],
         scratch_shapes=[
             pltpu.VMEM((2 * rows, depth), right0.dtype),
             pltpu.VMEM((tail, BLOCK), jnp.float32),
-            pltpu.SemaphoreType.DMA((len(one),)),
+            pltpu.SemaphoreType.DMA((max(len(one), len(other)),)),
             pltpu.SemaphoreType.DMA((max(len(given), 1),)),
         ],
         compiler_params=params(),
         cost_estimate=cost(6 * rows * depth * columns, 4 * rows * depth + 4 * depth * columns),
         name="partial_products",
-    )(diag, right0, right1, *arrays, *given, *gates)
-
-
-def finish_kernel(start, many, keep, coded, square, tangent, *rest):
+    )(diag, right0, right1, *arrays, *(x for x, _, _ in given), *gates)
+
+
+def finish_kernel(start, cuts, keep, coded, square, tangent, *rest):
+    many = len(cuts)
     given, outs, passed = rest[:many], rest[-5 - many : -3 - many], rest[-3 - many : -3]
     made, out_sems, sems = rest[-3:]
     rows, columns = square.shape
     across = columns // BLOCK
     others = [
-        pltpu.make_async_copy(x, y, sems.at[i]) for i, (x, y) in enumerate(zip(given, passed))
+        pltpu.make_async_copy(x.at[pl.ds(lo, hi - lo)], y, sems.at[i])
+        for i, (x, y, (lo, hi)) in enumerate(zip(given, passed, cuts))
     ]
     results = [
         pltpu.make_async_copy(made.at[i], x.at[pl.ds(start, rows)], out_sems.at[i])
@@ -371,10 +374,10 @@
     rows, columns = square.shape
     out = jax.ShapeDtypeStruct((all_rows, columns), jnp.bfloat16)
     held, before = list(held), list(before)
-    passed = [jax.ShapeDtypeStruct(x.shape, x.dtype) for x in held]
+    passed = [jax.ShapeDtypeStruct((hi - lo, x.shape[1]), x.dtype) for x, lo, hi in held]
     many = len(held)
     return pl.pallas_call(
-        functools.partial(finish_kernel, start, many),
+        functools.partial(finish_kernel, start, [cut for _, *cut in held]),
         in_specs=[SM(), VM(), VM(), VM()] + [HB() for _ in (*held, *before, *after)],
         out_specs=[HB() for _ in range(2 + many)],
         out_shape=[out, out] + passed,
@@ -387,7 +390,7 @@
         compiler_params=params(),
         cost_estimate=cost(0, 16 * rows * columns),
         name="finish",
-    )(keep, coded, square, tangent, *held, *before, *after)
+    )(keep, coded, square, tangent, *(x for x, _, _ in held), *before, *after)
 
 
 def per_device_pair(
@@ -450,14 +453,18 @@
     back = move(coded, over_z)
     far2 = move(near2, over_y)
     sums = own(parts(joint, a1, b1), parts(near0, got1, passed1))
-    coded, a2 = partials(
-        (piece(near2), piece(far2)), (piece(far2), piece(near2)), given=(a2,), gates=sums[:1]
+    late = a2.shape[0] * 3 // 4
+    coded, top2, low2 = partials(
+        (piece(near2), piece(far2)),
+        (piece(far2), piece(near2)),
+        given=(piece(a2, 0, late), piece(a2, late)),
+        gates=sums[:1],
     )
-    (coded,) = handed_on((coded,), (back,))
+    (low2,) = handed_on((low2,), (back,))
     outs = finished(keep, *sums, back, (), 0, all_rows)
     back = move(coded, over_z)
-    got2 = move(a2, over_y)
-    sums = own((piece(a2), piece(b2)), (piece(got2), piece(passed2)))
+    got2 = (piece(move(top2, over_y)), piece(move(low2, over_y)))
+    sums = own((piece(a2), piece(b2)), (*got2, piece(passed2)))
     return tuple(finished(keep, *sums, back, outs, split, all_rows))
 
 

time: 106 us -> 109 us (1.028)
  the two profiles are of different devices: /device:TPU:24 before, /device:TPU:10 now
where the time goes in v9:
time: 109 us; the launch traced here: 108 us
  waiting for transfers between devices  39.7 us (36%)
  starting transfers between devices  34 us (31%)
  Pallas kernels  32.2 us (30%)
  local copies, waits for them, and re-layouts  1.2 us (1%)
    ppermute x13, waiting for transfers between devices, move(): return lax.ppermute(values, ('row', 'col'), pairs)  39.7 us
    ppermute x13, starting transfers between devices, move(): return lax.ppermute(values, ('row', 'col'), pairs)  34 us
    pallas_call x2, Pallas kernels, partial_products(): pl.pallas_call(functools.partial(partial_kernel, one, other, len(arrays),...  9.13 us
    pallas_call x2, Pallas kernels, local_products(): pl.pallas_call(functools.partial(local_kernel, one, other), grid=(columns...  8.41 us
    pallas_call x1, Pallas kernels, masked_right(): pl.pallas_call(right_kernel, grid=(depth // tall,), in_specs=[SM(), SM(),...  6.99 us
    pallas_call x2, Pallas kernels, masked_chunks(): pl.pallas_call(functools.partial(chunk_kernel, spans, int(stacked), panel...  3.9 us
    pallas_call x2, Pallas kernels, finished(): pl.pallas_call(functools.partial(finish_kernel, start, [cut for _, *cut i...  2.84 us
  transfers between devices with their start and end apart: 13, of which 6 were waited for; matrix products, arithmetic and copies ran while one was open for 0% of the time, Pallas kernels for 26%

profile of v9, /device:TPU:10, one launch (start us, length us, event | category | flops | bytes accessed | tf_op | source)
XLA Modules:
  0.0 107.9 jit_solution(6539639216551261100)
XLA Ops:
  0.7 2.4 %left_chunks.2 = (bf16[64,2048]{1,0:T(8,128)(2,1)}, bf16[96,2048]{1,0:T(8,128)(2,1)}, bf16[96,2048]{1,0:T(8,128)(2,1)}) custom-call(s32[1]{0:T(128)} %bitcast.1.refs_0_, s32[2,128]{1,0:T(2,128)} %refs_1_.3, s32[2,128]{1,0:T(2,128)} %refs_2_.3, bf16[256,16384]{1,0:T(8,128)(2,1)} %refs_3_.3, bf16[256,16384]{1,0:T(8,128)(2,1)} %refs_4_.3), custom_call_target="tpu_custom_call" | custom-call | bytes 32768 | tf_op jit(solution)/shard_map/left_chunks/pallas_call | solution.py:80
  3.1 1.6 %collective-permute-start.1 = (bf16[96,2048]{1,0:T(8,128)(2,1)}, bf16[96,2048]{1,0:T(8,128)(2,1)S(1)}, u32[]{:S(2)}, u32[]{:S(2)}) collective-permute-start(bf16[96,2048]{1,0:T(8,128)(2,1)} %get-tuple-element.29.refs_2_), channel_id=1, source_target_pairs={{0,1},{1,0},{2,3},{3,2},{4,5},{5,4},{6,7},{7,6},{8,9},{9,8},{10,11... | collective-permute-start | bytes 1179656 | tf_op jit(solution)/shard_map/ppermute | solution.py:422
  5.3 1.0 copy-done
  6.3 1.5 %left_chunks.3 = (bf16[128,2048]{1,0:T(8,128)(2,1)S(1)}, bf16[128,2048]{1,0:T(8,128)(2,1)S(1)}) custom-call(s32[1]{0:T(128)} %bitcast.1.refs_0_, s32[2,128]{1,0:T(2,128)S(1)} %copy-done.5, s32[2,128]{1,0:T(2,128)S(1)} %copy-done.6, bf16[256,16384]{1,0:T(8,128)(2,1)} %refs_3_.3, bf16[256,16384]{1,0:T(8,128)(2,1)} %refs_4_.3, bf16[96,2048]{1,0:T(8,128)(2,1)S(1)} %copy-done), custom_call_target="tpu_custom_call" | custom-call | bytes 32768 | tf_op jit(solution)/shard_map/left_chunks/pallas_call | solution.py:80
  7.9 7.0 %right_panels.1 = (bf16[2048,768]{1,0:T(8,128)(2,1)S(1)}, bf16[2048,768]{1,0:T(8,128)(2,1)}) custom-call(s32[16,6]{1,0:T(8,128)S(1)} %copy.13.mask0, s32[16,6]{1,0:T(8,128)S(1)} %copy.14.mask1, bf16[2048,768]{1,0:T(8,128)(2,1)} %x0.1, bf16[2048,768]{1,0:T(8,128)(2,1)} %x1.1, bf16[128,2048]{1,0:T(8,128)(2,1)S(1)} %get-tuple-element.25.rest_0_.refs_2_.refs_3_.refs_0_), custom_call_target="tpu_custom_call" | custom-call | bytes 196608 | tf_op jit(solution)/shard_map/right_panels/pallas_call | solution.py:179
  14.9 4.1 %collective-permute-done.refs_0_.refs_3_ = bf16[64,2048]{1,0:T(8,128)(2,1)S(1)} collective-permute-done((bf16[64,2048]{1,0:T(8,128)(2,1)}, bf16[64,2048]{1,0:T(8,128)(2,1)S(1)}, u32[]{:S(2)}, u32[]{:S(2)}) %collective-permute-start) | collective-permute-done | bytes 262176 | tf_op jit(solution)/shard_map/ppermute | solution.py:422
  19.2 2.4 %collective-permute-start.5 = (bf16[128,2048]{1,0:T(8,128)(2,1)S(1)}, bf16[128,2048]{1,0:T(8,128)(2,1)S(1)}, u32[]{:S(2)}, u32[]{:S(2)}) collective-permute-start(bf16[128,2048]{1,0:T(8,128)(2,1)S(1)} %get-tuple-element.32.refs_1_), channel_id=1, source_target_pairs={{0,1},{1,0},{2,3},{3,2},{4,5},{5,4},{6,7},{7,6},{8,9},{9,8},{10,11... | collective-permute-start | bytes 1572872 | tf_op jit(solution)/shard_map/ppermute | solution.py:422
  21.7 1.1 %collective-permute-start.2 = (bf16[96,2048]{1,0:T(8,128)(2,1)S(1)}, bf16[96,2048]{1,0:T(8,128)(2,1)S(1)}, u32[]{:S(2)}, u32[]{:S(2)}) collective-permute-start(bf16[96,2048]{1,0:T(8,128)(2,1)S(1)} %get-tuple-element.31), channel_id=1, source_target_pairs={{0,16},{1,17},{2,18},{3,19},{4,20},{5,21},{6,22},{7,23},{8,24},{9,... | collective-permute-start | bytes 1179656 | tf_op jit(solution)/shard_map/ppermute | solution.py:422
  22.8 1.9 %collective-permute-start.4 = (bf16[64,2048]{1,0:T(8,128)(2,1)S(1)}, bf16[64,2048]{1,0:T(8,128)(2,1)S(1)}, u32[]{:S(2)}, u32[]{:S(2)}) collective-permute-start(bf16[64,2048]{1,0:T(8,128)(2,1)S(1)} %collective-permute-done.refs_0_.refs_3_), channel_id=1, source_target_pairs={{0,1},{1,0},{2,3},{3,2},{4,5},{5,4},{6,7},{7,6},{8,9},{9,8},{10,11... | collective-permute-start | bytes 786440 | tf_op jit(solution)/shard_map/ppermute | solution.py:422
  24.8 13.6 %collective-permute-done.4.refs_3_.refs_0_ = bf16[64,2048]{1,0:T(8,128)(2,1)S(1)} collective-permute-done((bf16[64,2048]{1,0:T(8,128)(2,1)S(1)}, bf16[64,2048]{1,0:T(8,128)(2,1)S(1)}, u32[]{:S(2)}, u32[]{:S(2)}) %collective-permute-start.4) | collective-permute-done | bytes 262176 | tf_op jit(solution)/shard_map/ppermute | solution.py:422
  38.6 2.9 %collective-permute-start.6 = (bf16[128,2048]{1,0:T(8,128)(2,1)S(1)}, bf16[128,2048]{1,0:T(8,128)(2,1)S(1)}, u32[]{:S(2)}, u32[]{:S(2)}) collective-permute-start(bf16[128,2048]{1,0:T(8,128)(2,1)S(1)} %get-tuple-element.33), channel_id=1, source_target_pairs={{0,16},{1,17},{2,18},{3,19},{4,20},{5,21},{6,22},{7,23},{8,24},{9,... | collective-permute-start | bytes 1572872 | tf_op jit(solution)/shard_map/ppermute | solution.py:422
  42.2 1.3 %collective-permute-start.7 = (bf16[96,2048]{1,0:T(8,128)(2,1)S(1)}, bf16[96,2048]{1,0:T(8,128)(2,1)S(1)}, u32[]{:S(2)}, u32[]{:S(2)}) collective-permute-start(bf16[96,2048]{1,0:T(8,128)(2,1)S(1)} %get-tuple-element.34.refs_1_), channel_id=1, source_target_pairs={{0,1},{1,0},{2,3},{3,2},{4,5},{5,4},{6,7},{7,6},{8,9},{9,8},{10,11... | collective-permute-start | bytes 1179656 | tf_op jit(solution)/shard_map/ppermute | solution.py:422
  43.5 10.0 %collective-permute-done.3.refs_2_ = bf16[96,2048]{1,0:T(8,128)(2,1)S(1)} collective-permute-done((bf16[96,2048]{1,0:T(8,128)(2,1)S(1)}, bf16[96,2048]{1,0:T(8,128)(2,1)S(1)}, u32[]{:S(2)}, u32[]{:S(2)}) %collective-permute-start.3) | collective-permute-done | bytes 393248 | tf_op jit(solution)/shard_map/ppermute | solution.py:422
  53.5 4.7 %partial_products.2.refs_0_ = s16[1552,128]{1,0:T(8,128)(2,1)S(1)} custom-call(s32[1]{0:T(128)} %bitcast.diag, bf16[2048,768]{1,0:T(8,128)(2,1)S(1)} %get-tuple-element.26.refs_1_.right0, bf16[2048,768]{1,0:T(8,128)(2,1)} %get-tuple-element.27.right1, bf16[64,2048]{1,0:T(8,128)(2,1)S(1)} %collective-permute-done.refs_0_.refs_3_, ...), custom_call_target="tpu_custom_call" | custom-call | flops 18874368 | bytes 114688 | tf_op jit(solution)/shard_map/partial_products/pallas_call | solution.py:315
  58.7 3.3 %collective-permute-done.6.refs_1_ = bf16[128,2048]{1,0:T(8,128)(2,1)S(1)} collective-permute-done((bf16[128,2048]{1,0:T(8,128)(2,1)S(1)}, bf16[128,2048]{1,0:T(8,128)(2,1)S(1)}, u32[]{:S(2)}, u32[]{:S(2)}) %collective-permute-start.6) | collective-permute-done | bytes 524320 | tf_op jit(solution)/shard_map/ppermute | solution.py:422
  63.1 11.6 %collective-permute-start.11 = (s16[1552,128]{1,0:T(8,128)(2,1)S(1)}, s16[1552,128]{1,0:T(8,128)(2,1)S(1)}, u32[]{:S(2)}, u32[]{:S(2)}) collective-permute-start(s16[1552,128]{1,0:T(8,128)(2,1)S(1)} %get-tuple-element.40), channel_id=1, source_target_pairs={{0,16},{1,17},{2,18},{3,19},{4,20},{5,21},{6,22},{7,23},{8,24},{9,... | collective-permute-start | bytes 1191944 | tf_op jit(solution)/shard_map/ppermute | solution.py:422
  74.7 4.5 %own_products.2 = (f32[128,768]{1,0:T(8,128)S(1)}, f32[128,768]{1,0:T(8,128)S(1)}) custom-call(s32[1]{0:T(128)} %bitcast.diag, bf16[2048,768]{1,0:T(8,128)(2,1)S(1)} %get-tuple-element.26.refs_1_.right0, bf16[2048,768]{1,0:T(8,128)(2,1)} %get-tuple-element.27.right1, bf16[64,2048]{1,0:T(8,128)(2,1)S(1)} %copy-done.3, ...), custom_call_target="tpu_custom_call" | custom-call | flops 18874368 | bytes 131072 | tf_op jit(solution)/shard_map/own_products/pallas_call | solution.py:250
  79.2 4.4 %partial_products.3 = (s16[1552,128]{1,0:T(8,128)(2,1)S(1)}, bf16[96,2048]{1,0:T(8,128)(2,1)S(1)}, bf16[32,2048]{1,0:T(8,128)(2,1)S(1)}) custom-call(s32[1]{0:T(128)} %bitcast.diag, bf16[2048,768]{1,0:T(8,128)(2,1)S(1)} %get-tuple-element.26.refs_1_.right0, bf16[2048,768]{1,0:T(8,128)(2,1)} %get-tuple-element.27.right1, ...), custom_call_target="tpu_custom_call" | custom-call | flops 18874368 | bytes 114688 | tf_op jit(solution)/shard_map/partial_products/pallas_call | solution.py:315
  83.6 7.0 %collective-permute-start.9 = (s16[1552,128]{1,0:T(8,128)(2,1)S(1)}, s16[1552,128]{1,0:T(8,128)(2,1)S(1)}, u32[]{:S(2)}, u32[]{:S(2)}) collective-permute-start(s16[1552,128]{1,0:T(8,128)(2,1)S(1)} %get-tuple-element.37), channel_id=1, source_target_pairs={{0,16},{1,17},{2,18},{3,19},{4,20},{5,21},{6,22},{7,23},{8,24},{9,... | collective-permute-start | bytes 1191944 | tf_op jit(solution)/shard_map/ppermute | solution.py:422
  90.6 1.4 %collective-permute-start.10 = (bf16[96,2048]{1,0:T(8,128)(2,1)S(1)}, bf16[96,2048]{1,0:T(8,128)(2,1)S(1)}, u32[]{:S(2)}, u32[]{:S(2)}) collective-permute-start(bf16[96,2048]{1,0:T(8,128)(2,1)S(1)} %get-tuple-element.38), channel_id=1, source_target_pairs={{0,1},{1,0},{2,3},{3,2},{4,5},{5,4},{6,7},{7,6},{8,9},{9,8},{10,11... | collective-permute-start | bytes 1179656 | tf_op jit(solution)/shard_map/ppermute | solution.py:422
  92.9 1.4 %finish.2 = (bf16[256,768]{1,0:T(8,128)(2,1)}, bf16[256,768]{1,0:T(8,128)(2,1)}) custom-call(s32[2,6]{1,0:T(2,128)S(1)} %copy-done.4, s16[1552,128]{1,0:T(8,128)(2,1)S(1)} %collective-permute-done.11.refs_1_.coded, f32[128,768]{1,0:T(8,128)S(1)} %get-tuple-element.36.refs_4_.square, f32[128,768]{1,0:T(8,128)S(1)} %get-tuple-element.43.tangent), custom_call_target="tpu_custom_call" | custom-call | bytes 24576 | tf_op jit(solution)/shard_map/finish/pallas_call | solution.py:379
  94.3 8.3 %collective-permute-done.12.refs_3_ = bf16[32,2048]{1,0:T(8,128)(2,1)S(1)} collective-permute-done((bf16[32,2048]{1,0:T(8,128)(2,1)S(1)}, bf16[32,2048]{1,0:T(8,128)(2,1)S(1)}, u32[]{:S(2)}, u32[]{:S(2)}) %collective-permute-start.12) | collective-permute-done | bytes 131104 | tf_op jit(solution)/shard_map/ppermute | solution.py:422
  102.6 3.9 %own_products.3 = (f32[128,768]{1,0:T(8,128)S(1)}, f32[128,768]{1,0:T(8,128)S(1)}) custom-call(s32[1]{0:T(128)} %bitcast.diag, bf16[2048,768]{1,0:T(8,128)(2,1)S(1)} %get-tuple-element.26.refs_1_.right0, bf16[2048,768]{1,0:T(8,128)(2,1)} %get-tuple-element.27.right1, bf16[128,2048]{1,0:T(8,128)(2,1)S(1)} %get-tuple-element.25.rest_0_.refs_2_.refs_3_.refs_0_, ...), custom_call_target="tpu_custom_call" | custom-call | flops 18874368 | bytes 131072 | tf_op jit(solution)/shard_map/own_products/pallas_call | solution.py:250
  106.5 1.4 %finish.3 = (bf16[256,768]{1,0:T(8,128)(2,1)}, bf16[256,768]{1,0:T(8,128)(2,1)}) custom-call(s32[2,6]{1,0:T(2,128)S(1)} %copy-done.4, s16[1552,128]{1,0:T(8,128)(2,1)S(1)} %collective-permute-done.9.coded, f32[128,768]{1,0:T(8,128)S(1)} %get-tuple-element.41.square, ...), custom_call_target="tpu_custom_call", output_to_operand_aliasing={{0}: (4, {}), {1}: (5, {})} | custom-call | bytes 24576 | tf_op jit(solution)/shard_map/finish/pallas_call | solution.py:379
  (35 shorter events, 4.3 us)
Async XLA Ops:
  0.6 4.5 %copy-start.7 = (s32[16,6]{0,1:T(8,128)S(1)}, s32[16,6]{0,1:T(8,128)}, u32[]{:S(2)}) copy-start(s32[16,6]{0,1:T(8,128)} %param.15) | copy-start | bytes 1156
  0.7 4.6 %copy-start.8 = (s32[16,6]{0,1:T(8,128)S(1)}, s32[16,6]{0,1:T(8,128)}, u32[]{:S(2)}) copy-start(s32[16,6]{0,1:T(8,128)} %param.16) | copy-start | bytes 1156
  0.7 4.7 %copy-start.5 = (s32[2,128]{1,0:T(2,128)S(1)}, s32[2,128]{1,0:T(2,128)}, u32[]{:S(2)}) copy-start(s32[2,128]{1,0:T(2,128)} %refs_1_.3) | copy-start | bytes 3076
  0.7 4.7 %copy-start.6 = (s32[2,128]{1,0:T(2,128)S(1)}, s32[2,128]{1,0:T(2,128)}, u32[]{:S(2)}) copy-start(s32[2,128]{1,0:T(2,128)} %refs_2_.3) | copy-start | bytes 3076
  3.1 15.9 %collective-permute-start.1 = (bf16[96,2048]{1,0:T(8,128)(2,1)}, bf16[96,2048]{1,0:T(8,128)(2,1)S(1)}, u32[]{:S(2)}, u32[]{:S(2)}) collective-permute-start(bf16[96,2048]{1,0:T(8,128)(2,1)} %get-tuple-element.29.refs_2_), channel_id=1, source_target_pairs={{0,1},{1,0},{2,3},{3,2},{4,5},{5,4},{6,7},{7,6},{8,9},{9,8},{10,11... | collective-permute-start | bytes 1179656 | tf_op jit(solution)/shard_map/ppermute | solution.py:422
  4.6 14.3 %collective-permute-start = (bf16[64,2048]{1,0:T(8,128)(2,1)}, bf16[64,2048]{1,0:T(8,128)(2,1)S(1)}, u32[]{:S(2)}, u32[]{:S(2)}) collective-permute-start(bf16[64,2048]{1,0:T(8,128)(2,1)} %get-tuple-element.28.refs_0_), channel_id=1, source_target_pairs={{0,1},{1,17},{2,3},{3,19},{4,5},{5,21},{6,7},{7,23},{8,9},{9,25},{... | collective-permute-start | bytes 786440 | tf_op jit(solution)/shard_map/ppermute | solution.py:422
  5.3 1.0 copy-start
  7.9 11.1 %copy-start.1 = (bf16[96,2048]{1,0:T(8,128)(2,1)S(1)}, bf16[96,2048]{1,0:T(8,128)(2,1)}, u32[]{:S(2)}) copy-start(bf16[96,2048]{1,0:T(8,128)(2,1)} %get-tuple-element.24.refs_5_.refs_3_) | copy-start | bytes 1179652
  19.2 19.1 %collective-permute-start.5 = (bf16[128,2048]{1,0:T(8,128)(2,1)S(1)}, bf16[128,2048]{1,0:T(8,128)(2,1)S(1)}, u32[]{:S(2)}, u32[]{:S(2)}) collective-permute-start(bf16[128,2048]{1,0:T(8,128)(2,1)S(1)} %get-tuple-element.32.refs_1_), channel_id=1, source_target_pairs={{0,1},{1,0},{2,3},{3,2},{4,5},{5,4},{6,7},{7,6},{8,9},{9,8},{10,11... | collective-permute-start | bytes 1572872 | tf_op jit(solution)/shard_map/ppermute | solution.py:422
  21.7 19.8 %collective-permute-start.2 = (bf16[96,2048]{1,0:T(8,128)(2,1)S(1)}, bf16[96,2048]{1,0:T(8,128)(2,1)S(1)}, u32[]{:S(2)}, u32[]{:S(2)}) collective-permute-start(bf16[96,2048]{1,0:T(8,128)(2,1)S(1)} %get-tuple-element.31), channel_id=1, source_target_pairs={{0,16},{1,17},{2,18},{3,19},{4,20},{5,21},{6,22},{7,23},{8,24},{9,... | collective-permute-start | bytes 1179656 | tf_op jit(solution)/shard_map/ppermute | solution.py:422
  22.8 15.5 %collective-permute-start.4 = (bf16[64,2048]{1,0:T(8,128)(2,1)S(1)}, bf16[64,2048]{1,0:T(8,128)(2,1)S(1)}, u32[]{:S(2)}, u32[]{:S(2)}) collective-permute-start(bf16[64,2048]{1,0:T(8,128)(2,1)S(1)} %collective-permute-done.refs_0_.refs_3_), channel_id=1, source_target_pairs={{0,1},{1,0},{2,3},{3,2},{4,5},{5,4},{6,7},{7,6},{8,9},{9,8},{10,11... | collective-permute-start | bytes 786440 | tf_op jit(solution)/shard_map/ppermute | solution.py:422
  38.6 23.4 %collective-permute-start.6 = (bf16[128,2048]{1,0:T(8,128)(2,1)S(1)}, bf16[128,2048]{1,0:T(8,128)(2,1)S(1)}, u32[]{:S(2)}, u32[]{:S(2)}) collective-permute-start(bf16[128,2048]{1,0:T(8,128)(2,1)S(1)} %get-tuple-element.33), channel_id=1, source_target_pairs={{0,16},{1,17},{2,18},{3,19},{4,20},{5,21},{6,22},{7,23},{8,24},{9,... | collective-permute-start | bytes 1572872 | tf_op jit(solution)/shard_map/ppermute | solution.py:422
  41.5 12.1 %collective-permute-start.3 = (bf16[96,2048]{1,0:T(8,128)(2,1)S(1)}, bf16[96,2048]{1,0:T(8,128)(2,1)S(1)}, u32[]{:S(2)}, u32[]{:S(2)}) collective-permute-start(bf16[96,2048]{1,0:T(8,128)(2,1)S(1)} %collective-permute-done.2.refs_1_), channel_id=1, source_target_pairs={{0,1},{1,0},{2,3},{3,2},{4,5},{5,4},{6,7},{7,6},{8,9},{9,8},{10,11... | collective-permute-start | bytes 1179656 | tf_op jit(solution)/shard_map/ppermute | solution.py:422
  42.2 16.4 %collective-permute-start.7 = (bf16[96,2048]{1,0:T(8,128)(2,1)S(1)}, bf16[96,2048]{1,0:T(8,128)(2,1)S(1)}, u32[]{:S(2)}, u32[]{:S(2)}) collective-permute-start(bf16[96,2048]{1,0:T(8,128)(2,1)S(1)} %get-tuple-element.34.refs_1_), channel_id=1, source_target_pairs={{0,1},{1,0},{2,3},{3,2},{4,5},{5,4},{6,7},{7,6},{8,9},{9,8},{10,11... | collective-permute-start | bytes 1179656 | tf_op jit(solution)/shard_map/ppermute | solution.py:422
  53.5 21.2 %copy-start.2 = (bf16[96,2048]{1,0:T(8,128)(2,1)S(1)}, bf16[96,2048]{1,0:T(8,128)(2,1)}, u32[]{:S(2)}) copy-start(bf16[96,2048]{1,0:T(8,128)(2,1)} %get-tuple-element.29.refs_2_) | copy-start | bytes 1179652
  53.5 21.2 %copy-start.3 = (bf16[64,2048]{1,0:T(8,128)(2,1)S(1)}, bf16[64,2048]{1,0:T(8,128)(2,1)}, u32[]{:S(2)}) copy-start(bf16[64,2048]{1,0:T(8,128)(2,1)} %get-tuple-element.28.refs_0_) | copy-start | bytes 786436
  62.2 17.0 %collective-permute-start.8 = (bf16[128,2048]{1,0:T(8,128)(2,1)S(1)}, bf16[128,2048]{1,0:T(8,128)(2,1)S(1)}, u32[]{:S(2)}, u32[]{:S(2)}) collective-permute-start(bf16[128,2048]{1,0:T(8,128)(2,1)S(1)} %get-tuple-element.35.refs_0_), channel_id=1, source_target_pairs={{0,1},{1,0},{2,3},{3,2},{4,5},{5,4},{6,7},{7,6},{8,9},{9,8},{10,11... | collective-permute-start | bytes 1572872 | tf_op jit(solution)/shard_map/ppermute | solution.py:422
  63.1 29.0 %collective-permute-start.11 = (s16[1552,128]{1,0:T(8,128)(2,1)S(1)}, s16[1552,128]{1,0:T(8,128)(2,1)S(1)}, u32[]{:S(2)}, u32[]{:S(2)}) collective-permute-start(s16[1552,128]{1,0:T(8,128)(2,1)S(1)} %get-tuple-element.40), channel_id=1, source_target_pairs={{0,16},{1,17},{2,18},{3,19},{4,20},{5,21},{6,22},{7,23},{8,24},{9,... | collective-permute-start | bytes 1191944 | tf_op jit(solution)/shard_map/ppermute | solution.py:422
  79.2 13.6 %copy-start.4 = (s32[2,6]{1,0:T(2,128)S(1)}, s32[2,6]{1,0:T(2,128)}, u32[]{:S(2)}) copy-start(s32[2,6]{1,0:T(2,128)} %keep.3) | copy-start | bytes 148
  83.6 22.9 %collective-permute-start.9 = (s16[1552,128]{1,0:T(8,128)(2,1)S(1)}, s16[1552,128]{1,0:T(8,128)(2,1)S(1)}, u32[]{:S(2)}, u32[]{:S(2)}) collective-permute-start(s16[1552,128]{1,0:T(8,128)(2,1)S(1)} %get-tuple-element.37), channel_id=1, source_target_pairs={{0,16},{1,17},{2,18},{3,19},{4,20},{5,21},{6,22},{7,23},{8,24},{9,... | collective-permute-start | bytes 1191944 | tf_op jit(solution)/shard_map/ppermute | solution.py:422
  90.6 12.0 %collective-permute-start.10 = (bf16[96,2048]{1,0:T(8,128)(2,1)S(1)}, bf16[96,2048]{1,0:T(8,128)(2,1)S(1)}, u32[]{:S(2)}, u32[]{:S(2)}) collective-permute-start(bf16[96,2048]{1,0:T(8,128)(2,1)S(1)} %get-tuple-element.38), channel_id=1, source_target_pairs={{0,1},{1,0},{2,3},{3,2},{4,5},{5,4},{6,7},{7,6},{8,9},{9,8},{10,11... | collective-permute-start | bytes 1179656 | tf_op jit(solution)/shard_map/ppermute | solution.py:422
  92.2 10.4 %collective-permute-start.12 = (bf16[32,2048]{1,0:T(8,128)(2,1)S(1)}, bf16[32,2048]{1,0:T(8,128)(2,1)S(1)}, u32[]{:S(2)}, u32[]{:S(2)}) collective-permute-start(bf16[32,2048]{1,0:T(8,128)(2,1)S(1)} %handed_on.3), channel_id=1, source_target_pairs={{0,1},{1,0},{2,3},{3,2},{4,5},{5,4},{6,7},{7,6},{8,9},{9,8},{10,11... | collective-permute-start | bytes 393224 | tf_op jit(solution)/shard_map/ppermute | solution.py:422

commit v10 on v9

--- a/solution.py
+++ b/solution.py
@@ -95,25 +95,28 @@
     )(place, mask0, mask1, x0, x1, *after)
 
 
-def choose_kernel(gates, many, diag, *refs):
+def choose_kernel(gates, cuts, diag, *refs):
     one, other = refs[gates : gates + 2]
-    held, outs, sems = refs[gates + 2 : gates + 2 + many], refs[-many - 2 : -1], refs[-1]
-    others = [
-        pltpu.make_async_copy(x, out, sems.at[1 + i])
-        for i, (x, out) in enumerate(zip(held, outs[1:]))
-    ]
+    held = refs[gates + 2 : gates + 2 + len(cuts)]
+    send, joint, sems = refs[-3:]
+    others = []
+    top = 0
+    for i, (x, (lo, hi)) in enumerate(zip(held, cuts)):
+        target = joint.at[pl.ds(top, hi - lo)]
+        others.append(pltpu.make_async_copy(x.at[pl.ds(lo, hi - lo)], target, sems.at[1 + i]))
+        top += hi - lo
     for copy in others:
         copy.start()
 
     @pl.when(diag[0] == 1)
     def _():
-        copy = pltpu.make_async_copy(one, outs[0], sems.at[0])
+        copy = pltpu.make_async_copy(one, send, sems.at[0])
         copy.start()
         copy.wait()
 
     @pl.when(diag[0] == 0)
     def _():
-        copy = pltpu.make_async_copy(other, outs[0], sems.at[0])
+        copy = pltpu.make_async_copy(other, send, sems.at[0])
         copy.start()
         copy.wait()
 
@@ -121,18 +124,22 @@
         copy.wait()
 
 
-def chosen(diag, one, other, held=(), after=()):
-    outs = [jax.ShapeDtypeStruct(x.shape, x.dtype) for x in (one, *held)]
-    return pl.pallas_call(
-        functools.partial(choose_kernel, len(after), len(held)),
+def chosen(diag, one, other, held, after=()):
+    rows = sum(hi - lo for _, lo, hi in held)
+    outs = [
+        jax.ShapeDtypeStruct(one.shape, one.dtype),
+        jax.ShapeDtypeStruct((rows, one.shape[1]), one.dtype),
+    ]
+    return pl.pallas_call(
+        functools.partial(choose_kernel, len(after), [cut for _, *cut in held]),
         in_specs=[SM()] + [HB() for _ in (*after, one, other, *held)],
         out_specs=[HB() for _ in outs],
         out_shape=outs,
-        scratch_shapes=[pltpu.SemaphoreType.DMA((len(outs),))],
+        scratch_shapes=[pltpu.SemaphoreType.DMA((1 + len(held),))],
         compiler_params=params(),
         cost_estimate=cost(0, 4 * one.size),
         name="to_send",
-    )(diag, *after, one, other, *held)
+    )(diag, *after, one, other, *(x for x, _, _ in held))
 
 
 def hand_kernel(many, *refs):
@@ -337,15 +344,13 @@
     )(diag, right0, right1, *arrays, *(x for x, _, _ in given), *gates)
 
 
-def finish_kernel(start, cuts, keep, coded, square, tangent, *rest):
-    many = len(cuts)
+def finish_kernel(start, many, keep, coded, square, tangent, *rest):
     given, outs, passed = rest[:many], rest[-5 - many : -3 - many], rest[-3 - many : -3]
     made, out_sems, sems = rest[-3:]
     rows, columns = square.shape
     across = columns // BLOCK
     others = [
-        pltpu.make_async_copy(x.at[pl.ds(lo, hi - lo)], y, sems.at[i])
-        for i, (x, y, (lo, hi)) in enumerate(zip(given, passed, cuts))
+        pltpu.make_async_copy(x, y, sems.at[i]) for i, (x, y) in enumerate(zip(given, passed))
     ]
     results = [
         pltpu.make_async_copy(made.at[i], x.at[pl.ds(start, rows)], out_sems.at[i])
@@ -374,10 +379,10 @@
     rows, columns = square.shape
     out = jax.ShapeDtypeStruct((all_rows, columns), jnp.bfloat16)
     held, before = list(held), list(before)
-    passed = [jax.ShapeDtypeStruct((hi - lo, x.shape[1]), x.dtype) for x, lo, hi in held]
+    passed = [jax.ShapeDtypeStruct(x.shape, x.dtype) for x in held]
     many = len(held)
     return pl.pallas_call(
-        functools.partial(finish_kernel, start, [cut for _, *cut in held]),
+        functools.partial(finish_kernel, start, many),
         in_specs=[SM(), VM(), VM(), VM()] + [HB() for _ in (*held, *before, *after)],
         out_specs=[HB() for _ in range(2 + many)],
         out_shape=[out, out] + passed,
@@ -390,7 +395,7 @@
         compiler_params=params(),
         cost_estimate=cost(0, 16 * rows * columns),
         name="finish",
-    )(keep, coded, square, tangent, *(x for x, _, _ in held), *before, *after)
+    )(keep, coded, square, tangent, *held, *before, *after)
 
 
 def per_device_pair(
@@ -404,8 +409,8 @@
     half = row_index // group
     diag = (half == lax.axis_index("col")).astype(jnp.int32).reshape(1)
     place = (row_index % group).astype(jnp.int32).reshape(1)
-    direct = all_rows // 8
-    split = all_rows // 2
+    split = all_rows * 7 // 16
+    ahead = all_rows // 8
     wide = 256
 
     def device(h, q, c):
@@ -414,10 +419,6 @@
     spots = [(h, q, c) for h in range(2) for q in range(group) for c in range(2)]
     over_y = [(device(h, q, c), device(h, q, 1 - c)) for h, q, c in spots]
     over_z = [(device(h, q, c), device(1 - h, q, c)) for h, q, c in spots]
-    ring = [
-        (device(h, q, c), device(h, q, 1 - c) if h == c else device(1 - h, q, c))
-        for h, q, c in spots
-    ]
     def move(values, pairs):
         return lax.ppermute(values, ("row", "col"), pairs)
 
@@ -431,40 +432,33 @@
     def own(one, other):
         return local_products(diag, one, other, right0, right1, wide)
 
-    def parts(joint, a, b):
-        top, low = piece(joint, 0, direct), piece(joint, direct)
-        return (top, piece(a), low, piece(b))
-
-    joint, a1, b1 = chunks(((0, direct), (direct, split)), True, ALL_VMEM_BYTES)
+    a1, b1 = chunks(((0, split),), False, ALL_VMEM_BYTES)
     passed1 = move(b1, over_y)
-    near0 = move(joint, ring)
     a2, b2 = chunks(((split, all_rows),), False, VMEM_BYTES, (a1,))
     right0, right1 = masked_right(mask0_cols, mask1_cols, x0_cols, x1_cols, (a2,))
-    send, b2 = chosen(diag, passed1, a1, (b2,), (near0, right0))
+    send, b2 = chosen(diag, passed1, a1, (piece(b2),), (right0,))
     near1 = move(send, over_z)
     passed2 = move(b2, over_y)
-    far0 = move(near0, over_y)
-    send, a1 = chosen(diag, passed2, a2, (a1,), (far0,))
+    send, most = chosen(diag, passed2, a2, (piece(a1), piece(a2, 0, ahead)))
     near2 = move(send, over_z)
-    got1 = move(a1, over_y)
+    got1 = move(most, over_y)
     far1 = move(near1, over_y)
-    (coded,) = partials(parts(near0, near1, far1), parts(far0, far1, near1))
+    (coded,) = partials((piece(near1), piece(far1)), (piece(far1), piece(near1)))
     coded, near2 = handed_on((coded, near2), (got1,))
     back = move(coded, over_z)
     far2 = move(near2, over_y)
-    sums = own(parts(joint, a1, b1), parts(near0, got1, passed1))
-    late = a2.shape[0] * 3 // 4
-    coded, top2, low2 = partials(
+    sums = own((piece(a1), piece(b1)), (piece(got1, 0, split), piece(passed1)))
+    coded, rest = partials(
         (piece(near2), piece(far2)),
         (piece(far2), piece(near2)),
-        given=(piece(a2, 0, late), piece(a2, late)),
+        given=(piece(a2, ahead),),
         gates=sums[:1],
     )
-    (low2,) = handed_on((low2,), (back,))
+    (coded,) = handed_on((coded,), (back,))
     outs = finished(keep, *sums, back, (), 0, all_rows)
     back = move(coded, over_z)
-    got2 = (piece(move(top2, over_y)), piece(move(low2, over_y)))
-    sums = own((piece(a2), piece(b2)), (*got2, piece(passed2)))
+    got2 = move(rest, over_y)
+    sums = own((piece(a2), piece(b2)), (piece(got1, split), piece(got2), piece(passed2)))
     return tuple(finished(keep, *sums, back, outs, split, all_rows))
 
 

time: 109 us -> 108 us (level)
  the two profiles are of different devices: /device:TPU:10 before, /device:TPU:0 now
where the time goes in v10:
time: 108 us
  waiting for transfers between devices  58.7 us (54%)
  Pallas kernels  33.2 us (31%)
  starting transfers between devices  13.8 us (13%)
  local copies, waits for them, and re-layouts  1.22 us (1%)
    ppermute x10, waiting for transfers between devices, move(): return lax.ppermute(values, ('row', 'col'), pairs)  58.7 us
    ppermute x10, starting transfers between devices, move(): return lax.ppermute(values, ('row', 'col'), pairs)  13.8 us
    pallas_call x2, Pallas kernels, local_products(): pl.pallas_call(functools.partial(local_kernel, one, other), grid=(columns...  9 us
    pallas_call x2, Pallas kernels, partial_products(): pl.pallas_call(functools.partial(partial_kernel, one, other, len(arrays),...  8.96 us
    pallas_call x1, Pallas kernels, masked_right(): pl.pallas_call(right_kernel, grid=(depth // tall,), in_specs=[SM(), SM(),...  7.01 us
    pallas_call x2, Pallas kernels, masked_chunks(): pl.pallas_call(functools.partial(chunk_kernel, spans, int(stacked), panel...  3.84 us
    pallas_call x2, Pallas kernels, finished(): pl.pallas_call(functools.partial(finish_kernel, start, many), in_specs=[S...  2.84 us
  transfers between devices with their start and end apart: 10, of which 7 were waited for; matrix products, arithmetic and copies ran while one was open for 0% of the time, Pallas kernels for 27%

profile of v10, /device:TPU:0, one launch (start us, length us, event | category | flops | bytes accessed | tf_op | source)
XLA Modules:
  0.0 107.8 jit_solution(11146881105237985663)
XLA Ops:
  0.7 2.3 %left_chunks.2 = (bf16[112,2048]{1,0:T(8,128)(2,1)}, bf16[112,2048]{1,0:T(8,128)(2,1)}) custom-call(s32[1]{0:T(128)} %bitcast.1.refs_0_, s32[2,128]{1,0:T(2,128)} %refs_1_.3, s32[2,128]{1,0:T(2,128)} %refs_2_.3, bf16[256,16384]{1,0:T(8,128)(2,1)} %refs_3_.3, bf16[256,16384]{1,0:T(8,128)(2,1)} %refs_4_.3), custom_call_target="tpu_custom_call" | custom-call | bytes 28672 | tf_op jit(solution)/shard_map/left_chunks/pallas_call | solution.py:80
  3.0 3.0 %collective-permute-start = (bf16[112,2048]{1,0:T(8,128)(2,1)}, bf16[112,2048]{1,0:T(8,128)(2,1)S(1)}, u32[]{:S(2)}, u32[]{:S(2)}) collective-permute-start(bf16[112,2048]{1,0:T(8,128)(2,1)} %get-tuple-element.26.refs_1_), channel_id=1, source_target_pairs={{0,1},{1,0},{2,3},{3,2},{4,5},{5,4},{6,7},{7,6},{8,9},{9,8},{10,11... | collective-permute-start | bytes 1376264 | tf_op jit(solution)/shard_map/ppermute | solution.py:423
  6.2 1.0 copy-done.1
  7.2 1.6 %left_chunks.3 = (bf16[144,2048]{1,0:T(8,128)(2,1)S(1)}, bf16[144,2048]{1,0:T(8,128)(2,1)S(1)}) custom-call(s32[1]{0:T(128)} %bitcast.1.refs_0_, s32[2,128]{1,0:T(2,128)S(1)} %copy-done.5, s32[2,128]{1,0:T(2,128)S(1)} %copy-done.6, bf16[256,16384]{1,0:T(8,128)(2,1)} %refs_3_.3, bf16[256,16384]{1,0:T(8,128)(2,1)} %refs_4_.3, bf16[112,2048]{1,0:T(8,128)(2,1)S(1)} %copy-done.1), custom_call_target="tpu_custom_call" | custom-call | bytes 36864 | tf_op jit(solution)/shard_map/left_chunks/pallas_call | solution.py:80
  8.8 7.0 %right_panels.1 = (bf16[2048,768]{1,0:T(8,128)(2,1)S(1)}, bf16[2048,768]{1,0:T(8,128)(2,1)}) custom-call(s32[16,6]{1,0:T(8,128)S(1)} %copy.13.mask0, s32[16,6]{1,0:T(8,128)S(1)} %copy.14.mask1, bf16[2048,768]{1,0:T(8,128)(2,1)} %x0.1, bf16[2048,768]{1,0:T(8,128)(2,1)} %x1.1, bf16[144,2048]{1,0:T(8,128)(2,1)S(1)} %get-tuple-element.23.rest_0_.refs_1_.refs_3_.refs_2_.refs_0_), custom_call_target="tpu_custom_call" | custom-call | bytes 196608 | tf_op jit(solution)/shard_map/right_panels/pallas_call | solution.py:186
  15.8 0.9 collective-permute-done.refs_1_.refs_3_
  17.1 1.8 %collective-permute-start.3 = (bf16[144,2048]{1,0:T(8,128)(2,1)S(1)}, bf16[144,2048]{1,0:T(8,128)(2,1)S(1)}, u32[]{:S(2)}, u32[]{:S(2)}) collective-permute-start(bf16[144,2048]{1,0:T(8,128)(2,1)S(1)} %get-tuple-element.29.refs_1_), channel_id=1, source_target_pairs={{0,1},{1,0},{2,3},{3,2},{4,5},{5,4},{6,7},{7,6},{8,9},{9,8},{10,11... | collective-permute-start | bytes 1769480 | tf_op jit(solution)/shard_map/ppermute | solution.py:423
  19.0 2.6 %collective-permute-start.1 = (bf16[112,2048]{1,0:T(8,128)(2,1)S(1)}, bf16[112,2048]{1,0:T(8,128)(2,1)S(1)}, u32[]{:S(2)}, u32[]{:S(2)}) collective-permute-start(bf16[112,2048]{1,0:T(8,128)(2,1)S(1)} %get-tuple-element.28), channel_id=1, source_target_pairs={{0,16},{1,17},{2,18},{3,19},{4,20},{5,21},{6,22},{7,23},{8,24},{9,... | collective-permute-start | bytes 1376264 | tf_op jit(solution)/shard_map/ppermute | solution.py:423
  21.5 10.2 %collective-permute-done.3.refs_0_.refs_4_ = bf16[144,2048]{1,0:T(8,128)(2,1)S(1)} collective-permute-done((bf16[144,2048]{1,0:T(8,128)(2,1)S(1)}, bf16[144,2048]{1,0:T(8,128)(2,1)S(1)}, u32[]{:S(2)}, u32[]{:S(2)}) %collective-permute-start.3) | collective-permute-done | bytes 589856 | tf_op jit(solution)/shard_map/ppermute | solution.py:423
  32.3 2.6 %collective-permute-start.4 = (bf16[144,2048]{1,0:T(8,128)(2,1)S(1)}, bf16[144,2048]{1,0:T(8,128)(2,1)S(1)}, u32[]{:S(2)}, u32[]{:S(2)}) collective-permute-start(bf16[144,2048]{1,0:T(8,128)(2,1)S(1)} %get-tuple-element.30), channel_id=1, source_target_pairs={{0,16},{1,17},{2,18},{3,19},{4,20},{5,21},{6,22},{7,23},{8,24},{9,... | collective-permute-start | bytes 1769480 | tf_op jit(solution)/shard_map/ppermute | solution.py:423
  34.9 1.5 %collective-permute-start.5 = (bf16[144,2048]{1,0:T(8,128)(2,1)S(1)}, bf16[144,2048]{1,0:T(8,128)(2,1)S(1)}, u32[]{:S(2)}, u32[]{:S(2)}) collective-permute-start(bf16[144,2048]{1,0:T(8,128)(2,1)S(1)} %get-tuple-element.31), channel_id=1, source_target_pairs={{0,1},{1,0},{2,3},{3,2},{4,5},{5,4},{6,7},{7,6},{8,9},{9,8},{10,11... | collective-permute-start | bytes 1769480 | tf_op jit(solution)/shard_map/ppermute | solution.py:423
  36.4 18.2 %collective-permute-done.1.refs_0_ = bf16[112,2048]{1,0:T(8,128)(2,1)S(1)} collective-permute-done((bf16[112,2048]{1,0:T(8,128)(2,1)S(1)}, bf16[112,2048]{1,0:T(8,128)(2,1)S(1)}, u32[]{:S(2)}, u32[]{:S(2)}) %collective-permute-start.1) | collective-permute-done | bytes 458784 | tf_op jit(solution)/shard_map/ppermute | solution.py:423
  55.1 9.7 %collective-permute-done.2.refs_1_ = bf16[112,2048]{1,0:T(8,128)(2,1)S(1)} collective-permute-done((bf16[112,2048]{1,0:T(8,128)(2,1)S(1)}, bf16[112,2048]{1,0:T(8,128)(2,1)S(1)}, u32[]{:S(2)}, u32[]{:S(2)}) %collective-permute-start.2) | collective-permute-done | bytes 458784 | tf_op jit(solution)/shard_map/ppermute | solution.py:423
  64.8 4.4 %partial_products.2.refs_0_ = s16[1360,128]{1,0:T(8,128)(2,1)S(1)} custom-call(s32[1]{0:T(128)} %bitcast.diag, bf16[2048,768]{1,0:T(8,128)(2,1)S(1)} %get-tuple-element.24.refs_0_.right0, bf16[2048,768]{1,0:T(8,128)(2,1)} %get-tuple-element.25.right1, bf16[112,2048]{1,0:T(8,128)(2,1)S(1)} %collective-permute-done.1.refs_0_, ...), custom_call_target="tpu_custom_call" | custom-call | flops 16515072 | bytes 112640 | tf_op jit(solution)/shard_map/partial_products/pallas_call | solution.py:322
  69.5 0.8 collective-permute-start.6
  70.3 4.3 %own_products.2 = (f32[112,768]{1,0:T(8,128)S(1)}, f32[112,768]{1,0:T(8,128)S(1)}) custom-call(s32[1]{0:T(128)} %bitcast.diag, bf16[2048,768]{1,0:T(8,128)(2,1)S(1)} %get-tuple-element.24.refs_0_.right0, bf16[2048,768]{1,0:T(8,128)(2,1)} %get-tuple-element.25.right1, bf16[112,2048]{1,0:T(8,128)(2,1)S(1)} %copy-done.2, bf16[112,2048]{1,0:T(8,128)(2,1)S(1)} %copy-done.3, ...), custom_call_target="tpu_custom_call" | custom-call | flops 16515072 | bytes 126976 | tf_op jit(solution)/shard_map/own_products/pallas_call | solution.py:257
  74.6 7.1 %collective-permute-done.6.refs_1_ = bf16[144,2048]{1,0:T(8,128)(2,1)S(1)} collective-permute-done((bf16[144,2048]{1,0:T(8,128)(2,1)S(1)}, bf16[144,2048]{1,0:T(8,128)(2,1)S(1)}, u32[]{:S(2)}, u32[]{:S(2)}) %collective-permute-start.6) | collective-permute-done | bytes 589856 | tf_op jit(solution)/shard_map/ppermute | solution.py:423
  81.7 4.5 %partial_products.3 = (s16[1744,128]{1,0:T(8,128)(2,1)S(1)}, bf16[112,2048]{1,0:T(8,128)(2,1)S(1)}) custom-call(s32[1]{0:T(128)} %bitcast.diag, bf16[2048,768]{1,0:T(8,128)(2,1)S(1)} %get-tuple-element.24.refs_0_.right0, bf16[2048,768]{1,0:T(8,128)(2,1)} %get-tuple-element.25.right1, bf16[144,2048]{1,0:T(8,128)(2,1)S(1)} %get-tuple-element.32.refs_0_, ...), custom_call_target="tpu_custom_call" | custom-call | flops 21233664 | bytes 116736 | tf_op jit(solution)/shard_map/partial_products/pallas_call | solution.py:322
  86.2 1.0 collective-permute-start.9
  87.5 1.4 %finish.2 = (bf16[256,768]{1,0:T(8,128)(2,1)}, bf16[256,768]{1,0:T(8,128)(2,1)}) custom-call(s32[2,6]{1,0:T(2,128)S(1)} %copy-done.4, s16[1360,128]{1,0:T(8,128)(2,1)S(1)} %collective-permute-done.7.refs_1_.coded, f32[112,768]{1,0:T(8,128)S(1)} %get-tuple-element.33.refs_3_.square, f32[112,768]{1,0:T(8,128)S(1)} %get-tuple-element.39.tangent), custom_call_target="tpu_custom_call" | custom-call | bytes 21504 | tf_op jit(solution)/shard_map/finish/pallas_call | solution.py:384
  88.9 5.8 %collective-permute-done.9.refs_3_ = bf16[112,2048]{1,0:T(8,128)(2,1)S(1)} collective-permute-done((bf16[112,2048]{1,0:T(8,128)(2,1)S(1)}, bf16[112,2048]{1,0:T(8,128)(2,1)S(1)}, u32[]{:S(2)}, u32[]{:S(2)}) %collective-permute-start.9) | collective-permute-done | bytes 458784 | tf_op jit(solution)/shard_map/ppermute | solution.py:423
  94.8 4.7 %own_products.3 = (f32[144,768]{1,0:T(8,128)S(1)}, f32[144,768]{1,0:T(8,128)S(1)}) custom-call(s32[1]{0:T(128)} %bitcast.diag, bf16[2048,768]{1,0:T(8,128)(2,1)} %copy-done, bf16[2048,768]{1,0:T(8,128)(2,1)} %get-tuple-element.25.right1, bf16[144,2048]{1,0:T(8,128)(2,1)S(1)} %get-tuple-element.23.rest_0_.refs_1_.refs_3_.refs_2_.refs_0_, ...), custom_call_target="tpu_custom_call" | custom-call | flops 21233664 | bytes 135168 | tf_op jit(solution)/shard_map/own_products/pallas_call | solution.py:257
  99.5 6.8 %collective-permute-done.8.coded = s16[1744,128]{1,0:T(8,128)(2,1)S(1)} collective-permute-done((s16[1744,128]{1,0:T(8,128)(2,1)S(1)}, s16[1744,128]{1,0:T(8,128)(2,1)S(1)}, u32[]{:S(2)}, u32[]{:S(2)}) %collective-permute-start.8) | collective-permute-done | bytes 446496 | tf_op jit(solution)/shard_map/ppermute | solution.py:423
  106.3 1.4 %finish.3 = (bf16[256,768]{1,0:T(8,128)(2,1)}, bf16[256,768]{1,0:T(8,128)(2,1)}) custom-call(s32[2,6]{1,0:T(2,128)S(1)} %copy-done.4, s16[1744,128]{1,0:T(8,128)(2,1)S(1)} %collective-permute-done.8.coded, f32[144,768]{1,0:T(8,128)S(1)} %get-tuple-element.37.square, ...), custom_call_target="tpu_custom_call", output_to_operand_aliasing={{0}: (4, {}), {1}: (5, {})} | custom-call | bytes 27648 | tf_op jit(solution)/shard_map/finish/pallas_call | solution.py:384
  (29 shorter events, 2.3 us)
Async XLA Ops:
  0.6 5.3 %copy-start.7 = (s32[16,6]{0,1:T(8,128)S(1)}, s32[16,6]{0,1:T(8,128)}, u32[]{:S(2)}) copy-start(s32[16,6]{0,1:T(8,128)} %param.15) | copy-start | bytes 1156
  0.7 5.4 %copy-start.8 = (s32[16,6]{0,1:T(8,128)S(1)}, s32[16,6]{0,1:T(8,128)}, u32[]{:S(2)}) copy-start(s32[16,6]{0,1:T(8,128)} %param.16) | copy-start | bytes 1156
  0.7 5.5 %copy-start.5 = (s32[2,128]{1,0:T(2,128)S(1)}, s32[2,128]{1,0:T(2,128)}, u32[]{:S(2)}) copy-start(s32[2,128]{1,0:T(2,128)} %refs_1_.3) | copy-start | bytes 3076
  0.7 5.5 %copy-start.6 = (s32[2,128]{1,0:T(2,128)S(1)}, s32[2,128]{1,0:T(2,128)}, u32[]{:S(2)}) copy-start(s32[2,128]{1,0:T(2,128)} %refs_2_.3) | copy-start | bytes 3076
  3.0 13.8 %collective-permute-start = (bf16[112,2048]{1,0:T(8,128)(2,1)}, bf16[112,2048]{1,0:T(8,128)(2,1)S(1)}, u32[]{:S(2)}, u32[]{:S(2)}) collective-permute-start(bf16[112,2048]{1,0:T(8,128)(2,1)} %get-tuple-element.26.refs_1_), channel_id=1, source_target_pairs={{0,1},{1,0},{2,3},{3,2},{4,5},{5,4},{6,7},{7,6},{8,9},{9,8},{10,11... | collective-permute-start | bytes 1376264 | tf_op jit(solution)/shard_map/ppermute | solution.py:423
  6.2 1.0 copy-start.1
  8.8 7.9 %copy-start.2 = (bf16[112,2048]{1,0:T(8,128)(2,1)S(1)}, bf16[112,2048]{1,0:T(8,128)(2,1)}, u32[]{:S(2)}) copy-start(bf16[112,2048]{1,0:T(8,128)(2,1)} %get-tuple-element.22.refs_5_.refs_2_.refs_0_) | copy-start | bytes 1376260
  15.8 65.9 %copy-start = (bf16[2048,768]{1,0:T(8,128)(2,1)}, bf16[2048,768]{1,0:T(8,128)(2,1)S(1)}, u32[]{:S(2)}) copy-start(bf16[2048,768]{1,0:T(8,128)(2,1)S(1)} %get-tuple-element.24.refs_0_.right0) | copy-start | bytes 9437188
  17.1 14.6 %collective-permute-start.3 = (bf16[144,2048]{1,0:T(8,128)(2,1)S(1)}, bf16[144,2048]{1,0:T(8,128)(2,1)S(1)}, u32[]{:S(2)}, u32[]{:S(2)}) collective-permute-start(bf16[144,2048]{1,0:T(8,128)(2,1)S(1)} %get-tuple-element.29.refs_1_), channel_id=1, source_target_pairs={{0,1},{1,0},{2,3},{3,2},{4,5},{5,4},{6,7},{7,6},{8,9},{9,8},{10,11... | collective-permute-start | bytes 1769480 | tf_op jit(solution)/shard_map/ppermute | solution.py:423
  19.0 35.7 %collective-permute-start.1 = (bf16[112,2048]{1,0:T(8,128)(2,1)S(1)}, bf16[112,2048]{1,0:T(8,128)(2,1)S(1)}, u32[]{:S(2)}, u32[]{:S(2)}) collective-permute-start(bf16[112,2048]{1,0:T(8,128)(2,1)S(1)} %get-tuple-element.28), channel_id=1, source_target_pairs={{0,16},{1,17},{2,18},{3,19},{4,20},{5,21},{6,22},{7,23},{8,24},{9,... | collective-permute-start | bytes 1376264 | tf_op jit(solution)/shard_map/ppermute | solution.py:423
  32.3 36.9 %collective-permute-start.4 = (bf16[144,2048]{1,0:T(8,128)(2,1)S(1)}, bf16[144,2048]{1,0:T(8,128)(2,1)S(1)}, u32[]{:S(2)}, u32[]{:S(2)}) collective-permute-start(bf16[144,2048]{1,0:T(8,128)(2,1)S(1)} %get-tuple-element.30), channel_id=1, source_target_pairs={{0,16},{1,17},{2,18},{3,19},{4,20},{5,21},{6,22},{7,23},{8,24},{9,... | collective-permute-start | bytes 1769480 | tf_op jit(solution)/shard_map/ppermute | solution.py:423
  34.9 34.3 %collective-permute-start.5 = (bf16[144,2048]{1,0:T(8,128)(2,1)S(1)}, bf16[144,2048]{1,0:T(8,128)(2,1)S(1)}, u32[]{:S(2)}, u32[]{:S(2)}) collective-permute-start(bf16[144,2048]{1,0:T(8,128)(2,1)S(1)} %get-tuple-element.31), channel_id=1, source_target_pairs={{0,1},{1,0},{2,3},{3,2},{4,5},{5,4},{6,7},{7,6},{8,9},{9,8},{10,11... | collective-permute-start | bytes 1769480 | tf_op jit(solution)/shard_map/ppermute | solution.py:423
  54.6 10.2 %collective-permute-start.2 = (bf16[112,2048]{1,0:T(8,128)(2,1)S(1)}, bf16[112,2048]{1,0:T(8,128)(2,1)S(1)}, u32[]{:S(2)}, u32[]{:S(2)}) collective-permute-start(bf16[112,2048]{1,0:T(8,128)(2,1)S(1)} %collective-permute-done.1.refs_0_), channel_id=1, source_target_pairs={{0,1},{1,0},{2,3},{3,2},{4,5},{5,4},{6,7},{7,6},{8,9},{9,8},{10,11... | collective-permute-start | bytes 1376264 | tf_op jit(solution)/shard_map/ppermute | solution.py:423
  64.8 5.5 %copy-start.3 = (bf16[112,2048]{1,0:T(8,128)(2,1)S(1)}, bf16[112,2048]{1,0:T(8,128)(2,1)}, u32[]{:S(2)}) copy-start(bf16[112,2048]{1,0:T(8,128)(2,1)} %get-tuple-element.26.refs_1_) | copy-start | bytes 1376260
  69.5 12.1 %collective-permute-start.6 = (bf16[144,2048]{1,0:T(8,128)(2,1)S(1)}, bf16[144,2048]{1,0:T(8,128)(2,1)S(1)}, u32[]{:S(2)}, u32[]{:S(2)}) collective-permute-start(bf16[144,2048]{1,0:T(8,128)(2,1)S(1)} %get-tuple-element.32.refs_0_), channel_id=1, source_target_pairs={{0,1},{1,0},{2,3},{3,2},{4,5},{5,4},{6,7},{7,6},{8,9},{9,8},{10,11... | collective-permute-start | bytes 1769480 | tf_op jit(solution)/shard_map/ppermute | solution.py:423
  70.3 16.9 %collective-permute-start.7 = (s16[1360,128]{1,0:T(8,128)(2,1)S(1)}, s16[1360,128]{1,0:T(8,128)(2,1)S(1)}, u32[]{:S(2)}, u32[]{:S(2)}) collective-permute-start(s16[1360,128]{1,0:T(8,128)(2,1)S(1)} %get-tuple-element.35), channel_id=1, source_target_pairs={{0,16},{1,17},{2,18},{3,19},{4,20},{5,21},{6,22},{7,23},{8,24},{9,... | collective-permute-start | bytes 1044488 | tf_op jit(solution)/shard_map/ppermute | solution.py:423
  81.7 5.9 %copy-start.4 = (s32[2,6]{1,0:T(2,128)S(1)}, s32[2,6]{1,0:T(2,128)}, u32[]{:S(2)}) copy-start(s32[2,6]{1,0:T(2,128)} %keep.3) | copy-start | bytes 148
  86.2 8.5 %collective-permute-start.9 = (bf16[112,2048]{1,0:T(8,128)(2,1)S(1)}, bf16[112,2048]{1,0:T(8,128)(2,1)S(1)}, u32[]{:S(2)}, u32[]{:S(2)}) collective-permute-start(bf16[112,2048]{1,0:T(8,128)(2,1)S(1)} %get-tuple-element.36), channel_id=1, source_target_pairs={{0,1},{1,0},{2,3},{3,2},{4,5},{5,4},{6,7},{7,6},{8,9},{9,8},{10,11... | collective-permute-start | bytes 1376264 | tf_op jit(solution)/shard_map/ppermute | solution.py:423
  87.4 18.9 %collective-permute-start.8 = (s16[1744,128]{1,0:T(8,128)(2,1)S(1)}, s16[1744,128]{1,0:T(8,128)(2,1)S(1)}, u32[]{:S(2)}, u32[]{:S(2)}) collective-permute-start(s16[1744,128]{1,0:T(8,128)(2,1)S(1)} %handed_on.3), channel_id=1, source_target_pairs={{0,16},{1,17},{2,18},{3,19},{4,20},{5,21},{6,22},{7,23},{8,24},{9,... | collective-permute-start | bytes 1339400 | tf_op jit(solution)/shard_map/ppermute | solution.py:423

commit v11 on v9

--- a/solution.py
+++ b/solution.py
@@ -404,7 +404,7 @@
     half = row_index // group
     diag = (half == lax.axis_index("col")).astype(jnp.int32).reshape(1)
     place = (row_index % group).astype(jnp.int32).reshape(1)
-    direct = all_rows // 8
+    direct = all_rows // 16
     split = all_rows // 2
     wide = 256
 
@@ -418,6 +418,8 @@
         (device(h, q, c), device(h, q, 1 - c) if h == c else device(1 - h, q, c))
         for h, q, c in spots
     ]
+    in_chip = [(device(h, q, c), device(h, q ^ 1, c)) for h, q, c in spots]
+
     def move(values, pairs):
         return lax.ppermute(values, ("row", "col"), pairs)
 
@@ -453,19 +455,19 @@
     back = move(coded, over_z)
     far2 = move(near2, over_y)
     sums = own(parts(joint, a1, b1), parts(near0, got1, passed1))
-    late = a2.shape[0] * 3 // 4
-    coded, top2, low2 = partials(
+    coded, rest, mark = partials(
         (piece(near2), piece(far2)),
         (piece(far2), piece(near2)),
-        given=(piece(a2, 0, late), piece(a2, late)),
+        given=(piece(a2), piece(near1, 0, all_rows // 4)),
         gates=sums[:1],
     )
-    (low2,) = handed_on((low2,), (back,))
+    (mark,) = handed_on((mark,), (back,))
+    mark = move(mark, in_chip)
     outs = finished(keep, *sums, back, (), 0, all_rows)
     back = move(coded, over_z)
-    got2 = (piece(move(top2, over_y)), piece(move(low2, over_y)))
-    sums = own((piece(a2), piece(b2)), (*got2, piece(passed2)))
-    return tuple(finished(keep, *sums, back, outs, split, all_rows))
+    got2 = move(rest, over_y)
+    sums = own((piece(a2), piece(b2)), (piece(got2), piece(passed2)))
+    return tuple(finished(keep, *sums, back, outs, split, all_rows, after=(mark,)))
 
 
 def passed_along(shard, axis, by):

time: 109 us -> 113 us (1.037)
  the two profiles are of different devices: /device:TPU:10 before, /device:TPU:0 now
where the time goes in v11:
time: 113 us; the launch traced here: 112 us
  waiting for transfers between devices  63.2 us (56%)
  Pallas kernels  32.5 us (29%)
  starting transfers between devices  14.7 us (13%)
  local copies, waits for them, and re-layouts  1.22 us (1%)
    ppermute x13, waiting for transfers between devices, move(): return lax.ppermute(values, ('row', 'col'), pairs)  63.2 us
    ppermute x13, starting transfers between devices, move(): return lax.ppermute(values, ('row', 'col'), pairs)  14.7 us
    pallas_call x2, Pallas kernels, partial_products(): pl.pallas_call(functools.partial(partial_kernel, one, other, len(arrays),...  9.42 us
    pallas_call x2, Pallas kernels, local_products(): pl.pallas_call(functools.partial(local_kernel, one, other), grid=(columns...  8.41 us
    pallas_call x1, Pallas kernels, masked_right(): pl.pallas_call(right_kernel, grid=(depth // tall,), in_specs=[SM(), SM(),...  6.97 us
    pallas_call x2, Pallas kernels, masked_chunks(): pl.pallas_call(functools.partial(chunk_kernel, spans, int(stacked), panel...  3.9 us
    pallas_call x2, Pallas kernels, finished(): pl.pallas_call(functools.partial(finish_kernel, start, [cut for _, *cut i...  2.83 us
  transfers between devices with their start and end apart: 13, of which 9 were waited for; matrix products, arithmetic and copies ran while one was open for 0% of the time, Pallas kernels for 25%

profile of v11, /device:TPU:0, one launch (start us, length us, event | category | flops | bytes accessed | tf_op | source)
XLA Modules:
  0.0 112.3 jit_solution(13970621561327194879)
XLA Ops:
  0.7 2.4 %left_chunks.2 = (bf16[32,2048]{1,0:T(8,128)(2,1)}, bf16[112,2048]{1,0:T(8,128)(2,1)}, bf16[112,2048]{1,0:T(8,128)(2,1)}) custom-call(s32[1]{0:T(128)} %bitcast.1.refs_0_, s32[2,128]{1,0:T(2,128)} %refs_1_.3, s32[2,128]{1,0:T(2,128)} %refs_2_.3, bf16[256,16384]{1,0:T(8,128)(2,1)} %refs_3_.3, bf16[256,16384]{1,0:T(8,128)(2,1)} %refs_4_.3), custom_call_target="tpu_custom_call" | custom-call | bytes 32768 | tf_op jit(solution)/shard_map/left_chunks/pallas_call | solution.py:80
  3.0 3.0 %collective-permute-start.1 = (bf16[112,2048]{1,0:T(8,128)(2,1)}, bf16[112,2048]{1,0:T(8,128)(2,1)S(1)}, u32[]{:S(2)}, u32[]{:S(2)}) collective-permute-start(bf16[112,2048]{1,0:T(8,128)(2,1)} %get-tuple-element.29.refs_2_), channel_id=1, source_target_pairs={{0,1},{1,0},{2,3},{3,2},{4,5},{5,4},{6,7},{7,6},{8,9},{9,8},{10,11... | collective-permute-start | bytes 1376264 | tf_op jit(solution)/shard_map/ppermute | solution.py:424
  7.2 1.5 %left_chunks.3 = (bf16[128,2048]{1,0:T(8,128)(2,1)S(1)}, bf16[128,2048]{1,0:T(8,128)(2,1)S(1)}) custom-call(s32[1]{0:T(128)} %bitcast.1.refs_0_, s32[2,128]{1,0:T(2,128)S(1)} %copy-done.7, s32[2,128]{1,0:T(2,128)S(1)} %copy-done.8, bf16[256,16384]{1,0:T(8,128)(2,1)} %refs_3_.3, bf16[256,16384]{1,0:T(8,128)(2,1)} %refs_4_.3, bf16[112,2048]{1,0:T(8,128)(2,1)S(1)} %copy-done.2), custom_call_target="tpu_custom_call" | custom-call | bytes 32768 | tf_op jit(solution)/shard_map/left_chunks/pallas_call | solution.py:80
  8.9 7.0 %right_panels.1 = (bf16[2048,768]{1,0:T(8,128)(2,1)S(1)}, bf16[2048,768]{1,0:T(8,128)(2,1)}) custom-call(s32[16,6]{1,0:T(8,128)S(1)} %copy.13.mask0, s32[16,6]{1,0:T(8,128)S(1)} %copy.14.mask1, bf16[2048,768]{1,0:T(8,128)(2,1)} %x0.1, bf16[2048,768]{1,0:T(8,128)(2,1)} %x1.1, bf16[128,2048]{1,0:T(8,128)(2,1)S(1)} %get-tuple-element.25.rest_0_.refs_2_.refs_0_), custom_call_target="tpu_custom_call" | custom-call | bytes 196608 | tf_op jit(solution)/shard_map/right_panels/pallas_call | solution.py:179
  15.9 3.1 %collective-permute-done.refs_0_.refs_3_ = bf16[32,2048]{1,0:T(8,128)(2,1)S(1)} collective-permute-done((bf16[32,2048]{1,0:T(8,128)(2,1)}, bf16[32,2048]{1,0:T(8,128)(2,1)S(1)}, u32[]{:S(2)}, u32[]{:S(2)}) %collective-permute-start) | collective-permute-done | bytes 131104 | tf_op jit(solution)/shard_map/ppermute | solution.py:424
  19.3 2.4 %collective-permute-start.5 = (bf16[128,2048]{1,0:T(8,128)(2,1)S(1)}, bf16[128,2048]{1,0:T(8,128)(2,1)S(1)}, u32[]{:S(2)}, u32[]{:S(2)}) collective-permute-start(bf16[128,2048]{1,0:T(8,128)(2,1)S(1)} %get-tuple-element.32.refs_1_), channel_id=1, source_target_pairs={{0,1},{1,0},{2,3},{3,2},{4,5},{5,4},{6,7},{7,6},{8,9},{9,8},{10,11... | collective-permute-start | bytes 1572872 | tf_op jit(solution)/shard_map/ppermute | solution.py:424
  21.8 1.1 %collective-permute-start.2 = (bf16[112,2048]{1,0:T(8,128)(2,1)S(1)}, bf16[112,2048]{1,0:T(8,128)(2,1)S(1)}, u32[]{:S(2)}, u32[]{:S(2)}) collective-permute-start(bf16[112,2048]{1,0:T(8,128)(2,1)S(1)} %get-tuple-element.31), channel_id=1, source_target_pairs={{0,16},{1,17},{2,18},{3,19},{4,20},{5,21},{6,22},{7,23},{8,24},{9,... | collective-permute-start | bytes 1376264 | tf_op jit(solution)/shard_map/ppermute | solution.py:424
  22.9 1.9 %collective-permute-start.4 = (bf16[32,2048]{1,0:T(8,128)(2,1)S(1)}, bf16[32,2048]{1,0:T(8,128)(2,1)S(1)}, u32[]{:S(2)}, u32[]{:S(2)}) collective-permute-start(bf16[32,2048]{1,0:T(8,128)(2,1)S(1)} %collective-permute-done.refs_0_.refs_3_), channel_id=1, source_target_pairs={{0,1},{1,0},{2,3},{3,2},{4,5},{5,4},{6,7},{7,6},{8,9},{9,8},{10,11... | collective-permute-start | bytes 393224 | tf_op jit(solution)/shard_map/ppermute | solution.py:424
  24.9 10.8 %collective-permute-done.4.refs_3_.refs_0_ = bf16[32,2048]{1,0:T(8,128)(2,1)S(1)} collective-permute-done((bf16[32,2048]{1,0:T(8,128)(2,1)S(1)}, bf16[32,2048]{1,0:T(8,128)(2,1)S(1)}, u32[]{:S(2)}, u32[]{:S(2)}) %collective-permute-start.4) | collective-permute-done | bytes 131104 | tf_op jit(solution)/shard_map/ppermute | solution.py:424
  36.0 2.9 %collective-permute-start.6 = (bf16[128,2048]{1,0:T(8,128)(2,1)S(1)}, bf16[128,2048]{1,0:T(8,128)(2,1)S(1)}, u32[]{:S(2)}, u32[]{:S(2)}) collective-permute-start(bf16[128,2048]{1,0:T(8,128)(2,1)S(1)} %get-tuple-element.33), channel_id=1, source_target_pairs={{0,16},{1,17},{2,18},{3,19},{4,20},{5,21},{6,22},{7,23},{8,24},{9,... | collective-permute-start | bytes 1572872 | tf_op jit(solution)/shard_map/ppermute | solution.py:424
  38.8 17.2 %collective-permute-done.2.refs_1_.refs_3_ = bf16[112,2048]{1,0:T(8,128)(2,1)S(1)} collective-permute-done((bf16[112,2048]{1,0:T(8,128)(2,1)S(1)}, bf16[112,2048]{1,0:T(8,128)(2,1)S(1)}, u32[]{:S(2)}, u32[]{:S(2)}) %collective-permute-start.2) | collective-permute-done | bytes 458784 | tf_op jit(solution)/shard_map/ppermute | solution.py:424
  56.5 1.6 %collective-permute-start.7 = (bf16[112,2048]{1,0:T(8,128)(2,1)S(1)}, bf16[112,2048]{1,0:T(8,128)(2,1)S(1)}, u32[]{:S(2)}, u32[]{:S(2)}) collective-permute-start(bf16[112,2048]{1,0:T(8,128)(2,1)S(1)} %get-tuple-element.34.refs_1_), channel_id=1, source_target_pairs={{0,1},{1,0},{2,3},{3,2},{4,5},{5,4},{6,7},{7,6},{8,9},{9,8},{10,11... | collective-permute-start | bytes 1376264 | tf_op jit(solution)/shard_map/ppermute | solution.py:424
  58.0 11.4 %collective-permute-done.3.refs_2_ = bf16[112,2048]{1,0:T(8,128)(2,1)S(1)} collective-permute-done((bf16[112,2048]{1,0:T(8,128)(2,1)S(1)}, bf16[112,2048]{1,0:T(8,128)(2,1)S(1)}, u32[]{:S(2)}, u32[]{:S(2)}) %collective-permute-start.3) | collective-permute-done | bytes 458784 | tf_op jit(solution)/shard_map/ppermute | solution.py:424
  69.5 4.7 %partial_products.2.refs_0_ = s16[1552,128]{1,0:T(8,128)(2,1)S(1)} custom-call(s32[1]{0:T(128)} %bitcast.diag, bf16[2048,768]{1,0:T(8,128)(2,1)S(1)} %get-tuple-element.26.refs_1_.right0, bf16[2048,768]{1,0:T(8,128)(2,1)} %get-tuple-element.27.right1, bf16[32,2048]{1,0:T(8,128)(2,1)S(1)} %collective-permute-done.refs_0_.refs_3_, ...), custom_call_target="tpu_custom_call" | custom-call | flops 18874368 | bytes 114688 | tf_op jit(solution)/shard_map/partial_products/pallas_call | solution.py:315
  74.1 2.1 %collective-permute-done.7.refs_2_.refs_4_ = bf16[112,2048]{1,0:T(8,128)(2,1)S(1)} collective-permute-done((bf16[112,2048]{1,0:T(8,128)(2,1)S(1)}, bf16[112,2048]{1,0:T(8,128)(2,1)S(1)}, u32[]{:S(2)}, u32[]{:S(2)}) %collective-permute-start.7) | collective-permute-done | bytes 458784 | tf_op jit(solution)/shard_map/ppermute | solution.py:424
  77.0 4.5 %own_products.2 = (f32[128,768]{1,0:T(8,128)S(1)}, f32[128,768]{1,0:T(8,128)S(1)}) custom-call(s32[1]{0:T(128)} %bitcast.diag, bf16[2048,768]{1,0:T(8,128)(2,1)S(1)} %get-tuple-element.26.refs_1_.right0, bf16[2048,768]{1,0:T(8,128)(2,1)} %get-tuple-element.27.right1, bf16[32,2048]{1,0:T(8,128)(2,1)S(1)} %copy-done.5, ...), custom_call_target="tpu_custom_call" | custom-call | flops 18874368 | bytes 131072 | tf_op jit(solution)/shard_map/own_products/pallas_call | solution.py:250
  81.5 5.7 %collective-permute-done.8.refs_1_ = bf16[128,2048]{1,0:T(8,128)(2,1)S(1)} collective-permute-done((bf16[128,2048]{1,0:T(8,128)(2,1)S(1)}, bf16[128,2048]{1,0:T(8,128)(2,1)S(1)}, u32[]{:S(2)}, u32[]{:S(2)}) %collective-permute-start.8) | collective-permute-done | bytes 524320 | tf_op jit(solution)/shard_map/ppermute | solution.py:424
  87.3 4.8 %partial_products.3 = (s16[1552,128]{1,0:T(8,128)(2,1)S(1)}, bf16[128,2048]{1,0:T(8,128)(2,1)S(1)}, bf16[64,2048]{1,0:T(8,128)(2,1)S(1)}) custom-call(s32[1]{0:T(128)} %bitcast.diag, bf16[2048,768]{1,0:T(8,128)(2,1)} %copy-done, bf16[2048,768]{1,0:T(8,128)(2,1)} %get-tuple-element.27.right1, bf16[128,2048]{1,0:T(8,128)(2,1)S(1)} %get-tuple-element.35.refs_0_, ...), custom_call_target="tpu_custom_call" | custom-call | flops 18874368 | bytes 114688 | tf_op jit(solution)/shard_map/partial_products/pallas_call | solution.py:315
  92.6 3.4 %collective-permute-done.11.coded.refs_1_ = s16[1552,128]{1,0:T(8,128)(2,1)S(1)} collective-permute-done((s16[1552,128]{1,0:T(8,128)(2,1)S(1)}, s16[1552,128]{1,0:T(8,128)(2,1)S(1)}, u32[]{:S(2)}, u32[]{:S(2)}) %collective-permute-start.11) | collective-permute-done | bytes 397344 | tf_op jit(solution)/shard_map/ppermute | solution.py:424
  96.1 1.4 %finish.2 = (bf16[256,768]{1,0:T(8,128)(2,1)}, bf16[256,768]{1,0:T(8,128)(2,1)}) custom-call(s32[2,6]{1,0:T(2,128)S(1)} %copy-done.6, s16[1552,128]{1,0:T(8,128)(2,1)S(1)} %collective-permute-done.11.coded.refs_1_, f32[128,768]{1,0:T(8,128)S(1)} %get-tuple-element.36.refs_4_.square, f32[128,768]{1,0:T(8,128)S(1)} %get-tuple-element.42.tangent), custom_call_target="tpu_custom_call" | custom-call | bytes 24576 | tf_op jit(solution)/shard_map/finish/pallas_call | solution.py:379
  97.5 4.4 %collective-permute-done.10.refs_2_ = bf16[128,2048]{1,0:T(8,128)(2,1)S(1)} collective-permute-done((bf16[128,2048]{1,0:T(8,128)(2,1)S(1)}, bf16[128,2048]{1,0:T(8,128)(2,1)S(1)}, u32[]{:S(2)}, u32[]{:S(2)}) %collective-permute-start.10) | collective-permute-done | bytes 524320 | tf_op jit(solution)/shard_map/ppermute | solution.py:424
  101.9 3.9 %own_products.3 = (f32[128,768]{1,0:T(8,128)S(1)}, f32[128,768]{1,0:T(8,128)S(1)}) custom-call(s32[1]{0:T(128)} %bitcast.diag, bf16[2048,768]{1,0:T(8,128)(2,1)S(1)} %copy-done.1, bf16[2048,768]{1,0:T(8,128)(2,1)} %get-tuple-element.27.right1, bf16[128,2048]{1,0:T(8,128)(2,1)S(1)} %get-tuple-element.25.rest_0_.refs_2_.refs_0_, ...), custom_call_target="tpu_custom_call" | custom-call | flops 18874368 | bytes 131072 | tf_op jit(solution)/shard_map/own_products/pallas_call | solution.py:250
  105.8 5.1 %collective-permute-done.9.coded = s16[1552,128]{1,0:T(8,128)(2,1)S(1)} collective-permute-done((s16[1552,128]{1,0:T(8,128)(2,1)S(1)}, s16[1552,128]{1,0:T(8,128)(2,1)S(1)}, u32[]{:S(2)}, u32[]{:S(2)}) %collective-permute-start.9) | collective-permute-done | bytes 397344 | tf_op jit(solution)/shard_map/ppermute | solution.py:424
  110.9 1.4 %finish.3 = (bf16[256,768]{1,0:T(8,128)(2,1)}, bf16[256,768]{1,0:T(8,128)(2,1)}) custom-call(s32[2,6]{1,0:T(2,128)S(1)} %copy-done.6, s16[1552,128]{1,0:T(8,128)(2,1)S(1)} %collective-permute-done.9.coded, f32[128,768]{1,0:T(8,128)S(1)} %get-tuple-element.39.square, ...), custom_call_target="tpu_custom_call", output_to_operand_aliasing={{0}: (4, {}), {1}: (5, {})} | custom-call | bytes 24576 | tf_op jit(solution)/shard_map/finish/pallas_call | solution.py:379
  (39 shorter events, 3.8 us)
Async XLA Ops:
  0.6 5.5 %copy-start.7 = (s32[2,128]{1,0:T(2,128)S(1)}, s32[2,128]{1,0:T(2,128)}, u32[]{:S(2)}) copy-start(s32[2,128]{1,0:T(2,128)} %refs_1_.3) | copy-start | bytes 3076
  0.7 5.5 %copy-start.8 = (s32[2,128]{1,0:T(2,128)S(1)}, s32[2,128]{1,0:T(2,128)}, u32[]{:S(2)}) copy-start(s32[2,128]{1,0:T(2,128)} %refs_2_.3) | copy-start | bytes 3076
  3.0 15.9 %collective-permute-start.1 = (bf16[112,2048]{1,0:T(8,128)(2,1)}, bf16[112,2048]{1,0:T(8,128)(2,1)S(1)}, u32[]{:S(2)}, u32[]{:S(2)}) collective-permute-start(bf16[112,2048]{1,0:T(8,128)(2,1)} %get-tuple-element.29.refs_2_), channel_id=1, source_target_pairs={{0,1},{1,0},{2,3},{3,2},{4,5},{5,4},{6,7},{7,6},{8,9},{9,8},{10,11... | collective-permute-start | bytes 1376264 | tf_op jit(solution)/shard_map/ppermute | solution.py:424
  6.1 12.9 %collective-permute-start = (bf16[32,2048]{1,0:T(8,128)(2,1)}, bf16[32,2048]{1,0:T(8,128)(2,1)S(1)}, u32[]{:S(2)}, u32[]{:S(2)}) collective-permute-start(bf16[32,2048]{1,0:T(8,128)(2,1)} %get-tuple-element.28.refs_0_), channel_id=1, source_target_pairs={{0,1},{1,17},{2,3},{3,19},{4,5},{5,21},{6,7},{7,23},{8,9},{9,25},{... | collective-permute-start | bytes 393224 | tf_op jit(solution)/shard_map/ppermute | solution.py:424
  6.1 1.0 copy-start.2
  7.2 1.6 %copy-start.9 = (s32[16,6]{0,1:T(8,128)S(1)}, s32[16,6]{0,1:T(8,128)}, u32[]{:S(2)}) copy-start(s32[16,6]{0,1:T(8,128)} %param.15) | copy-start | bytes 1156
  7.2 1.6 %copy-start.10 = (s32[16,6]{0,1:T(8,128)S(1)}, s32[16,6]{0,1:T(8,128)}, u32[]{:S(2)}) copy-start(s32[16,6]{0,1:T(8,128)} %param.16) | copy-start | bytes 1156
  8.9 10.1 %copy-start.3 = (bf16[112,2048]{1,0:T(8,128)(2,1)S(1)}, bf16[112,2048]{1,0:T(8,128)(2,1)}, u32[]{:S(2)}) copy-start(bf16[112,2048]{1,0:T(8,128)(2,1)} %get-tuple-element.24.refs_5_.refs_3_) | copy-start | bytes 1376260
  15.9 61.1 %copy-start = (bf16[2048,768]{1,0:T(8,128)(2,1)}, bf16[2048,768]{1,0:T(8,128)(2,1)S(1)}, u32[]{:S(2)}) copy-start(bf16[2048,768]{1,0:T(8,128)(2,1)S(1)} %get-tuple-element.26.refs_1_.right0) | copy-start | bytes 9437188
  19.3 16.3 %collective-permute-start.5 = (bf16[128,2048]{1,0:T(8,128)(2,1)S(1)}, bf16[128,2048]{1,0:T(8,128)(2,1)S(1)}, u32[]{:S(2)}, u32[]{:S(2)}) collective-permute-start(bf16[128,2048]{1,0:T(8,128)(2,1)S(1)} %get-tuple-element.32.refs_1_), channel_id=1, source_target_pairs={{0,1},{1,0},{2,3},{3,2},{4,5},{5,4},{6,7},{7,6},{8,9},{9,8},{10,11... | collective-permute-start | bytes 1572872 | tf_op jit(solution)/shard_map/ppermute | solution.py:424
  21.8 34.2 %collective-permute-start.2 = (bf16[112,2048]{1,0:T(8,128)(2,1)S(1)}, bf16[112,2048]{1,0:T(8,128)(2,1)S(1)}, u32[]{:S(2)}, u32[]{:S(2)}) collective-permute-start(bf16[112,2048]{1,0:T(8,128)(2,1)S(1)} %get-tuple-element.31), channel_id=1, source_target_pairs={{0,16},{1,17},{2,18},{3,19},{4,20},{5,21},{6,22},{7,23},{8,24},{9,... | collective-permute-start | bytes 1376264 | tf_op jit(solution)/shard_map/ppermute | solution.py:424
  22.9 12.7 %collective-permute-start.4 = (bf16[32,2048]{1,0:T(8,128)(2,1)S(1)}, bf16[32,2048]{1,0:T(8,128)(2,1)S(1)}, u32[]{:S(2)}, u32[]{:S(2)}) collective-permute-start(bf16[32,2048]{1,0:T(8,128)(2,1)S(1)} %collective-permute-done.refs_0_.refs_3_), channel_id=1, source_target_pairs={{0,1},{1,0},{2,3},{3,2},{4,5},{5,4},{6,7},{7,6},{8,9},{9,8},{10,11... | collective-permute-start | bytes 393224 | tf_op jit(solution)/shard_map/ppermute | solution.py:424
  36.0 40.2 %collective-permute-start.6 = (bf16[128,2048]{1,0:T(8,128)(2,1)S(1)}, bf16[128,2048]{1,0:T(8,128)(2,1)S(1)}, u32[]{:S(2)}, u32[]{:S(2)}) collective-permute-start(bf16[128,2048]{1,0:T(8,128)(2,1)S(1)} %get-tuple-element.33), channel_id=1, source_target_pairs={{0,16},{1,17},{2,18},{3,19},{4,20},{5,21},{6,22},{7,23},{8,24},{9,... | collective-permute-start | bytes 1572872 | tf_op jit(solution)/shard_map/ppermute | solution.py:424
  56.0 13.5 %collective-permute-start.3 = (bf16[112,2048]{1,0:T(8,128)(2,1)S(1)}, bf16[112,2048]{1,0:T(8,128)(2,1)S(1)}, u32[]{:S(2)}, u32[]{:S(2)}) collective-permute-start(bf16[112,2048]{1,0:T(8,128)(2,1)S(1)} %collective-permute-done.2.refs_1_.refs_3_), channel_id=1, source_target_pairs={{0,1},{1,0},{2,3},{3,2},{4,5},{5,4},{6,7},{7,6},{8,9},{9,8},{10,11... | collective-permute-start | bytes 1376264 | tf_op jit(solution)/shard_map/ppermute | solution.py:424
  56.5 19.7 %collective-permute-start.7 = (bf16[112,2048]{1,0:T(8,128)(2,1)S(1)}, bf16[112,2048]{1,0:T(8,128)(2,1)S(1)}, u32[]{:S(2)}, u32[]{:S(2)}) collective-permute-start(bf16[112,2048]{1,0:T(8,128)(2,1)S(1)} %get-tuple-element.34.refs_1_), channel_id=1, source_target_pairs={{0,1},{1,0},{2,3},{3,2},{4,5},{5,4},{6,7},{7,6},{8,9},{9,8},{10,11... | collective-permute-start | bytes 1376264 | tf_op jit(solution)/shard_map/ppermute | solution.py:424
  69.5 7.5 %copy-start.4 = (bf16[112,2048]{1,0:T(8,128)(2,1)S(1)}, bf16[112,2048]{1,0:T(8,128)(2,1)}, u32[]{:S(2)}) copy-start(bf16[112,2048]{1,0:T(8,128)(2,1)} %get-tuple-element.29.refs_2_) | copy-start | bytes 1376260
  69.5 7.5 %copy-start.5 = (bf16[32,2048]{1,0:T(8,128)(2,1)S(1)}, bf16[32,2048]{1,0:T(8,128)(2,1)}, u32[]{:S(2)}) copy-start(bf16[32,2048]{1,0:T(8,128)(2,1)} %get-tuple-element.28.refs_0_) | copy-start | bytes 393220
  76.5 10.8 %collective-permute-start.8 = (bf16[128,2048]{1,0:T(8,128)(2,1)S(1)}, bf16[128,2048]{1,0:T(8,128)(2,1)S(1)}, u32[]{:S(2)}, u32[]{:S(2)}) collective-permute-start(bf16[128,2048]{1,0:T(8,128)(2,1)S(1)} %get-tuple-element.35.refs_0_), channel_id=1, source_target_pairs={{0,1},{1,0},{2,3},{3,2},{4,5},{5,4},{6,7},{7,6},{8,9},{9,8},{10,11... | collective-permute-start | bytes 1572872 | tf_op jit(solution)/shard_map/ppermute | solution.py:424
  77.0 19.0 %collective-permute-start.11 = (s16[1552,128]{1,0:T(8,128)(2,1)S(1)}, s16[1552,128]{1,0:T(8,128)(2,1)S(1)}, u32[]{:S(2)}, u32[]{:S(2)}) collective-permute-start(s16[1552,128]{1,0:T(8,128)(2,1)S(1)} %get-tuple-element.41), channel_id=1, source_target_pairs={{0,16},{1,17},{2,18},{3,19},{4,20},{5,21},{6,22},{7,23},{8,24},{9,... | collective-permute-start | bytes 1191944 | tf_op jit(solution)/shard_map/ppermute | solution.py:424
  87.3 8.8 %copy-start.6 = (s32[2,6]{1,0:T(2,128)S(1)}, s32[2,6]{1,0:T(2,128)}, u32[]{:S(2)}) copy-start(s32[2,6]{1,0:T(2,128)} %keep.3) | copy-start | bytes 148
  87.3 14.6 %copy-start.1 = (bf16[2048,768]{1,0:T(8,128)(2,1)S(1)}, bf16[2048,768]{1,0:T(8,128)(2,1)}, u32[]{:S(2)}) copy-start(bf16[2048,768]{1,0:T(8,128)(2,1)} %copy-done) | copy-start | bytes 9437188
  92.0 9.9 %collective-permute-start.10 = (bf16[128,2048]{1,0:T(8,128)(2,1)S(1)}, bf16[128,2048]{1,0:T(8,128)(2,1)S(1)}, u32[]{:S(2)}, u32[]{:S(2)}) collective-permute-start(bf16[128,2048]{1,0:T(8,128)(2,1)S(1)} %get-tuple-element.38), channel_id=1, source_target_pairs={{0,1},{1,0},{2,3},{3,2},{4,5},{5,4},{6,7},{7,6},{8,9},{9,8},{10,11... | collective-permute-start | bytes 1572872 | tf_op jit(solution)/shard_map/ppermute | solution.py:424
  92.6 18.4 %collective-permute-start.9 = (s16[1552,128]{1,0:T(8,128)(2,1)S(1)}, s16[1552,128]{1,0:T(8,128)(2,1)S(1)}, u32[]{:S(2)}, u32[]{:S(2)}) collective-permute-start(s16[1552,128]{1,0:T(8,128)(2,1)S(1)} %get-tuple-element.37), channel_id=1, source_target_pairs={{0,16},{1,17},{2,18},{3,19},{4,20},{5,21},{6,22},{7,23},{8,24},{9,... | collective-permute-start | bytes 1191944 | tf_op jit(solution)/shard_map/ppermute | solution.py:424
  96.0 9.8 %collective-permute-start.12 = (bf16[64,2048]{1,0:T(8,128)(2,1)S(1)}, bf16[64,2048]{1,0:T(8,128)(2,1)S(1)}, u32[]{:S(2)}, u32[]{:S(2)}) collective-permute-start(bf16[64,2048]{1,0:T(8,128)(2,1)S(1)} %handed_on.3), channel_id=1, source_target_pairs={{0,2},{1,3},{2,0},{3,1},{4,6},{5,7},{6,4},{7,5},{8,10},{9,11},{10,... | collective-permute-start | bytes 786440 | tf_op jit(solution)/shard_map/ppermute | solution.py:424

commit v12 on v11

--- a/solution.py
+++ b/solution.py
@@ -404,7 +404,7 @@
     half = row_index // group
     diag = (half == lax.axis_index("col")).astype(jnp.int32).reshape(1)
     place = (row_index % group).astype(jnp.int32).reshape(1)
-    direct = all_rows // 16
+    direct = all_rows // 8
     split = all_rows // 2
     wide = 256
 
@@ -446,7 +446,7 @@
     near1 = move(send, over_z)
     passed2 = move(b2, over_y)
     far0 = move(near0, over_y)
-    send, a1 = chosen(diag, passed2, a2, (a1,), (far0,))
+    send, a1 = chosen(diag, passed2, a2, (a1,), (far0, near1))
     near2 = move(send, over_z)
     got1 = move(a1, over_y)
     far1 = move(near1, over_y)

time: 113 us -> 106 us (0.938)
  waiting for transfers between devices: 63.2 us -> 59.4 us
  starting transfers between devices: 14.7 us -> 12 us
    ppermute x13, waiting for transfers between devices: 63.2 us -> 59.4 us  [move(): return lax.ppermute(values, ('row', 'col'), pairs)]
    ppermute x13, starting transfers between devices: 14.7 us -> 12 us  [move(): return lax.ppermute(values, ('row', 'col'), pairs)]
  transfers between devices with their start and end apart: 13 -> 13, of which waited for: 9 -> 10; matrix products, arithmetic and copies ran while one was open for 0% -> 0% of each run, Pallas kernels for 25% -> 26%
where the time goes in v12:
time: 106 us
  waiting for transfers between devices  59.4 us (56%)
  Pallas kernels  32.4 us (31%)
  starting transfers between devices  12 us (11%)
  local copies, waits for them, and re-layouts  1.2 us (1%)
    ppermute x13, waiting for transfers between devices, move(): return lax.ppermute(values, ('row', 'col'), pairs)  59.4 us
    ppermute x13, starting transfers between devices, move(): return lax.ppermute(values, ('row', 'col'), pairs)  12 us
    pallas_call x2, Pallas kernels, partial_products(): pl.pallas_call(functools.partial(partial_kernel, one, other, len(arrays),...  9.49 us
    pallas_call x2, Pallas kernels, local_products(): pl.pallas_call(functools.partial(local_kernel, one, other), grid=(columns...  8.41 us
    pallas_call x1, Pallas kernels, masked_right(): pl.pallas_call(right_kernel, grid=(depth // tall,), in_specs=[SM(), SM(),...  6.96 us
    pallas_call x2, Pallas kernels, masked_chunks(): pl.pallas_call(functools.partial(chunk_kernel, spans, int(stacked), panel...  3.89 us
    pallas_call x2, Pallas kernels, finished(): pl.pallas_call(functools.partial(finish_kernel, start, [cut for _, *cut i...  2.83 us
  transfers between devices with their start and end apart: 13, of which 10 were waited for; matrix products, arithmetic and copies ran while one was open for 0% of the time, Pallas kernels for 26%

profile of v12, /device:TPU:0, one launch (start us, length us, event | category | flops | bytes accessed | tf_op | source)
XLA Modules:
  0.0 105.8 jit_solution(12203926677649796538)
XLA Ops:
  0.7 2.4 %left_chunks.2 = (bf16[64,2048]{1,0:T(8,128)(2,1)}, bf16[96,2048]{1,0:T(8,128)(2,1)}, bf16[96,2048]{1,0:T(8,128)(2,1)}) custom-call(s32[1]{0:T(128)} %bitcast.1.refs_0_, s32[2,128]{1,0:T(2,128)} %refs_1_.3, s32[2,128]{1,0:T(2,128)} %refs_2_.3, bf16[256,16384]{1,0:T(8,128)(2,1)} %refs_3_.3, bf16[256,16384]{1,0:T(8,128)(2,1)} %refs_4_.3), custom_call_target="tpu_custom_call" | custom-call | bytes 32768 | tf_op jit(solution)/shard_map/left_chunks/pallas_call | solution.py:80
  3.0 3.0 %collective-permute-start.1 = (bf16[96,2048]{1,0:T(8,128)(2,1)}, bf16[96,2048]{1,0:T(8,128)(2,1)S(1)}, u32[]{:S(2)}, u32[]{:S(2)}) collective-permute-start(bf16[96,2048]{1,0:T(8,128)(2,1)} %get-tuple-element.29.refs_2_), channel_id=1, source_target_pairs={{0,1},{1,0},{2,3},{3,2},{4,5},{5,4},{6,7},{7,6},{8,9},{9,8},{10,11... | collective-permute-start | bytes 1179656 | tf_op jit(solution)/shard_map/ppermute | solution.py:424
  7.1 1.5 %left_chunks.3 = (bf16[128,2048]{1,0:T(8,128)(2,1)S(1)}, bf16[128,2048]{1,0:T(8,128)(2,1)S(1)}) custom-call(s32[1]{0:T(128)} %bitcast.1.refs_0_, s32[2,128]{1,0:T(2,128)S(1)} %copy-done.7, s32[2,128]{1,0:T(2,128)S(1)} %copy-done.8, bf16[256,16384]{1,0:T(8,128)(2,1)} %refs_3_.3, bf16[256,16384]{1,0:T(8,128)(2,1)} %refs_4_.3, bf16[96,2048]{1,0:T(8,128)(2,1)S(1)} %copy-done.2), custom_call_target="tpu_custom_call" | custom-call | bytes 32768 | tf_op jit(solution)/shard_map/left_chunks/pallas_call | solution.py:80
  8.9 7.0 %right_panels.1 = (bf16[2048,768]{1,0:T(8,128)(2,1)S(1)}, bf16[2048,768]{1,0:T(8,128)(2,1)}) custom-call(s32[16,6]{1,0:T(8,128)S(1)} %copy.13.mask0, s32[16,6]{1,0:T(8,128)S(1)} %copy.14.mask1, bf16[2048,768]{1,0:T(8,128)(2,1)} %x0.1, bf16[2048,768]{1,0:T(8,128)(2,1)} %x1.1, bf16[128,2048]{1,0:T(8,128)(2,1)S(1)} %get-tuple-element.25.rest_0_.refs_3_.refs_2_.refs_0_), custom_call_target="tpu_custom_call" | custom-call | bytes 196608 | tf_op jit(solution)/shard_map/right_panels/pallas_call | solution.py:179
  15.8 4.7 %collective-permute-done.refs_0_.refs_3_ = bf16[64,2048]{1,0:T(8,128)(2,1)S(1)} collective-permute-done((bf16[64,2048]{1,0:T(8,128)(2,1)}, bf16[64,2048]{1,0:T(8,128)(2,1)S(1)}, u32[]{:S(2)}, u32[]{:S(2)}) %collective-permute-start) | collective-permute-done | bytes 262176 | tf_op jit(solution)/shard_map/ppermute | solution.py:424
  20.8 2.3 %collective-permute-start.5 = (bf16[128,2048]{1,0:T(8,128)(2,1)S(1)}, bf16[128,2048]{1,0:T(8,128)(2,1)S(1)}, u32[]{:S(2)}, u32[]{:S(2)}) collective-permute-start(bf16[128,2048]{1,0:T(8,128)(2,1)S(1)} %get-tuple-element.32.refs_1_), channel_id=1, source_target_pairs={{0,1},{1,0},{2,3},{3,2},{4,5},{5,4},{6,7},{7,6},{8,9},{9,8},{10,11... | collective-permute-start | bytes 1572872 | tf_op jit(solution)/shard_map/ppermute | solution.py:424
  23.1 1.1 %collective-permute-start.2 = (bf16[96,2048]{1,0:T(8,128)(2,1)S(1)}, bf16[96,2048]{1,0:T(8,128)(2,1)S(1)}, u32[]{:S(2)}, u32[]{:S(2)}) collective-permute-start(bf16[96,2048]{1,0:T(8,128)(2,1)S(1)} %get-tuple-element.31), channel_id=1, source_target_pairs={{0,16},{1,17},{2,18},{3,19},{4,20},{5,21},{6,22},{7,23},{8,24},{9,... | collective-permute-start | bytes 1179656 | tf_op jit(solution)/shard_map/ppermute | solution.py:424
  24.2 1.9 %collective-permute-start.4 = (bf16[64,2048]{1,0:T(8,128)(2,1)S(1)}, bf16[64,2048]{1,0:T(8,128)(2,1)S(1)}, u32[]{:S(2)}, u32[]{:S(2)}) collective-permute-start(bf16[64,2048]{1,0:T(8,128)(2,1)S(1)} %collective-permute-done.refs_0_.refs_3_), channel_id=1, source_target_pairs={{0,1},{1,0},{2,3},{3,2},{4,5},{5,4},{6,7},{7,6},{8,9},{9,8},{10,11... | collective-permute-start | bytes 786440 | tf_op jit(solution)/shard_map/ppermute | solution.py:424
  26.2 13.6 %collective-permute-done.4.refs_3_.refs_0_ = bf16[64,2048]{1,0:T(8,128)(2,1)S(1)} collective-permute-done((bf16[64,2048]{1,0:T(8,128)(2,1)S(1)}, bf16[64,2048]{1,0:T(8,128)(2,1)S(1)}, u32[]{:S(2)}, u32[]{:S(2)}) %collective-permute-start.4) | collective-permute-done | bytes 262176 | tf_op jit(solution)/shard_map/ppermute | solution.py:424
  39.7 2.4 %collective-permute-done.2.refs_1_.refs_3_ = bf16[96,2048]{1,0:T(8,128)(2,1)S(1)} collective-permute-done((bf16[96,2048]{1,0:T(8,128)(2,1)S(1)}, bf16[96,2048]{1,0:T(8,128)(2,1)S(1)}, u32[]{:S(2)}, u32[]{:S(2)}) %collective-permute-start.2) | collective-permute-done | bytes 393248 | tf_op jit(solution)/shard_map/ppermute | solution.py:424
  43.2 1.7 %collective-permute-start.7 = (bf16[96,2048]{1,0:T(8,128)(2,1)S(1)}, bf16[96,2048]{1,0:T(8,128)(2,1)S(1)}, u32[]{:S(2)}, u32[]{:S(2)}) collective-permute-start(bf16[96,2048]{1,0:T(8,128)(2,1)S(1)} %get-tuple-element.34.refs_1_), channel_id=1, source_target_pairs={{0,1},{1,0},{2,3},{3,2},{4,5},{5,4},{6,7},{7,6},{8,9},{9,8},{10,11... | collective-permute-start | bytes 1179656 | tf_op jit(solution)/shard_map/ppermute | solution.py:424
  44.9 10.0 %collective-permute-done.3.refs_2_ = bf16[96,2048]{1,0:T(8,128)(2,1)S(1)} collective-permute-done((bf16[96,2048]{1,0:T(8,128)(2,1)S(1)}, bf16[96,2048]{1,0:T(8,128)(2,1)S(1)}, u32[]{:S(2)}, u32[]{:S(2)}) %collective-permute-start.3) | collective-permute-done | bytes 393248 | tf_op jit(solution)/shard_map/ppermute | solution.py:424
  54.9 4.7 %partial_products.2.refs_0_ = s16[1552,128]{1,0:T(8,128)(2,1)S(1)} custom-call(s32[1]{0:T(128)} %bitcast.diag, bf16[2048,768]{1,0:T(8,128)(2,1)S(1)} %get-tuple-element.26.refs_1_.right0, bf16[2048,768]{1,0:T(8,128)(2,1)} %get-tuple-element.27.right1, bf16[64,2048]{1,0:T(8,128)(2,1)S(1)} %collective-permute-done.refs_0_.refs_3_, ...), custom_call_target="tpu_custom_call" | custom-call | flops 18874368 | bytes 114688 | tf_op jit(solution)/shard_map/partial_products/pallas_call | solution.py:315
  59.7 1.2 %collective-permute-done.7.refs_2_.refs_4_ = bf16[96,2048]{1,0:T(8,128)(2,1)S(1)} collective-permute-done((bf16[96,2048]{1,0:T(8,128)(2,1)S(1)}, bf16[96,2048]{1,0:T(8,128)(2,1)S(1)}, u32[]{:S(2)}, u32[]{:S(2)}) %collective-permute-start.7) | collective-permute-done | bytes 393248 | tf_op jit(solution)/shard_map/ppermute | solution.py:424
  60.9 6.4 %collective-permute-done.6.refs_1_ = bf16[128,2048]{1,0:T(8,128)(2,1)S(1)} collective-permute-done((bf16[128,2048]{1,0:T(8,128)(2,1)S(1)}, bf16[128,2048]{1,0:T(8,128)(2,1)S(1)}, u32[]{:S(2)}, u32[]{:S(2)}) %collective-permute-start.6) | collective-permute-done | bytes 524320 | tf_op jit(solution)/shard_map/ppermute | solution.py:424
  68.1 4.5 %own_products.2 = (f32[128,768]{1,0:T(8,128)S(1)}, f32[128,768]{1,0:T(8,128)S(1)}) custom-call(s32[1]{0:T(128)} %bitcast.diag, bf16[2048,768]{1,0:T(8,128)(2,1)S(1)} %get-tuple-element.26.refs_1_.right0, bf16[2048,768]{1,0:T(8,128)(2,1)} %get-tuple-element.27.right1, bf16[64,2048]{1,0:T(8,128)(2,1)S(1)} %copy-done.5, ...), custom_call_target="tpu_custom_call" | custom-call | flops 18874368 | bytes 131072 | tf_op jit(solution)/shard_map/own_products/pallas_call | solution.py:250
  72.7 8.0 %collective-permute-done.8.refs_1_ = bf16[128,2048]{1,0:T(8,128)(2,1)S(1)} collective-permute-done((bf16[128,2048]{1,0:T(8,128)(2,1)S(1)}, bf16[128,2048]{1,0:T(8,128)(2,1)S(1)}, u32[]{:S(2)}, u32[]{:S(2)}) %collective-permute-start.8) | collective-permute-done | bytes 524320 | tf_op jit(solution)/shard_map/ppermute | solution.py:424
  80.7 4.8 %partial_products.3 = (s16[1552,128]{1,0:T(8,128)(2,1)S(1)}, bf16[128,2048]{1,0:T(8,128)(2,1)S(1)}, bf16[64,2048]{1,0:T(8,128)(2,1)S(1)}) custom-call(s32[1]{0:T(128)} %bitcast.diag, bf16[2048,768]{1,0:T(8,128)(2,1)} %copy-done, bf16[2048,768]{1,0:T(8,128)(2,1)} %get-tuple-element.27.right1, bf16[128,2048]{1,0:T(8,128)(2,1)S(1)} %get-tuple-element.35.refs_0_, ...), custom_call_target="tpu_custom_call" | custom-call | flops 18874368 | bytes 114688 | tf_op jit(solution)/shard_map/partial_products/pallas_call | solution.py:315
  85.8 1.1 %collective-permute-done.11.coded.refs_1_ = s16[1552,128]{1,0:T(8,128)(2,1)S(1)} collective-permute-done((s16[1552,128]{1,0:T(8,128)(2,1)S(1)}, s16[1552,128]{1,0:T(8,128)(2,1)S(1)}, u32[]{:S(2)}, u32[]{:S(2)}) %collective-permute-start.11) | collective-permute-done | bytes 397344 | tf_op jit(solution)/shard_map/ppermute | solution.py:424
  87.0 1.4 %finish.2 = (bf16[256,768]{1,0:T(8,128)(2,1)}, bf16[256,768]{1,0:T(8,128)(2,1)}) custom-call(s32[2,6]{1,0:T(2,128)S(1)} %copy-done.6, s16[1552,128]{1,0:T(8,128)(2,1)S(1)} %collective-permute-done.11.coded.refs_1_, f32[128,768]{1,0:T(8,128)S(1)} %get-tuple-element.36.refs_4_.square, f32[128,768]{1,0:T(8,128)S(1)} %get-tuple-element.42.tangent), custom_call_target="tpu_custom_call" | custom-call | bytes 24576 | tf_op jit(solution)/shard_map/finish/pallas_call | solution.py:379
  88.5 9.1 %collective-permute-done.10.refs_2_ = bf16[128,2048]{1,0:T(8,128)(2,1)S(1)} collective-permute-done((bf16[128,2048]{1,0:T(8,128)(2,1)S(1)}, bf16[128,2048]{1,0:T(8,128)(2,1)S(1)}, u32[]{:S(2)}, u32[]{:S(2)}) %collective-permute-start.10) | collective-permute-done | bytes 524320 | tf_op jit(solution)/shard_map/ppermute | solution.py:424
  97.6 3.9 %own_products.3 = (f32[128,768]{1,0:T(8,128)S(1)}, f32[128,768]{1,0:T(8,128)S(1)}) custom-call(s32[1]{0:T(128)} %bitcast.diag, bf16[2048,768]{1,0:T(8,128)(2,1)S(1)} %copy-done.1, bf16[2048,768]{1,0:T(8,128)(2,1)} %get-tuple-element.27.right1, bf16[128,2048]{1,0:T(8,128)(2,1)S(1)} %get-tuple-element.25.rest_0_.refs_3_.refs_2_.refs_0_, ...), custom_call_target="tpu_custom_call" | custom-call | flops 18874368 | bytes 131072 | tf_op jit(solution)/shard_map/own_products/pallas_call | solution.py:250
  101.5 2.9 %collective-permute-done.9.coded = s16[1552,128]{1,0:T(8,128)(2,1)S(1)} collective-permute-done((s16[1552,128]{1,0:T(8,128)(2,1)S(1)}, s16[1552,128]{1,0:T(8,128)(2,1)S(1)}, u32[]{:S(2)}, u32[]{:S(2)}) %collective-permute-start.9) | collective-permute-done | bytes 397344 | tf_op jit(solution)/shard_map/ppermute | solution.py:424
  104.3 1.4 %finish.3 = (bf16[256,768]{1,0:T(8,128)(2,1)}, bf16[256,768]{1,0:T(8,128)(2,1)}) custom-call(s32[2,6]{1,0:T(2,128)S(1)} %copy-done.6, s16[1552,128]{1,0:T(8,128)(2,1)S(1)} %collective-permute-done.9.coded, f32[128,768]{1,0:T(8,128)S(1)} %get-tuple-element.39.square, ...), custom_call_target="tpu_custom_call", output_to_operand_aliasing={{0}: (4, {}), {1}: (5, {})} | custom-call | bytes 24576 | tf_op jit(solution)/shard_map/finish/pallas_call | solution.py:379
  (39 shorter events, 3.8 us)
Async XLA Ops:
  0.6 5.5 %copy-start.7 = (s32[2,128]{1,0:T(2,128)S(1)}, s32[2,128]{1,0:T(2,128)}, u32[]{:S(2)}) copy-start(s32[2,128]{1,0:T(2,128)} %refs_1_.3) | copy-start | bytes 3076
  0.7 5.5 %copy-start.8 = (s32[2,128]{1,0:T(2,128)S(1)}, s32[2,128]{1,0:T(2,128)}, u32[]{:S(2)}) copy-start(s32[2,128]{1,0:T(2,128)} %refs_2_.3) | copy-start | bytes 3076
  3.0 17.5 %collective-permute-start.1 = (bf16[96,2048]{1,0:T(8,128)(2,1)}, bf16[96,2048]{1,0:T(8,128)(2,1)S(1)}, u32[]{:S(2)}, u32[]{:S(2)}) collective-permute-start(bf16[96,2048]{1,0:T(8,128)(2,1)} %get-tuple-element.29.refs_2_), channel_id=1, source_target_pairs={{0,1},{1,0},{2,3},{3,2},{4,5},{5,4},{6,7},{7,6},{8,9},{9,8},{10,11... | collective-permute-start | bytes 1179656 | tf_op jit(solution)/shard_map/ppermute | solution.py:424
  6.1 14.5 %collective-permute-start = (bf16[64,2048]{1,0:T(8,128)(2,1)}, bf16[64,2048]{1,0:T(8,128)(2,1)S(1)}, u32[]{:S(2)}, u32[]{:S(2)}) collective-permute-start(bf16[64,2048]{1,0:T(8,128)(2,1)} %get-tuple-element.28.refs_0_), channel_id=1, source_target_pairs={{0,1},{1,17},{2,3},{3,19},{4,5},{5,21},{6,7},{7,23},{8,9},{9,25},{... | collective-permute-start | bytes 786440 | tf_op jit(solution)/shard_map/ppermute | solution.py:424
  6.1 1.0 copy-start.2
  7.1 1.6 %copy-start.9 = (s32[16,6]{0,1:T(8,128)S(1)}, s32[16,6]{0,1:T(8,128)}, u32[]{:S(2)}) copy-start(s32[16,6]{0,1:T(8,128)} %param.15) | copy-start | bytes 1156
  7.1 1.6 %copy-start.10 = (s32[16,6]{0,1:T(8,128)S(1)}, s32[16,6]{0,1:T(8,128)}, u32[]{:S(2)}) copy-start(s32[16,6]{0,1:T(8,128)} %param.16) | copy-start | bytes 1156
  8.9 11.7 %copy-start.3 = (bf16[96,2048]{1,0:T(8,128)(2,1)S(1)}, bf16[96,2048]{1,0:T(8,128)(2,1)}, u32[]{:S(2)}) copy-start(bf16[96,2048]{1,0:T(8,128)(2,1)} %get-tuple-element.24.refs_5_.refs_3_.refs_4_) | copy-start | bytes 1179652
  15.8 52.3 %copy-start = (bf16[2048,768]{1,0:T(8,128)(2,1)}, bf16[2048,768]{1,0:T(8,128)(2,1)S(1)}, u32[]{:S(2)}) copy-start(bf16[2048,768]{1,0:T(8,128)(2,1)S(1)} %get-tuple-element.26.refs_1_.right0) | copy-start | bytes 9437188
  20.8 21.3 %collective-permute-start.5 = (bf16[128,2048]{1,0:T(8,128)(2,1)S(1)}, bf16[128,2048]{1,0:T(8,128)(2,1)S(1)}, u32[]{:S(2)}, u32[]{:S(2)}) collective-permute-start(bf16[128,2048]{1,0:T(8,128)(2,1)S(1)} %get-tuple-element.32.refs_1_), channel_id=1, source_target_pairs={{0,1},{1,0},{2,3},{3,2},{4,5},{5,4},{6,7},{7,6},{8,9},{9,8},{10,11... | collective-permute-start | bytes 1572872 | tf_op jit(solution)/shard_map/ppermute | solution.py:424
  23.1 19.0 %collective-permute-start.2 = (bf16[96,2048]{1,0:T(8,128)(2,1)S(1)}, bf16[96,2048]{1,0:T(8,128)(2,1)S(1)}, u32[]{:S(2)}, u32[]{:S(2)}) collective-permute-start(bf16[96,2048]{1,0:T(8,128)(2,1)S(1)} %get-tuple-element.31), channel_id=1, source_target_pairs={{0,16},{1,17},{2,18},{3,19},{4,20},{5,21},{6,22},{7,23},{8,24},{9,... | collective-permute-start | bytes 1179656 | tf_op jit(solution)/shard_map/ppermute | solution.py:424
  24.2 15.5 %collective-permute-start.4 = (bf16[64,2048]{1,0:T(8,128)(2,1)S(1)}, bf16[64,2048]{1,0:T(8,128)(2,1)S(1)}, u32[]{:S(2)}, u32[]{:S(2)}) collective-permute-start(bf16[64,2048]{1,0:T(8,128)(2,1)S(1)} %collective-permute-done.refs_0_.refs_3_), channel_id=1, source_target_pairs={{0,1},{1,0},{2,3},{3,2},{4,5},{5,4},{6,7},{7,6},{8,9},{9,8},{10,11... | collective-permute-start | bytes 786440 | tf_op jit(solution)/shard_map/ppermute | solution.py:424
  42.4 25.0 %collective-permute-start.6 = (bf16[128,2048]{1,0:T(8,128)(2,1)S(1)}, bf16[128,2048]{1,0:T(8,128)(2,1)S(1)}, u32[]{:S(2)}, u32[]{:S(2)}) collective-permute-start(bf16[128,2048]{1,0:T(8,128)(2,1)S(1)} %get-tuple-element.33), channel_id=1, source_target_pairs={{0,16},{1,17},{2,18},{3,19},{4,20},{5,21},{6,22},{7,23},{8,24},{9,... | collective-permute-start | bytes 1572872 | tf_op jit(solution)/shard_map/ppermute | solution.py:424
  42.9 12.1 %collective-permute-start.3 = (bf16[96,2048]{1,0:T(8,128)(2,1)S(1)}, bf16[96,2048]{1,0:T(8,128)(2,1)S(1)}, u32[]{:S(2)}, u32[]{:S(2)}) collective-permute-start(bf16[96,2048]{1,0:T(8,128)(2,1)S(1)} %collective-permute-done.2.refs_1_.refs_3_), channel_id=1, source_target_pairs={{0,1},{1,0},{2,3},{3,2},{4,5},{5,4},{6,7},{7,6},{8,9},{9,8},{10,11... | collective-permute-start | bytes 1179656 | tf_op jit(solution)/shard_map/ppermute | solution.py:424
  43.2 17.7 %collective-permute-start.7 = (bf16[96,2048]{1,0:T(8,128)(2,1)S(1)}, bf16[96,2048]{1,0:T(8,128)(2,1)S(1)}, u32[]{:S(2)}, u32[]{:S(2)}) collective-permute-start(bf16[96,2048]{1,0:T(8,128)(2,1)S(1)} %get-tuple-element.34.refs_1_), channel_id=1, source_target_pairs={{0,1},{1,0},{2,3},{3,2},{4,5},{5,4},{6,7},{7,6},{8,9},{9,8},{10,11... | collective-permute-start | bytes 1179656 | tf_op jit(solution)/shard_map/ppermute | solution.py:424
  54.9 13.2 %copy-start.4 = (bf16[96,2048]{1,0:T(8,128)(2,1)S(1)}, bf16[96,2048]{1,0:T(8,128)(2,1)}, u32[]{:S(2)}) copy-start(bf16[96,2048]{1,0:T(8,128)(2,1)} %get-tuple-element.29.refs_2_) | copy-start | bytes 1179652
  54.9 13.2 %copy-start.5 = (bf16[64,2048]{1,0:T(8,128)(2,1)S(1)}, bf16[64,2048]{1,0:T(8,128)(2,1)}, u32[]{:S(2)}) copy-start(bf16[64,2048]{1,0:T(8,128)(2,1)} %get-tuple-element.28.refs_0_) | copy-start | bytes 786436
  67.6 13.1 %collective-permute-start.8 = (bf16[128,2048]{1,0:T(8,128)(2,1)S(1)}, bf16[128,2048]{1,0:T(8,128)(2,1)S(1)}, u32[]{:S(2)}, u32[]{:S(2)}) collective-permute-start(bf16[128,2048]{1,0:T(8,128)(2,1)S(1)} %get-tuple-element.35.refs_0_), channel_id=1, source_target_pairs={{0,1},{1,0},{2,3},{3,2},{4,5},{5,4},{6,7},{7,6},{8,9},{9,8},{10,11... | collective-permute-start | bytes 1572872 | tf_op jit(solution)/shard_map/ppermute | solution.py:424
  68.1 18.8 %collective-permute-start.11 = (s16[1552,128]{1,0:T(8,128)(2,1)S(1)}, s16[1552,128]{1,0:T(8,128)(2,1)S(1)}, u32[]{:S(2)}, u32[]{:S(2)}) collective-permute-start(s16[1552,128]{1,0:T(8,128)(2,1)S(1)} %get-tuple-element.41), channel_id=1, source_target_pairs={{0,16},{1,17},{2,18},{3,19},{4,20},{5,21},{6,22},{7,23},{8,24},{9,... | collective-permute-start | bytes 1191944 | tf_op jit(solution)/shard_map/ppermute | solution.py:424
  80.7 6.4 %copy-start.6 = (s32[2,6]{1,0:T(2,128)S(1)}, s32[2,6]{1,0:T(2,128)}, u32[]{:S(2)}) copy-start(s32[2,6]{1,0:T(2,128)} %keep.3) | copy-start | bytes 148
  80.7 16.9 %copy-start.1 = (bf16[2048,768]{1,0:T(8,128)(2,1)S(1)}, bf16[2048,768]{1,0:T(8,128)(2,1)}, u32[]{:S(2)}) copy-start(bf16[2048,768]{1,0:T(8,128)(2,1)} %copy-done) | copy-start | bytes 9437188
  85.4 12.2 %collective-permute-start.10 = (bf16[128,2048]{1,0:T(8,128)(2,1)S(1)}, bf16[128,2048]{1,0:T(8,128)(2,1)S(1)}, u32[]{:S(2)}, u32[]{:S(2)}) collective-permute-start(bf16[128,2048]{1,0:T(8,128)(2,1)S(1)} %get-tuple-element.38), channel_id=1, source_target_pairs={{0,1},{1,0},{2,3},{3,2},{4,5},{5,4},{6,7},{7,6},{8,9},{9,8},{10,11... | collective-permute-start | bytes 1572872 | tf_op jit(solution)/shard_map/ppermute | solution.py:424
  85.8 18.6 %collective-permute-start.9 = (s16[1552,128]{1,0:T(8,128)(2,1)S(1)}, s16[1552,128]{1,0:T(8,128)(2,1)S(1)}, u32[]{:S(2)}, u32[]{:S(2)}) collective-permute-start(s16[1552,128]{1,0:T(8,128)(2,1)S(1)} %get-tuple-element.37), channel_id=1, source_target_pairs={{0,16},{1,17},{2,18},{3,19},{4,20},{5,21},{6,22},{7,23},{8,24},{9,... | collective-permute-start | bytes 1191944 | tf_op jit(solution)/shard_map/ppermute | solution.py:424
  86.9 14.5 %collective-permute-start.12 = (bf16[64,2048]{1,0:T(8,128)(2,1)S(1)}, bf16[64,2048]{1,0:T(8,128)(2,1)S(1)}, u32[]{:S(2)}, u32[]{:S(2)}) collective-permute-start(bf16[64,2048]{1,0:T(8,128)(2,1)S(1)} %handed_on.3), channel_id=1, source_target_pairs={{0,2},{1,3},{2,0},{3,1},{4,6},{5,7},{6,4},{7,5},{8,10},{9,11},{10,... | collective-permute-start | bytes 786440 | tf_op jit(solution)/shard_map/ppermute | solution.py:424

commit v13 on v12

--- a/solution.py
+++ b/solution.py
@@ -95,44 +95,43 @@
     )(place, mask0, mask1, x0, x1, *after)
 
 
-def choose_kernel(gates, many, diag, *refs):
-    one, other = refs[gates : gates + 2]
-    held, outs, sems = refs[gates + 2 : gates + 2 + many], refs[-many - 2 : -1], refs[-1]
+def choose_kernel(gates, many, cuts, diag, *refs):
+    one, other = refs[gates : gates + many], refs[gates + many]
+    held = refs[gates + many + 1 : gates + many + 1 + len(cuts)]
+    outs, sems = refs[-len(cuts) - 2 : -1], refs[-1]
+    send = outs[0]
     others = [
-        pltpu.make_async_copy(x, out, sems.at[1 + i])
-        for i, (x, out) in enumerate(zip(held, outs[1:]))
+        pltpu.make_async_copy(x.at[pl.ds(lo, hi - lo)], out, sems.at[many + i])
+        for i, (x, out, (lo, hi)) in enumerate(zip(held, outs[1:], cuts))
     ]
     for copy in others:
         copy.start()
 
     @pl.when(diag[0] == 1)
     def _():
-        copy = pltpu.make_async_copy(one, outs[0], sems.at[0])
-        copy.start()
-        copy.wait()
+        fetched([(i, 0, x.shape[0]) for i, x in enumerate(one)], one, send, sems)
 
     @pl.when(diag[0] == 0)
     def _():
-        copy = pltpu.make_async_copy(other, outs[0], sems.at[0])
-        copy.start()
-        copy.wait()
+        fetched([(0, 0, other.shape[0])], [other], send, sems)
 
     for copy in others:
         copy.wait()
 
 
 def chosen(diag, one, other, held=(), after=()):
-    outs = [jax.ShapeDtypeStruct(x.shape, x.dtype) for x in (one, *held)]
-    return pl.pallas_call(
-        functools.partial(choose_kernel, len(after), len(held)),
-        in_specs=[SM()] + [HB() for _ in (*after, one, other, *held)],
+    outs = [jax.ShapeDtypeStruct(other.shape, other.dtype)]
+    outs += [jax.ShapeDtypeStruct((hi - lo, x.shape[1]), x.dtype) for x, lo, hi in held]
+    return pl.pallas_call(
+        functools.partial(choose_kernel, len(after), len(one), [cut for _, *cut in held]),
+        in_specs=[SM()] + [HB() for _ in (*after, *one, other, *held)],
         out_specs=[HB() for _ in outs],
         out_shape=outs,
-        scratch_shapes=[pltpu.SemaphoreType.DMA((len(outs),))],
+        scratch_shapes=[pltpu.SemaphoreType.DMA((len(one) + len(held),))],
         compiler_params=params(),
-        cost_estimate=cost(0, 4 * one.size),
+        cost_estimate=cost(0, 4 * other.size),
         name="to_send",
-    )(diag, *after, one, other, *held)
+    )(diag, *after, *one, other, *(x for x, _, _ in held))
 
 
 def hand_kernel(many, *refs):
@@ -442,11 +441,14 @@
     near0 = move(joint, ring)
     a2, b2 = chunks(((split, all_rows),), False, VMEM_BYTES, (a1,))
     right0, right1 = masked_right(mask0_cols, mask1_cols, x0_cols, x1_cols, (a2,))
-    send, b2 = chosen(diag, passed1, a1, (b2,), (near0, right0))
+    middle = b2.shape[0] // 2
+    send, top2, low2 = chosen(
+        diag, (passed1,), a1, (piece(b2, 0, middle), piece(b2, middle)), (near0, right0)
+    )
     near1 = move(send, over_z)
-    passed2 = move(b2, over_y)
+    passed2 = (move(top2, over_y), move(low2, over_y))
     far0 = move(near0, over_y)
-    send, a1 = chosen(diag, passed2, a2, (a1,), (far0, near1))
+    send, a1 = chosen(diag, passed2, a2, (piece(a1),), (far0, near1))
     near2 = move(send, over_z)
     got1 = move(a1, over_y)
     far1 = move(near1, over_y)
@@ -455,18 +457,18 @@
     back = move(coded, over_z)
     far2 = move(near2, over_y)
     sums = own(parts(joint, a1, b1), parts(near0, got1, passed1))
-    coded, rest, mark = partials(
+    coded, *rest, mark = partials(
         (piece(near2), piece(far2)),
         (piece(far2), piece(near2)),
-        given=(piece(a2), piece(near1, 0, all_rows // 4)),
+        given=(piece(a2, 0, middle), piece(a2, middle), piece(near1, 0, all_rows // 4)),
         gates=sums[:1],
     )
     (mark,) = handed_on((mark,), (back,))
     mark = move(mark, in_chip)
     outs = finished(keep, *sums, back, (), 0, all_rows)
     back = move(coded, over_z)
-    got2 = move(rest, over_y)
-    sums = own((piece(a2), piece(b2)), (piece(got2), piece(passed2)))
+    got2 = [move(part, over_y) for part in rest]
+    sums = own((piece(a2), piece(b2)), (*map(piece, got2), *map(piece, passed2)))
     return tuple(finished(keep, *sums, back, outs, split, all_rows, after=(mark,)))
 
 

time: 106 us -> 106 us (level)
  waiting for transfers between devices: 59.4 us -> 56.3 us
  starting transfers between devices: 12 us -> 14.5 us
    ppermute x13 -> x15, waiting for transfers between devices: 59.4 us -> 56.3 us  [move(): return lax.ppermute(values, ('row', 'col'), pairs)]
    ppermute x13 -> x15, starting transfers between devices: 12 us -> 14.5 us  [move(): return lax.ppermute(values, ('row', 'col'), pairs)]
  transfers between devices with their start and end apart: 13 -> 15, of which waited for: 10 -> 10; matrix products, arithmetic and copies ran while one was open for 0% -> 0% of each run, Pallas kernels for 26% -> 27%
where the time goes in v13:
time: 106 us; the launch traced here: 105 us
  waiting for transfers between devices  56.3 us (53%)
  Pallas kernels  32.5 us (31%)
  starting transfers between devices  14.5 us (14%)
  local copies, waits for them, and re-layouts  1.2 us (1%)
    ppermute x15, waiting for transfers between devices, move(): return lax.ppermute(values, ('row', 'col'), pairs)  56.3 us
    ppermute x15, starting transfers between devices, move(): return lax.ppermute(values, ('row', 'col'), pairs)  14.5 us
    pallas_call x2, Pallas kernels, partial_products(): pl.pallas_call(functools.partial(partial_kernel, one, other, len(arrays),...  9.5 us
    pallas_call x2, Pallas kernels, local_products(): pl.pallas_call(functools.partial(local_kernel, one, other), grid=(columns...  8.45 us
    pallas_call x1, Pallas kernels, masked_right(): pl.pallas_call(right_kernel, grid=(depth // tall,), in_specs=[SM(), SM(),...  6.97 us
    pallas_call x2, Pallas kernels, masked_chunks(): pl.pallas_call(functools.partial(chunk_kernel, spans, int(stacked), panel...  3.89 us
    pallas_call x2, Pallas kernels, finished(): pl.pallas_call(functools.partial(finish_kernel, start, [cut for _, *cut i...  2.83 us
  transfers between devices with their start and end apart: 15, of which 10 were waited for; matrix products, arithmetic and copies ran while one was open for 0% of the time, Pallas kernels for 27%

profile of v13, /device:TPU:0, one launch (start us, length us, event | category | flops | bytes accessed | tf_op | source)
XLA Modules:
  0.0 105.3 jit_solution(5510949682420612532)
XLA Ops:
  0.7 2.4 %left_chunks.2 = (bf16[64,2048]{1,0:T(8,128)(2,1)}, bf16[96,2048]{1,0:T(8,128)(2,1)}, bf16[96,2048]{1,0:T(8,128)(2,1)}) custom-call(s32[1]{0:T(128)} %bitcast.1.refs_0_, s32[2,128]{1,0:T(2,128)} %refs_1_.3, s32[2,128]{1,0:T(2,128)} %refs_2_.3, bf16[256,16384]{1,0:T(8,128)(2,1)} %refs_3_.3, bf16[256,16384]{1,0:T(8,128)(2,1)} %refs_4_.3), custom_call_target="tpu_custom_call" | custom-call | bytes 32768 | tf_op jit(solution)/shard_map/left_chunks/pallas_call | solution.py:80
  3.0 3.0 %collective-permute-start.1 = (bf16[96,2048]{1,0:T(8,128)(2,1)}, bf16[96,2048]{1,0:T(8,128)(2,1)S(1)}, u32[]{:S(2)}, u32[]{:S(2)}) collective-permute-start(bf16[96,2048]{1,0:T(8,128)(2,1)} %get-tuple-element.31.refs_2_), channel_id=1, source_target_pairs={{0,1},{1,0},{2,3},{3,2},{4,5},{5,4},{6,7},{7,6},{8,9},{9,8},{10,11... | collective-permute-start | bytes 1179656 | tf_op jit(solution)/shard_map/ppermute | solution.py:423
  7.1 1.5 %left_chunks.3 = (bf16[128,2048]{1,0:T(8,128)(2,1)S(1)}, bf16[128,2048]{1,0:T(8,128)(2,1)S(1)}) custom-call(s32[1]{0:T(128)} %bitcast.1.refs_0_, s32[2,128]{1,0:T(2,128)S(1)} %copy-done.7, s32[2,128]{1,0:T(2,128)S(1)} %copy-done.8, bf16[256,16384]{1,0:T(8,128)(2,1)} %refs_3_.3, bf16[256,16384]{1,0:T(8,128)(2,1)} %refs_4_.3, bf16[96,2048]{1,0:T(8,128)(2,1)S(1)} %copy-done.2), custom_call_target="tpu_custom_call" | custom-call | bytes 32768 | tf_op jit(solution)/shard_map/left_chunks/pallas_call | solution.py:80
  8.9 7.0 %right_panels.1 = (bf16[2048,768]{1,0:T(8,128)(2,1)S(1)}, bf16[2048,768]{1,0:T(8,128)(2,1)}) custom-call(s32[16,6]{1,0:T(8,128)S(1)} %copy.13.mask0, s32[16,6]{1,0:T(8,128)S(1)} %copy.14.mask1, bf16[2048,768]{1,0:T(8,128)(2,1)} %x0.1, bf16[2048,768]{1,0:T(8,128)(2,1)} %x1.1, bf16[128,2048]{1,0:T(8,128)(2,1)S(1)} %get-tuple-element.27.rest_0_.refs_4_.refs_2_.refs_3_.refs_0_), custom_call_target="tpu_custom_call" | custom-call | bytes 196608 | tf_op jit(solution)/shard_map/right_panels/pallas_call | solution.py:178
  15.8 4.7 %collective-permute-done.refs_0_.refs_3_ = bf16[64,2048]{1,0:T(8,128)(2,1)S(1)} collective-permute-done((bf16[64,2048]{1,0:T(8,128)(2,1)}, bf16[64,2048]{1,0:T(8,128)(2,1)S(1)}, u32[]{:S(2)}, u32[]{:S(2)}) %collective-permute-start) | collective-permute-done | bytes 262176 | tf_op jit(solution)/shard_map/ppermute | solution.py:423
  20.8 3.3 %collective-permute-start.2 = (bf16[96,2048]{1,0:T(8,128)(2,1)S(1)}, bf16[96,2048]{1,0:T(8,128)(2,1)S(1)}, u32[]{:S(2)}, u32[]{:S(2)}) collective-permute-start(bf16[96,2048]{1,0:T(8,128)(2,1)S(1)} %get-tuple-element.33), channel_id=1, source_target_pairs={{0,16},{1,17},{2,18},{3,19},{4,20},{5,21},{6,22},{7,23},{8,24},{9,... | collective-permute-start | bytes 1179656 | tf_op jit(solution)/shard_map/ppermute | solution.py:423
  24.2 2.0 %collective-permute-start.5 = (bf16[64,2048]{1,0:T(8,128)(2,1)S(1)}, bf16[64,2048]{1,0:T(8,128)(2,1)S(1)}, u32[]{:S(2)}, u32[]{:S(2)}) collective-permute-start(bf16[64,2048]{1,0:T(8,128)(2,1)S(1)} %get-tuple-element.34), channel_id=1, source_target_pairs={{0,1},{1,0},{2,3},{3,2},{4,5},{5,4},{6,7},{7,6},{8,9},{9,8},{10,11... | collective-permute-start | bytes 786440 | tf_op jit(solution)/shard_map/ppermute | solution.py:423
  26.2 7.2 %collective-permute-done.4.refs_3_.refs_0_ = bf16[64,2048]{1,0:T(8,128)(2,1)S(1)} collective-permute-done((bf16[64,2048]{1,0:T(8,128)(2,1)S(1)}, bf16[64,2048]{1,0:T(8,128)(2,1)S(1)}, u32[]{:S(2)}, u32[]{:S(2)}) %collective-permute-start.4) | collective-permute-done | bytes 262176 | tf_op jit(solution)/shard_map/ppermute | solution.py:423
  33.4 5.6 %collective-permute-done.5.refs_2_.refs_4_ = bf16[64,2048]{1,0:T(8,128)(2,1)S(1)} collective-permute-done((bf16[64,2048]{1,0:T(8,128)(2,1)S(1)}, bf16[64,2048]{1,0:T(8,128)(2,1)S(1)}, u32[]{:S(2)}, u32[]{:S(2)}) %collective-permute-start.5) | collective-permute-done | bytes 262176 | tf_op jit(solution)/shard_map/ppermute | solution.py:423
  39.0 3.3 %collective-permute-done.6.refs_3_.refs_5_ = bf16[64,2048]{1,0:T(8,128)(2,1)S(1)} collective-permute-done((bf16[64,2048]{1,0:T(8,128)(2,1)S(1)}, bf16[64,2048]{1,0:T(8,128)(2,1)S(1)}, u32[]{:S(2)}, u32[]{:S(2)}) %collective-permute-start.6) | collective-permute-done | bytes 262176 | tf_op jit(solution)/shard_map/ppermute | solution.py:423
  43.0 1.5 %collective-permute-start.3 = (bf16[96,2048]{1,0:T(8,128)(2,1)S(1)}, bf16[96,2048]{1,0:T(8,128)(2,1)S(1)}, u32[]{:S(2)}, u32[]{:S(2)}) collective-permute-start(bf16[96,2048]{1,0:T(8,128)(2,1)S(1)} %collective-permute-done.2.refs_1_.refs_4_), channel_id=1, source_target_pairs={{0,1},{1,0},{2,3},{3,2},{4,5},{5,4},{6,7},{7,6},{8,9},{9,8},{10,11... | collective-permute-start | bytes 1179656 | tf_op jit(solution)/shard_map/ppermute | solution.py:423
  45.0 10.0 %collective-permute-done.3.refs_2_ = bf16[96,2048]{1,0:T(8,128)(2,1)S(1)} collective-permute-done((bf16[96,2048]{1,0:T(8,128)(2,1)S(1)}, bf16[96,2048]{1,0:T(8,128)(2,1)S(1)}, u32[]{:S(2)}, u32[]{:S(2)}) %collective-permute-start.3) | collective-permute-done | bytes 393248 | tf_op jit(solution)/shard_map/ppermute | solution.py:423
  55.0 4.7 %partial_products.2.refs_0_ = s16[1552,128]{1,0:T(8,128)(2,1)S(1)} custom-call(s32[1]{0:T(128)} %bitcast.diag, bf16[2048,768]{1,0:T(8,128)(2,1)S(1)} %get-tuple-element.28.refs_1_.right0, bf16[2048,768]{1,0:T(8,128)(2,1)} %get-tuple-element.29.right1, bf16[64,2048]{1,0:T(8,128)(2,1)S(1)} %collective-permute-done.refs_0_.refs_3_, ...), custom_call_target="tpu_custom_call" | custom-call | flops 18874368 | bytes 114688 | tf_op jit(solution)/shard_map/partial_products/pallas_call | solution.py:314
  60.2 6.2 %collective-permute-done.7.refs_1_ = bf16[128,2048]{1,0:T(8,128)(2,1)S(1)} collective-permute-done((bf16[128,2048]{1,0:T(8,128)(2,1)S(1)}, bf16[128,2048]{1,0:T(8,128)(2,1)S(1)}, u32[]{:S(2)}, u32[]{:S(2)}) %collective-permute-start.7) | collective-permute-done | bytes 524320 | tf_op jit(solution)/shard_map/ppermute | solution.py:423
  66.6 1.3 %collective-permute-start.9 = (bf16[128,2048]{1,0:T(8,128)(2,1)S(1)}, bf16[128,2048]{1,0:T(8,128)(2,1)S(1)}, u32[]{:S(2)}, u32[]{:S(2)}) collective-permute-start(bf16[128,2048]{1,0:T(8,128)(2,1)S(1)} %get-tuple-element.38.refs_0_), channel_id=1, source_target_pairs={{0,1},{1,0},{2,3},{3,2},{4,5},{5,4},{6,7},{7,6},{8,9},{9,8},{10,11... | collective-permute-start | bytes 1572872 | tf_op jit(solution)/shard_map/ppermute | solution.py:423
  68.0 4.5 %own_products.2 = (f32[128,768]{1,0:T(8,128)S(1)}, f32[128,768]{1,0:T(8,128)S(1)}) custom-call(s32[1]{0:T(128)} %bitcast.diag, bf16[2048,768]{1,0:T(8,128)(2,1)S(1)} %get-tuple-element.28.refs_1_.right0, bf16[2048,768]{1,0:T(8,128)(2,1)} %get-tuple-element.29.right1, bf16[64,2048]{1,0:T(8,128)(2,1)S(1)} %copy-done.5, ...), custom_call_target="tpu_custom_call" | custom-call | flops 18874368 | bytes 131072 | tf_op jit(solution)/shard_map/own_products/pallas_call | solution.py:249
  72.5 6.2 %collective-permute-done.9.refs_1_ = bf16[128,2048]{1,0:T(8,128)(2,1)S(1)} collective-permute-done((bf16[128,2048]{1,0:T(8,128)(2,1)S(1)}, bf16[128,2048]{1,0:T(8,128)(2,1)S(1)}, u32[]{:S(2)}, u32[]{:S(2)}) %collective-permute-start.9) | collective-permute-done | bytes 524320 | tf_op jit(solution)/shard_map/ppermute | solution.py:423
  78.8 4.8 %partial_products.3 = (s16[1552,128]{1,0:T(8,128)(2,1)S(1)}, bf16[64,2048]{1,0:T(8,128)(2,1)S(1)}, bf16[64,2048]{1,0:T(8,128)(2,1)S(1)}, bf16[64,2048]{1,0:T(8,128)(2,1)S(1)}) custom-call(s32[1]{0:T(128)} %bitcast.diag, bf16[2048,768]{1,0:T(8,128)(2,1)} %copy-done, bf16[2048,768]{1,0:T(8,128)(2,1)} %get-tuple-element.29.right1, ...), custom_call_target="tpu_custom_call" | custom-call | flops 18874368 | bytes 114688 | tf_op jit(solution)/shard_map/partial_products/pallas_call | solution.py:314
  83.6 1.8 %collective-permute-start.11 = (bf16[64,2048]{1,0:T(8,128)(2,1)S(1)}, bf16[64,2048]{1,0:T(8,128)(2,1)S(1)}, u32[]{:S(2)}, u32[]{:S(2)}) collective-permute-start(bf16[64,2048]{1,0:T(8,128)(2,1)S(1)} %get-tuple-element.41), channel_id=1, source_target_pairs={{0,1},{1,0},{2,3},{3,2},{4,5},{5,4},{6,7},{7,6},{8,9},{9,8},{10,11... | collective-permute-start | bytes 786440 | tf_op jit(solution)/shard_map/ppermute | solution.py:423
  85.7 9.9 %collective-permute-done.13.coded.refs_1_ = s16[1552,128]{1,0:T(8,128)(2,1)S(1)} collective-permute-done((s16[1552,128]{1,0:T(8,128)(2,1)S(1)}, s16[1552,128]{1,0:T(8,128)(2,1)S(1)}, u32[]{:S(2)}, u32[]{:S(2)}) %collective-permute-start.13) | collective-permute-done | bytes 397344 | tf_op jit(solution)/shard_map/ppermute | solution.py:423
  95.8 1.4 %finish.2 = (bf16[256,768]{1,0:T(8,128)(2,1)}, bf16[256,768]{1,0:T(8,128)(2,1)}) custom-call(s32[2,6]{1,0:T(2,128)S(1)} %copy-done.6, s16[1552,128]{1,0:T(8,128)(2,1)S(1)} %collective-permute-done.13.coded.refs_1_, f32[128,768]{1,0:T(8,128)S(1)} %get-tuple-element.39.refs_5_.square, f32[128,768]{1,0:T(8,128)S(1)} %get-tuple-element.46.tangent), custom_call_target="tpu_custom_call" | custom-call | bytes 24576 | tf_op jit(solution)/shard_map/finish/pallas_call | solution.py:378
  97.2 3.9 %own_products.3 = (f32[128,768]{1,0:T(8,128)S(1)}, f32[128,768]{1,0:T(8,128)S(1)}) custom-call(s32[1]{0:T(128)} %bitcast.diag, bf16[2048,768]{1,0:T(8,128)(2,1)S(1)} %copy-done.1, bf16[2048,768]{1,0:T(8,128)(2,1)} %get-tuple-element.29.right1, bf16[128,2048]{1,0:T(8,128)(2,1)S(1)} %get-tuple-element.27.rest_0_.refs_4_.refs_2_.refs_3_.refs_0_, ...), custom_call_target="tpu_custom_call" | custom-call | flops 18874368 | bytes 131072 | tf_op jit(solution)/shard_map/own_products/pallas_call | solution.py:249
  101.2 2.7 %collective-permute-done.10.coded = s16[1552,128]{1,0:T(8,128)(2,1)S(1)} collective-permute-done((s16[1552,128]{1,0:T(8,128)(2,1)S(1)}, s16[1552,128]{1,0:T(8,128)(2,1)S(1)}, u32[]{:S(2)}, u32[]{:S(2)}) %collective-permute-start.10) | collective-permute-done | bytes 397344 | tf_op jit(solution)/shard_map/ppermute | solution.py:423
  103.9 1.4 %finish.3 = (bf16[256,768]{1,0:T(8,128)(2,1)}, bf16[256,768]{1,0:T(8,128)(2,1)}) custom-call(s32[2,6]{1,0:T(2,128)S(1)} %copy-done.6, s16[1552,128]{1,0:T(8,128)(2,1)S(1)} %collective-permute-done.10.coded, f32[128,768]{1,0:T(8,128)S(1)} %get-tuple-element.43.square, ...), custom_call_target="tpu_custom_call", output_to_operand_aliasing={{0}: (4, {}), {1}: (5, {})} | custom-call | bytes 24576 | tf_op jit(solution)/shard_map/finish/pallas_call | solution.py:378
  (43 shorter events, 4.0 us)
Async XLA Ops:
  0.6 5.5 %copy-start.7 = (s32[2,128]{1,0:T(2,128)S(1)}, s32[2,128]{1,0:T(2,128)}, u32[]{:S(2)}) copy-start(s32[2,128]{1,0:T(2,128)} %refs_1_.3) | copy-start | bytes 3076
  0.7 5.5 %copy-start.8 = (s32[2,128]{1,0:T(2,128)S(1)}, s32[2,128]{1,0:T(2,128)}, u32[]{:S(2)}) copy-start(s32[2,128]{1,0:T(2,128)} %refs_2_.3) | copy-start | bytes 3076
  3.0 17.5 %collective-permute-start.1 = (bf16[96,2048]{1,0:T(8,128)(2,1)}, bf16[96,2048]{1,0:T(8,128)(2,1)S(1)}, u32[]{:S(2)}, u32[]{:S(2)}) collective-permute-start(bf16[96,2048]{1,0:T(8,128)(2,1)} %get-tuple-element.31.refs_2_), channel_id=1, source_target_pairs={{0,1},{1,0},{2,3},{3,2},{4,5},{5,4},{6,7},{7,6},{8,9},{9,8},{10,11... | collective-permute-start | bytes 1179656 | tf_op jit(solution)/shard_map/ppermute | solution.py:423
  6.1 14.5 %collective-permute-start = (bf16[64,2048]{1,0:T(8,128)(2,1)}, bf16[64,2048]{1,0:T(8,128)(2,1)S(1)}, u32[]{:S(2)}, u32[]{:S(2)}) collective-permute-start(bf16[64,2048]{1,0:T(8,128)(2,1)} %get-tuple-element.30.refs_0_), channel_id=1, source_target_pairs={{0,1},{1,17},{2,3},{3,19},{4,5},{5,21},{6,7},{7,23},{8,9},{9,25},{... | collective-permute-start | bytes 786440 | tf_op jit(solution)/shard_map/ppermute | solution.py:423
  7.1 1.6 %copy-start.10 = (s32[16,6]{0,1:T(8,128)S(1)}, s32[16,6]{0,1:T(8,128)}, u32[]{:S(2)}) copy-start(s32[16,6]{0,1:T(8,128)} %param.16) | copy-start | bytes 1156
  8.9 11.7 %copy-start.3 = (bf16[96,2048]{1,0:T(8,128)(2,1)S(1)}, bf16[96,2048]{1,0:T(8,128)(2,1)}, u32[]{:S(2)}) copy-start(bf16[96,2048]{1,0:T(8,128)(2,1)} %get-tuple-element.26.refs_5_.refs_3_) | copy-start | bytes 1179652
  15.8 52.1 %copy-start = (bf16[2048,768]{1,0:T(8,128)(2,1)}, bf16[2048,768]{1,0:T(8,128)(2,1)S(1)}, u32[]{:S(2)}) copy-start(bf16[2048,768]{1,0:T(8,128)(2,1)S(1)} %get-tuple-element.28.refs_1_.right0) | copy-start | bytes 9437188
  20.8 21.5 %collective-permute-start.2 = (bf16[96,2048]{1,0:T(8,128)(2,1)S(1)}, bf16[96,2048]{1,0:T(8,128)(2,1)S(1)}, u32[]{:S(2)}, u32[]{:S(2)}) collective-permute-start(bf16[96,2048]{1,0:T(8,128)(2,1)S(1)} %get-tuple-element.33), channel_id=1, source_target_pairs={{0,16},{1,17},{2,18},{3,19},{4,20},{5,21},{6,22},{7,23},{8,24},{9,... | collective-permute-start | bytes 1179656 | tf_op jit(solution)/shard_map/ppermute | solution.py:423
  24.2 9.2 %collective-permute-start.4 = (bf16[64,2048]{1,0:T(8,128)(2,1)S(1)}, bf16[64,2048]{1,0:T(8,128)(2,1)S(1)}, u32[]{:S(2)}, u32[]{:S(2)}) collective-permute-start(bf16[64,2048]{1,0:T(8,128)(2,1)S(1)} %collective-permute-done.refs_0_.refs_3_), channel_id=1, source_target_pairs={{0,1},{1,0},{2,3},{3,2},{4,5},{5,4},{6,7},{7,6},{8,9},{9,8},{10,11... | collective-permute-start | bytes 786440 | tf_op jit(solution)/shard_map/ppermute | solution.py:423
  24.2 14.9 %collective-permute-start.5 = (bf16[64,2048]{1,0:T(8,128)(2,1)S(1)}, bf16[64,2048]{1,0:T(8,128)(2,1)S(1)}, u32[]{:S(2)}, u32[]{:S(2)}) collective-permute-start(bf16[64,2048]{1,0:T(8,128)(2,1)S(1)} %get-tuple-element.34), channel_id=1, source_target_pairs={{0,1},{1,0},{2,3},{3,2},{4,5},{5,4},{6,7},{7,6},{8,9},{9,8},{10,11... | collective-permute-start | bytes 786440 | tf_op jit(solution)/shard_map/ppermute | solution.py:423
  26.2 16.1 %collective-permute-start.6 = (bf16[64,2048]{1,0:T(8,128)(2,1)S(1)}, bf16[64,2048]{1,0:T(8,128)(2,1)S(1)}, u32[]{:S(2)}, u32[]{:S(2)}) collective-permute-start(bf16[64,2048]{1,0:T(8,128)(2,1)S(1)} %get-tuple-element.35), channel_id=1, source_target_pairs={{0,1},{1,0},{2,3},{3,2},{4,5},{5,4},{6,7},{7,6},{8,9},{9,8},{10,11... | collective-permute-start | bytes 786440 | tf_op jit(solution)/shard_map/ppermute | solution.py:423
  42.6 23.8 %collective-permute-start.7 = (bf16[128,2048]{1,0:T(8,128)(2,1)S(1)}, bf16[128,2048]{1,0:T(8,128)(2,1)S(1)}, u32[]{:S(2)}, u32[]{:S(2)}) collective-permute-start(bf16[128,2048]{1,0:T(8,128)(2,1)S(1)} %get-tuple-element.36), channel_id=1, source_target_pairs={{0,16},{1,17},{2,18},{3,19},{4,20},{5,21},{6,22},{7,23},{8,24},{9,... | collective-permute-start | bytes 1572872 | tf_op jit(solution)/shard_map/ppermute | solution.py:423
  43.0 12.1 %collective-permute-start.3 = (bf16[96,2048]{1,0:T(8,128)(2,1)S(1)}, bf16[96,2048]{1,0:T(8,128)(2,1)S(1)}, u32[]{:S(2)}, u32[]{:S(2)}) collective-permute-start(bf16[96,2048]{1,0:T(8,128)(2,1)S(1)} %collective-permute-done.2.refs_1_.refs_4_), channel_id=1, source_target_pairs={{0,1},{1,0},{2,3},{3,2},{4,5},{5,4},{6,7},{7,6},{8,9},{9,8},{10,11... | collective-permute-start | bytes 1179656 | tf_op jit(solution)/shard_map/ppermute | solution.py:423
  44.5 15.7 %collective-permute-start.8 = (bf16[96,2048]{1,0:T(8,128)(2,1)S(1)}, bf16[96,2048]{1,0:T(8,128)(2,1)S(1)}, u32[]{:S(2)}, u32[]{:S(2)}) collective-permute-start(bf16[96,2048]{1,0:T(8,128)(2,1)S(1)} %get-tuple-element.37.refs_1_), channel_id=1, source_target_pairs={{0,1},{1,0},{2,3},{3,2},{4,5},{5,4},{6,7},{7,6},{8,9},{9,8},{10,11... | collective-permute-start | bytes 1179656 | tf_op jit(solution)/shard_map/ppermute | solution.py:423
  55.0 12.9 %copy-start.4 = (bf16[96,2048]{1,0:T(8,128)(2,1)S(1)}, bf16[96,2048]{1,0:T(8,128)(2,1)}, u32[]{:S(2)}) copy-start(bf16[96,2048]{1,0:T(8,128)(2,1)} %get-tuple-element.31.refs_2_) | copy-start | bytes 1179652
  55.0 12.9 %copy-start.5 = (bf16[64,2048]{1,0:T(8,128)(2,1)S(1)}, bf16[64,2048]{1,0:T(8,128)(2,1)}, u32[]{:S(2)}) copy-start(bf16[64,2048]{1,0:T(8,128)(2,1)} %get-tuple-element.30.refs_0_) | copy-start | bytes 786436
  66.6 12.2 %collective-permute-start.9 = (bf16[128,2048]{1,0:T(8,128)(2,1)S(1)}, bf16[128,2048]{1,0:T(8,128)(2,1)S(1)}, u32[]{:S(2)}, u32[]{:S(2)}) collective-permute-start(bf16[128,2048]{1,0:T(8,128)(2,1)S(1)} %get-tuple-element.38.refs_0_), channel_id=1, source_target_pairs={{0,1},{1,0},{2,3},{3,2},{4,5},{5,4},{6,7},{7,6},{8,9},{9,8},{10,11... | collective-permute-start | bytes 1572872 | tf_op jit(solution)/shard_map/ppermute | solution.py:423
  67.9 27.7 %collective-permute-start.13 = (s16[1552,128]{1,0:T(8,128)(2,1)S(1)}, s16[1552,128]{1,0:T(8,128)(2,1)S(1)}, u32[]{:S(2)}, u32[]{:S(2)}) collective-permute-start(s16[1552,128]{1,0:T(8,128)(2,1)S(1)} %get-tuple-element.45), channel_id=1, source_target_pairs={{0,16},{1,17},{2,18},{3,19},{4,20},{5,21},{6,22},{7,23},{8,24},{9,... | collective-permute-start | bytes 1191944 | tf_op jit(solution)/shard_map/ppermute | solution.py:423
  78.8 17.0 %copy-start.6 = (s32[2,6]{1,0:T(2,128)S(1)}, s32[2,6]{1,0:T(2,128)}, u32[]{:S(2)}) copy-start(s32[2,6]{1,0:T(2,128)} %keep.3) | copy-start | bytes 148
  78.8 18.5 %copy-start.1 = (bf16[2048,768]{1,0:T(8,128)(2,1)S(1)}, bf16[2048,768]{1,0:T(8,128)(2,1)}, u32[]{:S(2)}) copy-start(bf16[2048,768]{1,0:T(8,128)(2,1)} %copy-done) | copy-start | bytes 9437188
  83.5 20.4 %collective-permute-start.10 = (s16[1552,128]{1,0:T(8,128)(2,1)S(1)}, s16[1552,128]{1,0:T(8,128)(2,1)S(1)}, u32[]{:S(2)}, u32[]{:S(2)}) collective-permute-start(s16[1552,128]{1,0:T(8,128)(2,1)S(1)} %get-tuple-element.40), channel_id=1, source_target_pairs={{0,16},{1,17},{2,18},{3,19},{4,20},{5,21},{6,22},{7,23},{8,24},{9,... | collective-permute-start | bytes 1191944 | tf_op jit(solution)/shard_map/ppermute | solution.py:423
  83.6 13.6 %collective-permute-start.11 = (bf16[64,2048]{1,0:T(8,128)(2,1)S(1)}, bf16[64,2048]{1,0:T(8,128)(2,1)S(1)}, u32[]{:S(2)}, u32[]{:S(2)}) collective-permute-start(bf16[64,2048]{1,0:T(8,128)(2,1)S(1)} %get-tuple-element.41), channel_id=1, source_target_pairs={{0,1},{1,0},{2,3},{3,2},{4,5},{5,4},{6,7},{7,6},{8,9},{9,8},{10,11... | collective-permute-start | bytes 786440 | tf_op jit(solution)/shard_map/ppermute | solution.py:423
  85.4 11.8 %collective-permute-start.12 = (bf16[64,2048]{1,0:T(8,128)(2,1)S(1)}, bf16[64,2048]{1,0:T(8,128)(2,1)S(1)}, u32[]{:S(2)}, u32[]{:S(2)}) collective-permute-start(bf16[64,2048]{1,0:T(8,128)(2,1)S(1)} %get-tuple-element.42), channel_id=1, source_target_pairs={{0,1},{1,0},{2,3},{3,2},{4,5},{5,4},{6,7},{7,6},{8,9},{9,8},{10,11... | collective-permute-start | bytes 786440 | tf_op jit(solution)/shard_map/ppermute | solution.py:423
  95.7 5.5 %collective-permute-start.14 = (bf16[64,2048]{1,0:T(8,128)(2,1)S(1)}, bf16[64,2048]{1,0:T(8,128)(2,1)S(1)}, u32[]{:S(2)}, u32[]{:S(2)}) collective-permute-start(bf16[64,2048]{1,0:T(8,128)(2,1)S(1)} %handed_on.3), channel_id=1, source_target_pairs={{0,2},{1,3},{2,0},{3,1},{4,6},{5,7},{6,4},{7,5},{8,10},{9,11},{10,... | collective-permute-start | bytes 786440 | tf_op jit(solution)/shard_map/ppermute | solution.py:423
  (2 other events, 2.5 us)

commit v14 on v13

--- a/solution.py
+++ b/solution.py
@@ -403,8 +403,8 @@
     half = row_index // group
     diag = (half == lax.axis_index("col")).astype(jnp.int32).reshape(1)
     place = (row_index % group).astype(jnp.int32).reshape(1)
-    direct = all_rows // 8
-    split = all_rows // 2
+    direct = all_rows // 16
+    split = all_rows * 7 // 16
     wide = 256
 
     def device(h, q, c):
@@ -441,7 +441,7 @@
     near0 = move(joint, ring)
     a2, b2 = chunks(((split, all_rows),), False, VMEM_BYTES, (a1,))
     right0, right1 = masked_right(mask0_cols, mask1_cols, x0_cols, x1_cols, (a2,))
-    middle = b2.shape[0] // 2
+    middle = b2.shape[0] // 32 * 16
     send, top2, low2 = chosen(
         diag, (passed1,), a1, (piece(b2, 0, middle), piece(b2, middle)), (near0, right0)
     )

time: 106 us -> 109 us (1.028)
  waiting for transfers between devices: 56.3 us -> 58.4 us
    ppermute x15, waiting for transfers between devices: 56.3 us -> 58.4 us  [move(): return lax.ppermute(values, ('row', 'col'), pairs)]
  transfers between devices with their start and end apart: 15 -> 15, of which waited for: 10 -> 8; matrix products, arithmetic and copies ran while one was open for 0% -> 0% of each run, Pallas kernels for 27% -> 26%
where the time goes in v14:
time: 109 us
  waiting for transfers between devices  58.4 us (54%)
  Pallas kernels  33.1 us (30%)
  starting transfers between devices  15 us (14%)
  local copies, waits for them, and re-layouts  1.2 us (1%)
    ppermute x15, waiting for transfers between devices, move(): return lax.ppermute(values, ('row', 'col'), pairs)  58.4 us
    ppermute x15, starting transfers between devices, move(): return lax.ppermute(values, ('row', 'col'), pairs)  15 us
    pallas_call x2, Pallas kernels, partial_products(): pl.pallas_call(functools.partial(partial_kernel, one, other, len(arrays),...  9.4 us
    pallas_call x2, Pallas kernels, local_products(): pl.pallas_call(functools.partial(local_kernel, one, other), grid=(columns...  9.02 us
    pallas_call x1, Pallas kernels, masked_right(): pl.pallas_call(right_kernel, grid=(depth // tall,), in_specs=[SM(), SM(),...  6.99 us
    pallas_call x2, Pallas kernels, masked_chunks(): pl.pallas_call(functools.partial(chunk_kernel, spans, int(stacked), panel...  3.86 us
    pallas_call x2, Pallas kernels, finished(): pl.pallas_call(functools.partial(finish_kernel, start, [cut for _, *cut i...  2.84 us
  transfers between devices with their start and end apart: 15, of which 8 were waited for; matrix products, arithmetic and copies ran while one was open for 0% of the time, Pallas kernels for 26%

profile of v14, /device:TPU:0, one launch (start us, length us, event | category | flops | bytes accessed | tf_op | source)
XLA Modules:
  0.0 108.6 jit_solution(7089861840602963978)
XLA Ops:
  0.7 2.2 %left_chunks.2 = (bf16[32,2048]{1,0:T(8,128)(2,1)}, bf16[96,2048]{1,0:T(8,128)(2,1)}, bf16[96,2048]{1,0:T(8,128)(2,1)}) custom-call(s32[1]{0:T(128)} %bitcast.1.refs_0_, s32[2,128]{1,0:T(2,128)} %refs_1_.3, s32[2,128]{1,0:T(2,128)} %refs_2_.3, bf16[256,16384]{1,0:T(8,128)(2,1)} %refs_3_.3, bf16[256,16384]{1,0:T(8,128)(2,1)} %refs_4_.3), custom_call_target="tpu_custom_call" | custom-call | bytes 28672 | tf_op jit(solution)/shard_map/left_chunks/pallas_call | solution.py:80
  2.9 3.0 %collective-permute-start.1 = (bf16[96,2048]{1,0:T(8,128)(2,1)}, bf16[96,2048]{1,0:T(8,128)(2,1)S(1)}, u32[]{:S(2)}, u32[]{:S(2)}) collective-permute-start(bf16[96,2048]{1,0:T(8,128)(2,1)} %get-tuple-element.31.refs_2_), channel_id=1, source_target_pairs={{0,1},{1,0},{2,3},{3,2},{4,5},{5,4},{6,7},{7,6},{8,9},{9,8},{10,11... | collective-permute-start | bytes 1179656 | tf_op jit(solution)/shard_map/ppermute | solution.py:423
  6.0 1.0 copy-done.1
  7.0 1.6 %left_chunks.3 = (bf16[144,2048]{1,0:T(8,128)(2,1)S(1)}, bf16[144,2048]{1,0:T(8,128)(2,1)S(1)}) custom-call(s32[1]{0:T(128)} %bitcast.1.refs_0_, s32[2,128]{1,0:T(2,128)S(1)} %copy-done.6, s32[2,128]{1,0:T(2,128)S(1)} %copy-done.7, bf16[256,16384]{1,0:T(8,128)(2,1)} %refs_3_.3, bf16[256,16384]{1,0:T(8,128)(2,1)} %refs_4_.3, bf16[96,2048]{1,0:T(8,128)(2,1)S(1)} %copy-done.1), custom_call_target="tpu_custom_call" | custom-call | bytes 36864 | tf_op jit(solution)/shard_map/left_chunks/pallas_call | solution.py:80
  8.8 7.0 %right_panels.1 = (bf16[2048,768]{1,0:T(8,128)(2,1)S(1)}, bf16[2048,768]{1,0:T(8,128)(2,1)}) custom-call(s32[16,6]{1,0:T(8,128)S(1)} %copy.13.mask0, s32[16,6]{1,0:T(8,128)S(1)} %copy.14.mask1, bf16[2048,768]{1,0:T(8,128)(2,1)} %x0.1, bf16[2048,768]{1,0:T(8,128)(2,1)} %x1.1, bf16[144,2048]{1,0:T(8,128)(2,1)S(1)} %get-tuple-element.27.rest_0_.refs_4_.refs_2_.refs_3_.refs_0_), custom_call_target="tpu_custom_call" | custom-call | bytes 196608 | tf_op jit(solution)/shard_map/right_panels/pallas_call | solution.py:178
  15.8 1.6 %collective-permute-done.refs_0_.refs_3_ = bf16[32,2048]{1,0:T(8,128)(2,1)S(1)} collective-permute-done((bf16[32,2048]{1,0:T(8,128)(2,1)}, bf16[32,2048]{1,0:T(8,128)(2,1)S(1)}, u32[]{:S(2)}, u32[]{:S(2)}) %collective-permute-start) | collective-permute-done | bytes 131104 | tf_op jit(solution)/shard_map/ppermute | solution.py:423
  17.8 3.5 %collective-permute-start.2 = (bf16[96,2048]{1,0:T(8,128)(2,1)S(1)}, bf16[96,2048]{1,0:T(8,128)(2,1)S(1)}, u32[]{:S(2)}, u32[]{:S(2)}) collective-permute-start(bf16[96,2048]{1,0:T(8,128)(2,1)S(1)} %get-tuple-element.33), channel_id=1, source_target_pairs={{0,16},{1,17},{2,18},{3,19},{4,20},{5,21},{6,22},{7,23},{8,24},{9,... | collective-permute-start | bytes 1179656 | tf_op jit(solution)/shard_map/ppermute | solution.py:423
  21.3 2.0 %collective-permute-start.5 = (bf16[64,2048]{1,0:T(8,128)(2,1)S(1)}, bf16[64,2048]{1,0:T(8,128)(2,1)S(1)}, u32[]{:S(2)}, u32[]{:S(2)}) collective-permute-start(bf16[64,2048]{1,0:T(8,128)(2,1)S(1)} %get-tuple-element.34), channel_id=1, source_target_pairs={{0,1},{1,0},{2,3},{3,2},{4,5},{5,4},{6,7},{7,6},{8,9},{9,8},{10,11... | collective-permute-start | bytes 786440 | tf_op jit(solution)/shard_map/ppermute | solution.py:423
  23.4 14.7 %collective-permute-done.4.refs_3_.refs_0_ = bf16[32,2048]{1,0:T(8,128)(2,1)S(1)} collective-permute-done((bf16[32,2048]{1,0:T(8,128)(2,1)S(1)}, bf16[32,2048]{1,0:T(8,128)(2,1)S(1)}, u32[]{:S(2)}, u32[]{:S(2)}) %collective-permute-start.4) | collective-permute-done | bytes 131104 | tf_op jit(solution)/shard_map/ppermute | solution.py:423
  38.9 1.5 %collective-permute-start.3 = (bf16[96,2048]{1,0:T(8,128)(2,1)S(1)}, bf16[96,2048]{1,0:T(8,128)(2,1)S(1)}, u32[]{:S(2)}, u32[]{:S(2)}) collective-permute-start(bf16[96,2048]{1,0:T(8,128)(2,1)S(1)} %collective-permute-done.2.refs_1_.refs_4_), channel_id=1, source_target_pairs={{0,1},{1,0},{2,3},{3,2},{4,5},{5,4},{6,7},{7,6},{8,9},{9,8},{10,11... | collective-permute-start | bytes 1179656 | tf_op jit(solution)/shard_map/ppermute | solution.py:423
  40.9 10.0 %collective-permute-done.3.refs_2_ = bf16[96,2048]{1,0:T(8,128)(2,1)S(1)} collective-permute-done((bf16[96,2048]{1,0:T(8,128)(2,1)S(1)}, bf16[96,2048]{1,0:T(8,128)(2,1)S(1)}, u32[]{:S(2)}, u32[]{:S(2)}) %collective-permute-start.3) | collective-permute-done | bytes 393248 | tf_op jit(solution)/shard_map/ppermute | solution.py:423
  50.9 4.4 %partial_products.2.refs_0_ = s16[1360,128]{1,0:T(8,128)(2,1)S(1)} custom-call(s32[1]{0:T(128)} %bitcast.diag, bf16[2048,768]{1,0:T(8,128)(2,1)S(1)} %get-tuple-element.28.refs_1_.right0, bf16[2048,768]{1,0:T(8,128)(2,1)} %get-tuple-element.29.right1, bf16[32,2048]{1,0:T(8,128)(2,1)S(1)} %collective-permute-done.refs_0_.refs_3_, ...), custom_call_target="tpu_custom_call" | custom-call | flops 16515072 | bytes 112640 | tf_op jit(solution)/shard_map/partial_products/pallas_call | solution.py:314
  55.3 1.6 %collective-permute-done.8.refs_2_.refs_4_ = bf16[96,2048]{1,0:T(8,128)(2,1)S(1)} collective-permute-done((bf16[96,2048]{1,0:T(8,128)(2,1)S(1)}, bf16[96,2048]{1,0:T(8,128)(2,1)S(1)}, u32[]{:S(2)}, u32[]{:S(2)}) %collective-permute-start.8) | collective-permute-done | bytes 393248 | tf_op jit(solution)/shard_map/ppermute | solution.py:423
  56.9 9.2 %collective-permute-done.7.refs_1_ = bf16[144,2048]{1,0:T(8,128)(2,1)S(1)} collective-permute-done((bf16[144,2048]{1,0:T(8,128)(2,1)S(1)}, bf16[144,2048]{1,0:T(8,128)(2,1)S(1)}, u32[]{:S(2)}, u32[]{:S(2)}) %collective-permute-start.7) | collective-permute-done | bytes 589856 | tf_op jit(solution)/shard_map/ppermute | solution.py:423
  66.4 1.6 %collective-permute-start.9 = (bf16[144,2048]{1,0:T(8,128)(2,1)S(1)}, bf16[144,2048]{1,0:T(8,128)(2,1)S(1)}, u32[]{:S(2)}, u32[]{:S(2)}) collective-permute-start(bf16[144,2048]{1,0:T(8,128)(2,1)S(1)} %get-tuple-element.38.refs_0_), channel_id=1, source_target_pairs={{0,1},{1,0},{2,3},{3,2},{4,5},{5,4},{6,7},{7,6},{8,9},{9,8},{10,11... | collective-permute-start | bytes 1769480 | tf_op jit(solution)/shard_map/ppermute | solution.py:423
  68.0 4.3 %own_products.2 = (f32[112,768]{1,0:T(8,128)S(1)}, f32[112,768]{1,0:T(8,128)S(1)}) custom-call(s32[1]{0:T(128)} %bitcast.diag, bf16[2048,768]{1,0:T(8,128)(2,1)S(1)} %get-tuple-element.28.refs_1_.right0, bf16[2048,768]{1,0:T(8,128)(2,1)} %get-tuple-element.29.right1, bf16[32,2048]{1,0:T(8,128)(2,1)S(1)} %copy-done.4, ...), custom_call_target="tpu_custom_call" | custom-call | flops 16515072 | bytes 126976 | tf_op jit(solution)/shard_map/own_products/pallas_call | solution.py:249
  72.4 8.9 %collective-permute-done.9.refs_1_ = bf16[144,2048]{1,0:T(8,128)(2,1)S(1)} collective-permute-done((bf16[144,2048]{1,0:T(8,128)(2,1)S(1)}, bf16[144,2048]{1,0:T(8,128)(2,1)S(1)}, u32[]{:S(2)}, u32[]{:S(2)}) %collective-permute-start.9) | collective-permute-done | bytes 589856 | tf_op jit(solution)/shard_map/ppermute | solution.py:423
  81.3 5.0 %partial_products.3 = (s16[1744,128]{1,0:T(8,128)(2,1)S(1)}, bf16[64,2048]{1,0:T(8,128)(2,1)S(1)}, bf16[80,2048]{1,0:T(8,128)(2,1)S(1)}, bf16[64,2048]{1,0:T(8,128)(2,1)S(1)}) custom-call(s32[1]{0:T(128)} %bitcast.diag, bf16[2048,768]{1,0:T(8,128)(2,1)} %copy-done, bf16[2048,768]{1,0:T(8,128)(2,1)} %get-tuple-element.29.right1, ...), custom_call_target="tpu_custom_call" | custom-call | flops 21233664 | bytes 116736 | tf_op jit(solution)/shard_map/partial_products/pallas_call | solution.py:314
  86.4 1.8 %collective-permute-start.12 = (bf16[80,2048]{1,0:T(8,128)(2,1)S(1)}, bf16[80,2048]{1,0:T(8,128)(2,1)S(1)}, u32[]{:S(2)}, u32[]{:S(2)}) collective-permute-start(bf16[80,2048]{1,0:T(8,128)(2,1)S(1)} %get-tuple-element.42), channel_id=1, source_target_pairs={{0,1},{1,0},{2,3},{3,2},{4,5},{5,4},{6,7},{7,6},{8,9},{9,8},{10,11... | collective-permute-start | bytes 983048 | tf_op jit(solution)/shard_map/ppermute | solution.py:423
  88.6 1.4 %finish.2 = (bf16[256,768]{1,0:T(8,128)(2,1)}, bf16[256,768]{1,0:T(8,128)(2,1)}) custom-call(s32[2,6]{1,0:T(2,128)S(1)} %copy-done.5, s16[1360,128]{1,0:T(8,128)(2,1)S(1)} %collective-permute-done.13.coded.refs_1_, f32[112,768]{1,0:T(8,128)S(1)} %get-tuple-element.39.refs_5_.square, f32[112,768]{1,0:T(8,128)S(1)} %get-tuple-element.46.tangent), custom_call_target="tpu_custom_call" | custom-call | bytes 21504 | tf_op jit(solution)/shard_map/finish/pallas_call | solution.py:378
  90.0 10.6 %collective-permute-done.11.refs_2_ = bf16[64,2048]{1,0:T(8,128)(2,1)S(1)} collective-permute-done((bf16[64,2048]{1,0:T(8,128)(2,1)S(1)}, bf16[64,2048]{1,0:T(8,128)(2,1)S(1)}, u32[]{:S(2)}, u32[]{:S(2)}) %collective-permute-start.11) | collective-permute-done | bytes 262176 | tf_op jit(solution)/shard_map/ppermute | solution.py:423
  100.6 4.7 %own_products.3 = (f32[144,768]{1,0:T(8,128)S(1)}, f32[144,768]{1,0:T(8,128)S(1)}) custom-call(s32[1]{0:T(128)} %bitcast.diag, bf16[2048,768]{1,0:T(8,128)(2,1)} %copy-done, bf16[2048,768]{1,0:T(8,128)(2,1)} %get-tuple-element.29.right1, bf16[144,2048]{1,0:T(8,128)(2,1)S(1)} %get-tuple-element.27.rest_0_.refs_4_.refs_2_.refs_3_.refs_0_, ...), custom_call_target="tpu_custom_call" | custom-call | flops 21233664 | bytes 135168 | tf_op jit(solution)/shard_map/own_products/pallas_call | solution.py:249
  105.3 1.8 %collective-permute-done.10.coded = s16[1744,128]{1,0:T(8,128)(2,1)S(1)} collective-permute-done((s16[1744,128]{1,0:T(8,128)(2,1)S(1)}, s16[1744,128]{1,0:T(8,128)(2,1)S(1)}, u32[]{:S(2)}, u32[]{:S(2)}) %collective-permute-start.10) | collective-permute-done | bytes 446496 | tf_op jit(solution)/shard_map/ppermute | solution.py:423
  107.1 1.4 %finish.3 = (bf16[256,768]{1,0:T(8,128)(2,1)}, bf16[256,768]{1,0:T(8,128)(2,1)}) custom-call(s32[2,6]{1,0:T(2,128)S(1)} %copy-done.5, s16[1744,128]{1,0:T(8,128)(2,1)S(1)} %collective-permute-done.10.coded, f32[144,768]{1,0:T(8,128)S(1)} %get-tuple-element.43.square, ...), custom_call_target="tpu_custom_call", output_to_operand_aliasing={{0}: (4, {}), {1}: (5, {})} | custom-call | bytes 27648 | tf_op jit(solution)/shard_map/finish/pallas_call | solution.py:378
  (41 shorter events, 2.7 us)
Async XLA Ops:
  0.6 5.4 %copy-start.6 = (s32[2,128]{1,0:T(2,128)S(1)}, s32[2,128]{1,0:T(2,128)}, u32[]{:S(2)}) copy-start(s32[2,128]{1,0:T(2,128)} %refs_1_.3) | copy-start | bytes 3076
  0.7 5.4 %copy-start.7 = (s32[2,128]{1,0:T(2,128)S(1)}, s32[2,128]{1,0:T(2,128)}, u32[]{:S(2)}) copy-start(s32[2,128]{1,0:T(2,128)} %refs_2_.3) | copy-start | bytes 3076
  2.9 14.5 %collective-permute-start.1 = (bf16[96,2048]{1,0:T(8,128)(2,1)}, bf16[96,2048]{1,0:T(8,128)(2,1)S(1)}, u32[]{:S(2)}, u32[]{:S(2)}) collective-permute-start(bf16[96,2048]{1,0:T(8,128)(2,1)} %get-tuple-element.31.refs_2_), channel_id=1, source_target_pairs={{0,1},{1,0},{2,3},{3,2},{4,5},{5,4},{6,7},{7,6},{8,9},{9,8},{10,11... | collective-permute-start | bytes 1179656 | tf_op jit(solution)/shard_map/ppermute | solution.py:423
  6.0 11.5 %collective-permute-start = (bf16[32,2048]{1,0:T(8,128)(2,1)}, bf16[32,2048]{1,0:T(8,128)(2,1)S(1)}, u32[]{:S(2)}, u32[]{:S(2)}) collective-permute-start(bf16[32,2048]{1,0:T(8,128)(2,1)} %get-tuple-element.30.refs_0_), channel_id=1, source_target_pairs={{0,1},{1,17},{2,3},{3,19},{4,5},{5,21},{6,7},{7,23},{8,9},{9,25},{... | collective-permute-start | bytes 393224 | tf_op jit(solution)/shard_map/ppermute | solution.py:423
  7.0 1.6 %copy-start.8 = (s32[16,6]{0,1:T(8,128)S(1)}, s32[16,6]{0,1:T(8,128)}, u32[]{:S(2)}) copy-start(s32[16,6]{0,1:T(8,128)} %param.15) | copy-start | bytes 1156
  7.0 1.7 %copy-start.9 = (s32[16,6]{0,1:T(8,128)S(1)}, s32[16,6]{0,1:T(8,128)}, u32[]{:S(2)}) copy-start(s32[16,6]{0,1:T(8,128)} %param.16) | copy-start | bytes 1156
  8.8 8.6 %copy-start.2 = (bf16[96,2048]{1,0:T(8,128)(2,1)S(1)}, bf16[96,2048]{1,0:T(8,128)(2,1)}, u32[]{:S(2)}) copy-start(bf16[96,2048]{1,0:T(8,128)(2,1)} %get-tuple-element.26.refs_5_.refs_3_) | copy-start | bytes 1179652
  15.8 52.2 %copy-start = (bf16[2048,768]{1,0:T(8,128)(2,1)}, bf16[2048,768]{1,0:T(8,128)(2,1)S(1)}, u32[]{:S(2)}) copy-start(bf16[2048,768]{1,0:T(8,128)(2,1)S(1)} %get-tuple-element.28.refs_1_.right0) | copy-start | bytes 9437188
  17.8 20.2 %collective-permute-start.2 = (bf16[96,2048]{1,0:T(8,128)(2,1)S(1)}, bf16[96,2048]{1,0:T(8,128)(2,1)S(1)}, u32[]{:S(2)}, u32[]{:S(2)}) collective-permute-start(bf16[96,2048]{1,0:T(8,128)(2,1)S(1)} %get-tuple-element.33), channel_id=1, source_target_pairs={{0,16},{1,17},{2,18},{3,19},{4,20},{5,21},{6,22},{7,23},{8,24},{9,... | collective-permute-start | bytes 1179656 | tf_op jit(solution)/shard_map/ppermute | solution.py:423
  21.3 16.7 %collective-permute-start.6 = (bf16[80,2048]{1,0:T(8,128)(2,1)S(1)}, bf16[80,2048]{1,0:T(8,128)(2,1)S(1)}, u32[]{:S(2)}, u32[]{:S(2)}) collective-permute-start(bf16[80,2048]{1,0:T(8,128)(2,1)S(1)} %get-tuple-element.35), channel_id=1, source_target_pairs={{0,1},{1,0},{2,3},{3,2},{4,5},{5,4},{6,7},{7,6},{8,9},{9,8},{10,11... | collective-permute-start | bytes 983048 | tf_op jit(solution)/shard_map/ppermute | solution.py:423
  21.3 16.7 %collective-permute-start.5 = (bf16[64,2048]{1,0:T(8,128)(2,1)S(1)}, bf16[64,2048]{1,0:T(8,128)(2,1)S(1)}, u32[]{:S(2)}, u32[]{:S(2)}) collective-permute-start(bf16[64,2048]{1,0:T(8,128)(2,1)S(1)} %get-tuple-element.34), channel_id=1, source_target_pairs={{0,1},{1,0},{2,3},{3,2},{4,5},{5,4},{6,7},{7,6},{8,9},{9,8},{10,11... | collective-permute-start | bytes 786440 | tf_op jit(solution)/shard_map/ppermute | solution.py:423
  23.4 14.7 %collective-permute-start.4 = (bf16[32,2048]{1,0:T(8,128)(2,1)S(1)}, bf16[32,2048]{1,0:T(8,128)(2,1)S(1)}, u32[]{:S(2)}, u32[]{:S(2)}) collective-permute-start(bf16[32,2048]{1,0:T(8,128)(2,1)S(1)} %collective-permute-done.refs_0_.refs_3_), channel_id=1, source_target_pairs={{0,1},{1,0},{2,3},{3,2},{4,5},{5,4},{6,7},{7,6},{8,9},{9,8},{10,11... | collective-permute-start | bytes 393224 | tf_op jit(solution)/shard_map/ppermute | solution.py:423
  38.4 27.7 %collective-permute-start.7 = (bf16[144,2048]{1,0:T(8,128)(2,1)S(1)}, bf16[144,2048]{1,0:T(8,128)(2,1)S(1)}, u32[]{:S(2)}, u32[]{:S(2)}) collective-permute-start(bf16[144,2048]{1,0:T(8,128)(2,1)S(1)} %get-tuple-element.36), channel_id=1, source_target_pairs={{0,16},{1,17},{2,18},{3,19},{4,20},{5,21},{6,22},{7,23},{8,24},{9,... | collective-permute-start | bytes 1769480 | tf_op jit(solution)/shard_map/ppermute | solution.py:423
  38.9 12.1 %collective-permute-start.3 = (bf16[96,2048]{1,0:T(8,128)(2,1)S(1)}, bf16[96,2048]{1,0:T(8,128)(2,1)S(1)}, u32[]{:S(2)}, u32[]{:S(2)}) collective-permute-start(bf16[96,2048]{1,0:T(8,128)(2,1)S(1)} %collective-permute-done.2.refs_1_.refs_4_), channel_id=1, source_target_pairs={{0,1},{1,0},{2,3},{3,2},{4,5},{5,4},{6,7},{7,6},{8,9},{9,8},{10,11... | collective-permute-start | bytes 1179656 | tf_op jit(solution)/shard_map/ppermute | solution.py:423
  40.3 16.5 %collective-permute-start.8 = (bf16[96,2048]{1,0:T(8,128)(2,1)S(1)}, bf16[96,2048]{1,0:T(8,128)(2,1)S(1)}, u32[]{:S(2)}, u32[]{:S(2)}) collective-permute-start(bf16[96,2048]{1,0:T(8,128)(2,1)S(1)} %get-tuple-element.37.refs_1_), channel_id=1, source_target_pairs={{0,1},{1,0},{2,3},{3,2},{4,5},{5,4},{6,7},{7,6},{8,9},{9,8},{10,11... | collective-permute-start | bytes 1179656 | tf_op jit(solution)/shard_map/ppermute | solution.py:423
  50.9 17.1 %copy-start.3 = (bf16[96,2048]{1,0:T(8,128)(2,1)S(1)}, bf16[96,2048]{1,0:T(8,128)(2,1)}, u32[]{:S(2)}) copy-start(bf16[96,2048]{1,0:T(8,128)(2,1)} %get-tuple-element.31.refs_2_) | copy-start | bytes 1179652
  50.9 17.1 %copy-start.4 = (bf16[32,2048]{1,0:T(8,128)(2,1)S(1)}, bf16[32,2048]{1,0:T(8,128)(2,1)}, u32[]{:S(2)}) copy-start(bf16[32,2048]{1,0:T(8,128)(2,1)} %get-tuple-element.30.refs_0_) | copy-start | bytes 393220
  66.4 14.9 %collective-permute-start.9 = (bf16[144,2048]{1,0:T(8,128)(2,1)S(1)}, bf16[144,2048]{1,0:T(8,128)(2,1)S(1)}, u32[]{:S(2)}, u32[]{:S(2)}) collective-permute-start(bf16[144,2048]{1,0:T(8,128)(2,1)S(1)} %get-tuple-element.38.refs_0_), channel_id=1, source_target_pairs={{0,1},{1,0},{2,3},{3,2},{4,5},{5,4},{6,7},{7,6},{8,9},{9,8},{10,11... | collective-permute-start | bytes 1769480 | tf_op jit(solution)/shard_map/ppermute | solution.py:423
  68.0 20.5 %collective-permute-start.13 = (s16[1360,128]{1,0:T(8,128)(2,1)S(1)}, s16[1360,128]{1,0:T(8,128)(2,1)S(1)}, u32[]{:S(2)}, u32[]{:S(2)}) collective-permute-start(s16[1360,128]{1,0:T(8,128)(2,1)S(1)} %get-tuple-element.45), channel_id=1, source_target_pairs={{0,16},{1,17},{2,18},{3,19},{4,20},{5,21},{6,22},{7,23},{8,24},{9,... | collective-permute-start | bytes 1044488 | tf_op jit(solution)/shard_map/ppermute | solution.py:423
  81.3 7.3 %copy-start.5 = (s32[2,6]{1,0:T(2,128)S(1)}, s32[2,6]{1,0:T(2,128)}, u32[]{:S(2)}) copy-start(s32[2,6]{1,0:T(2,128)} %keep.3) | copy-start | bytes 148
  86.3 20.8 %collective-permute-start.10 = (s16[1744,128]{1,0:T(8,128)(2,1)S(1)}, s16[1744,128]{1,0:T(8,128)(2,1)S(1)}, u32[]{:S(2)}, u32[]{:S(2)}) collective-permute-start(s16[1744,128]{1,0:T(8,128)(2,1)S(1)} %get-tuple-element.40), channel_id=1, source_target_pairs={{0,16},{1,17},{2,18},{3,19},{4,20},{5,21},{6,22},{7,23},{8,24},{9,... | collective-permute-start | bytes 1339400 | tf_op jit(solution)/shard_map/ppermute | solution.py:423
  86.4 14.2 %collective-permute-start.12 = (bf16[80,2048]{1,0:T(8,128)(2,1)S(1)}, bf16[80,2048]{1,0:T(8,128)(2,1)S(1)}, u32[]{:S(2)}, u32[]{:S(2)}) collective-permute-start(bf16[80,2048]{1,0:T(8,128)(2,1)S(1)} %get-tuple-element.42), channel_id=1, source_target_pairs={{0,1},{1,0},{2,3},{3,2},{4,5},{5,4},{6,7},{7,6},{8,9},{9,8},{10,11... | collective-permute-start | bytes 983048 | tf_op jit(solution)/shard_map/ppermute | solution.py:423
  88.2 12.4 %collective-permute-start.11 = (bf16[64,2048]{1,0:T(8,128)(2,1)S(1)}, bf16[64,2048]{1,0:T(8,128)(2,1)S(1)}, u32[]{:S(2)}, u32[]{:S(2)}) collective-permute-start(bf16[64,2048]{1,0:T(8,128)(2,1)S(1)} %get-tuple-element.41), channel_id=1, source_target_pairs={{0,1},{1,0},{2,3},{3,2},{4,5},{5,4},{6,7},{7,6},{8,9},{9,8},{10,11... | collective-permute-start | bytes 786440 | tf_op jit(solution)/shard_map/ppermute | solution.py:423
  88.5 16.8 %collective-permute-start.14 = (bf16[64,2048]{1,0:T(8,128)(2,1)S(1)}, bf16[64,2048]{1,0:T(8,128)(2,1)S(1)}, u32[]{:S(2)}, u32[]{:S(2)}) collective-permute-start(bf16[64,2048]{1,0:T(8,128)(2,1)S(1)} %handed_on.3), channel_id=1, source_target_pairs={{0,2},{1,3},{2,0},{3,1},{4,6},{5,7},{6,4},{7,5},{8,10},{9,11},{10,... | collective-permute-start | bytes 786440 | tf_op jit(solution)/shard_map/ppermute | solution.py:423
  (1 other events, 1.0 us)

commit v15 on v14

--- a/solution.py
+++ b/solution.py
@@ -404,7 +404,7 @@
     diag = (half == lax.axis_index("col")).astype(jnp.int32).reshape(1)
     place = (row_index % group).astype(jnp.int32).reshape(1)
     direct = all_rows // 16
-    split = all_rows * 7 // 16
+    split = all_rows // 2
     wide = 256
 
     def device(h, q, c):

time: 109 us -> 107 us (0.982)
  transfers between devices with their start and end apart: 15 -> 15, of which waited for: 8 -> 10; matrix products, arithmetic and copies ran while one was open for 0% -> 0% of each run, Pallas kernels for 26% -> 26%
where the time goes in v15:
time: 107 us
  waiting for transfers between devices  57.5 us (54%)
  Pallas kernels  32.5 us (30%)
  starting transfers between devices  14.7 us (14%)
  local copies, waits for them, and re-layouts  1.22 us (1%)
    ppermute x15, waiting for transfers between devices, move(): return lax.ppermute(values, ('row', 'col'), pairs)  57.5 us
    ppermute x15, starting transfers between devices, move(): return lax.ppermute(values, ('row', 'col'), pairs)  14.7 us
    pallas_call x2, Pallas kernels, partial_products(): pl.pallas_call(functools.partial(partial_kernel, one, other, len(arrays),...  9.43 us
    pallas_call x2, Pallas kernels, local_products(): pl.pallas_call(functools.partial(local_kernel, one, other), grid=(columns...  8.44 us
    pallas_call x1, Pallas kernels, masked_right(): pl.pallas_call(right_kernel, grid=(depth // tall,), in_specs=[SM(), SM(),...  6.98 us
    pallas_call x2, Pallas kernels, masked_chunks(): pl.pallas_call(functools.partial(chunk_kernel, spans, int(stacked), panel...  3.88 us
    pallas_call x2, Pallas kernels, finished(): pl.pallas_call(functools.partial(finish_kernel, start, [cut for _, *cut i...  2.84 us
  transfers between devices with their start and end apart: 15, of which 10 were waited for; matrix products, arithmetic and copies ran while one was open for 0% of the time, Pallas kernels for 26%

profile of v15, /device:TPU:0, one launch (start us, length us, event | category | flops | bytes accessed | tf_op | source)
XLA Modules:
  0.0 106.8 jit_solution(11308190655927500818)
XLA Ops:
  0.7 2.3 %left_chunks.2 = (bf16[32,2048]{1,0:T(8,128)(2,1)}, bf16[112,2048]{1,0:T(8,128)(2,1)}, bf16[112,2048]{1,0:T(8,128)(2,1)}) custom-call(s32[1]{0:T(128)} %bitcast.1.refs_0_, s32[2,128]{1,0:T(2,128)} %refs_1_.3, s32[2,128]{1,0:T(2,128)} %refs_2_.3, bf16[256,16384]{1,0:T(8,128)(2,1)} %refs_3_.3, bf16[256,16384]{1,0:T(8,128)(2,1)} %refs_4_.3), custom_call_target="tpu_custom_call" | custom-call | bytes 32768 | tf_op jit(solution)/shard_map/left_chunks/pallas_call | solution.py:80
  3.0 3.0 %collective-permute-start.1 = (bf16[112,2048]{1,0:T(8,128)(2,1)}, bf16[112,2048]{1,0:T(8,128)(2,1)S(1)}, u32[]{:S(2)}, u32[]{:S(2)}) collective-permute-start(bf16[112,2048]{1,0:T(8,128)(2,1)} %get-tuple-element.31.refs_2_), channel_id=1, source_target_pairs={{0,1},{1,0},{2,3},{3,2},{4,5},{5,4},{6,7},{7,6},{8,9},{9,8},{10,11... | collective-permute-start | bytes 1376264 | tf_op jit(solution)/shard_map/ppermute | solution.py:423
  7.1 1.5 %left_chunks.3 = (bf16[128,2048]{1,0:T(8,128)(2,1)S(1)}, bf16[128,2048]{1,0:T(8,128)(2,1)S(1)}) custom-call(s32[1]{0:T(128)} %bitcast.1.refs_0_, s32[2,128]{1,0:T(2,128)S(1)} %copy-done.7, s32[2,128]{1,0:T(2,128)S(1)} %copy-done.8, bf16[256,16384]{1,0:T(8,128)(2,1)} %refs_3_.3, bf16[256,16384]{1,0:T(8,128)(2,1)} %refs_4_.3, bf16[112,2048]{1,0:T(8,128)(2,1)S(1)} %copy-done.2), custom_call_target="tpu_custom_call" | custom-call | bytes 32768 | tf_op jit(solution)/shard_map/left_chunks/pallas_call | solution.py:80
  8.9 7.0 %right_panels.1 = (bf16[2048,768]{1,0:T(8,128)(2,1)S(1)}, bf16[2048,768]{1,0:T(8,128)(2,1)}) custom-call(s32[16,6]{1,0:T(8,128)S(1)} %copy.13.mask0, s32[16,6]{1,0:T(8,128)S(1)} %copy.14.mask1, bf16[2048,768]{1,0:T(8,128)(2,1)} %x0.1, bf16[2048,768]{1,0:T(8,128)(2,1)} %x1.1, bf16[128,2048]{1,0:T(8,128)(2,1)S(1)} %get-tuple-element.27.rest_0_.refs_4_.refs_2_.refs_3_.refs_0_), custom_call_target="tpu_custom_call" | custom-call | bytes 196608 | tf_op jit(solution)/shard_map/right_panels/pallas_call | solution.py:178
  15.9 3.1 %collective-permute-done.refs_0_.refs_3_ = bf16[32,2048]{1,0:T(8,128)(2,1)S(1)} collective-permute-done((bf16[32,2048]{1,0:T(8,128)(2,1)}, bf16[32,2048]{1,0:T(8,128)(2,1)S(1)}, u32[]{:S(2)}, u32[]{:S(2)}) %collective-permute-start) | collective-permute-done | bytes 131104 | tf_op jit(solution)/shard_map/ppermute | solution.py:423
  19.3 3.5 %collective-permute-start.2 = (bf16[112,2048]{1,0:T(8,128)(2,1)S(1)}, bf16[112,2048]{1,0:T(8,128)(2,1)S(1)}, u32[]{:S(2)}, u32[]{:S(2)}) collective-permute-start(bf16[112,2048]{1,0:T(8,128)(2,1)S(1)} %get-tuple-element.33), channel_id=1, source_target_pairs={{0,16},{1,17},{2,18},{3,19},{4,20},{5,21},{6,22},{7,23},{8,24},{9,... | collective-permute-start | bytes 1376264 | tf_op jit(solution)/shard_map/ppermute | solution.py:423
  22.8 2.0 %collective-permute-start.6 = (bf16[64,2048]{1,0:T(8,128)(2,1)S(1)}, bf16[64,2048]{1,0:T(8,128)(2,1)S(1)}, u32[]{:S(2)}, u32[]{:S(2)}) collective-permute-start(bf16[64,2048]{1,0:T(8,128)(2,1)S(1)} %get-tuple-element.35), channel_id=1, source_target_pairs={{0,1},{1,0},{2,3},{3,2},{4,5},{5,4},{6,7},{7,6},{8,9},{9,8},{10,11... | collective-permute-start | bytes 786440 | tf_op jit(solution)/shard_map/ppermute | solution.py:423
  24.9 13.2 %collective-permute-done.4.refs_3_.refs_0_ = bf16[32,2048]{1,0:T(8,128)(2,1)S(1)} collective-permute-done((bf16[32,2048]{1,0:T(8,128)(2,1)S(1)}, bf16[32,2048]{1,0:T(8,128)(2,1)S(1)}, u32[]{:S(2)}, u32[]{:S(2)}) %collective-permute-start.4) | collective-permute-done | bytes 131104 | tf_op jit(solution)/shard_map/ppermute | solution.py:423
  38.2 4.2 %collective-permute-done.2.refs_1_.refs_4_ = bf16[112,2048]{1,0:T(8,128)(2,1)S(1)} collective-permute-done((bf16[112,2048]{1,0:T(8,128)(2,1)S(1)}, bf16[112,2048]{1,0:T(8,128)(2,1)S(1)}, u32[]{:S(2)}, u32[]{:S(2)}) %collective-permute-start.2) | collective-permute-done | bytes 458784 | tf_op jit(solution)/shard_map/ppermute | solution.py:423
  42.7 1.6 %collective-permute-start.3 = (bf16[112,2048]{1,0:T(8,128)(2,1)S(1)}, bf16[112,2048]{1,0:T(8,128)(2,1)S(1)}, u32[]{:S(2)}, u32[]{:S(2)}) collective-permute-start(bf16[112,2048]{1,0:T(8,128)(2,1)S(1)} %collective-permute-done.2.refs_1_.refs_4_), channel_id=1, source_target_pairs={{0,1},{1,0},{2,3},{3,2},{4,5},{5,4},{6,7},{7,6},{8,9},{9,8},{10,11... | collective-permute-start | bytes 1376264 | tf_op jit(solution)/shard_map/ppermute | solution.py:423
  44.8 11.4 %collective-permute-done.3.refs_2_ = bf16[112,2048]{1,0:T(8,128)(2,1)S(1)} collective-permute-done((bf16[112,2048]{1,0:T(8,128)(2,1)S(1)}, bf16[112,2048]{1,0:T(8,128)(2,1)S(1)}, u32[]{:S(2)}, u32[]{:S(2)}) %collective-permute-start.3) | collective-permute-done | bytes 458784 | tf_op jit(solution)/shard_map/ppermute | solution.py:423
  56.3 4.7 %partial_products.2.refs_0_ = s16[1552,128]{1,0:T(8,128)(2,1)S(1)} custom-call(s32[1]{0:T(128)} %bitcast.diag, bf16[2048,768]{1,0:T(8,128)(2,1)S(1)} %get-tuple-element.28.refs_1_.right0, bf16[2048,768]{1,0:T(8,128)(2,1)} %get-tuple-element.29.right1, bf16[32,2048]{1,0:T(8,128)(2,1)S(1)} %collective-permute-done.refs_0_.refs_3_, ...), custom_call_target="tpu_custom_call" | custom-call | flops 18874368 | bytes 114688 | tf_op jit(solution)/shard_map/partial_products/pallas_call | solution.py:314
  60.9 3.1 %collective-permute-done.8.refs_2_.refs_4_ = bf16[112,2048]{1,0:T(8,128)(2,1)S(1)} collective-permute-done((bf16[112,2048]{1,0:T(8,128)(2,1)S(1)}, bf16[112,2048]{1,0:T(8,128)(2,1)S(1)}, u32[]{:S(2)}, u32[]{:S(2)}) %collective-permute-start.8) | collective-permute-done | bytes 458784 | tf_op jit(solution)/shard_map/ppermute | solution.py:423
  64.0 3.6 %collective-permute-done.7.refs_1_ = bf16[128,2048]{1,0:T(8,128)(2,1)S(1)} collective-permute-done((bf16[128,2048]{1,0:T(8,128)(2,1)S(1)}, bf16[128,2048]{1,0:T(8,128)(2,1)S(1)}, u32[]{:S(2)}, u32[]{:S(2)}) %collective-permute-start.7) | collective-permute-done | bytes 524320 | tf_op jit(solution)/shard_map/ppermute | solution.py:423
  67.9 1.6 %collective-permute-start.9 = (bf16[128,2048]{1,0:T(8,128)(2,1)S(1)}, bf16[128,2048]{1,0:T(8,128)(2,1)S(1)}, u32[]{:S(2)}, u32[]{:S(2)}) collective-permute-start(bf16[128,2048]{1,0:T(8,128)(2,1)S(1)} %get-tuple-element.38.refs_0_), channel_id=1, source_target_pairs={{0,1},{1,0},{2,3},{3,2},{4,5},{5,4},{6,7},{7,6},{8,9},{9,8},{10,11... | collective-permute-start | bytes 1572872 | tf_op jit(solution)/shard_map/ppermute | solution.py:423
  69.5 4.5 %own_products.2 = (f32[128,768]{1,0:T(8,128)S(1)}, f32[128,768]{1,0:T(8,128)S(1)}) custom-call(s32[1]{0:T(128)} %bitcast.diag, bf16[2048,768]{1,0:T(8,128)(2,1)S(1)} %get-tuple-element.28.refs_1_.right0, bf16[2048,768]{1,0:T(8,128)(2,1)} %get-tuple-element.29.right1, bf16[32,2048]{1,0:T(8,128)(2,1)S(1)} %copy-done.5, ...), custom_call_target="tpu_custom_call" | custom-call | flops 18874368 | bytes 131072 | tf_op jit(solution)/shard_map/own_products/pallas_call | solution.py:249
  74.1 7.5 %collective-permute-done.9.refs_1_ = bf16[128,2048]{1,0:T(8,128)(2,1)S(1)} collective-permute-done((bf16[128,2048]{1,0:T(8,128)(2,1)S(1)}, bf16[128,2048]{1,0:T(8,128)(2,1)S(1)}, u32[]{:S(2)}, u32[]{:S(2)}) %collective-permute-start.9) | collective-permute-done | bytes 524320 | tf_op jit(solution)/shard_map/ppermute | solution.py:423
  81.6 4.8 %partial_products.3 = (s16[1552,128]{1,0:T(8,128)(2,1)S(1)}, bf16[64,2048]{1,0:T(8,128)(2,1)S(1)}, bf16[64,2048]{1,0:T(8,128)(2,1)S(1)}, bf16[64,2048]{1,0:T(8,128)(2,1)S(1)}) custom-call(s32[1]{0:T(128)} %bitcast.diag, bf16[2048,768]{1,0:T(8,128)(2,1)} %copy-done, bf16[2048,768]{1,0:T(8,128)(2,1)} %get-tuple-element.29.right1, ...), custom_call_target="tpu_custom_call" | custom-call | flops 18874368 | bytes 114688 | tf_op jit(solution)/shard_map/partial_products/pallas_call | solution.py:314
  86.4 1.8 %collective-permute-start.11 = (bf16[64,2048]{1,0:T(8,128)(2,1)S(1)}, bf16[64,2048]{1,0:T(8,128)(2,1)S(1)}, u32[]{:S(2)}, u32[]{:S(2)}) collective-permute-start(bf16[64,2048]{1,0:T(8,128)(2,1)S(1)} %get-tuple-element.41), channel_id=1, source_target_pairs={{0,1},{1,0},{2,3},{3,2},{4,5},{5,4},{6,7},{7,6},{8,9},{9,8},{10,11... | collective-permute-start | bytes 786440 | tf_op jit(solution)/shard_map/ppermute | solution.py:423
  88.5 8.4 %collective-permute-done.13.coded.refs_1_ = s16[1552,128]{1,0:T(8,128)(2,1)S(1)} collective-permute-done((s16[1552,128]{1,0:T(8,128)(2,1)S(1)}, s16[1552,128]{1,0:T(8,128)(2,1)S(1)}, u32[]{:S(2)}, u32[]{:S(2)}) %collective-permute-start.13) | collective-permute-done | bytes 397344 | tf_op jit(solution)/shard_map/ppermute | solution.py:423
  97.0 1.4 %finish.2 = (bf16[256,768]{1,0:T(8,128)(2,1)}, bf16[256,768]{1,0:T(8,128)(2,1)}) custom-call(s32[2,6]{1,0:T(2,128)S(1)} %copy-done.6, s16[1552,128]{1,0:T(8,128)(2,1)S(1)} %collective-permute-done.13.coded.refs_1_, f32[128,768]{1,0:T(8,128)S(1)} %get-tuple-element.39.refs_5_.square, f32[128,768]{1,0:T(8,128)S(1)} %get-tuple-element.46.tangent), custom_call_target="tpu_custom_call" | custom-call | bytes 24576 | tf_op jit(solution)/shard_map/finish/pallas_call | solution.py:378
  99.4 3.9 %own_products.3 = (f32[128,768]{1,0:T(8,128)S(1)}, f32[128,768]{1,0:T(8,128)S(1)}) custom-call(s32[1]{0:T(128)} %bitcast.diag, bf16[2048,768]{1,0:T(8,128)(2,1)S(1)} %copy-done.1, bf16[2048,768]{1,0:T(8,128)(2,1)} %get-tuple-element.29.right1, bf16[128,2048]{1,0:T(8,128)(2,1)S(1)} %get-tuple-element.27.rest_0_.refs_4_.refs_2_.refs_3_.refs_0_, ...), custom_call_target="tpu_custom_call" | custom-call | flops 18874368 | bytes 131072 | tf_op jit(solution)/shard_map/own_products/pallas_call | solution.py:249
  103.3 2.0 %collective-permute-done.10.coded = s16[1552,128]{1,0:T(8,128)(2,1)S(1)} collective-permute-done((s16[1552,128]{1,0:T(8,128)(2,1)S(1)}, s16[1552,128]{1,0:T(8,128)(2,1)S(1)}, u32[]{:S(2)}, u32[]{:S(2)}) %collective-permute-start.10) | collective-permute-done | bytes 397344 | tf_op jit(solution)/shard_map/ppermute | solution.py:423
  105.3 1.4 %finish.3 = (bf16[256,768]{1,0:T(8,128)(2,1)}, bf16[256,768]{1,0:T(8,128)(2,1)}) custom-call(s32[2,6]{1,0:T(2,128)S(1)} %copy-done.6, s16[1552,128]{1,0:T(8,128)(2,1)S(1)} %collective-permute-done.10.coded, f32[128,768]{1,0:T(8,128)S(1)} %get-tuple-element.43.square, ...), custom_call_target="tpu_custom_call", output_to_operand_aliasing={{0}: (4, {}), {1}: (5, {})} | custom-call | bytes 24576 | tf_op jit(solution)/shard_map/finish/pallas_call | solution.py:378
  (43 shorter events, 4.2 us)
Async XLA Ops:
  0.6 5.5 %copy-start.7 = (s32[2,128]{1,0:T(2,128)S(1)}, s32[2,128]{1,0:T(2,128)}, u32[]{:S(2)}) copy-start(s32[2,128]{1,0:T(2,128)} %refs_1_.3) | copy-start | bytes 3076
  0.7 5.5 %copy-start.8 = (s32[2,128]{1,0:T(2,128)S(1)}, s32[2,128]{1,0:T(2,128)}, u32[]{:S(2)}) copy-start(s32[2,128]{1,0:T(2,128)} %refs_2_.3) | copy-start | bytes 3076
  3.0 15.9 %collective-permute-start.1 = (bf16[112,2048]{1,0:T(8,128)(2,1)}, bf16[112,2048]{1,0:T(8,128)(2,1)S(1)}, u32[]{:S(2)}, u32[]{:S(2)}) collective-permute-start(bf16[112,2048]{1,0:T(8,128)(2,1)} %get-tuple-element.31.refs_2_), channel_id=1, source_target_pairs={{0,1},{1,0},{2,3},{3,2},{4,5},{5,4},{6,7},{7,6},{8,9},{9,8},{10,11... | collective-permute-start | bytes 1376264 | tf_op jit(solution)/shard_map/ppermute | solution.py:423
  6.0 12.9 %collective-permute-start = (bf16[32,2048]{1,0:T(8,128)(2,1)}, bf16[32,2048]{1,0:T(8,128)(2,1)S(1)}, u32[]{:S(2)}, u32[]{:S(2)}) collective-permute-start(bf16[32,2048]{1,0:T(8,128)(2,1)} %get-tuple-element.30.refs_0_), channel_id=1, source_target_pairs={{0,1},{1,17},{2,3},{3,19},{4,5},{5,21},{6,7},{7,23},{8,9},{9,25},{... | collective-permute-start | bytes 393224 | tf_op jit(solution)/shard_map/ppermute | solution.py:423
  7.1 1.6 %copy-start.10 = (s32[16,6]{0,1:T(8,128)S(1)}, s32[16,6]{0,1:T(8,128)}, u32[]{:S(2)}) copy-start(s32[16,6]{0,1:T(8,128)} %param.16) | copy-start | bytes 1156
  8.9 10.1 %copy-start.3 = (bf16[112,2048]{1,0:T(8,128)(2,1)S(1)}, bf16[112,2048]{1,0:T(8,128)(2,1)}, u32[]{:S(2)}) copy-start(bf16[112,2048]{1,0:T(8,128)(2,1)} %get-tuple-element.26.refs_5_.refs_3_) | copy-start | bytes 1376260
  15.8 53.7 %copy-start = (bf16[2048,768]{1,0:T(8,128)(2,1)}, bf16[2048,768]{1,0:T(8,128)(2,1)S(1)}, u32[]{:S(2)}) copy-start(bf16[2048,768]{1,0:T(8,128)(2,1)S(1)} %get-tuple-element.28.refs_1_.right0) | copy-start | bytes 9437188
  19.3 23.0 %collective-permute-start.2 = (bf16[112,2048]{1,0:T(8,128)(2,1)S(1)}, bf16[112,2048]{1,0:T(8,128)(2,1)S(1)}, u32[]{:S(2)}, u32[]{:S(2)}) collective-permute-start(bf16[112,2048]{1,0:T(8,128)(2,1)S(1)} %get-tuple-element.33), channel_id=1, source_target_pairs={{0,16},{1,17},{2,18},{3,19},{4,20},{5,21},{6,22},{7,23},{8,24},{9,... | collective-permute-start | bytes 1376264 | tf_op jit(solution)/shard_map/ppermute | solution.py:423
  22.8 15.3 %collective-permute-start.5 = (bf16[64,2048]{1,0:T(8,128)(2,1)S(1)}, bf16[64,2048]{1,0:T(8,128)(2,1)S(1)}, u32[]{:S(2)}, u32[]{:S(2)}) collective-permute-start(bf16[64,2048]{1,0:T(8,128)(2,1)S(1)} %get-tuple-element.34), channel_id=1, source_target_pairs={{0,1},{1,0},{2,3},{3,2},{4,5},{5,4},{6,7},{7,6},{8,9},{9,8},{10,11... | collective-permute-start | bytes 786440 | tf_op jit(solution)/shard_map/ppermute | solution.py:423
  22.8 15.3 %collective-permute-start.6 = (bf16[64,2048]{1,0:T(8,128)(2,1)S(1)}, bf16[64,2048]{1,0:T(8,128)(2,1)S(1)}, u32[]{:S(2)}, u32[]{:S(2)}) collective-permute-start(bf16[64,2048]{1,0:T(8,128)(2,1)S(1)} %get-tuple-element.35), channel_id=1, source_target_pairs={{0,1},{1,0},{2,3},{3,2},{4,5},{5,4},{6,7},{7,6},{8,9},{9,8},{10,11... | collective-permute-start | bytes 786440 | tf_op jit(solution)/shard_map/ppermute | solution.py:423
  24.9 13.3 %collective-permute-start.4 = (bf16[32,2048]{1,0:T(8,128)(2,1)S(1)}, bf16[32,2048]{1,0:T(8,128)(2,1)S(1)}, u32[]{:S(2)}, u32[]{:S(2)}) collective-permute-start(bf16[32,2048]{1,0:T(8,128)(2,1)S(1)} %collective-permute-done.refs_0_.refs_3_), channel_id=1, source_target_pairs={{0,1},{1,0},{2,3},{3,2},{4,5},{5,4},{6,7},{7,6},{8,9},{9,8},{10,11... | collective-permute-start | bytes 393224 | tf_op jit(solution)/shard_map/ppermute | solution.py:423
  42.7 25.0 %collective-permute-start.7 = (bf16[128,2048]{1,0:T(8,128)(2,1)S(1)}, bf16[128,2048]{1,0:T(8,128)(2,1)S(1)}, u32[]{:S(2)}, u32[]{:S(2)}) collective-permute-start(bf16[128,2048]{1,0:T(8,128)(2,1)S(1)} %get-tuple-element.36), channel_id=1, source_target_pairs={{0,16},{1,17},{2,18},{3,19},{4,20},{5,21},{6,22},{7,23},{8,24},{9,... | collective-permute-start | bytes 1572872 | tf_op jit(solution)/shard_map/ppermute | solution.py:423
  42.7 13.5 %collective-permute-start.3 = (bf16[112,2048]{1,0:T(8,128)(2,1)S(1)}, bf16[112,2048]{1,0:T(8,128)(2,1)S(1)}, u32[]{:S(2)}, u32[]{:S(2)}) collective-permute-start(bf16[112,2048]{1,0:T(8,128)(2,1)S(1)} %collective-permute-done.2.refs_1_.refs_4_), channel_id=1, source_target_pairs={{0,1},{1,0},{2,3},{3,2},{4,5},{5,4},{6,7},{7,6},{8,9},{9,8},{10,11... | collective-permute-start | bytes 1376264 | tf_op jit(solution)/shard_map/ppermute | solution.py:423
  44.4 19.6 %collective-permute-start.8 = (bf16[112,2048]{1,0:T(8,128)(2,1)S(1)}, bf16[112,2048]{1,0:T(8,128)(2,1)S(1)}, u32[]{:S(2)}, u32[]{:S(2)}) collective-permute-start(bf16[112,2048]{1,0:T(8,128)(2,1)S(1)} %get-tuple-element.37.refs_1_), channel_id=1, source_target_pairs={{0,1},{1,0},{2,3},{3,2},{4,5},{5,4},{6,7},{7,6},{8,9},{9,8},{10,11... | collective-permute-start | bytes 1376264 | tf_op jit(solution)/shard_map/ppermute | solution.py:423
  56.3 13.3 %copy-start.4 = (bf16[112,2048]{1,0:T(8,128)(2,1)S(1)}, bf16[112,2048]{1,0:T(8,128)(2,1)}, u32[]{:S(2)}) copy-start(bf16[112,2048]{1,0:T(8,128)(2,1)} %get-tuple-element.31.refs_2_) | copy-start | bytes 1376260
  56.3 13.3 %copy-start.5 = (bf16[32,2048]{1,0:T(8,128)(2,1)S(1)}, bf16[32,2048]{1,0:T(8,128)(2,1)}, u32[]{:S(2)}) copy-start(bf16[32,2048]{1,0:T(8,128)(2,1)} %get-tuple-element.30.refs_0_) | copy-start | bytes 393220
  67.9 13.7 %collective-permute-start.9 = (bf16[128,2048]{1,0:T(8,128)(2,1)S(1)}, bf16[128,2048]{1,0:T(8,128)(2,1)S(1)}, u32[]{:S(2)}, u32[]{:S(2)}) collective-permute-start(bf16[128,2048]{1,0:T(8,128)(2,1)S(1)} %get-tuple-element.38.refs_0_), channel_id=1, source_target_pairs={{0,1},{1,0},{2,3},{3,2},{4,5},{5,4},{6,7},{7,6},{8,9},{9,8},{10,11... | collective-permute-start | bytes 1572872 | tf_op jit(solution)/shard_map/ppermute | solution.py:423
  69.5 27.4 %collective-permute-start.13 = (s16[1552,128]{1,0:T(8,128)(2,1)S(1)}, s16[1552,128]{1,0:T(8,128)(2,1)S(1)}, u32[]{:S(2)}, u32[]{:S(2)}) collective-permute-start(s16[1552,128]{1,0:T(8,128)(2,1)S(1)} %get-tuple-element.45), channel_id=1, source_target_pairs={{0,16},{1,17},{2,18},{3,19},{4,20},{5,21},{6,22},{7,23},{8,24},{9,... | collective-permute-start | bytes 1191944 | tf_op jit(solution)/shard_map/ppermute | solution.py:423
  81.5 15.5 %copy-start.6 = (s32[2,6]{1,0:T(2,128)S(1)}, s32[2,6]{1,0:T(2,128)}, u32[]{:S(2)}) copy-start(s32[2,6]{1,0:T(2,128)} %keep.3) | copy-start | bytes 148
  81.5 17.8 %copy-start.1 = (bf16[2048,768]{1,0:T(8,128)(2,1)S(1)}, bf16[2048,768]{1,0:T(8,128)(2,1)}, u32[]{:S(2)}) copy-start(bf16[2048,768]{1,0:T(8,128)(2,1)} %copy-done) | copy-start | bytes 9437188
  86.3 19.0 %collective-permute-start.10 = (s16[1552,128]{1,0:T(8,128)(2,1)S(1)}, s16[1552,128]{1,0:T(8,128)(2,1)S(1)}, u32[]{:S(2)}, u32[]{:S(2)}) collective-permute-start(s16[1552,128]{1,0:T(8,128)(2,1)S(1)} %get-tuple-element.40), channel_id=1, source_target_pairs={{0,16},{1,17},{2,18},{3,19},{4,20},{5,21},{6,22},{7,23},{8,24},{9,... | collective-permute-start | bytes 1191944 | tf_op jit(solution)/shard_map/ppermute | solution.py:423
  86.4 12.1 %collective-permute-start.11 = (bf16[64,2048]{1,0:T(8,128)(2,1)S(1)}, bf16[64,2048]{1,0:T(8,128)(2,1)S(1)}, u32[]{:S(2)}, u32[]{:S(2)}) collective-permute-start(bf16[64,2048]{1,0:T(8,128)(2,1)S(1)} %get-tuple-element.41), channel_id=1, source_target_pairs={{0,1},{1,0},{2,3},{3,2},{4,5},{5,4},{6,7},{7,6},{8,9},{9,8},{10,11... | collective-permute-start | bytes 786440 | tf_op jit(solution)/shard_map/ppermute | solution.py:423
  88.2 11.2 %collective-permute-start.12 = (bf16[64,2048]{1,0:T(8,128)(2,1)S(1)}, bf16[64,2048]{1,0:T(8,128)(2,1)S(1)}, u32[]{:S(2)}, u32[]{:S(2)}) collective-permute-start(bf16[64,2048]{1,0:T(8,128)(2,1)S(1)} %get-tuple-element.42), channel_id=1, source_target_pairs={{0,1},{1,0},{2,3},{3,2},{4,5},{5,4},{6,7},{7,6},{8,9},{9,8},{10,11... | collective-permute-start | bytes 786440 | tf_op jit(solution)/shard_map/ppermute | solution.py:423
  97.0 6.4 %collective-permute-start.14 = (bf16[64,2048]{1,0:T(8,128)(2,1)S(1)}, bf16[64,2048]{1,0:T(8,128)(2,1)S(1)}, u32[]{:S(2)}, u32[]{:S(2)}) collective-permute-start(bf16[64,2048]{1,0:T(8,128)(2,1)S(1)} %handed_on.3), channel_id=1, source_target_pairs={{0,2},{1,3},{2,0},{3,1},{4,6},{5,7},{6,4},{7,5},{8,10},{9,11},{10,... | collective-permute-start | bytes 786440 | tf_op jit(solution)/shard_map/ppermute | solution.py:423
  (2 other events, 2.6 us)

commit v16 on v8

--- a/solution.py
+++ b/solution.py
@@ -441,7 +441,7 @@
     near1 = move(send, over_z)
     passed2 = move(b2, over_y)
     far0 = move(near0, over_y)
-    send, a1 = chosen(diag, passed2, a2, (a1,), (far0,))
+    send, a1 = chosen(diag, passed2, a2, (a1,), (far0, near1))
     near2 = move(send, over_z)
     got1 = move(a1, over_y)
     far1 = move(near1, over_y)

time: 106 us -> 109 us (1.028)
  the two profiles are of different devices: /device:TPU:24 before, /device:TPU:0 now
where the time goes in v16:
time: 109 us; the launch traced here: 108 us
  waiting for transfers between devices  62.4 us (57%)
  Pallas kernels  31.8 us (29%)
  starting transfers between devices  11.9 us (11%)
  local copies, waits for them, and re-layouts  1.2 us (1%)
    ppermute x12, waiting for transfers between devices, move(): return lax.ppermute(values, ('row', 'col'), pairs)  62.4 us
    ppermute x12, starting transfers between devices, move(): return lax.ppermute(values, ('row', 'col'), pairs)  11.9 us
    pallas_call x2, Pallas kernels, partial_products(): pl.pallas_call(functools.partial(partial_kernel, one, other, len(arrays),...  8.77 us
    pallas_call x2, Pallas kernels, local_products(): pl.pallas_call(functools.partial(local_kernel, one, other), grid=(columns...  8.41 us
    pallas_call x1, Pallas kernels, masked_right(): pl.pallas_call(right_kernel, grid=(depth // tall,), in_specs=[SM(), SM(),...  6.99 us
    pallas_call x2, Pallas kernels, masked_chunks(): pl.pallas_call(functools.partial(chunk_kernel, spans, int(stacked), panel...  3.9 us
    pallas_call x2, Pallas kernels, finished(): pl.pallas_call(functools.partial(finish_kernel, start, many), in_specs=[S...  2.83 us
  transfers between devices with their start and end apart: 12, of which 10 were waited for; matrix products, arithmetic and copies ran while one was open for 0% of the time, Pallas kernels for 25%

profile of v16, /device:TPU:0, one launch (start us, length us, event | category | flops | bytes accessed | tf_op | source)
XLA Modules:
  0.0 108.2 jit_solution(4592390659350815109)
XLA Ops:
  0.7 2.4 %left_chunks.2 = (bf16[64,2048]{1,0:T(8,128)(2,1)}, bf16[96,2048]{1,0:T(8,128)(2,1)}, bf16[96,2048]{1,0:T(8,128)(2,1)}) custom-call(s32[1]{0:T(128)} %bitcast.1.refs_0_, s32[2,128]{1,0:T(2,128)} %refs_1_.3, s32[2,128]{1,0:T(2,128)} %refs_2_.3, bf16[256,16384]{1,0:T(8,128)(2,1)} %refs_3_.3, bf16[256,16384]{1,0:T(8,128)(2,1)} %refs_4_.3), custom_call_target="tpu_custom_call" | custom-call | bytes 32768 | tf_op jit(solution)/shard_map/left_chunks/pallas_call | solution.py:80
  3.1 3.0 %collective-permute-start.1 = (bf16[96,2048]{1,0:T(8,128)(2,1)}, bf16[96,2048]{1,0:T(8,128)(2,1)S(1)}, u32[]{:S(2)}, u32[]{:S(2)}) collective-permute-start(bf16[96,2048]{1,0:T(8,128)(2,1)} %get-tuple-element.28.refs_2_), channel_id=1, source_target_pairs={{0,1},{1,0},{2,3},{3,2},{4,5},{5,4},{6,7},{7,6},{8,9},{9,8},{10,11... | collective-permute-start | bytes 1179656 | tf_op jit(solution)/shard_map/ppermute | solution.py:419
  7.3 1.5 %left_chunks.3 = (bf16[128,2048]{1,0:T(8,128)(2,1)S(1)}, bf16[128,2048]{1,0:T(8,128)(2,1)S(1)}) custom-call(s32[1]{0:T(128)} %bitcast.1.refs_0_, s32[2,128]{1,0:T(2,128)S(1)} %copy-done.5, s32[2,128]{1,0:T(2,128)S(1)} %copy-done.6, bf16[256,16384]{1,0:T(8,128)(2,1)} %refs_3_.3, bf16[256,16384]{1,0:T(8,128)(2,1)} %refs_4_.3, bf16[96,2048]{1,0:T(8,128)(2,1)S(1)} %copy-done), custom_call_target="tpu_custom_call" | custom-call | bytes 32768 | tf_op jit(solution)/shard_map/left_chunks/pallas_call | solution.py:80
  8.9 7.0 %right_panels.1 = (bf16[2048,768]{1,0:T(8,128)(2,1)S(1)}, bf16[2048,768]{1,0:T(8,128)(2,1)}) custom-call(s32[16,6]{1,0:T(8,128)S(1)} %copy.13.mask0, s32[16,6]{1,0:T(8,128)S(1)} %copy.14.mask1, bf16[2048,768]{1,0:T(8,128)(2,1)} %x0.1, bf16[2048,768]{1,0:T(8,128)(2,1)} %x1.1, bf16[128,2048]{1,0:T(8,128)(2,1)S(1)} %get-tuple-element.24.rest_0_.refs_3_.refs_2_), custom_call_target="tpu_custom_call" | custom-call | bytes 196608 | tf_op jit(solution)/shard_map/right_panels/pallas_call | solution.py:179
  15.9 4.7 %collective-permute-done.refs_0_.refs_3_ = bf16[64,2048]{1,0:T(8,128)(2,1)S(1)} collective-permute-done((bf16[64,2048]{1,0:T(8,128)(2,1)}, bf16[64,2048]{1,0:T(8,128)(2,1)S(1)}, u32[]{:S(2)}, u32[]{:S(2)}) %collective-permute-start) | collective-permute-done | bytes 262176 | tf_op jit(solution)/shard_map/ppermute | solution.py:419
  20.9 2.3 %collective-permute-start.5 = (bf16[128,2048]{1,0:T(8,128)(2,1)S(1)}, bf16[128,2048]{1,0:T(8,128)(2,1)S(1)}, u32[]{:S(2)}, u32[]{:S(2)}) collective-permute-start(bf16[128,2048]{1,0:T(8,128)(2,1)S(1)} %get-tuple-element.31.refs_1_), channel_id=1, source_target_pairs={{0,1},{1,0},{2,3},{3,2},{4,5},{5,4},{6,7},{7,6},{8,9},{9,8},{10,11... | collective-permute-start | bytes 1572872 | tf_op jit(solution)/shard_map/ppermute | solution.py:419
  23.1 1.1 %collective-permute-start.2 = (bf16[96,2048]{1,0:T(8,128)(2,1)S(1)}, bf16[96,2048]{1,0:T(8,128)(2,1)S(1)}, u32[]{:S(2)}, u32[]{:S(2)}) collective-permute-start(bf16[96,2048]{1,0:T(8,128)(2,1)S(1)} %get-tuple-element.30), channel_id=1, source_target_pairs={{0,16},{1,17},{2,18},{3,19},{4,20},{5,21},{6,22},{7,23},{8,24},{9,... | collective-permute-start | bytes 1179656 | tf_op jit(solution)/shard_map/ppermute | solution.py:419
  24.3 1.9 %collective-permute-start.4 = (bf16[64,2048]{1,0:T(8,128)(2,1)S(1)}, bf16[64,2048]{1,0:T(8,128)(2,1)S(1)}, u32[]{:S(2)}, u32[]{:S(2)}) collective-permute-start(bf16[64,2048]{1,0:T(8,128)(2,1)S(1)} %collective-permute-done.refs_0_.refs_3_), channel_id=1, source_target_pairs={{0,1},{1,0},{2,3},{3,2},{4,5},{5,4},{6,7},{7,6},{8,9},{9,8},{10,11... | collective-permute-start | bytes 786440 | tf_op jit(solution)/shard_map/ppermute | solution.py:419
  26.2 13.6 %collective-permute-done.4.refs_3_.refs_0_ = bf16[64,2048]{1,0:T(8,128)(2,1)S(1)} collective-permute-done((bf16[64,2048]{1,0:T(8,128)(2,1)S(1)}, bf16[64,2048]{1,0:T(8,128)(2,1)S(1)}, u32[]{:S(2)}, u32[]{:S(2)}) %collective-permute-start.4) | collective-permute-done | bytes 262176 | tf_op jit(solution)/shard_map/ppermute | solution.py:419
  39.8 2.4 %collective-permute-done.2.refs_1_ = bf16[96,2048]{1,0:T(8,128)(2,1)S(1)} collective-permute-done((bf16[96,2048]{1,0:T(8,128)(2,1)S(1)}, bf16[96,2048]{1,0:T(8,128)(2,1)S(1)}, u32[]{:S(2)}, u32[]{:S(2)}) %collective-permute-start.2) | collective-permute-done | bytes 393248 | tf_op jit(solution)/shard_map/ppermute | solution.py:419
  43.2 1.7 %collective-permute-start.7 = (bf16[96,2048]{1,0:T(8,128)(2,1)S(1)}, bf16[96,2048]{1,0:T(8,128)(2,1)S(1)}, u32[]{:S(2)}, u32[]{:S(2)}) collective-permute-start(bf16[96,2048]{1,0:T(8,128)(2,1)S(1)} %get-tuple-element.33.refs_1_), channel_id=1, source_target_pairs={{0,1},{1,0},{2,3},{3,2},{4,5},{5,4},{6,7},{7,6},{8,9},{9,8},{10,11... | collective-permute-start | bytes 1179656 | tf_op jit(solution)/shard_map/ppermute | solution.py:419
  44.9 10.0 %collective-permute-done.3.refs_2_ = bf16[96,2048]{1,0:T(8,128)(2,1)S(1)} collective-permute-done((bf16[96,2048]{1,0:T(8,128)(2,1)S(1)}, bf16[96,2048]{1,0:T(8,128)(2,1)S(1)}, u32[]{:S(2)}, u32[]{:S(2)}) %collective-permute-start.3) | collective-permute-done | bytes 393248 | tf_op jit(solution)/shard_map/ppermute | solution.py:419
  55.0 4.7 %partial_products.2.refs_0_ = s16[1552,128]{1,0:T(8,128)(2,1)S(1)} custom-call(s32[1]{0:T(128)} %bitcast.diag, bf16[2048,768]{1,0:T(8,128)(2,1)S(1)} %get-tuple-element.25.refs_1_.right0, bf16[2048,768]{1,0:T(8,128)(2,1)} %get-tuple-element.26.right1, bf16[64,2048]{1,0:T(8,128)(2,1)S(1)} %collective-permute-done.refs_0_.refs_3_, ...), custom_call_target="tpu_custom_call" | custom-call | flops 18874368 | bytes 114688 | tf_op jit(solution)/shard_map/partial_products/pallas_call | solution.py:314
  59.7 1.2 %collective-permute-done.7.refs_2_.refs_4_ = bf16[96,2048]{1,0:T(8,128)(2,1)S(1)} collective-permute-done((bf16[96,2048]{1,0:T(8,128)(2,1)S(1)}, bf16[96,2048]{1,0:T(8,128)(2,1)S(1)}, u32[]{:S(2)}, u32[]{:S(2)}) %collective-permute-start.7) | collective-permute-done | bytes 393248 | tf_op jit(solution)/shard_map/ppermute | solution.py:419
  60.9 6.4 %collective-permute-done.6.refs_1_ = bf16[128,2048]{1,0:T(8,128)(2,1)S(1)} collective-permute-done((bf16[128,2048]{1,0:T(8,128)(2,1)S(1)}, bf16[128,2048]{1,0:T(8,128)(2,1)S(1)}, u32[]{:S(2)}, u32[]{:S(2)}) %collective-permute-start.6) | collective-permute-done | bytes 524320 | tf_op jit(solution)/shard_map/ppermute | solution.py:419
  68.1 4.5 %own_products.2 = (f32[128,768]{1,0:T(8,128)S(1)}, f32[128,768]{1,0:T(8,128)S(1)}) custom-call(s32[1]{0:T(128)} %bitcast.diag, bf16[2048,768]{1,0:T(8,128)(2,1)S(1)} %get-tuple-element.25.refs_1_.right0, bf16[2048,768]{1,0:T(8,128)(2,1)} %get-tuple-element.26.right1, bf16[64,2048]{1,0:T(8,128)(2,1)S(1)} %copy-done.3, ...), custom_call_target="tpu_custom_call" | custom-call | flops 18874368 | bytes 131072 | tf_op jit(solution)/shard_map/own_products/pallas_call | solution.py:250
  72.7 8.0 %collective-permute-done.8.refs_1_ = bf16[128,2048]{1,0:T(8,128)(2,1)S(1)} collective-permute-done((bf16[128,2048]{1,0:T(8,128)(2,1)S(1)}, bf16[128,2048]{1,0:T(8,128)(2,1)S(1)}, u32[]{:S(2)}, u32[]{:S(2)}) %collective-permute-start.8) | collective-permute-done | bytes 524320 | tf_op jit(solution)/shard_map/ppermute | solution.py:419
  80.7 4.0 %partial_products.3 = (s16[1552,128]{1,0:T(8,128)(2,1)S(1)}, bf16[128,2048]{1,0:T(8,128)(2,1)S(1)}) custom-call(s32[1]{0:T(128)} %bitcast.diag, bf16[2048,768]{1,0:T(8,128)(2,1)S(1)} %get-tuple-element.25.refs_1_.right0, bf16[2048,768]{1,0:T(8,128)(2,1)} %get-tuple-element.26.right1, bf16[128,2048]{1,0:T(8,128)(2,1)S(1)} %get-tuple-element.34.refs_0_, ...), custom_call_target="tpu_custom_call" | custom-call | flops 18874368 | bytes 114688 | tf_op jit(solution)/shard_map/partial_products/pallas_call | solution.py:314
  85.1 1.9 %collective-permute-done.9.refs_1_.coded = s16[1552,128]{1,0:T(8,128)(2,1)S(1)} collective-permute-done((s16[1552,128]{1,0:T(8,128)(2,1)S(1)}, s16[1552,128]{1,0:T(8,128)(2,1)S(1)}, u32[]{:S(2)}, u32[]{:S(2)}) %collective-permute-start.9) | collective-permute-done | bytes 397344 | tf_op jit(solution)/shard_map/ppermute | solution.py:419
  87.2 1.4 %finish.2 = (bf16[256,768]{1,0:T(8,128)(2,1)}, bf16[256,768]{1,0:T(8,128)(2,1)}) custom-call(s32[2,6]{1,0:T(2,128)S(1)} %copy-done.4, s16[1552,128]{1,0:T(8,128)(2,1)S(1)} %collective-permute-done.9.refs_1_.coded, f32[128,768]{1,0:T(8,128)S(1)} %get-tuple-element.35.refs_3_.square, f32[128,768]{1,0:T(8,128)S(1)} %get-tuple-element.41.tangent), custom_call_target="tpu_custom_call" | custom-call | bytes 24576 | tf_op jit(solution)/shard_map/finish/pallas_call | solution.py:376
  88.7 8.2 %collective-permute-done.11.refs_2_ = bf16[128,2048]{1,0:T(8,128)(2,1)S(1)} collective-permute-done((bf16[128,2048]{1,0:T(8,128)(2,1)S(1)}, bf16[128,2048]{1,0:T(8,128)(2,1)S(1)}, u32[]{:S(2)}, u32[]{:S(2)}) %collective-permute-start.11) | collective-permute-done | bytes 524320 | tf_op jit(solution)/shard_map/ppermute | solution.py:419
  96.9 3.9 %own_products.3 = (f32[128,768]{1,0:T(8,128)S(1)}, f32[128,768]{1,0:T(8,128)S(1)}) custom-call(s32[1]{0:T(128)} %bitcast.diag, bf16[2048,768]{1,0:T(8,128)(2,1)S(1)} %get-tuple-element.25.refs_1_.right0, bf16[2048,768]{1,0:T(8,128)(2,1)} %get-tuple-element.26.right1, bf16[128,2048]{1,0:T(8,128)(2,1)S(1)} %get-tuple-element.38.refs_0_, ...), custom_call_target="tpu_custom_call" | custom-call | flops 18874368 | bytes 131072 | tf_op jit(solution)/shard_map/own_products/pallas_call | solution.py:250
  100.8 6.0 %collective-permute-done.10.coded = s16[1552,128]{1,0:T(8,128)(2,1)S(1)} collective-permute-done((s16[1552,128]{1,0:T(8,128)(2,1)S(1)}, s16[1552,128]{1,0:T(8,128)(2,1)S(1)}, u32[]{:S(2)}, u32[]{:S(2)}) %collective-permute-start.10) | collective-permute-done | bytes 397344 | tf_op jit(solution)/shard_map/ppermute | solution.py:419
  106.8 1.4 %finish.3 = (bf16[256,768]{1,0:T(8,128)(2,1)}, bf16[256,768]{1,0:T(8,128)(2,1)}) custom-call(s32[2,6]{1,0:T(2,128)S(1)} %copy-done.4, s16[1552,128]{1,0:T(8,128)(2,1)S(1)} %collective-permute-done.10.coded, f32[128,768]{1,0:T(8,128)S(1)} %get-tuple-element.39.square, ...), custom_call_target="tpu_custom_call", output_to_operand_aliasing={{0}: (4, {}), {1}: (5, {})} | custom-call | bytes 24576 | tf_op jit(solution)/shard_map/finish/pallas_call | solution.py:376
  (33 shorter events, 4.0 us)
Async XLA Ops:
  0.6 5.5 %copy-start.7 = (s32[16,6]{0,1:T(8,128)S(1)}, s32[16,6]{0,1:T(8,128)}, u32[]{:S(2)}) copy-start(s32[16,6]{0,1:T(8,128)} %param.15) | copy-start | bytes 1156
  0.7 5.6 %copy-start.8 = (s32[16,6]{0,1:T(8,128)S(1)}, s32[16,6]{0,1:T(8,128)}, u32[]{:S(2)}) copy-start(s32[16,6]{0,1:T(8,128)} %param.16) | copy-start | bytes 1156
  0.7 5.7 %copy-start.5 = (s32[2,128]{1,0:T(2,128)S(1)}, s32[2,128]{1,0:T(2,128)}, u32[]{:S(2)}) copy-start(s32[2,128]{1,0:T(2,128)} %refs_1_.3) | copy-start | bytes 3076
  0.7 5.7 %copy-start.6 = (s32[2,128]{1,0:T(2,128)S(1)}, s32[2,128]{1,0:T(2,128)}, u32[]{:S(2)}) copy-start(s32[2,128]{1,0:T(2,128)} %refs_2_.3) | copy-start | bytes 3076
  3.1 17.5 %collective-permute-start.1 = (bf16[96,2048]{1,0:T(8,128)(2,1)}, bf16[96,2048]{1,0:T(8,128)(2,1)S(1)}, u32[]{:S(2)}, u32[]{:S(2)}) collective-permute-start(bf16[96,2048]{1,0:T(8,128)(2,1)} %get-tuple-element.28.refs_2_), channel_id=1, source_target_pairs={{0,1},{1,0},{2,3},{3,2},{4,5},{5,4},{6,7},{7,6},{8,9},{9,8},{10,11... | collective-permute-start | bytes 1179656 | tf_op jit(solution)/shard_map/ppermute | solution.py:419
  6.1 14.5 %collective-permute-start = (bf16[64,2048]{1,0:T(8,128)(2,1)}, bf16[64,2048]{1,0:T(8,128)(2,1)S(1)}, u32[]{:S(2)}, u32[]{:S(2)}) collective-permute-start(bf16[64,2048]{1,0:T(8,128)(2,1)} %get-tuple-element.27.refs_0_), channel_id=1, source_target_pairs={{0,1},{1,17},{2,3},{3,19},{4,5},{5,21},{6,7},{7,23},{8,9},{9,25},{... | collective-permute-start | bytes 786440 | tf_op jit(solution)/shard_map/ppermute | solution.py:419
  6.3 1.0 copy-start
  8.9 11.7 %copy-start.1 = (bf16[96,2048]{1,0:T(8,128)(2,1)S(1)}, bf16[96,2048]{1,0:T(8,128)(2,1)}, u32[]{:S(2)}) copy-start(bf16[96,2048]{1,0:T(8,128)(2,1)} %get-tuple-element.23.refs_5_.refs_3_.refs_4_) | copy-start | bytes 1179652
  20.9 21.3 %collective-permute-start.5 = (bf16[128,2048]{1,0:T(8,128)(2,1)S(1)}, bf16[128,2048]{1,0:T(8,128)(2,1)S(1)}, u32[]{:S(2)}, u32[]{:S(2)}) collective-permute-start(bf16[128,2048]{1,0:T(8,128)(2,1)S(1)} %get-tuple-element.31.refs_1_), channel_id=1, source_target_pairs={{0,1},{1,0},{2,3},{3,2},{4,5},{5,4},{6,7},{7,6},{8,9},{9,8},{10,11... | collective-permute-start | bytes 1572872 | tf_op jit(solution)/shard_map/ppermute | solution.py:419
  23.1 19.0 %collective-permute-start.2 = (bf16[96,2048]{1,0:T(8,128)(2,1)S(1)}, bf16[96,2048]{1,0:T(8,128)(2,1)S(1)}, u32[]{:S(2)}, u32[]{:S(2)}) collective-permute-start(bf16[96,2048]{1,0:T(8,128)(2,1)S(1)} %get-tuple-element.30), channel_id=1, source_target_pairs={{0,16},{1,17},{2,18},{3,19},{4,20},{5,21},{6,22},{7,23},{8,24},{9,... | collective-permute-start | bytes 1179656 | tf_op jit(solution)/shard_map/ppermute | solution.py:419
  24.3 15.5 %collective-permute-start.4 = (bf16[64,2048]{1,0:T(8,128)(2,1)S(1)}, bf16[64,2048]{1,0:T(8,128)(2,1)S(1)}, u32[]{:S(2)}, u32[]{:S(2)}) collective-permute-start(bf16[64,2048]{1,0:T(8,128)(2,1)S(1)} %collective-permute-done.refs_0_.refs_3_), channel_id=1, source_target_pairs={{0,1},{1,0},{2,3},{3,2},{4,5},{5,4},{6,7},{7,6},{8,9},{9,8},{10,11... | collective-permute-start | bytes 786440 | tf_op jit(solution)/shard_map/ppermute | solution.py:419
  42.4 25.0 %collective-permute-start.6 = (bf16[128,2048]{1,0:T(8,128)(2,1)S(1)}, bf16[128,2048]{1,0:T(8,128)(2,1)S(1)}, u32[]{:S(2)}, u32[]{:S(2)}) collective-permute-start(bf16[128,2048]{1,0:T(8,128)(2,1)S(1)} %get-tuple-element.32), channel_id=1, source_target_pairs={{0,16},{1,17},{2,18},{3,19},{4,20},{5,21},{6,22},{7,23},{8,24},{9,... | collective-permute-start | bytes 1572872 | tf_op jit(solution)/shard_map/ppermute | solution.py:419
  42.9 12.1 %collective-permute-start.3 = (bf16[96,2048]{1,0:T(8,128)(2,1)S(1)}, bf16[96,2048]{1,0:T(8,128)(2,1)S(1)}, u32[]{:S(2)}, u32[]{:S(2)}) collective-permute-start(bf16[96,2048]{1,0:T(8,128)(2,1)S(1)} %collective-permute-done.2.refs_1_), channel_id=1, source_target_pairs={{0,1},{1,0},{2,3},{3,2},{4,5},{5,4},{6,7},{7,6},{8,9},{9,8},{10,11... | collective-permute-start | bytes 1179656 | tf_op jit(solution)/shard_map/ppermute | solution.py:419
  43.2 17.7 %collective-permute-start.7 = (bf16[96,2048]{1,0:T(8,128)(2,1)S(1)}, bf16[96,2048]{1,0:T(8,128)(2,1)S(1)}, u32[]{:S(2)}, u32[]{:S(2)}) collective-permute-start(bf16[96,2048]{1,0:T(8,128)(2,1)S(1)} %get-tuple-element.33.refs_1_), channel_id=1, source_target_pairs={{0,1},{1,0},{2,3},{3,2},{4,5},{5,4},{6,7},{7,6},{8,9},{9,8},{10,11... | collective-permute-start | bytes 1179656 | tf_op jit(solution)/shard_map/ppermute | solution.py:419
  55.0 13.2 %copy-start.2 = (bf16[96,2048]{1,0:T(8,128)(2,1)S(1)}, bf16[96,2048]{1,0:T(8,128)(2,1)}, u32[]{:S(2)}) copy-start(bf16[96,2048]{1,0:T(8,128)(2,1)} %get-tuple-element.28.refs_2_) | copy-start | bytes 1179652
  55.0 13.2 %copy-start.3 = (bf16[64,2048]{1,0:T(8,128)(2,1)S(1)}, bf16[64,2048]{1,0:T(8,128)(2,1)}, u32[]{:S(2)}) copy-start(bf16[64,2048]{1,0:T(8,128)(2,1)} %get-tuple-element.27.refs_0_) | copy-start | bytes 786436
  67.6 13.1 %collective-permute-start.8 = (bf16[128,2048]{1,0:T(8,128)(2,1)S(1)}, bf16[128,2048]{1,0:T(8,128)(2,1)S(1)}, u32[]{:S(2)}, u32[]{:S(2)}) collective-permute-start(bf16[128,2048]{1,0:T(8,128)(2,1)S(1)} %get-tuple-element.34.refs_0_), channel_id=1, source_target_pairs={{0,1},{1,0},{2,3},{3,2},{4,5},{5,4},{6,7},{7,6},{8,9},{9,8},{10,11... | collective-permute-start | bytes 1572872 | tf_op jit(solution)/shard_map/ppermute | solution.py:419
  68.1 18.8 %collective-permute-start.9 = (s16[1552,128]{1,0:T(8,128)(2,1)S(1)}, s16[1552,128]{1,0:T(8,128)(2,1)S(1)}, u32[]{:S(2)}, u32[]{:S(2)}) collective-permute-start(s16[1552,128]{1,0:T(8,128)(2,1)S(1)} %get-tuple-element.37), channel_id=1, source_target_pairs={{0,16},{1,17},{2,18},{3,19},{4,20},{5,21},{6,22},{7,23},{8,24},{9,... | collective-permute-start | bytes 1191944 | tf_op jit(solution)/shard_map/ppermute | solution.py:419
  80.7 6.5 %copy-start.4 = (s32[2,6]{1,0:T(2,128)S(1)}, s32[2,6]{1,0:T(2,128)}, u32[]{:S(2)}) copy-start(s32[2,6]{1,0:T(2,128)} %keep.3) | copy-start | bytes 148
  84.7 12.1 %collective-permute-start.11 = (bf16[128,2048]{1,0:T(8,128)(2,1)S(1)}, bf16[128,2048]{1,0:T(8,128)(2,1)S(1)}, u32[]{:S(2)}, u32[]{:S(2)}) collective-permute-start(bf16[128,2048]{1,0:T(8,128)(2,1)S(1)} %get-tuple-element.38.refs_0_), channel_id=1, source_target_pairs={{0,1},{1,0},{2,3},{3,2},{4,5},{5,4},{6,7},{7,6},{8,9},{9,8},{10,11... | collective-permute-start | bytes 1572872 | tf_op jit(solution)/shard_map/ppermute | solution.py:419
  87.1 19.7 %collective-permute-start.10 = (s16[1552,128]{1,0:T(8,128)(2,1)S(1)}, s16[1552,128]{1,0:T(8,128)(2,1)S(1)}, u32[]{:S(2)}, u32[]{:S(2)}) collective-permute-start(s16[1552,128]{1,0:T(8,128)(2,1)S(1)} %handed_on.3), channel_id=1, source_target_pairs={{0,16},{1,17},{2,18},{3,19},{4,20},{5,21},{6,22},{7,23},{8,24},{9,... | collective-permute-start | bytes 1191944 | tf_op jit(solution)/shard_map/ppermute | solution.py:419
